TPU v7x, 32 devices: a whole 2x2x4 slice. The times are simulated.
32 devices in a mesh: row: 4 (over z), col: 8 (over y, x, core).
Axes of the slice: x: 2, y: 2, z: 4, core: 2. Of those that a mesh axis runs over, the one named last changes fastest.
Arguments:
- tile_data: bfloat16 [4, 8, 32, 256, 256], P('row', 'col'), may hold values from -0.125 to 0.125
- tile_row_block: int32 [4, 8, 32], P('row', 'col'), may hold values from 0 to 63
- tile_column_block: int32 [4, 8, 32], P('row', 'col'), may hold values from 0 to 63
- tile_count: int32 [4, 8], P('row', 'col'), may hold values from 1 to 32, as said below
- saved_primal: float32 [3, 131072], P(None, 'col'), may hold values from 0 to 1
- saved_dual: float32 [3, 65536], P(None, 'row'), may hold values from 0 to 1
- primal_mask: int32 [3, 131072], P(None, 'col'), may hold values 0 or 1
- dual_mask: int32 [3, 65536], P(None, 'row'), may hold values 0 or 1
- cost_vector: float32 [131072], P('col'), may hold values from -6 to 6
- demand: float32 [65536], P('row'), may hold values from -6 to 6
- upper_bound: float32 [131072], P('col'), may hold values from 0.5 to 1.5
- step_sizes: float32 [2], replicated, may hold values from 0.2 to 0.4
- primal_cotangent: float32 [131072], P('col'), may hold values from -6 to 6
- dual_cotangent: float32 [65536], P('row'), may hold values from -6 to 6
Outputs:
- primal_adjoint: float32 [131072], P('col')
- dual_adjoint: float32 [65536], P(('row', 'col'))
- step_gradients: float32 [2], replicated
Inputs may be any that keep to these rules, and one draw needn't show every extreme that they name: `tile_count`: block positions may repeat, and tiles at one position add; slots at and beyond a device's count are ignored. In every index of row some device has 32 live slots.
All inputs are finite; a program needn't handle non-finite values. No bound on the sum of `primal_mask` or of `dual_mask` on one device may be relied on, other than what follows from the above.
Results may differ from a plain program's by a relative error of at most 0.00071.
Values may be sent and summed in bfloat16 or wider, within the bound.
No kernel may reach another device: no remote copies, remote signals or barrier semaphores. Data moves between devices by JAX's collectives and lax.ppermute only.
A program may use at most 64 MiB of HBM per device.

v0:
```python
import math

import jax
import jax.numpy as jnp
from jax import lax
from jax.sharding import PartitionSpec as P


def block_terms(tile_part, in_part, out_part, live_part, vectors, out_blocks, transpose):
    tile_width = tile_part.shape[-1]
    blocks = vectors.reshape(vectors.shape[0], -1, tile_width)
    picked = jnp.take(blocks, in_part, axis=1)
    einsum_form = "sij,bsi->bsj" if transpose else "sij,bsj->bsi"
    products = jnp.einsum(einsum_form, tile_part, picked, preferred_element_type=jnp.float32)
    products = products * live_part[None, :, None]
    selector = (out_part[:, None] == jnp.arange(out_blocks, dtype=jnp.int32)[None, :]).astype(
        jnp.float32
    )
    summed = jnp.einsum("sn,bsi->bni", selector, products, precision=lax.Precision.HIGHEST)
    return summed.reshape(vectors.shape[0], out_blocks * tile_width)


def tile_apply(tile_stack, in_index, out_index, live_count, vectors, out_blocks, transpose):
    slot_count = tile_stack.shape[0]
    live_slots = (jnp.arange(slot_count, dtype=jnp.int32) < live_count).astype(jnp.float32)
    return block_terms(tile_stack, in_index, out_index, live_slots, vectors, out_blocks, transpose)


def local(
    tile_data,
    tile_row_block,
    tile_column_block,
    tile_count,
    saved_primal,
    saved_dual,
    primal_mask,
    dual_mask,
    cost_vector,
    demand,
    upper_bound,
    step_sizes,
    primal_cotangent,
    dual_cotangent,
):
    slot_count = tile_data.shape[2]
    tile_width = tile_data.shape[-1]
    tile_stack = tile_data.reshape(slot_count, tile_width, tile_width)
    row_blocks = tile_row_block.reshape(slot_count)
    column_blocks = tile_column_block.reshape(slot_count)
    live_count = tile_count.reshape(())
    iterations = saved_primal.shape[0]
    row_length = saved_dual.shape[1]
    column_length = saved_primal.shape[1]
    share_rows = row_length // lax.axis_size("col")
    share_start = lax.axis_index("col") * share_rows
    column_part = column_length // lax.axis_size("row")
    column_start = lax.axis_index("row") * column_part
    tau = step_sizes[0]
    sigma = step_sizes[1]

    def forward(vectors):
        return tile_apply(
            tile_stack,
            column_blocks,
            row_blocks,
            live_count,
            vectors,
            row_length // tile_width,
            False,
        )

    def backward(vectors):
        return tile_apply(
            tile_stack,
            row_blocks,
            column_blocks,
            live_count,
            vectors,
            column_length // tile_width,
            True,
        )

    def row_share(array):
        return lax.dynamic_slice_in_dim(array, share_start, share_rows, array.ndim - 1)

    def column_share(array):
        return lax.dynamic_slice_in_dim(array, column_start, column_part, array.ndim - 1)

    dual_partial = backward(saved_dual.astype(jnp.bfloat16))
    reduced = cost_vector[None, :] - lax.psum(dual_partial, "row")
    half = jnp.clip(saved_primal - tau * reduced, 0.0, upper_bound[None, :])
    extrapolated = (2.0 * half - saved_primal).astype(jnp.bfloat16)
    masks_x = primal_mask.astype(jnp.float32)
    adjoint_x = primal_cotangent
    partial_value = forward(extrapolated)
    residual_share = row_share(demand[None, :] - lax.psum(partial_value, "col"))
    adjoint_y = dual_cotangent
    masks_y = dual_mask.astype(jnp.float32)
    anchor_x = jnp.zeros_like(adjoint_x)
    anchor_y = jnp.zeros_like(adjoint_y)
    tau_sum = jnp.zeros((), jnp.float32)
    sigma_sum = jnp.zeros((), jnp.float32)
    for step in reversed(range(iterations)):
        weight = (step + 1.0) / (step + 2.0)
        anchor_x = anchor_x + (1.0 - weight) * adjoint_x
        anchor_y = anchor_y + (1.0 - weight) * adjoint_y
        dual_term = masks_y[step] * weight * adjoint_y
        sigma_local = jnp.sum(row_share(dual_term) * residual_share[step])
        spread = dual_term.astype(jnp.bfloat16)
        back_partial = backward(spread[None, :])
        back = lax.psum(back_partial, "row")[0]
        primal_term = masks_x[step] * (weight * adjoint_x - 2.0 * sigma * back)
        tau_local = jnp.sum(-column_share(primal_term) * column_share(reduced[step]))
        primal_input = primal_term.astype(jnp.bfloat16)
        adjoint_x = primal_term + sigma * back
        image = forward(primal_input[None, :])
        image_rows = lax.psum(image, "col")[0]
        adjoint_y = dual_term + tau * image_rows
        tau_total, sigma_total = lax.psum((tau_local, sigma_local), ("row", "col"))
        tau_sum = tau_sum + tau_total
        sigma_sum = sigma_sum + sigma_total
    primal_adjoint = adjoint_x + anchor_x
    dual_adjoint = row_share(adjoint_y + anchor_y)
    total_columns = column_length * lax.axis_size("col")
    total_rows = row_length * lax.axis_size("row")
    gradients = jnp.stack([tau_sum / math.sqrt(total_columns), sigma_sum / math.sqrt(total_rows)])
    return (primal_adjoint, dual_adjoint, gradients)


def solution(mesh):
    placed = (
        P("row", "col", None, None, None),
        P("row", "col", None),
        P("row", "col", None),
        P("row", "col"),
        P(None, "col"),
        P(None, "row"),
        P(None, "col"),
        P(None, "row"),
        P("col"),
        P("row"),
        P("col"),
        P(),
        P("col"),
        P("row"),
    )
    return jax.shard_map(
        local,
        mesh=mesh,
        in_specs=placed,
        out_specs=(P("col"), P(("row", "col")), P()),
        check_vma=False,
    )
```

profile of v0, /device:TPU:0, one launch (start us, length us, event | category | flops | bytes accessed | tf_op | source)
XLA Modules:
  0.0 377.2 jit_solution(5014077306665207104)
XLA Ops:
  7.3 0.7 compare_select_fusion
  8.0 0.7 compare_and_fusion
  8.7 1.0 convert_element_type.25
  9.7 0.2 slice_multiply_fusion.2
  9.9 0.9 fusion.74
  11.4 0.6 gather_fusion
  12.0 0.1 fusion.45
  12.1 2.8 fusion.14
  15.0 0.3 convolution_bitcast_fusion.7
  15.3 0.7 copy.31
  16.0 0.6 fusion.78
  16.7 0.1 fusion.76
  17.5 35.3 %all-reduce.10.cloned.1.call-done = f32[1,16384]{1,0:T(1,128)} async-done(((f32[1,16384]{1,0:T(1,128)}), f32[1,16384]{1,0:T(1,128)}) %all-reduce.10.cloned.1.call-update) | async-done | bytes 65552 | tf_op jit(solution)/shard_map/psum | solution.py:111
  52.8 1.6 broadcast_multiply_fusion.5
  54.4 0.6 gather_fusion.1
  55.1 3.4 fusion.12
  58.5 0.3 convolution_bitcast_fusion.6
  58.8 0.7 copy.32
  59.7 0.6 gather_fusion.6
  60.3 51.6 %all-reduce.12.cloned.1.call-done = f32[1,16384]{1,0:T(1,128)} async-done(((f32[1,16384]{1,0:T(1,128)}), f32[1,16384]{1,0:T(1,128)}) %all-reduce.12.cloned.1.call-update) | async-done | bytes 65552 | tf_op jit(solution)/shard_map/psum | solution.py:117
  111.8 1.5 broadcast_multiply_fusion.2
  113.4 0.6 gather_fusion.2
  114.1 2.8 fusion.10
  117.0 0.3 convolution_bitcast_fusion.5
  117.3 0.7 copy.33
  118.1 2.9 fusion.2
  120.9 30.6 %all-reduce.14.cloned.1.call-done = f32[1,16384]{1,0:T(1,128)} async-done(((f32[1,16384]{1,0:T(1,128)}), f32[1,16384]{1,0:T(1,128)}) %all-reduce.14.cloned.1.call-update) | async-done | bytes 65552 | tf_op jit(solution)/shard_map/psum | solution.py:111
  151.5 1.6 broadcast_multiply_fusion.4
  153.1 0.6 gather_fusion.3
  153.8 3.4 fusion.8
  157.2 0.3 convolution_bitcast_fusion.4
  157.5 0.7 copy.34
  158.3 0.4 convolution_bitcast_fusion.1
  158.7 0.8 copy.37
  159.5 51.1 %all-reduce.16.cloned.1.call-done = f32[1,16384]{1,0:T(1,128)} async-done(((f32[1,16384]{1,0:T(1,128)}), f32[1,16384]{1,0:T(1,128)}) %all-reduce.16.cloned.1.call-update) | async-done | bytes 65552 | tf_op jit(solution)/shard_map/psum | solution.py:117
  210.6 1.5 broadcast_multiply_fusion.1
  212.2 0.6 gather_fusion.4
  212.9 2.8 fusion.6
  215.7 0.3 convolution_bitcast_fusion.3
  216.0 0.7 copy.35
  216.8 35.8 %all-reduce.20.cloned.1.call-done = (f32[1,16384]{1,0:T(1,128)}, f32[3,16384]{1,0:T(4,128)}) async-done(((f32[1,16384]{1,0:T(1,128)}, f32[3,16384]{1,0:T(4,128)}), (f32[1,16384]{1,0:T(1,128)}, f32[3,16384]{1,0:T(4,128)})) %all-reduce.20.cloned.1.call-update) | async-done | bytes 262160 | tf_op jit(solution)/shard_map/psum | solution.py:111
  252.6 1.8 subtract_convert_fusion
  254.4 0.1 fusion.75
  254.5 1.6 broadcast_multiply_fusion.3
  256.1 0.6 gather_fusion.7
  256.8 3.4 fusion
  260.1 0.4 convolution_bitcast_fusion
  260.5 0.8 copy.38
  261.4 0.7 multiply_reduce_fusion.1
  262.1 0.6 gather_fusion.5
  262.8 3.4 fusion.4
  266.1 0.3 convolution_bitcast_fusion.2
  266.5 0.7 copy.36
  267.2 0.6 multiply_reduce_fusion.2
  269.1 0.6 multiply_reduce_fusion
  270.3 50.9 %all-reduce.18.cloned.1.call-done = (f32[1,16384]{1,0:T(1,128)}, f32[3,16384]{1,0:T(4,128)}) async-done(((f32[1,16384]{1,0:T(1,128)}, f32[3,16384]{1,0:T(4,128)}), (f32[1,16384]{1,0:T(1,128)}, f32[3,16384]{1,0:T(4,128)})) %all-reduce.18.cloned.1.call-update) | async-done | bytes 262160 | tf_op jit(solution)/shard_map/psum | solution.py:117
  321.2 0.8 dynamic-slice_subtract_fusion
  322.0 0.6 multiply_reduce_fusion.4
  322.6 0.6 multiply_reduce_fusion.5
  323.2 1.5 broadcast_multiply_fusion
  326.1 1.9 multiply_reduce_fusion.3
  328.6 0.7 add_add_fusion
  329.3 39.2 %all-reduce = (f32[]{:T(128)}, f32[]{:T(128)}) all-reduce(f32[]{:T(128)S(6)} %add.120, f32[]{:T(128)S(6)} %add.118), channel_id=1, replica_groups=mesh['row'=4,'col'=8] {'row','col'}, use_global_device_ids=true, to_apply=%region_15.18 | all-reduce | flops 2 | bytes 16 | tf_op jit(solution)/shard_map/psum | solution.py:119
  369.8 0.6 pad_maximum_fusion
  (57 shorter events, 1.1 us)
Async XLA Ops:
  7.2 7.8 %copy-start.6 = (s32[1,1,32]{2,1,0:T(1,128)S(1)}, s32[1,1,32]{2,1,0:T(1,128)}, u32[]{:S(2)}) copy-start(s32[1,1,32]{2,1,0:T(1,128)} %param.20) | copy-start | bytes 388
  7.2 8.9 %copy-start.8 = (f32[2]{0:T(128)S(1)}, f32[2]{0:T(128)}, u32[]{:S(2)}) copy-start(f32[2]{0:T(128)} %param.29) | copy-start | bytes 28
  7.2 9.4 %copy-start.1 = (s32[3,16384]{1,0:T(4,128)S(1)}, s32[3,16384]{1,0:T(4,128)}, u32[]{:S(2)}) copy-start(s32[3,16384]{1,0:T(4,128)} %param.24) | copy-start | bytes 589828
  7.2 47.2 %copy-start.3 = (f32[16384]{0:T(1024)S(1)}, f32[16384]{0:T(1024)}, u32[]{:S(2)}) copy-start(f32[16384]{0:T(1024)} %param.30) | copy-start | bytes 196612
  7.2 45.6 %all-reduce.10.cloned.1.call-start = ((), (), s32[]{:S(2)}) async-start(), calls=%async_computation | async-start | bytes 131072 | tf_op jit(solution)/shard_map/psum | solution.py:111
  14.9 43.6 %copy-start.7 = (s32[1,1,32]{2,1,0:T(1,128)S(1)}, s32[1,1,32]{2,1,0:T(1,128)}, u32[]{:S(2)}) copy-start(s32[1,1,32]{2,1,0:T(1,128)} %param.19) | copy-start | bytes 388
  14.9 44.7 %copy-start = (f32[3,16384]{1,0:T(4,128)S(1)}, f32[3,16384]{1,0:T(4,128)}, u32[]{:S(2)}) copy-start(f32[3,16384]{1,0:T(4,128)} %param.23) | copy-start | bytes 589828
  16.0 95.9 %all-reduce.12.cloned.1.call-start = ((), (), s32[]{:S(2)}) async-start(), calls=%async_computation.1 | async-start | bytes 131072 | tf_op jit(solution)/shard_map/psum | solution.py:117
  59.5 92.0 %all-reduce.14.cloned.1.call-start = ((), (), s32[]{:S(2)}) async-start(), calls=%async_computation.2 | async-start | bytes 131072 | tf_op jit(solution)/shard_map/psum | solution.py:111
  118.0 92.6 %all-reduce.16.cloned.1.call-start = ((), (), s32[]{:S(2)}) async-start(), calls=%async_computation.3 | async-start | bytes 131072 | tf_op jit(solution)/shard_map/psum | solution.py:117
  157.2 95.4 %copy-start.2 = (f32[3,16384]{1,0:T(4,128)S(1)}, f32[3,16384]{1,0:T(4,128)}, u32[]{:S(2)}) copy-start(f32[3,16384]{1,0:T(4,128)} %param.22) | copy-start | bytes 589828
  157.2 95.4 %copy-start.4 = (f32[16384]{0:T(1024)S(1)}, f32[16384]{0:T(1024)}, u32[]{:S(2)}) copy-start(f32[16384]{0:T(1024)} %param.28) | copy-start | bytes 196612
  157.2 95.4 %copy-start.5 = (f32[16384]{0:T(1024)S(1)}, f32[16384]{0:T(1024)}, u32[]{:S(2)}) copy-start(f32[16384]{0:T(1024)} %param.26) | copy-start | bytes 196612
  158.2 94.3 %all-reduce.20.cloned.1.call-start = ((), (), s32[]{:S(2)}) async-start(), calls=%async_computation.5 | async-start | bytes 655360 | tf_op jit(solution)/shard_map/psum | solution.py:111
  216.7 104.5 %all-reduce.18.cloned.1.call-start = ((), (), s32[]{:S(2)}) async-start(), calls=%async_computation.4 | async-start | bytes 655360 | tf_op jit(solution)/shard_map/psum | solution.py:117
  260.1 61.1 %dynamic-slice-start = ((f32[16384]{0:T(1024)}, s32[]{:T(128)}), f32[2048]{0:T(1024)S(1)}, s32[]{:S(2)}) async-start(f32[16384]{0:T(1024)} %param.27, s32[]{:T(128)} %select_n.36), calls=%async_computation.6 | async-start | bytes 16896 | tf_op jit(solution)/shard_map/dynamic_slice | solution.py:84
Sparse Core Ops, SparseCore 0:
  16.1 36.6 all-reduce.9
  59.7 52.1 all-reduce.11
  118.1 33.3 all-reduce.13
  158.4 52.1 all-reduce.15
  216.9 35.6 all-reduce.19
  267.3 53.8 all-reduce.17
where the time goes:
time: 378 us; the launch traced here: 377 us
  waiting for transfers between devices  255 us (67%)
  blocking collectives  39.2 us (10%)
  matrix products  27.4 us (7%)
  other arithmetic  22.1 us (6%)
  between operations  20.9 us (6%)
  local copies, waits for them, and re-layouts  11.9 us (3%)
    psum x3, waiting for transfers between devices, local(): image_rows = lax.psum(image, 'col')[0]  154 us
    psum x3, waiting for transfers between devices, local(): back = lax.psum(back_partial, 'row')[0]  102 us
    psum x1, blocking collectives, local(): tau_total, sigma_total = lax.psum((tau_local, sigma_local), ('row', 'col'))  39.2 us
    dot_general x8, matrix products, block_terms(): jnp.einsum(einsum_form, tile_part, picked, preferred_element_type=jnp.flo...  24.9 us
  transfers between devices with their start and end apart: 6, of which 6 were waited for; matrix products, arithmetic and copies ran while one was open for 2% of the time, Pallas kernels for 0%

commit v1 on v0

v1 whole, which is shorter than its diff:
```python
import functools
import math

import jax
import jax.numpy as jnp
from jax import lax
from jax.experimental import pallas as pl
from jax.experimental.pallas import tpu as pltpu
from jax.sharding import PartitionSpec as P

LANES = 128
VMEM = pl.BlockSpec(memory_space=pltpu.VMEM)
SMEM = pl.BlockSpec(memory_space=pltpu.SMEM)
GRANT = 32 * 1024 * 1024


def accumulate(transpose, in_index, out_index, count, tiles, source, slot_of, total):
    slots, width, _ = tiles.shape
    per_block = width // LANES
    vectors = total.shape[0]
    total[...] = jnp.zeros_like(total)
    live_count = count[0, 0]
    rows = max(8, vectors)
    for slot in range(slots):
        start = slot_of(in_index[0, 0, slot] * per_block)
        place = out_index[0, 0, slot] * per_block
        live = (live_count > slot).astype(jnp.float32)
        halves = []
        for half in range(per_block):
            if vectors == 1:
                halves.append(source[0, pl.ds(start + half, 1), :])
            else:
                which = lax.broadcasted_iota(jnp.int32, (rows, LANES), 0)
                stacked = jnp.zeros((rows, LANES), jnp.float32)
                for vector in range(vectors):
                    line = source[vector, pl.ds(start + half, 1), :]
                    stacked = jnp.where(which == vector, line, stacked)
                halves.append(stacked)
        block = (jnp.concatenate(halves, axis=1) * live).astype(jnp.bfloat16)
        contract = ((1,), (0,)) if transpose else ((1,), (1,))
        product = lax.dot_general(
            block, tiles[slot], (contract, ((), ())), preferred_element_type=jnp.float32
        )
        for vector in range(vectors):
            for half in range(per_block):
                at = pl.ds(place + half, 1)
                total[vector, at, :] += product[
                    vector : vector + 1, half * LANES : (half + 1) * LANES
                ]


def apply_body(transpose, parts_in, parts_out, vectors, *refs):
    in_index, out_index, count, place_in, place_out, tiles = refs[:6]
    parts = refs[6 : 6 + parts_in]
    outs = refs[6 + parts_in : 6 + parts_in + parts_out]
    source, total = refs[6 + parts_in + parts_out :]
    length = source.shape[1] // parts_in
    for part in range(parts_in):
        source[:, part * length : (part + 1) * length, :] = (
            parts[part][...].astype(jnp.float32).reshape(vectors, length, LANES)
        )

    def slot_of(row):
        if parts_in == 1:
            return row
        owner = row // length
        return (owner ^ place_in[0]) * length + (row - owner * length)

    accumulate(transpose, in_index, out_index, count, tiles, source, slot_of, total)
    size = total.shape[1] // parts_out
    for part in range(parts_out):
        first = pl.multiple_of((place_out[0] ^ part) * size, size)
        outs[part][...] = total[:, pl.ds(first, size), :].reshape(outs[part].shape)


def apply_tiles(transpose, grid, place_in, place_out, parts, out_rows, parts_out, vectors, name):
    tiles, row_blocks, column_blocks, count = grid
    in_rows = sum(part.size for part in parts) // (vectors * LANES)
    size = out_rows // parts_out
    shape = (size, LANES) if vectors == 1 else (vectors, size, LANES)
    order = (row_blocks, column_blocks) if transpose else (column_blocks, row_blocks)
    return pl.pallas_call(
        functools.partial(apply_body, transpose, len(parts), parts_out, vectors),
        out_shape=[jax.ShapeDtypeStruct(shape, jnp.float32)] * parts_out,
        in_specs=[SMEM] * 5 + [VMEM] * (1 + len(parts)),
        out_specs=[VMEM] * parts_out,
        scratch_shapes=[
            pltpu.VMEM((vectors, in_rows, LANES), jnp.float32),
            pltpu.VMEM((vectors, out_rows, LANES), jnp.float32),
        ],
        compiler_params=pltpu.CompilerParams(vmem_limit_bytes=GRANT),
        cost_estimate=pl.CostEstimate(
            flops=2 * tiles.size * vectors, bytes_accessed=2 * tiles.size, transcendentals=0
        ),
        name=name,
    )(*order, count, place_in, place_out, tiles, *parts)


def exchange(parts, axis):
    size = len(parts)
    return [parts[0]] + [
        lax.ppermute(parts[k], axis, [(i, i ^ k) for i in range(size)]) for k in range(1, size)
    ]


def tree_sum(parts):
    while len(parts) > 1:
        parts = [parts[i] + parts[i + 1] for i in range(0, len(parts), 2)]
    return parts[0]


def local(
    tile_data,
    tile_row_block,
    tile_column_block,
    tile_count,
    saved_primal,
    saved_dual,
    primal_mask,
    dual_mask,
    cost_vector,
    demand,
    upper_bound,
    step_sizes,
    primal_cotangent,
    dual_cotangent,
):
    slot_count = tile_data.shape[2]
    tile_width = tile_data.shape[-1]
    tiles = tile_data.reshape(slot_count, tile_width, tile_width)
    grid = (tiles, tile_row_block, tile_column_block, tile_count)
    iterations = saved_primal.shape[0]
    row_length = saved_dual.shape[1]
    column_length = saved_primal.shape[1]
    n_row = lax.axis_size("row")
    n_col = lax.axis_size("col")
    me_row = lax.axis_index("row")
    me_col = lax.axis_index("col")
    at_row = me_row.reshape(1).astype(jnp.int32)
    at_col = me_col.reshape(1).astype(jnp.int32)
    lines_y = row_length // LANES
    lines_x = column_length // LANES
    share_y = lines_y // n_col
    share_x = lines_x // n_row
    tau = step_sizes[0]
    sigma = step_sizes[1]

    def own_y(array):
        lead = array.shape[:-1]
        array = array.reshape(lead + (lines_y, LANES))
        return lax.dynamic_slice_in_dim(array, me_col * share_y, share_y, len(lead))

    def own_x(array):
        lead = array.shape[:-1]
        array = array.reshape(lead + (lines_x, LANES))
        return lax.dynamic_slice_in_dim(array, me_row * share_x, share_x, len(lead))

    def weight_of(step):
        return (step + 1.0) / (step + 2.0)

    last = iterations - 1
    first_term = (
        dual_mask[last].astype(jnp.float32) * weight_of(last) * dual_cotangent
    ).reshape(lines_y, LANES)
    first_parts = [first_term.astype(jnp.bfloat16)]
    back_parts = apply_tiles(
        True, grid, at_col, at_row, first_parts, lines_x, n_row, 1, "back_first"
    )

    saved = saved_dual.astype(jnp.bfloat16).reshape(iterations, lines_y, LANES)
    saved_parts = apply_tiles(
        True, grid, at_col, at_row, [saved], lines_x, n_row, iterations, "back_saved"
    )

    adjoint_x = own_x(primal_cotangent)
    adjoint_y = own_y(dual_cotangent)
    masks_x = own_x(primal_mask).astype(jnp.float32)
    masks_y = own_y(dual_mask).astype(jnp.float32)
    anchor_x = jnp.zeros_like(adjoint_x)
    anchor_y = jnp.zeros_like(adjoint_y)
    tau_terms = []
    sigma_terms = []
    reduced = None
    for step in reversed(range(iterations)):
        weight = weight_of(step)
        anchor_x = anchor_x + (1.0 - weight) * adjoint_x
        anchor_y = anchor_y + (1.0 - weight) * adjoint_y
        dual_term = masks_y[step] * weight * adjoint_y
        sigma_terms.append((step, dual_term))
        if back_parts is None:
            gathered = exchange([dual_term.astype(jnp.bfloat16)] * n_col, "col")
            back_parts = apply_tiles(
                True, grid, at_col, at_row, gathered, lines_x, n_row, 1, f"back_{step}"
            )
        back = tree_sum(exchange(back_parts, "row"))
        back_parts = None
        primal_term = masks_x[step] * (weight * adjoint_x - 2.0 * sigma * back)
        tau_terms.append((step, primal_term))
        adjoint_x = primal_term + sigma * back
        gathered = exchange([primal_term.astype(jnp.bfloat16)] * n_row, "row")
        image_parts = apply_tiles(
            False, grid, at_row, at_col, gathered, lines_y, n_col, 1, f"image_{step}"
        )
        if reduced is None:
            reduced = own_x(cost_vector) - tree_sum(exchange(saved_parts, "row"))
            primal = own_x(saved_primal)
            half = jnp.clip(primal - tau * reduced, 0.0, own_x(upper_bound))
            extrapolated = (2.0 * half - primal).astype(jnp.bfloat16)
            extrapolated = exchange([extrapolated] * n_row, "row")
            residual_parts = apply_tiles(
                False,
                grid,
                at_row,
                at_col,
                extrapolated,
                lines_y,
                n_col,
                iterations,
                "image_saved",
            )
        image = tree_sum(exchange(image_parts, "col"))
        adjoint_y = dual_term + tau * image
    residual = own_y(demand) - tree_sum(exchange(residual_parts, "col"))

    tau_sum = -sum(jnp.sum(term * reduced[step]) for step, term in tau_terms)
    sigma_sum = sum(jnp.sum(term * residual[step]) for step, term in sigma_terms)
    sums = jnp.stack([tau_sum, sigma_sum])
    spots = lax.broadcasted_iota(jnp.int32, (8, LANES), 1)
    packed = jnp.where(spots == 0, sums[0], jnp.where(spots == 1, sums[1], 0.0))
    packed = tree_sum(exchange([packed] * n_row, "row"))
    packed = tree_sum(exchange([packed] * n_col, "col"))
    total_columns = column_length * n_col
    total_rows = row_length * n_row
    scales = jnp.array(
        [1.0 / math.sqrt(total_columns), 1.0 / math.sqrt(total_rows)], jnp.float32
    )
    gradients = packed[0, :2] * scales

    final_x = exchange([adjoint_x + anchor_x] * n_row, "row")
    primal_adjoint = jnp.zeros((n_row, share_x, LANES), jnp.float32)
    for part in range(n_row):
        primal_adjoint = lax.dynamic_update_index_in_dim(
            primal_adjoint, final_x[part], me_row ^ part, 0
        )
    primal_adjoint = primal_adjoint.reshape(column_length)
    dual_adjoint = (adjoint_y + anchor_y).reshape(row_length // n_col)
    return (primal_adjoint, dual_adjoint, gradients)


def solution(mesh):
    placed = (
        P("row", "col", None, None, None),
        P("row", "col", None),
        P("row", "col", None),
        P("row", "col"),
        P(None, "col"),
        P(None, "row"),
        P(None, "col"),
        P(None, "row"),
        P("col"),
        P("row"),
        P("col"),
        P(),
        P("col"),
        P("row"),
    )
    return jax.shard_map(
        local,
        mesh=mesh,
        in_specs=placed,
        out_specs=(P("col"), P(("row", "col")), P()),
        check_vma=False,
    )
```

time: 378 us -> 154 us (0.41)
  waiting for transfers between devices: 255 us -> 24.7 us
  starting transfers between devices: 0.25 us -> 87.8 us
  blocking collectives: 39.2 us -> 0 us
  matrix products: 27.4 us -> 0 us
  between operations: 20.9 us -> 6.28 us
  Pallas kernels: 0 us -> 11.9 us
  other arithmetic: 22.1 us -> 11 us
    psum x6 -> x0, waiting for transfers between devices: 255 us -> none  [the longest x3 154 us: local(): image_rows = lax.psum(image, 'col')[0]]
    ppermute x0 -> x79, starting transfers between devices: none -> 87.8 us  [exchange(): lax.ppermute(parts[k], axis, [(i, i ^ k) for i in range(size)])]
    psum x1 -> x0, blocking collectives: 39.2 us -> none  [local(): tau_total, sigma_total = lax.psum((tau_local, sigma_local), ('row', 'col'))]
    dot_general x16 -> x0, matrix products: 27.4 us -> none  [the longest x8 24.9 us: block_terms(): jnp.einsum(einsum_form, tile_part, picked, preferred_element_type=jnp.flo...]
    ppermute x0 -> x79, waiting for transfers between devices: none -> 24.7 us  [exchange(): lax.ppermute(parts[k], axis, [(i, i ^ k) for i in range(size)])]
    pallas_call x0 -> x8, Pallas kernels: none -> 11.9 us  [apply_tiles(): pl.pallas_call(functools.partial(apply_body, transpose, len(parts), parts...]
    mul x7 -> x2, other arithmetic: 9.44 us -> 1.55 us  [the longest x1 1.04 us: local(): dual_mask[last].astype(jnp.float32) * weight_of(last) * dual_cotangent]
    gather x8 -> x0, local copies, waits for them, and re-layouts: 5.01 us -> none  [block_terms(): picked = jnp.take(blocks, in_part, axis=1)]
  transfers between devices with their start and end apart: 6 -> 79, of which waited for: 6 -> 18; matrix products, arithmetic and copies ran while one was open for 2% -> 3% of each run, Pallas kernels for 0% -> 6%
where the time goes in v1:
time: 154 us; the launch traced here: 153 us
  starting transfers between devices  87.8 us (57%)
  waiting for transfers between devices  24.7 us (16%)
  Pallas kernels  11.9 us (8%)
  local copies, waits for them, and re-layouts  11.5 us (7%)
  other arithmetic  11 us (7%)
  between operations  6.28 us (4%)
    ppermute x79, starting transfers between devices, exchange(): lax.ppermute(parts[k], axis, [(i, i ^ k) for i in range(size)])  87.8 us
    ppermute x79, waiting for transfers between devices, exchange(): lax.ppermute(parts[k], axis, [(i, i ^ k) for i in range(size)])  24.7 us
    pallas_call x8, Pallas kernels, apply_tiles(): pl.pallas_call(functools.partial(apply_body, transpose, len(parts), parts...  11.9 us
    unnamed x38, local copies, waits for them, and re-layouts  10.2 us
  transfers between devices with their start and end apart: 79, of which 18 were waited for; matrix products, arithmetic and copies ran while one was open for 3% of the time, Pallas kernels for 6%

profile of v1, /device:TPU:0, one launch (start us, length us, event | category | flops | bytes accessed | tf_op | source)
XLA Modules:
  0.0 153.2 jit_solution(9626997004575475992)
XLA Ops:
  3.3 2.2 %copy-done.1 = bf16[1,1,32,256,256]{4,3,2,1,0:T(8,128)(2,1)S(1)} copy-done((bf16[1,1,32,256,256]{4,3,2,1,0:T(8,128)(2,1)S(1)}, bf16[1,1,32,256,256]{4,3,2,1,0:T(8,128)(2,1)}, u32[]{:S(2)}) %copy-start.1) | copy-done | bytes 4194328
  6.8 1.2 back_first.1
  8.0 3.1 %collective-permute-start = (f32[32,128]{1,0:T(8,128)S(1)}, f32[32,128]{1,0:T(8,128)S(1)}, u32[]{:S(2)}, u32[]{:S(2)}) collective-permute-start(f32[32,128]{1,0:T(8,128)S(1)} %get-tuple-element.52), channel_id=1, source_target_pairs={{0,8},{8,0},{16,24},{24,16},{1,9},{9,1},{17,25},{25,17},{2,10},{10... | collective-permute-start | bytes 49160 | tf_op jit(solution)/shard_map/ppermute | solution.py:102
  11.1 2.6 %collective-permute-start.1 = (f32[32,128]{1,0:T(8,128)S(1)}, f32[32,128]{1,0:T(8,128)S(1)}, u32[]{:S(2)}, u32[]{:S(2)}) collective-permute-start(f32[32,128]{1,0:T(8,128)S(1)} %get-tuple-element.53), channel_id=1, source_target_pairs={{0,16},{8,24},{16,0},{24,8},{1,17},{9,25},{17,1},{25,9},{2,18},{10... | collective-permute-start | bytes 49160 | tf_op jit(solution)/shard_map/ppermute | solution.py:102
  13.8 1.2 back_saved.1
  16.0 3.5 %collective-permute-start.57 = (f32[3,32,128]{2,1,0:T(8,128)S(1)}, f32[3,32,128]{2,1,0:T(8,128)S(1)}, u32[]{:S(2)}, u32[]{:S(2)}) collective-permute-start(f32[3,32,128]{2,1,0:T(8,128)S(1)} %get-tuple-element.89), channel_id=1, source_target_pairs={{0,16},{8,24},{16,0},{24,8},{1,17},{9,25},{17,1},{25,9},{2,18},{10... | collective-permute-start | bytes 147464 | tf_op jit(solution)/shard_map/ppermute | solution.py:102
  20.9 1.5 collective-permute-start.4
  22.4 2.8 %collective-permute-start.3 = (bf16[32,128]{1,0:T(8,128)(2,1)S(1)}, bf16[32,128]{1,0:T(8,128)(2,1)S(1)}, u32[]{:S(2)}, u32[]{:S(2)}) collective-permute-start(bf16[32,128]{1,0:T(8,128)(2,1)S(1)} %get-tuple-element.117.refs_6_), channel_id=1, source_target_pairs={{0,8},{8,0},{16,24},{24,16},{1,9},{9,1},{17,25},{25,17},{2,10},{10... | collective-permute-start | bytes 24584 | tf_op jit(solution)/shard_map/ppermute | solution.py:102
  26.9 2.2 %copy-done.2 = bf16[1,1,32,256,256]{4,3,2,1,0:T(8,128)(2,1)S(1)} copy-done((bf16[1,1,32,256,256]{4,3,2,1,0:T(8,128)(2,1)S(1)}, bf16[1,1,32,256,256]{4,3,2,1,0:T(8,128)(2,1)}, u32[]{:S(2)}) %copy-start.2) | copy-done | bytes 4194328
  29.1 1.7 %image_2.1 = (f32[16,128]{1,0:T(8,128)S(1)}, f32[16,128]{1,0:T(8,128)S(1)}, f32[16,128]{1,0:T(8,128)S(1)}, f32[16,128]{1,0:T(8,128)S(1)}, f32[16,128]{1,0:T(8,12...) custom-call(s32[1,1,32]{2,1,0:T(1,128)S(1)} %copy-done.8, s32[1,1,32]{2,1,0:T(1,128)S(1)} %copy-done.6, ...), custom_call_target="tpu_custom_call" | custom-call | flops 4194304 | bytes 4194304 | tf_op jit(solution)/shard_map/image_2/pallas_call | solution.py:82
  30.9 1.6 %collective-permute-start.7 = (f32[16,128]{1,0:T(8,128)S(1)}, f32[16,128]{1,0:T(8,128)S(1)}, u32[]{:S(2)}, u32[]{:S(2)}) collective-permute-start(f32[16,128]{1,0:T(8,128)S(1)} %get-tuple-element.57), channel_id=1, source_target_pairs={{0,2},{1,3},{2,0},{3,1},{4,6},{5,7},{6,4},{7,5},{8,10},{9,11},{10,... | collective-permute-start | bytes 24584 | tf_op jit(solution)/shard_map/ppermute | solution.py:102
  33.4 1.3 collective-permute-done.7
  34.7 1.5 collective-permute-start.9
  36.2 1.6 %collective-permute-start.11 = (f32[16,128]{1,0:T(8,128)S(1)}, f32[16,128]{1,0:T(8,128)S(1)}, u32[]{:S(2)}, u32[]{:S(2)}) collective-permute-start(f32[16,128]{1,0:T(8,128)S(1)} %get-tuple-element.61), channel_id=1, source_target_pairs={{0,6},{1,7},{2,4},{3,5},{4,2},{5,3},{6,0},{7,1},{8,14},{9,15},{10,... | collective-permute-start | bytes 24584 | tf_op jit(solution)/shard_map/ppermute | solution.py:102
  37.8 1.3 collective-permute-start.12
  39.7 3.4 %collective-permute-start.61 = (bf16[3,32,128]{2,1,0:T(8,128)(2,1)S(1)}, bf16[3,32,128]{2,1,0:T(8,128)(2,1)S(1)}, u32[]{:S(2)}, u32[]{:S(2)}) collective-permute-start(bf16[3,32,128]{2,1,0:T(8,128)(2,1)S(1)} %get-tuple-element.108.refs_6_), channel_id=1, source_target_pairs={{0,24},{8,16},{16,8},{24,0},{1,25},{9,17},{17,9},{25,1},{2,26},{10... | collective-permute-start | bytes 73736 | tf_op jit(solution)/shard_map/ppermute | solution.py:102
  43.2 1.3 fusion.23
  44.5 1.1 collective-permute-start.19
  45.6 1.5 collective-permute-start.18
  47.1 1.4 collective-permute-start.17
  48.6 2.3 %collective-permute-start.59 = (bf16[3,32,128]{2,1,0:T(8,128)(2,1)S(1)}, bf16[3,32,128]{2,1,0:T(8,128)(2,1)S(1)}, u32[]{:S(2)}, u32[]{:S(2)}) collective-permute-start(bf16[3,32,128]{2,1,0:T(8,128)(2,1)S(1)} %get-tuple-element.108.refs_6_), channel_id=1, source_target_pairs={{0,8},{8,0},{16,24},{24,16},{1,9},{9,1},{17,25},{25,17},{2,10},{10... | collective-permute-start | bytes 73736 | tf_op jit(solution)/shard_map/ppermute | solution.py:102
  52.3 2.2 %collective-permute-done.16.refs_10_ = bf16[16,128]{1,0:T(8,128)(2,1)S(1)} collective-permute-done((bf16[16,128]{1,0:T(8,128)(2,1)S(1)}, bf16[16,128]{1,0:T(8,128)(2,1)S(1)}, u32[]{:S(2)}, u32[]{:S(2)}) %collective-permute-start.16) | collective-permute-done | bytes 4128 | tf_op jit(solution)/shard_map/ppermute | solution.py:102
  55.2 2.9 %collective-permute-done.14.refs_8_ = bf16[16,128]{1,0:T(8,128)(2,1)S(1)} collective-permute-done((bf16[16,128]{1,0:T(8,128)(2,1)S(1)}, bf16[16,128]{1,0:T(8,128)(2,1)S(1)}, u32[]{:S(2)}, u32[]{:S(2)}) %collective-permute-start.14) | collective-permute-done | bytes 4128 | tf_op jit(solution)/shard_map/ppermute | solution.py:102
  58.1 1.2 back_1.1
  59.5 2.4 %collective-permute-start.21 = (f32[32,128]{1,0:T(8,128)S(1)}, f32[32,128]{1,0:T(8,128)S(1)}, u32[]{:S(2)}, u32[]{:S(2)}) collective-permute-start(f32[32,128]{1,0:T(8,128)S(1)} %get-tuple-element.65), channel_id=1, source_target_pairs={{0,16},{8,24},{16,0},{24,8},{1,17},{9,25},{17,1},{25,9},{2,18},{10... | collective-permute-start | bytes 49160 | tf_op jit(solution)/shard_map/ppermute | solution.py:102
  61.9 1.9 %collective-permute-start.22 = (f32[32,128]{1,0:T(8,128)S(1)}, f32[32,128]{1,0:T(8,128)S(1)}, u32[]{:S(2)}, u32[]{:S(2)}) collective-permute-start(f32[32,128]{1,0:T(8,128)S(1)} %get-tuple-element.66), channel_id=1, source_target_pairs={{0,24},{8,16},{16,8},{24,0},{1,25},{9,17},{17,9},{25,1},{2,26},{10... | collective-permute-start | bytes 49160 | tf_op jit(solution)/shard_map/ppermute | solution.py:102
  63.8 1.8 %image_saved.1 = (f32[3,16,128]{2,1,0:T(8,128)S(1)}, f32[3,16,128]{2,1,0:T(8,128)S(1)}, f32[3,16,128]{2,1,0:T(8,128)S(1)}, f32[3,16,128]{2,1,0:T(8,128)S(1)}, f3...) custom-call(s32[1,1,32]{2,1,0:T(1,128)S(1)} %copy-done.8, ...), custom_call_target="tpu_custom_call" | custom-call | flops 12582912 | bytes 4194304 | tf_op jit(solution)/shard_map/image_saved/pallas_call | solution.py:82
  66.2 1.2 collective-permute-done.22
  68.1 1.9 %collective-permute-start.25 = (bf16[32,128]{1,0:T(8,128)(2,1)S(1)}, bf16[32,128]{1,0:T(8,128)(2,1)S(1)}, u32[]{:S(2)}, u32[]{:S(2)}) collective-permute-start(bf16[32,128]{1,0:T(8,128)(2,1)S(1)} %get-tuple-element.112.refs_6_), channel_id=1, source_target_pairs={{0,24},{8,16},{16,8},{24,0},{1,25},{9,17},{17,9},{25,1},{2,26},{10... | collective-permute-start | bytes 24584 | tf_op jit(solution)/shard_map/ppermute | solution.py:102
  70.1 2.5 %collective-permute-start.23 = (bf16[32,128]{1,0:T(8,128)(2,1)S(1)}, bf16[32,128]{1,0:T(8,128)(2,1)S(1)}, u32[]{:S(2)}, u32[]{:S(2)}) collective-permute-start(bf16[32,128]{1,0:T(8,128)(2,1)S(1)} %get-tuple-element.112.refs_6_), channel_id=1, source_target_pairs={{0,8},{8,0},{16,24},{24,16},{1,9},{9,1},{17,25},{25,17},{2,10},{10... | collective-permute-start | bytes 24584 | tf_op jit(solution)/shard_map/ppermute | solution.py:102
  72.6 1.1 collective-permute-done.25.refs_9_
  74.6 1.8 %image_1.1 = (f32[16,128]{1,0:T(8,128)S(1)}, f32[16,128]{1,0:T(8,128)S(1)}, f32[16,128]{1,0:T(8,128)S(1)}, f32[16,128]{1,0:T(8,128)S(1)}, f32[16,128]{1,0:T(8,12...) custom-call(s32[1,1,32]{2,1,0:T(1,128)S(1)} %copy-done.8, s32[1,1,32]{2,1,0:T(1,128)S(1)} %copy-done.6, ...), custom_call_target="tpu_custom_call" | custom-call | flops 4194304 | bytes 4194304 | tf_op jit(solution)/shard_map/image_1/pallas_call | solution.py:82
  76.4 1.2 collective-permute-start.27
  80.2 1.5 collective-permute-start.67
  81.7 1.7 %collective-permute-start.68 = (f32[3,16,128]{2,1,0:T(8,128)S(1)}, f32[3,16,128]{2,1,0:T(8,128)S(1)}, u32[]{:S(2)}, u32[]{:S(2)}) collective-permute-start(f32[3,16,128]{2,1,0:T(8,128)S(1)} %get-tuple-element.98), channel_id=1, source_target_pairs={{0,7},{1,6},{2,5},{3,4},{4,3},{5,2},{6,1},{7,0},{8,15},{9,14},{10,... | collective-permute-start | bytes 73736 | tf_op jit(solution)/shard_map/ppermute | solution.py:102
  85.0 1.2 collective-permute-start.30
  86.1 1.4 collective-permute-start.31
  88.4 2.3 %collective-permute-done.31 = f32[16,128]{1,0:T(8,128)S(1)} collective-permute-done((f32[16,128]{1,0:T(8,128)S(1)}, f32[16,128]{1,0:T(8,128)S(1)}, u32[]{:S(2)}, u32[]{:S(2)}) %collective-permute-start.31) | collective-permute-done | bytes 8224 | tf_op jit(solution)/shard_map/ppermute | solution.py:102
  91.5 2.0 %fusion.11 = (f32[]{:T(128)}, f32[]{:T(128)}, f32[]{:T(128)}, f32[16,128]{1,0:T(8,128)S(1)}) fusion(f32[3,16,128]{2,1,0:T(8,128)S(1)} %add_subtract_fusion.1, f32[3,16,128]{2,1,0:T(8,128)S(1)} %dynamic-slice_convert_fusion.1, f32[16,128]{1,0:T(8,128)S(1)} %get-tuple-element.116, f32[128,128]{1,0:T(8,128)} %bitcast.142, s32[]{:T(128)S(6)} %select_n.35, ...), kind=kLoop, calls=%fused_computation.40 | loop fusion | flops 43005 | bytes 139284 | tf_op jit(solution)/shard_map/reduce_sum | solution.py:226
  94.4 1.3 collective-permute-start.38
  95.7 1.2 collective-permute-start.37
  96.8 1.1 collective-permute-start.36
  101.9 2.2 %copy-done.3 = bf16[1,1,32,256,256]{4,3,2,1,0:T(8,128)(2,1)S(1)} copy-done((bf16[1,1,32,256,256]{4,3,2,1,0:T(8,128)(2,1)S(1)}, bf16[1,1,32,256,256]{4,3,2,1,0:T(8,128)(2,1)}, u32[]{:S(2)}) %copy-start.3) | copy-done | bytes 4194328
  104.1 1.2 back_0.1
  105.3 2.2 %collective-permute-start.40 = (f32[32,128]{1,0:T(8,128)S(1)}, f32[32,128]{1,0:T(8,128)S(1)}, u32[]{:S(2)}, u32[]{:S(2)}) collective-permute-start(f32[32,128]{1,0:T(8,128)S(1)} %get-tuple-element.76), channel_id=1, source_target_pairs={{0,8},{8,0},{16,24},{24,16},{1,9},{9,1},{17,25},{25,17},{2,10},{10... | collective-permute-start | bytes 49160 | tf_op jit(solution)/shard_map/ppermute | solution.py:102
  108.4 1.5 %collective-permute-start.42 = (f32[32,128]{1,0:T(8,128)S(1)}, f32[32,128]{1,0:T(8,128)S(1)}, u32[]{:S(2)}, u32[]{:S(2)}) collective-permute-start(f32[32,128]{1,0:T(8,128)S(1)} %get-tuple-element.78), channel_id=1, source_target_pairs={{0,24},{8,16},{16,8},{24,0},{1,25},{9,17},{17,9},{25,1},{2,26},{10... | collective-permute-start | bytes 49160 | tf_op jit(solution)/shard_map/ppermute | solution.py:102
  109.9 2.2 %collective-permute-done.41 = f32[32,128]{1,0:T(8,128)S(1)} collective-permute-done((f32[32,128]{1,0:T(8,128)S(1)}, f32[32,128]{1,0:T(8,128)S(1)}, u32[]{:S(2)}, u32[]{:S(2)}) %collective-permute-start.41) | collective-permute-done | bytes 16416 | tf_op jit(solution)/shard_map/ppermute | solution.py:102
  112.1 1.8 %collective-permute-done.42 = f32[32,128]{1,0:T(8,128)S(1)} collective-permute-done((f32[32,128]{1,0:T(8,128)S(1)}, f32[32,128]{1,0:T(8,128)S(1)}, u32[]{:S(2)}, u32[]{:S(2)}) %collective-permute-start.42) | collective-permute-done | bytes 16416 | tf_op jit(solution)/shard_map/ppermute | solution.py:102
  113.9 1.3 fusion.2
  117.4 1.4 collective-permute-start.71
  118.8 1.9 %collective-permute-start.69 = (f32[8,128]{1,0:T(8,128)S(1)}, f32[8,128]{1,0:T(8,128)S(1)}, u32[]{:S(2)}, u32[]{:S(2)}) collective-permute-start(f32[8,128]{1,0:T(8,128)S(1)} %broadcast_select_fusion), channel_id=1, source_target_pairs={{0,8},{8,0},{16,24},{24,16},{1,9},{9,1},{17,25},{25,17},{2,10},{10... | collective-permute-start | bytes 12296 | tf_op jit(solution)/shard_map/ppermute | solution.py:102
  120.7 1.5 %collective-permute-start.48 = (bf16[32,128]{1,0:T(8,128)(2,1)S(1)}, bf16[32,128]{1,0:T(8,128)(2,1)S(1)}, u32[]{:S(2)}, u32[]{:S(2)}) collective-permute-start(bf16[32,128]{1,0:T(8,128)(2,1)S(1)} %convert_element_type.45.refs_6_), channel_id=1, source_target_pairs={{0,24},{8,16},{16,8},{24,0},{1,25},{9,17},{17,9},{25,1},{2,26},{10... | collective-permute-start | bytes 24584 | tf_op jit(solution)/shard_map/ppermute | solution.py:102
  122.3 2.8 %collective-permute-start.46 = (bf16[32,128]{1,0:T(8,128)(2,1)S(1)}, bf16[32,128]{1,0:T(8,128)(2,1)S(1)}, u32[]{:S(2)}, u32[]{:S(2)}) collective-permute-start(bf16[32,128]{1,0:T(8,128)(2,1)S(1)} %convert_element_type.45.refs_6_), channel_id=1, source_target_pairs={{0,8},{8,0},{16,24},{24,16},{1,9},{9,1},{17,25},{25,17},{2,10},{10... | collective-permute-start | bytes 24584 | tf_op jit(solution)/shard_map/ppermute | solution.py:102
  125.2 1.5 collective-permute-start.77
  126.7 2.4 %collective-permute-done.78 = f32[8,128]{1,0:T(8,128)S(1)} collective-permute-done((f32[8,128]{1,0:T(8,128)S(1)}, f32[8,128]{1,0:T(8,128)S(1)}, u32[]{:S(2)}, u32[]{:S(2)}) %collective-permute-start.78) | collective-permute-done | bytes 4128 | tf_op jit(solution)/shard_map/ppermute | solution.py:102
  129.8 1.0 collective-permute-start.75
  133.4 2.2 %copy-done.4 = bf16[1,1,32,256,256]{4,3,2,1,0:T(8,128)(2,1)S(1)} copy-done((bf16[1,1,32,256,256]{4,3,2,1,0:T(8,128)(2,1)S(1)}, bf16[1,1,32,256,256]{4,3,2,1,0:T(8,128)(2,1)}, u32[]{:S(2)}) %copy-start.4) | copy-done | bytes 4194328
  135.5 1.7 %image_0.1 = (f32[16,128]{1,0:T(8,128)S(1)}, f32[16,128]{1,0:T(8,128)S(1)}, f32[16,128]{1,0:T(8,128)S(1)}, f32[16,128]{1,0:T(8,128)S(1)}, f32[16,128]{1,0:T(8,12...) custom-call(s32[1,1,32]{2,1,0:T(1,128)S(1)} %copy-done.8, s32[1,1,32]{2,1,0:T(1,128)S(1)} %copy-done.6, ...), custom_call_target="tpu_custom_call" | custom-call | flops 4194304 | bytes 4194304 | tf_op jit(solution)/shard_map/image_0/pallas_call | solution.py:82
  137.6 1.9 %collective-permute-start.43 = (f32[32,128]{1,0:T(8,128)S(1)}, f32[32,128]{1,0:T(8,128)S(1)}, u32[]{:S(2)}, u32[]{:S(2)}) collective-permute-start(f32[32,128]{1,0:T(8,128)S(1)} %get-tuple-element.111), channel_id=1, source_target_pairs={{0,8},{8,0},{16,24},{24,16},{1,9},{9,1},{17,25},{25,17},{2,10},{10... | collective-permute-start | bytes 49160 | tf_op jit(solution)/shard_map/ppermute | solution.py:102
  139.5 2.3 %collective-permute-start.45 = (f32[32,128]{1,0:T(8,128)S(1)}, f32[32,128]{1,0:T(8,128)S(1)}, u32[]{:S(2)}, u32[]{:S(2)}) collective-permute-start(f32[32,128]{1,0:T(8,128)S(1)} %get-tuple-element.111), channel_id=1, source_target_pairs={{0,24},{8,16},{16,8},{24,0},{1,25},{9,17},{17,9},{25,1},{2,26},{10... | collective-permute-start | bytes 49160 | tf_op jit(solution)/shard_map/ppermute | solution.py:102
  145.9 1.4 collective-permute-start.54
  147.3 1.3 collective-permute-start.55
  148.6 1.8 %collective-permute-done.54 = f32[16,128]{1,0:T(8,128)S(1)} collective-permute-done((f32[16,128]{1,0:T(8,128)S(1)}, f32[16,128]{1,0:T(8,128)S(1)}, u32[]{:S(2)}, u32[]{:S(2)}) %collective-permute-start.54) | collective-permute-done | bytes 8224 | tf_op jit(solution)/shard_map/ppermute | solution.py:102
  151.3 1.9 %add_bitcast_fusion = f32[2048]{0:T(1024)} fusion(f32[16,128]{1,0:T(8,128)S(1)} %get-tuple-element.107, f32[16,128]{1,0:T(8,128)S(1)} %get-tuple-element.116, f32[16,128]{1,0:T(8,128)S(1)} %collective-permute-done.54, f32[16,128]{1,0:T(8,128)S(1)} %collective-permute-done.55, f32[16,128]{1,0:T(8,128)S(1)} %collective-permute-done.52, ...), kind=kLoop, calls=%fused_computation.56 | loop fusion | flops 34816 | bytes 106504 | tf_op jit(solution)/shard_map/reshape | solution.py:246
  (169 shorter events, 31.3 us)
Async XLA Ops:
  8.0 12.8 %collective-permute-start = (f32[32,128]{1,0:T(8,128)S(1)}, f32[32,128]{1,0:T(8,128)S(1)}, u32[]{:S(2)}, u32[]{:S(2)}) collective-permute-start(f32[32,128]{1,0:T(8,128)S(1)} %get-tuple-element.52), channel_id=1, source_target_pairs={{0,8},{8,0},{16,24},{24,16},{1,9},{9,1},{17,25},{25,17},{2,10},{10... | collective-permute-start | bytes 49160 | tf_op jit(solution)/shard_map/ppermute | solution.py:102
  11.1 9.7 %collective-permute-start.1 = (f32[32,128]{1,0:T(8,128)S(1)}, f32[32,128]{1,0:T(8,128)S(1)}, u32[]{:S(2)}, u32[]{:S(2)}) collective-permute-start(f32[32,128]{1,0:T(8,128)S(1)} %get-tuple-element.53), channel_id=1, source_target_pairs={{0,16},{8,24},{16,0},{24,8},{1,17},{9,25},{17,1},{25,9},{2,18},{10... | collective-permute-start | bytes 49160 | tf_op jit(solution)/shard_map/ppermute | solution.py:102
  13.7 7.1 %collective-permute-start.2 = (f32[32,128]{1,0:T(8,128)S(1)}, f32[32,128]{1,0:T(8,128)S(1)}, u32[]{:S(2)}, u32[]{:S(2)}) collective-permute-start(f32[32,128]{1,0:T(8,128)S(1)} %get-tuple-element.54), channel_id=1, source_target_pairs={{0,24},{8,16},{16,8},{24,0},{1,25},{9,17},{17,9},{25,1},{2,26},{10... | collective-permute-start | bytes 49160 | tf_op jit(solution)/shard_map/ppermute | solution.py:102
  15.0 21.2 %collective-permute-start.56 = (f32[3,32,128]{2,1,0:T(8,128)S(1)}, f32[3,32,128]{2,1,0:T(8,128)S(1)}, u32[]{:S(2)}, u32[]{:S(2)}) collective-permute-start(f32[3,32,128]{2,1,0:T(8,128)S(1)} %get-tuple-element.88), channel_id=1, source_target_pairs={{0,8},{8,0},{16,24},{24,16},{1,9},{9,1},{17,25},{25,17},{2,10},{10... | collective-permute-start | bytes 147464 | tf_op jit(solution)/shard_map/ppermute | solution.py:102
  16.0 20.2 %collective-permute-start.57 = (f32[3,32,128]{2,1,0:T(8,128)S(1)}, f32[3,32,128]{2,1,0:T(8,128)S(1)}, u32[]{:S(2)}, u32[]{:S(2)}) collective-permute-start(f32[3,32,128]{2,1,0:T(8,128)S(1)} %get-tuple-element.89), channel_id=1, source_target_pairs={{0,16},{8,24},{16,0},{24,8},{1,17},{9,25},{17,1},{25,9},{2,18},{10... | collective-permute-start | bytes 147464 | tf_op jit(solution)/shard_map/ppermute | solution.py:102
  20.8 5.6 %collective-permute-start.5 = (bf16[32,128]{1,0:T(8,128)(2,1)S(1)}, bf16[32,128]{1,0:T(8,128)(2,1)S(1)}, u32[]{:S(2)}, u32[]{:S(2)}) collective-permute-start(bf16[32,128]{1,0:T(8,128)(2,1)S(1)} %get-tuple-element.117.refs_6_), channel_id=1, source_target_pairs={{0,24},{8,16},{16,8},{24,0},{1,25},{9,17},{17,9},{25,1},{2,26},{10... | collective-permute-start | bytes 24584 | tf_op jit(solution)/shard_map/ppermute | solution.py:102
  20.9 5.5 %collective-permute-start.4 = (bf16[32,128]{1,0:T(8,128)(2,1)S(1)}, bf16[32,128]{1,0:T(8,128)(2,1)S(1)}, u32[]{:S(2)}, u32[]{:S(2)}) collective-permute-start(bf16[32,128]{1,0:T(8,128)(2,1)S(1)} %get-tuple-element.117.refs_6_), channel_id=1, source_target_pairs={{0,16},{8,24},{16,0},{24,8},{1,17},{9,25},{17,1},{25,9},{2,18},{10... | collective-permute-start | bytes 24584 | tf_op jit(solution)/shard_map/ppermute | solution.py:102
  22.4 4.5 %collective-permute-start.3 = (bf16[32,128]{1,0:T(8,128)(2,1)S(1)}, bf16[32,128]{1,0:T(8,128)(2,1)S(1)}, u32[]{:S(2)}, u32[]{:S(2)}) collective-permute-start(bf16[32,128]{1,0:T(8,128)(2,1)S(1)} %get-tuple-element.117.refs_6_), channel_id=1, source_target_pairs={{0,8},{8,0},{16,24},{24,16},{1,9},{9,1},{17,25},{25,17},{2,10},{10... | collective-permute-start | bytes 24584 | tf_op jit(solution)/shard_map/ppermute | solution.py:102
  26.4 11.3 %collective-permute-start.58 = (f32[3,32,128]{2,1,0:T(8,128)S(1)}, f32[3,32,128]{2,1,0:T(8,128)S(1)}, u32[]{:S(2)}, u32[]{:S(2)}) collective-permute-start(f32[3,32,128]{2,1,0:T(8,128)S(1)} %get-tuple-element.90), channel_id=1, source_target_pairs={{0,24},{8,16},{16,8},{24,0},{1,25},{9,17},{17,9},{25,1},{2,26},{10... | collective-permute-start | bytes 147464 | tf_op jit(solution)/shard_map/ppermute | solution.py:102
  32.5 7.2 %collective-permute-start.8 = (f32[16,128]{1,0:T(8,128)S(1)}, f32[16,128]{1,0:T(8,128)S(1)}, u32[]{:S(2)}, u32[]{:S(2)}) collective-permute-start(f32[16,128]{1,0:T(8,128)S(1)} %get-tuple-element.58), channel_id=1, source_target_pairs={{0,3},{1,2},{2,1},{3,0},{4,7},{5,6},{6,5},{7,4},{8,11},{9,10},{10,... | collective-permute-start | bytes 24584 | tf_op jit(solution)/shard_map/ppermute | solution.py:102
  34.7 8.5 %collective-permute-start.9 = (f32[16,128]{1,0:T(8,128)S(1)}, f32[16,128]{1,0:T(8,128)S(1)}, u32[]{:S(2)}, u32[]{:S(2)}) collective-permute-start(f32[16,128]{1,0:T(8,128)S(1)} %get-tuple-element.59), channel_id=1, source_target_pairs={{0,4},{1,5},{2,6},{3,7},{4,0},{5,1},{6,2},{7,3},{8,12},{9,13},{10,... | collective-permute-start | bytes 24584 | tf_op jit(solution)/shard_map/ppermute | solution.py:102
  36.2 7.0 %collective-permute-start.10 = (f32[16,128]{1,0:T(8,128)S(1)}, f32[16,128]{1,0:T(8,128)S(1)}, u32[]{:S(2)}, u32[]{:S(2)}) collective-permute-start(f32[16,128]{1,0:T(8,128)S(1)} %get-tuple-element.60), channel_id=1, source_target_pairs={{0,5},{1,4},{2,7},{3,6},{4,1},{5,0},{6,3},{7,2},{8,13},{9,12},{10,... | collective-permute-start | bytes 24584 | tf_op jit(solution)/shard_map/ppermute | solution.py:102
  36.2 7.0 %collective-permute-start.11 = (f32[16,128]{1,0:T(8,128)S(1)}, f32[16,128]{1,0:T(8,128)S(1)}, u32[]{:S(2)}, u32[]{:S(2)}) collective-permute-start(f32[16,128]{1,0:T(8,128)S(1)} %get-tuple-element.61), channel_id=1, source_target_pairs={{0,6},{1,7},{2,4},{3,5},{4,2},{5,3},{6,0},{7,1},{8,14},{9,15},{10,... | collective-permute-start | bytes 24584 | tf_op jit(solution)/shard_map/ppermute | solution.py:102
  37.8 5.4 %collective-permute-start.12 = (f32[16,128]{1,0:T(8,128)S(1)}, f32[16,128]{1,0:T(8,128)S(1)}, u32[]{:S(2)}, u32[]{:S(2)}) collective-permute-start(f32[16,128]{1,0:T(8,128)S(1)} %get-tuple-element.62), channel_id=1, source_target_pairs={{0,7},{1,6},{2,5},{3,4},{4,3},{5,2},{6,1},{7,0},{8,15},{9,14},{10,... | collective-permute-start | bytes 24584 | tf_op jit(solution)/shard_map/ppermute | solution.py:102
  39.7 22.2 %collective-permute-start.61 = (bf16[3,32,128]{2,1,0:T(8,128)(2,1)S(1)}, bf16[3,32,128]{2,1,0:T(8,128)(2,1)S(1)}, u32[]{:S(2)}, u32[]{:S(2)}) collective-permute-start(bf16[3,32,128]{2,1,0:T(8,128)(2,1)S(1)} %get-tuple-element.108.refs_6_), channel_id=1, source_target_pairs={{0,24},{8,16},{16,8},{24,0},{1,25},{9,17},{17,9},{25,1},{2,26},{10... | collective-permute-start | bytes 73736 | tf_op jit(solution)/shard_map/ppermute | solution.py:102
  44.5 4.1 %collective-permute-start.19 = (bf16[16,128]{1,0:T(8,128)(2,1)S(1)}, bf16[16,128]{1,0:T(8,128)(2,1)S(1)}, u32[]{:S(2)}, u32[]{:S(2)}) collective-permute-start(bf16[16,128]{1,0:T(8,128)(2,1)S(1)} %get-tuple-element.115.refs_6_), channel_id=1, source_target_pairs={{0,7},{1,6},{2,5},{3,4},{4,3},{5,2},{6,1},{7,0},{8,15},{9,14},{10,... | collective-permute-start | bytes 12296 | tf_op jit(solution)/shard_map/ppermute | solution.py:102
  45.6 5.3 %collective-permute-start.18 = (bf16[16,128]{1,0:T(8,128)(2,1)S(1)}, bf16[16,128]{1,0:T(8,128)(2,1)S(1)}, u32[]{:S(2)}, u32[]{:S(2)}) collective-permute-start(bf16[16,128]{1,0:T(8,128)(2,1)S(1)} %get-tuple-element.115.refs_6_), channel_id=1, source_target_pairs={{0,6},{1,7},{2,4},{3,5},{4,2},{5,3},{6,0},{7,1},{8,14},{9,15},{10,... | collective-permute-start | bytes 12296 | tf_op jit(solution)/shard_map/ppermute | solution.py:102
  47.1 4.5 %collective-permute-start.17 = (bf16[16,128]{1,0:T(8,128)(2,1)S(1)}, bf16[16,128]{1,0:T(8,128)(2,1)S(1)}, u32[]{:S(2)}, u32[]{:S(2)}) collective-permute-start(bf16[16,128]{1,0:T(8,128)(2,1)S(1)} %get-tuple-element.115.refs_6_), channel_id=1, source_target_pairs={{0,5},{1,4},{2,7},{3,6},{4,1},{5,0},{6,3},{7,2},{8,13},{9,12},{10,... | collective-permute-start | bytes 12296 | tf_op jit(solution)/shard_map/ppermute | solution.py:102
  48.4 15.3 %collective-permute-start.60 = (bf16[3,32,128]{2,1,0:T(8,128)(2,1)S(1)}, bf16[3,32,128]{2,1,0:T(8,128)(2,1)S(1)}, u32[]{:S(2)}, u32[]{:S(2)}) collective-permute-start(bf16[3,32,128]{2,1,0:T(8,128)(2,1)S(1)} %get-tuple-element.108.refs_6_), channel_id=1, source_target_pairs={{0,16},{8,24},{16,0},{24,8},{1,17},{9,25},{17,1},{25,9},{2,18},{10... | collective-permute-start | bytes 73736 | tf_op jit(solution)/shard_map/ppermute | solution.py:102
  48.6 15.2 %collective-permute-start.59 = (bf16[3,32,128]{2,1,0:T(8,128)(2,1)S(1)}, bf16[3,32,128]{2,1,0:T(8,128)(2,1)S(1)}, u32[]{:S(2)}, u32[]{:S(2)}) collective-permute-start(bf16[3,32,128]{2,1,0:T(8,128)(2,1)S(1)} %get-tuple-element.108.refs_6_), channel_id=1, source_target_pairs={{0,8},{8,0},{16,24},{24,16},{1,9},{9,1},{17,25},{25,17},{2,10},{10... | collective-permute-start | bytes 73736 | tf_op jit(solution)/shard_map/ppermute | solution.py:102
  59.3 6.9 %collective-permute-start.20 = (f32[32,128]{1,0:T(8,128)S(1)}, f32[32,128]{1,0:T(8,128)S(1)}, u32[]{:S(2)}, u32[]{:S(2)}) collective-permute-start(f32[32,128]{1,0:T(8,128)S(1)} %get-tuple-element.64), channel_id=1, source_target_pairs={{0,8},{8,0},{16,24},{24,16},{1,9},{9,1},{17,25},{25,17},{2,10},{10... | collective-permute-start | bytes 49160 | tf_op jit(solution)/shard_map/ppermute | solution.py:102
  59.5 6.8 %collective-permute-start.21 = (f32[32,128]{1,0:T(8,128)S(1)}, f32[32,128]{1,0:T(8,128)S(1)}, u32[]{:S(2)}, u32[]{:S(2)}) collective-permute-start(f32[32,128]{1,0:T(8,128)S(1)} %get-tuple-element.65), channel_id=1, source_target_pairs={{0,16},{8,24},{16,0},{24,8},{1,17},{9,25},{17,1},{25,9},{2,18},{10... | collective-permute-start | bytes 49160 | tf_op jit(solution)/shard_map/ppermute | solution.py:102
  61.9 5.5 %collective-permute-start.22 = (f32[32,128]{1,0:T(8,128)S(1)}, f32[32,128]{1,0:T(8,128)S(1)}, u32[]{:S(2)}, u32[]{:S(2)}) collective-permute-start(f32[32,128]{1,0:T(8,128)S(1)} %get-tuple-element.66), channel_id=1, source_target_pairs={{0,24},{8,16},{16,8},{24,0},{1,25},{9,17},{17,9},{25,1},{2,26},{10... | collective-permute-start | bytes 49160 | tf_op jit(solution)/shard_map/ppermute | solution.py:102
  65.6 14.6 %collective-permute-start.62 = (f32[3,16,128]{2,1,0:T(8,128)S(1)}, f32[3,16,128]{2,1,0:T(8,128)S(1)}, u32[]{:S(2)}, u32[]{:S(2)}) collective-permute-start(f32[3,16,128]{2,1,0:T(8,128)S(1)} %get-tuple-element.92), channel_id=1, source_target_pairs={{0,1},{1,0},{2,3},{3,2},{4,5},{5,4},{6,7},{7,6},{8,9},{9,8},{10,11... | collective-permute-start | bytes 73736 | tf_op jit(solution)/shard_map/ppermute | solution.py:102
  65.6 16.0 %collective-permute-start.63 = (f32[3,16,128]{2,1,0:T(8,128)S(1)}, f32[3,16,128]{2,1,0:T(8,128)S(1)}, u32[]{:S(2)}, u32[]{:S(2)}) collective-permute-start(f32[3,16,128]{2,1,0:T(8,128)S(1)} %get-tuple-element.93), channel_id=1, source_target_pairs={{0,2},{1,3},{2,0},{3,1},{4,6},{5,7},{6,4},{7,5},{8,10},{9,11},{10,... | collective-permute-start | bytes 73736 | tf_op jit(solution)/shard_map/ppermute | solution.py:102
  68.1 5.5 %collective-permute-start.25 = (bf16[32,128]{1,0:T(8,128)(2,1)S(1)}, bf16[32,128]{1,0:T(8,128)(2,1)S(1)}, u32[]{:S(2)}, u32[]{:S(2)}) collective-permute-start(bf16[32,128]{1,0:T(8,128)(2,1)S(1)} %get-tuple-element.112.refs_6_), channel_id=1, source_target_pairs={{0,24},{8,16},{16,8},{24,0},{1,25},{9,17},{17,9},{25,1},{2,26},{10... | collective-permute-start | bytes 24584 | tf_op jit(solution)/shard_map/ppermute | solution.py:102
  70.0 4.5 %collective-permute-start.24 = (bf16[32,128]{1,0:T(8,128)(2,1)S(1)}, bf16[32,128]{1,0:T(8,128)(2,1)S(1)}, u32[]{:S(2)}, u32[]{:S(2)}) collective-permute-start(bf16[32,128]{1,0:T(8,128)(2,1)S(1)} %get-tuple-element.112.refs_6_), channel_id=1, source_target_pairs={{0,16},{8,24},{16,0},{24,8},{1,17},{9,25},{17,1},{25,9},{2,18},{10... | collective-permute-start | bytes 24584 | tf_op jit(solution)/shard_map/ppermute | solution.py:102
  70.1 4.5 %collective-permute-start.23 = (bf16[32,128]{1,0:T(8,128)(2,1)S(1)}, bf16[32,128]{1,0:T(8,128)(2,1)S(1)}, u32[]{:S(2)}, u32[]{:S(2)}) collective-permute-start(bf16[32,128]{1,0:T(8,128)(2,1)S(1)} %get-tuple-element.112.refs_6_), channel_id=1, source_target_pairs={{0,8},{8,0},{16,24},{24,16},{1,9},{9,1},{17,25},{25,17},{2,10},{10... | collective-permute-start | bytes 24584 | tf_op jit(solution)/shard_map/ppermute | solution.py:102
  77.6 5.8 %collective-permute-start.64 = (f32[3,16,128]{2,1,0:T(8,128)S(1)}, f32[3,16,128]{2,1,0:T(8,128)S(1)}, u32[]{:S(2)}, u32[]{:S(2)}) collective-permute-start(f32[3,16,128]{2,1,0:T(8,128)S(1)} %get-tuple-element.94), channel_id=1, source_target_pairs={{0,3},{1,2},{2,1},{3,0},{4,7},{5,6},{6,5},{7,4},{8,11},{9,10},{10,... | collective-permute-start | bytes 73736 | tf_op jit(solution)/shard_map/ppermute | solution.py:102
  78.3 5.7 %collective-permute-start.65 = (f32[3,16,128]{2,1,0:T(8,128)S(1)}, f32[3,16,128]{2,1,0:T(8,128)S(1)}, u32[]{:S(2)}, u32[]{:S(2)}) collective-permute-start(f32[3,16,128]{2,1,0:T(8,128)S(1)} %get-tuple-element.95), channel_id=1, source_target_pairs={{0,4},{1,5},{2,6},{3,7},{4,0},{5,1},{6,2},{7,3},{8,12},{9,13},{10,... | collective-permute-start | bytes 73736 | tf_op jit(solution)/shard_map/ppermute | solution.py:102
  80.2 4.8 %collective-permute-start.66 = (f32[3,16,128]{2,1,0:T(8,128)S(1)}, f32[3,16,128]{2,1,0:T(8,128)S(1)}, u32[]{:S(2)}, u32[]{:S(2)}) collective-permute-start(f32[3,16,128]{2,1,0:T(8,128)S(1)} %get-tuple-element.96), channel_id=1, source_target_pairs={{0,5},{1,4},{2,7},{3,6},{4,1},{5,0},{6,3},{7,2},{8,13},{9,12},{10,... | collective-permute-start | bytes 73736 | tf_op jit(solution)/shard_map/ppermute | solution.py:102
  80.2 6.0 %collective-permute-start.67 = (f32[3,16,128]{2,1,0:T(8,128)S(1)}, f32[3,16,128]{2,1,0:T(8,128)S(1)}, u32[]{:S(2)}, u32[]{:S(2)}) collective-permute-start(f32[3,16,128]{2,1,0:T(8,128)S(1)} %get-tuple-element.97), channel_id=1, source_target_pairs={{0,6},{1,7},{2,4},{3,5},{4,2},{5,3},{6,0},{7,1},{8,14},{9,15},{10,... | collective-permute-start | bytes 73736 | tf_op jit(solution)/shard_map/ppermute | solution.py:102
  81.7 5.9 %collective-permute-start.68 = (f32[3,16,128]{2,1,0:T(8,128)S(1)}, f32[3,16,128]{2,1,0:T(8,128)S(1)}, u32[]{:S(2)}, u32[]{:S(2)}) collective-permute-start(f32[3,16,128]{2,1,0:T(8,128)S(1)} %get-tuple-element.98), channel_id=1, source_target_pairs={{0,7},{1,6},{2,5},{3,4},{4,3},{5,2},{6,1},{7,0},{8,15},{9,14},{10,... | collective-permute-start | bytes 73736 | tf_op jit(solution)/shard_map/ppermute | solution.py:102
  83.4 5.0 %collective-permute-start.28 = (f32[16,128]{1,0:T(8,128)S(1)}, f32[16,128]{1,0:T(8,128)S(1)}, u32[]{:S(2)}, u32[]{:S(2)}) collective-permute-start(f32[16,128]{1,0:T(8,128)S(1)} %get-tuple-element.70), channel_id=1, source_target_pairs={{0,3},{1,2},{2,1},{3,0},{4,7},{5,6},{6,5},{7,4},{8,11},{9,10},{10,... | collective-permute-start | bytes 24584 | tf_op jit(solution)/shard_map/ppermute | solution.py:102
  84.0 4.4 %collective-permute-start.29 = (f32[16,128]{1,0:T(8,128)S(1)}, f32[16,128]{1,0:T(8,128)S(1)}, u32[]{:S(2)}, u32[]{:S(2)}) collective-permute-start(f32[16,128]{1,0:T(8,128)S(1)} %get-tuple-element.71), channel_id=1, source_target_pairs={{0,4},{1,5},{2,6},{3,7},{4,0},{5,1},{6,2},{7,3},{8,12},{9,13},{10,... | collective-permute-start | bytes 24584 | tf_op jit(solution)/shard_map/ppermute | solution.py:102
  86.1 4.6 %collective-permute-start.31 = (f32[16,128]{1,0:T(8,128)S(1)}, f32[16,128]{1,0:T(8,128)S(1)}, u32[]{:S(2)}, u32[]{:S(2)}) collective-permute-start(f32[16,128]{1,0:T(8,128)S(1)} %get-tuple-element.73), channel_id=1, source_target_pairs={{0,6},{1,7},{2,4},{3,5},{4,2},{5,3},{6,0},{7,1},{8,14},{9,15},{10,... | collective-permute-start | bytes 24584 | tf_op jit(solution)/shard_map/ppermute | solution.py:102
  93.5 4.7 %collective-permute-start.39 = (bf16[16,128]{1,0:T(8,128)(2,1)S(1)}, bf16[16,128]{1,0:T(8,128)(2,1)S(1)}, u32[]{:S(2)}, u32[]{:S(2)}) collective-permute-start(bf16[16,128]{1,0:T(8,128)(2,1)S(1)} %fusion.22.refs_6_), channel_id=1, source_target_pairs={{0,7},{1,6},{2,5},{3,4},{4,3},{5,2},{6,1},{7,0},{8,15},{9,14},{10,... | collective-permute-start | bytes 12296 | tf_op jit(solution)/shard_map/ppermute | solution.py:102
  94.4 4.8 %collective-permute-start.38 = (bf16[16,128]{1,0:T(8,128)(2,1)S(1)}, bf16[16,128]{1,0:T(8,128)(2,1)S(1)}, u32[]{:S(2)}, u32[]{:S(2)}) collective-permute-start(bf16[16,128]{1,0:T(8,128)(2,1)S(1)} %fusion.22.refs_6_), channel_id=1, source_target_pairs={{0,6},{1,7},{2,4},{3,5},{4,2},{5,3},{6,0},{7,1},{8,14},{9,15},{10,... | collective-permute-start | bytes 12296 | tf_op jit(solution)/shard_map/ppermute | solution.py:102
  95.7 6.1 %collective-permute-start.37 = (bf16[16,128]{1,0:T(8,128)(2,1)S(1)}, bf16[16,128]{1,0:T(8,128)(2,1)S(1)}, u32[]{:S(2)}, u32[]{:S(2)}) collective-permute-start(bf16[16,128]{1,0:T(8,128)(2,1)S(1)} %fusion.22.refs_6_), channel_id=1, source_target_pairs={{0,5},{1,4},{2,7},{3,6},{4,1},{5,0},{6,3},{7,2},{8,13},{9,12},{10,... | collective-permute-start | bytes 12296 | tf_op jit(solution)/shard_map/ppermute | solution.py:102
  96.8 4.9 %collective-permute-start.36 = (bf16[16,128]{1,0:T(8,128)(2,1)S(1)}, bf16[16,128]{1,0:T(8,128)(2,1)S(1)}, u32[]{:S(2)}, u32[]{:S(2)}) collective-permute-start(bf16[16,128]{1,0:T(8,128)(2,1)S(1)} %fusion.22.refs_6_), channel_id=1, source_target_pairs={{0,4},{1,5},{2,6},{3,7},{4,0},{5,1},{6,2},{7,3},{8,12},{9,13},{10,... | collective-permute-start | bytes 12296 | tf_op jit(solution)/shard_map/ppermute | solution.py:102
  105.3 4.6 %collective-permute-start.40 = (f32[32,128]{1,0:T(8,128)S(1)}, f32[32,128]{1,0:T(8,128)S(1)}, u32[]{:S(2)}, u32[]{:S(2)}) collective-permute-start(f32[32,128]{1,0:T(8,128)S(1)} %get-tuple-element.76), channel_id=1, source_target_pairs={{0,8},{8,0},{16,24},{24,16},{1,9},{9,1},{17,25},{25,17},{2,10},{10... | collective-permute-start | bytes 49160 | tf_op jit(solution)/shard_map/ppermute | solution.py:102
  107.5 4.6 %collective-permute-start.41 = (f32[32,128]{1,0:T(8,128)S(1)}, f32[32,128]{1,0:T(8,128)S(1)}, u32[]{:S(2)}, u32[]{:S(2)}) collective-permute-start(f32[32,128]{1,0:T(8,128)S(1)} %get-tuple-element.77), channel_id=1, source_target_pairs={{0,16},{8,24},{16,0},{24,8},{1,17},{9,25},{17,1},{25,9},{2,18},{10... | collective-permute-start | bytes 49160 | tf_op jit(solution)/shard_map/ppermute | solution.py:102
  108.4 5.5 %collective-permute-start.42 = (f32[32,128]{1,0:T(8,128)S(1)}, f32[32,128]{1,0:T(8,128)S(1)}, u32[]{:S(2)}, u32[]{:S(2)}) collective-permute-start(f32[32,128]{1,0:T(8,128)S(1)} %get-tuple-element.78), channel_id=1, source_target_pairs={{0,24},{8,16},{16,8},{24,0},{1,25},{9,17},{17,9},{25,1},{2,26},{10... | collective-permute-start | bytes 49160 | tf_op jit(solution)/shard_map/ppermute | solution.py:102
  117.1 5.2 %collective-permute-start.70 = (f32[8,128]{1,0:T(8,128)S(1)}, f32[8,128]{1,0:T(8,128)S(1)}, u32[]{:S(2)}, u32[]{:S(2)}) collective-permute-start(f32[8,128]{1,0:T(8,128)S(1)} %broadcast_select_fusion), channel_id=1, source_target_pairs={{0,16},{8,24},{16,0},{24,8},{1,17},{9,25},{17,1},{25,9},{2,18},{10... | collective-permute-start | bytes 12296 | tf_op jit(solution)/shard_map/ppermute | solution.py:102
  117.4 7.7 %collective-permute-start.71 = (f32[8,128]{1,0:T(8,128)S(1)}, f32[8,128]{1,0:T(8,128)S(1)}, u32[]{:S(2)}, u32[]{:S(2)}) collective-permute-start(f32[8,128]{1,0:T(8,128)S(1)} %broadcast_select_fusion), channel_id=1, source_target_pairs={{0,24},{8,16},{16,8},{24,0},{1,25},{9,17},{17,9},{25,1},{2,26},{10... | collective-permute-start | bytes 12296 | tf_op jit(solution)/shard_map/ppermute | solution.py:102
  118.8 6.3 %collective-permute-start.69 = (f32[8,128]{1,0:T(8,128)S(1)}, f32[8,128]{1,0:T(8,128)S(1)}, u32[]{:S(2)}, u32[]{:S(2)}) collective-permute-start(f32[8,128]{1,0:T(8,128)S(1)} %broadcast_select_fusion), channel_id=1, source_target_pairs={{0,8},{8,0},{16,24},{24,16},{1,9},{9,1},{17,25},{25,17},{2,10},{10... | collective-permute-start | bytes 12296 | tf_op jit(solution)/shard_map/ppermute | solution.py:102
  120.7 10.1 %collective-permute-start.48 = (bf16[32,128]{1,0:T(8,128)(2,1)S(1)}, bf16[32,128]{1,0:T(8,128)(2,1)S(1)}, u32[]{:S(2)}, u32[]{:S(2)}) collective-permute-start(bf16[32,128]{1,0:T(8,128)(2,1)S(1)} %convert_element_type.45.refs_6_), channel_id=1, source_target_pairs={{0,24},{8,16},{16,8},{24,0},{1,25},{9,17},{17,9},{25,1},{2,26},{10... | collective-permute-start | bytes 24584 | tf_op jit(solution)/shard_map/ppermute | solution.py:102
  122.2 9.4 %collective-permute-start.47 = (bf16[32,128]{1,0:T(8,128)(2,1)S(1)}, bf16[32,128]{1,0:T(8,128)(2,1)S(1)}, u32[]{:S(2)}, u32[]{:S(2)}) collective-permute-start(bf16[32,128]{1,0:T(8,128)(2,1)S(1)} %convert_element_type.45.refs_6_), channel_id=1, source_target_pairs={{0,16},{8,24},{16,0},{24,8},{1,17},{9,25},{17,1},{25,9},{2,18},{10... | collective-permute-start | bytes 24584 | tf_op jit(solution)/shard_map/ppermute | solution.py:102
  122.3 10.3 %collective-permute-start.46 = (bf16[32,128]{1,0:T(8,128)(2,1)S(1)}, bf16[32,128]{1,0:T(8,128)(2,1)S(1)}, u32[]{:S(2)}, u32[]{:S(2)}) collective-permute-start(bf16[32,128]{1,0:T(8,128)(2,1)S(1)} %convert_element_type.45.refs_6_), channel_id=1, source_target_pairs={{0,8},{8,0},{16,24},{24,16},{1,9},{9,1},{17,25},{25,17},{2,10},{10... | collective-permute-start | bytes 24584 | tf_op jit(solution)/shard_map/ppermute | solution.py:102
  125.1 4.0 %collective-permute-start.78 = (f32[8,128]{1,0:T(8,128)S(1)}, f32[8,128]{1,0:T(8,128)S(1)}, u32[]{:S(2)}, u32[]{:S(2)}) collective-permute-start(f32[8,128]{1,0:T(8,128)S(1)} %add_add_fusion.5), channel_id=1, source_target_pairs={{0,7},{1,6},{2,5},{3,4},{4,3},{5,2},{6,1},{7,0},{8,15},{9,14},{10,... | collective-permute-start | bytes 12296 | tf_op jit(solution)/shard_map/ppermute | solution.py:102
  125.2 4.6 %collective-permute-start.77 = (f32[8,128]{1,0:T(8,128)S(1)}, f32[8,128]{1,0:T(8,128)S(1)}, u32[]{:S(2)}, u32[]{:S(2)}) collective-permute-start(f32[8,128]{1,0:T(8,128)S(1)} %add_add_fusion.5), channel_id=1, source_target_pairs={{0,6},{1,7},{2,4},{3,5},{4,2},{5,3},{6,0},{7,1},{8,14},{9,15},{10,... | collective-permute-start | bytes 12296 | tf_op jit(solution)/shard_map/ppermute | solution.py:102
  129.1 8.2 %collective-permute-start.76 = (f32[8,128]{1,0:T(8,128)S(1)}, f32[8,128]{1,0:T(8,128)S(1)}, u32[]{:S(2)}, u32[]{:S(2)}) collective-permute-start(f32[8,128]{1,0:T(8,128)S(1)} %add_add_fusion.5), channel_id=1, source_target_pairs={{0,5},{1,4},{2,7},{3,6},{4,1},{5,0},{6,3},{7,2},{8,13},{9,12},{10,... | collective-permute-start | bytes 12296 | tf_op jit(solution)/shard_map/ppermute | solution.py:102
  129.8 7.8 %collective-permute-start.75 = (f32[8,128]{1,0:T(8,128)S(1)}, f32[8,128]{1,0:T(8,128)S(1)}, u32[]{:S(2)}, u32[]{:S(2)}) collective-permute-start(f32[8,128]{1,0:T(8,128)S(1)} %add_add_fusion.5), channel_id=1, source_target_pairs={{0,4},{1,5},{2,6},{3,7},{4,0},{5,1},{6,2},{7,3},{8,12},{9,13},{10,... | collective-permute-start | bytes 12296 | tf_op jit(solution)/shard_map/ppermute | solution.py:102
  130.8 8.7 %collective-permute-start.74 = (f32[8,128]{1,0:T(8,128)S(1)}, f32[8,128]{1,0:T(8,128)S(1)}, u32[]{:S(2)}, u32[]{:S(2)}) collective-permute-start(f32[8,128]{1,0:T(8,128)S(1)} %add_add_fusion.5), channel_id=1, source_target_pairs={{0,3},{1,2},{2,1},{3,0},{4,7},{5,6},{6,5},{7,4},{8,11},{9,10},{10,... | collective-permute-start | bytes 12296 | tf_op jit(solution)/shard_map/ppermute | solution.py:102
  131.6 10.2 %collective-permute-start.73 = (f32[8,128]{1,0:T(8,128)S(1)}, f32[8,128]{1,0:T(8,128)S(1)}, u32[]{:S(2)}, u32[]{:S(2)}) collective-permute-start(f32[8,128]{1,0:T(8,128)S(1)} %add_add_fusion.5), channel_id=1, source_target_pairs={{0,2},{1,3},{2,0},{3,1},{4,6},{5,7},{6,4},{7,5},{8,10},{9,11},{10,... | collective-permute-start | bytes 12296 | tf_op jit(solution)/shard_map/ppermute | solution.py:102
  132.6 9.2 %collective-permute-start.72 = (f32[8,128]{1,0:T(8,128)S(1)}, f32[8,128]{1,0:T(8,128)S(1)}, u32[]{:S(2)}, u32[]{:S(2)}) collective-permute-start(f32[8,128]{1,0:T(8,128)S(1)} %add_add_fusion.5), channel_id=1, source_target_pairs={{0,1},{1,0},{2,3},{3,2},{4,5},{5,4},{6,7},{7,6},{8,9},{9,8},{10,11... | collective-permute-start | bytes 12296 | tf_op jit(solution)/shard_map/ppermute | solution.py:102
  137.3 6.9 %collective-permute-start.44 = (f32[32,128]{1,0:T(8,128)S(1)}, f32[32,128]{1,0:T(8,128)S(1)}, u32[]{:S(2)}, u32[]{:S(2)}) collective-permute-start(f32[32,128]{1,0:T(8,128)S(1)} %get-tuple-element.111), channel_id=1, source_target_pairs={{0,16},{8,24},{16,0},{24,8},{1,17},{9,25},{17,1},{25,9},{2,18},{10... | collective-permute-start | bytes 49160 | tf_op jit(solution)/shard_map/ppermute | solution.py:102
  137.6 5.7 %collective-permute-start.43 = (f32[32,128]{1,0:T(8,128)S(1)}, f32[32,128]{1,0:T(8,128)S(1)}, u32[]{:S(2)}, u32[]{:S(2)}) collective-permute-start(f32[32,128]{1,0:T(8,128)S(1)} %get-tuple-element.111), channel_id=1, source_target_pairs={{0,8},{8,0},{16,24},{24,16},{1,9},{9,1},{17,25},{25,17},{2,10},{10... | collective-permute-start | bytes 49160 | tf_op jit(solution)/shard_map/ppermute | solution.py:102
  139.5 5.7 %collective-permute-start.45 = (f32[32,128]{1,0:T(8,128)S(1)}, f32[32,128]{1,0:T(8,128)S(1)}, u32[]{:S(2)}, u32[]{:S(2)}) collective-permute-start(f32[32,128]{1,0:T(8,128)S(1)} %get-tuple-element.111), channel_id=1, source_target_pairs={{0,24},{8,16},{16,8},{24,0},{1,25},{9,17},{17,9},{25,1},{2,26},{10... | collective-permute-start | bytes 49160 | tf_op jit(solution)/shard_map/ppermute | solution.py:102
  141.8 4.1 %collective-permute-start.49 = (f32[16,128]{1,0:T(8,128)S(1)}, f32[16,128]{1,0:T(8,128)S(1)}, u32[]{:S(2)}, u32[]{:S(2)}) collective-permute-start(f32[16,128]{1,0:T(8,128)S(1)} %get-tuple-element.80), channel_id=1, source_target_pairs={{0,1},{1,0},{2,3},{3,2},{4,5},{5,4},{6,7},{7,6},{8,9},{9,8},{10,11... | collective-permute-start | bytes 24584 | tf_op jit(solution)/shard_map/ppermute | solution.py:102
  141.8 5.5 %collective-permute-start.50 = (f32[16,128]{1,0:T(8,128)S(1)}, f32[16,128]{1,0:T(8,128)S(1)}, u32[]{:S(2)}, u32[]{:S(2)}) collective-permute-start(f32[16,128]{1,0:T(8,128)S(1)} %get-tuple-element.81), channel_id=1, source_target_pairs={{0,2},{1,3},{2,0},{3,1},{4,6},{5,7},{6,4},{7,5},{8,10},{9,11},{10,... | collective-permute-start | bytes 24584 | tf_op jit(solution)/shard_map/ppermute | solution.py:102
  143.3 5.3 %collective-permute-start.51 = (f32[16,128]{1,0:T(8,128)S(1)}, f32[16,128]{1,0:T(8,128)S(1)}, u32[]{:S(2)}, u32[]{:S(2)}) collective-permute-start(f32[16,128]{1,0:T(8,128)S(1)} %get-tuple-element.82), channel_id=1, source_target_pairs={{0,3},{1,2},{2,1},{3,0},{4,7},{5,6},{6,5},{7,4},{8,11},{9,10},{10,... | collective-permute-start | bytes 24584 | tf_op jit(solution)/shard_map/ppermute | solution.py:102
  144.2 4.4 %collective-permute-start.52 = (f32[16,128]{1,0:T(8,128)S(1)}, f32[16,128]{1,0:T(8,128)S(1)}, u32[]{:S(2)}, u32[]{:S(2)}) collective-permute-start(f32[16,128]{1,0:T(8,128)S(1)} %get-tuple-element.83), channel_id=1, source_target_pairs={{0,4},{1,5},{2,6},{3,7},{4,0},{5,1},{6,2},{7,3},{8,12},{9,13},{10,... | collective-permute-start | bytes 24584 | tf_op jit(solution)/shard_map/ppermute | solution.py:102
  145.9 4.6 %collective-permute-start.54 = (f32[16,128]{1,0:T(8,128)S(1)}, f32[16,128]{1,0:T(8,128)S(1)}, u32[]{:S(2)}, u32[]{:S(2)}) collective-permute-start(f32[16,128]{1,0:T(8,128)S(1)} %get-tuple-element.85), channel_id=1, source_target_pairs={{0,6},{1,7},{2,4},{3,5},{4,2},{5,3},{6,0},{7,1},{8,14},{9,15},{10,... | collective-permute-start | bytes 24584 | tf_op jit(solution)/shard_map/ppermute | solution.py:102
  (32 other events, 319.8 us)

commit v2 on v1

v2 whole, which is shorter than its diff:
```python
import functools
import math

import jax
import jax.numpy as jnp
from jax import lax
from jax.experimental import pallas as pl
from jax.experimental.pallas import tpu as pltpu
from jax.sharding import PartitionSpec as P

LANES = 128
VMEM = pl.BlockSpec(memory_space=pltpu.VMEM)
SMEM = pl.BlockSpec(memory_space=pltpu.SMEM)
GRANT = 32 * 1024 * 1024


def accumulate(transpose, in_index, out_index, count, tiles, source, total):
    slots, width, _ = tiles.shape
    per_block = width // LANES
    vectors = total.shape[0]
    total[...] = jnp.zeros_like(total)
    live_count = count[0, 0]
    rows = max(8, vectors)
    for slot in range(slots):
        start = in_index[0, 0, slot] * per_block
        place = out_index[0, 0, slot] * per_block
        live = (live_count > slot).astype(jnp.float32)
        halves = []
        for half in range(per_block):
            if vectors == 1:
                halves.append(source[0, pl.ds(start + half, 1), :])
            else:
                which = lax.broadcasted_iota(jnp.int32, (rows, LANES), 0)
                stacked = jnp.zeros((rows, LANES), jnp.float32)
                for vector in range(vectors):
                    line = source[vector, pl.ds(start + half, 1), :]
                    stacked = jnp.where(which == vector, line, stacked)
                halves.append(stacked)
        block = (jnp.concatenate(halves, axis=1) * live).astype(jnp.bfloat16)
        contract = ((1,), (0,)) if transpose else ((1,), (1,))
        product = lax.dot_general(
            block, tiles[slot], (contract, ((), ())), preferred_element_type=jnp.float32
        )
        for vector in range(vectors):
            for half in range(per_block):
                at = pl.ds(place + half, 1)
                total[vector, at, :] += product[
                    vector : vector + 1, half * LANES : (half + 1) * LANES
                ]


def apply_body(transpose, in_index, out_index, count, tiles, parts, out, source, total):
    for part in range(parts.shape[0]):
        length = parts.shape[2]
        source[:, part * length : (part + 1) * length, :] = parts[part].astype(jnp.float32)
    accumulate(transpose, in_index, out_index, count, tiles, source, total)
    size = out.shape[2]
    for part in range(out.shape[0]):
        out[part] = total[:, part * size : (part + 1) * size, :]


def apply_tiles(transpose, grid, parts, out_rows, parts_out, name):
    tiles, row_blocks, column_blocks, count = grid
    parts_in, vectors, length, _ = parts.shape
    shape = (parts_out, vectors, out_rows // parts_out, LANES)
    order = (row_blocks, column_blocks) if transpose else (column_blocks, row_blocks)
    return pl.pallas_call(
        functools.partial(apply_body, transpose),
        out_shape=jax.ShapeDtypeStruct(shape, jnp.float32),
        in_specs=[SMEM] * 3 + [VMEM] * 2,
        out_specs=VMEM,
        scratch_shapes=[
            pltpu.VMEM((vectors, parts_in * length, LANES), jnp.float32),
            pltpu.VMEM((vectors, out_rows, LANES), jnp.float32),
        ],
        compiler_params=pltpu.CompilerParams(vmem_limit_bytes=GRANT),
        cost_estimate=pl.CostEstimate(
            flops=2 * tiles.size * vectors, bytes_accessed=2 * tiles.size, transcendentals=0
        ),
        name=name,
    )(*order, count, tiles, parts)


def scatter_sum(parts, axis):
    return lax.all_to_all(parts, axis, 0, 0).sum(axis=0)


def gather(part, axis):
    size = lax.axis_size(axis)
    return lax.all_to_all(jnp.broadcast_to(part, (size,) + part.shape), axis, 0, 0)


def local(
    tile_data,
    tile_row_block,
    tile_column_block,
    tile_count,
    saved_primal,
    saved_dual,
    primal_mask,
    dual_mask,
    cost_vector,
    demand,
    upper_bound,
    step_sizes,
    primal_cotangent,
    dual_cotangent,
):
    slot_count = tile_data.shape[2]
    tile_width = tile_data.shape[-1]
    tiles = tile_data.reshape(slot_count, tile_width, tile_width)
    grid = (tiles, tile_row_block, tile_column_block, tile_count)
    iterations = saved_primal.shape[0]
    row_length = saved_dual.shape[1]
    column_length = saved_primal.shape[1]
    n_row = lax.axis_size("row")
    n_col = lax.axis_size("col")
    me_row = lax.axis_index("row")
    me_col = lax.axis_index("col")
    lines_y = row_length // LANES
    lines_x = column_length // LANES
    share_y = lines_y // n_col
    share_x = lines_x // n_row
    tau = step_sizes[0]
    sigma = step_sizes[1]

    def own_y(array):
        lead = array.shape[:-1]
        array = array.reshape(lead + (lines_y, LANES))
        return lax.dynamic_slice_in_dim(array, me_col * share_y, share_y, len(lead))

    def own_x(array):
        lead = array.shape[:-1]
        array = array.reshape(lead + (lines_x, LANES))
        return lax.dynamic_slice_in_dim(array, me_row * share_x, share_x, len(lead))

    def weight_of(step):
        return (step + 1.0) / (step + 2.0)

    last = iterations - 1
    first_term = (
        dual_mask[last].astype(jnp.float32) * weight_of(last) * dual_cotangent
    ).reshape(1, 1, lines_y, LANES)
    first_part = first_term.astype(jnp.bfloat16)
    back_parts = apply_tiles(True, grid, first_part, lines_x, n_row, "back_first")

    saved = saved_dual.astype(jnp.bfloat16).reshape(1, iterations, lines_y, LANES)
    saved_parts = apply_tiles(True, grid, saved, lines_x, n_row, "back_saved")

    adjoint_x = own_x(primal_cotangent)
    adjoint_y = own_y(dual_cotangent)
    masks_x = own_x(primal_mask).astype(jnp.float32)
    masks_y = own_y(dual_mask).astype(jnp.float32)
    anchor_x = jnp.zeros_like(adjoint_x)
    anchor_y = jnp.zeros_like(adjoint_y)
    tau_terms = []
    sigma_terms = []
    reduced = None
    for step in reversed(range(iterations)):
        weight = weight_of(step)
        anchor_x = anchor_x + (1.0 - weight) * adjoint_x
        anchor_y = anchor_y + (1.0 - weight) * adjoint_y
        dual_term = masks_y[step] * weight * adjoint_y
        sigma_terms.append((step, dual_term))
        if back_parts is None:
            gathered = gather(dual_term.astype(jnp.bfloat16)[None], "col")
            back_parts = apply_tiles(True, grid, gathered, lines_x, n_row, f"back_{step}")
        back = scatter_sum(back_parts, "row")[0]
        back_parts = None
        primal_term = masks_x[step] * (weight * adjoint_x - 2.0 * sigma * back)
        tau_terms.append((step, primal_term))
        adjoint_x = primal_term + sigma * back
        gathered = gather(primal_term.astype(jnp.bfloat16)[None], "row")
        image_parts = apply_tiles(False, grid, gathered, lines_y, n_col, f"image_{step}")
        if reduced is None:
            reduced = own_x(cost_vector) - scatter_sum(saved_parts, "row")
            primal = own_x(saved_primal)
            half = jnp.clip(primal - tau * reduced, 0.0, own_x(upper_bound))
            extrapolated = (2.0 * half - primal).astype(jnp.bfloat16)
            extrapolated = gather(extrapolated, "row")
            residual_parts = apply_tiles(
                False, grid, extrapolated, lines_y, n_col, "image_saved"
            )
        image = scatter_sum(image_parts, "col")[0]
        adjoint_y = dual_term + tau * image
    residual = own_y(demand) - scatter_sum(residual_parts, "col")

    tau_sum = -sum(jnp.sum(term * reduced[step]) for step, term in tau_terms)
    sigma_sum = sum(jnp.sum(term * residual[step]) for step, term in sigma_terms)
    sums = jnp.stack([tau_sum, sigma_sum])
    spots = lax.broadcasted_iota(jnp.int32, (8, LANES), 1)
    packed = jnp.where(spots == 0, sums[0], jnp.where(spots == 1, sums[1], 0.0))
    packed = gather(packed, "row").sum(axis=0)
    packed = gather(packed, "col").sum(axis=0)
    total_columns = column_length * n_col
    total_rows = row_length * n_row
    scales = jnp.array(
        [1.0 / math.sqrt(total_columns), 1.0 / math.sqrt(total_rows)], jnp.float32
    )
    gradients = packed[0, :2] * scales

    primal_adjoint = gather(adjoint_x + anchor_x, "row").reshape(column_length)
    dual_adjoint = (adjoint_y + anchor_y).reshape(row_length // n_col)
    return (primal_adjoint, dual_adjoint, gradients)


def solution(mesh):
    placed = (
        P("row", "col", None, None, None),
        P("row", "col", None),
        P("row", "col", None),
        P("row", "col"),
        P(None, "col"),
        P(None, "row"),
        P(None, "col"),
        P(None, "row"),
        P("col"),
        P("row"),
        P("col"),
        P(),
        P("col"),
        P("row"),
    )
    return jax.shard_map(
        local,
        mesh=mesh,
        in_specs=placed,
        out_specs=(P("col"), P(("row", "col")), P()),
        check_vma=False,
    )
```

time: 154 us -> 189 us (1.23)
  waiting for transfers between devices: 24.7 us -> 61.7 us
  starting transfers between devices: 87.8 us -> 57.9 us
  local copies, waits for them, and re-layouts: 11.5 us -> 25.9 us
  blocking collectives: 0 us -> 7.2 us
  Pallas kernels: 11.9 us -> 17.1 us
    ppermute x79 -> x0, starting transfers between devices: 87.8 us -> none  [exchange(): lax.ppermute(parts[k], axis, [(i, i ^ k) for i in range(size)])]
    all_to_all x0 -> x16, waiting for transfers between devices: none -> 61.7 us  [the longest x8 34.8 us: scatter_sum(): return lax.all_to_all(parts, axis, 0, 0).sum(axis=0)]
    all_to_all x0 -> x16, starting transfers between devices: none -> 57.9 us  [the longest x8 31.5 us: scatter_sum(): return lax.all_to_all(parts, axis, 0, 0).sum(axis=0)]
    ppermute x79 -> x0, waiting for transfers between devices: 24.7 us -> none  [exchange(): lax.ppermute(parts[k], axis, [(i, i ^ k) for i in range(size)])]
    unnamed x38 -> x45, local copies, waits for them, and re-layouts: 10.2 us -> 19.5 us
    all_to_all x0 -> x1, blocking collectives: none -> 7.2 us  [gather(): lax.all_to_all(jnp.broadcast_to(part, (size,) + part.shape), axis, 0, 0)]
    pallas_call x8, Pallas kernels: 11.9 us -> 17.1 us  [apply_tiles(): pl.pallas_call(functools.partial(apply_body, transpose), out_shape=jax.Sh...]
    broadcast_in_dim x1 -> x9, local copies, waits for them, and re-layouts: 0.01 us -> 4.99 us  [gather(): jnp.broadcast_to(part, (size,) + part.shape)]
  transfers between devices with their start and end apart: 79 -> 16, of which waited for: 18 -> 16; matrix products, arithmetic and copies ran while one was open for 3% -> 2% of each run, Pallas kernels for 6% -> 6%
where the time goes in v2:
time: 189 us; the launch traced here: 186 us
  waiting for transfers between devices  61.7 us (33%)
  starting transfers between devices  57.9 us (31%)
  local copies, waits for them, and re-layouts  25.9 us (14%)
  Pallas kernels  17.1 us (9%)
  other arithmetic  10.6 us (6%)
  blocking collectives  7.2 us (4%)
  between operations  6.09 us (3%)
    all_to_all x8, waiting for transfers between devices, scatter_sum(): return lax.all_to_all(parts, axis, 0, 0).sum(axis=0)  34.8 us
    all_to_all x8, starting transfers between devices, scatter_sum(): return lax.all_to_all(parts, axis, 0, 0).sum(axis=0)  31.5 us
    all_to_all x8, waiting for transfers between devices, gather(): lax.all_to_all(jnp.broadcast_to(part, (size,) + part.shape), axis, 0, 0)  26.8 us
    all_to_all x8, starting transfers between devices, gather(): lax.all_to_all(jnp.broadcast_to(part, (size,) + part.shape), axis, 0, 0)  26.3 us
    unnamed x45, local copies, waits for them, and re-layouts  19.5 us
    pallas_call x8, Pallas kernels, apply_tiles(): pl.pallas_call(functools.partial(apply_body, transpose), out_shape=jax.Sh...  17.1 us
    all_to_all x1, blocking collectives, gather(): lax.all_to_all(jnp.broadcast_to(part, (size,) + part.shape), axis, 0, 0)  7.2 us
    broadcast_in_dim x9, local copies, waits for them, and re-layouts, gather(): jnp.broadcast_to(part, (size,) + part.shape)  4.99 us
  transfers between devices with their start and end apart: 16, of which 16 were waited for; matrix products, arithmetic and copies ran while one was open for 2% of the time, Pallas kernels for 6%

profile of v2, /device:TPU:0, one launch (start us, length us, event | category | flops | bytes accessed | tf_op | source)
XLA Modules:
  0.0 186.4 jit_solution(131276573561485340)
XLA Ops:
  1.4 1.0 convert_multiply_fusion
  2.4 0.9 fusion.parts
  3.3 2.2 %copy-done.1 = bf16[1,1,32,256,256]{4,3,2,1,0:T(8,128)(2,1)S(1)} copy-done((bf16[1,1,32,256,256]{4,3,2,1,0:T(8,128)(2,1)S(1)}, bf16[1,1,32,256,256]{4,3,2,1,0:T(8,128)(2,1)}, u32[]{:S(2)}) %copy-start.1) | copy-done | bytes 4194328
  5.5 0.7 copy-done.9
  6.1 0.7 copy-done.11
  6.8 1.8 back_first.1
  8.6 6.3 %all-to-all-start = ((f32[4,1,32,128]{3,2,1,0:T(8,128)}), f32[4,1,32,128]{3,2,1,0:T(8,128)S(1)}, u32[]{:S(2)}, u32[]{:S(2)}) async-start(f32[4,1,32,128]{3,2,1,0:T(8,128)} %back_first.1), calls=%async_computation | async-start | bytes 131072 | tf_op jit(solution)/shard_map/all_to_all | solution.py:85
  16.3 4.5 %all-to-all-done = f32[4,1,32,128]{3,2,1,0:T(8,128)S(1)} async-done(((f32[4,1,32,128]{3,2,1,0:T(8,128)}), f32[4,1,32,128]{3,2,1,0:T(8,128)S(1)}, u32[]{:S(2)}, u32[]{:S(2)}) %all-to-all-start) | async-done | bytes 65568 | tf_op jit(solution)/shard_map/all_to_all | solution.py:85
  21.4 3.3 %all-to-all-start.1 = ((bf16[4,1,32,128]{3,2,1,0:T(8,128)(2,1)}), bf16[4,1,32,128]{3,2,1,0:T(8,128)(2,1)S(1)}, u32[]{:S(2)}, u32[]{:S(2)}) async-start(bf16[4,1,32,128]{3,2,1,0:T(8,128)(2,1)} %broadcast_in_dim.48), calls=%async_computation.1 | async-start | bytes 65536 | tf_op jit(solution)/shard_map/all_to_all | solution.py:90
  24.7 5.6 %all-to-all-done.1.parts = bf16[4,1,32,128]{3,2,1,0:T(8,128)(2,1)S(1)} async-done(((bf16[4,1,32,128]{3,2,1,0:T(8,128)(2,1)}), bf16[4,1,32,128]{3,2,1,0:T(8,128)(2,1)S(1)}, u32[]{:S(2)}, u32[]{:S(2)}) %all-to-all-start.1) | async-done | bytes 32800 | tf_op jit(solution)/shard_map/all_to_all | solution.py:90
  30.3 2.2 %copy-done.2 = bf16[1,1,32,256,256]{4,3,2,1,0:T(8,128)(2,1)S(1)} copy-done((bf16[1,1,32,256,256]{4,3,2,1,0:T(8,128)(2,1)S(1)}, bf16[1,1,32,256,256]{4,3,2,1,0:T(8,128)(2,1)}, u32[]{:S(2)}) %copy-start.2) | copy-done | bytes 4194328
  32.5 2.4 %image_2.1 = f32[8,1,16,128]{3,2,1,0:T(8,128)} custom-call(s32[1,1,32]{2,1,0:T(1,128)S(1)} %copy-done.12, s32[1,1,32]{2,1,0:T(1,128)S(1)} %copy-done.10, s32[1,1]{1,0:T(1,128)S(6)} %copy.31.count, bf16[32,256,256]{2,1,0:T(8,128)(2,1)S(1)} %bitcast.102, bf16[4,1,32,128]{3,2,1,0:T(8,128)(2,1)S(1)} %all-to-all-done.1.parts), custom_call_target="tpu_custom_call" | custom-call | flops 4194304 | bytes 4194304 | tf_op jit(solution)/shard_map/image_2/pallas_call | solution.py:67
  34.9 3.7 %all-to-all-start.2 = ((f32[8,1,16,128]{3,2,1,0:T(8,128)}), f32[8,1,16,128]{3,2,1,0:T(8,128)S(1)}, u32[]{:S(2)}, u32[]{:S(2)}) async-start(f32[8,1,16,128]{3,2,1,0:T(8,128)} %image_2.1), calls=%async_computation.2 | async-start | bytes 131072 | tf_op jit(solution)/shard_map/all_to_all | solution.py:85
  38.6 5.0 %all-to-all-done.2 = f32[8,1,16,128]{3,2,1,0:T(8,128)S(1)} async-done(((f32[8,1,16,128]{3,2,1,0:T(8,128)}), f32[8,1,16,128]{3,2,1,0:T(8,128)S(1)}, u32[]{:S(2)}, u32[]{:S(2)}) %all-to-all-start.2) | async-done | bytes 65568 | tf_op jit(solution)/shard_map/all_to_all | solution.py:85
  43.6 1.4 fusion.26
  45.0 0.6 broadcast_in_dim.49
  45.6 3.3 %all-to-all-start.3 = ((bf16[8,1,16,128]{3,2,1,0:T(8,128)(2,1)}), bf16[8,1,16,128]{3,2,1,0:T(8,128)(2,1)S(1)}, u32[]{:S(2)}, u32[]{:S(2)}) async-start(bf16[8,1,16,128]{3,2,1,0:T(8,128)(2,1)} %broadcast_in_dim.49), calls=%async_computation.3 | async-start | bytes 65536 | tf_op jit(solution)/shard_map/all_to_all | solution.py:90
  49.1 2.2 %copy-done.3 = bf16[1,1,32,256,256]{4,3,2,1,0:T(8,128)(2,1)S(1)} copy-done((bf16[1,1,32,256,256]{4,3,2,1,0:T(8,128)(2,1)S(1)}, bf16[1,1,32,256,256]{4,3,2,1,0:T(8,128)(2,1)}, u32[]{:S(2)}) %copy-start.3) | copy-done | bytes 4194328
  51.3 1.9 %back_saved.1 = f32[4,3,32,128]{3,2,1,0:T(8,128)} custom-call(s32[1,1,32]{2,1,0:T(1,128)S(1)} %copy-done.10, s32[1,1,32]{2,1,0:T(1,128)S(1)} %copy-done.12, s32[1,1]{1,0:T(1,128)S(6)} %copy.31.count, bf16[32,256,256]{2,1,0:T(8,128)(2,1)S(1)} %bitcast.103, bf16[1,3,128,128]{3,2,1,0:T(8,128)(2,1)S(1)} %copy.29), custom_call_target="tpu_custom_call" | custom-call | flops 12582912 | bytes 4194304 | tf_op jit(solution)/shard_map/back_saved/pallas_call | solution.py:67
  53.8 3.4 %all-to-all-start.12 = ((f32[4,3,32,128]{3,2,1,0:T(8,128)}), f32[4,3,32,128]{3,2,1,0:T(8,128)S(1)}, u32[]{:S(2)}, u32[]{:S(2)}) async-start(f32[4,3,32,128]{3,2,1,0:T(8,128)} %back_saved.1), calls=%async_computation.12 | async-start | bytes 393216 | tf_op jit(solution)/shard_map/all_to_all | solution.py:85
  57.2 2.2 %copy-done.4 = bf16[1,1,32,256,256]{4,3,2,1,0:T(8,128)(2,1)S(1)} copy-done((bf16[1,1,32,256,256]{4,3,2,1,0:T(8,128)(2,1)S(1)}, bf16[1,1,32,256,256]{4,3,2,1,0:T(8,128)(2,1)}, u32[]{:S(2)}) %copy-start.4) | copy-done | bytes 4194328
  59.4 1.8 back_1.1
  61.2 3.7 %all-to-all-done.12 = f32[4,3,32,128]{3,2,1,0:T(8,128)S(1)} async-done(((f32[4,3,32,128]{3,2,1,0:T(8,128)}), f32[4,3,32,128]{3,2,1,0:T(8,128)S(1)}, u32[]{:S(2)}, u32[]{:S(2)}) %all-to-all-start.12) | async-done | bytes 196640 | tf_op jit(solution)/shard_map/all_to_all | solution.py:85
  64.9 3.3 %all-to-all-start.4 = ((f32[4,1,32,128]{3,2,1,0:T(8,128)}), f32[4,1,32,128]{3,2,1,0:T(8,128)S(1)}, u32[]{:S(2)}, u32[]{:S(2)}) async-start(f32[4,1,32,128]{3,2,1,0:T(8,128)} %back_1.1), calls=%async_computation.4 | async-start | bytes 131072 | tf_op jit(solution)/shard_map/all_to_all | solution.py:85
  68.2 0.7 constant_dynamic-slice_fusion
  68.9 4.9 %all-to-all-done.4 = f32[4,1,32,128]{3,2,1,0:T(8,128)S(1)} async-done(((f32[4,1,32,128]{3,2,1,0:T(8,128)}), f32[4,1,32,128]{3,2,1,0:T(8,128)S(1)}, u32[]{:S(2)}, u32[]{:S(2)}) %all-to-all-start.4) | async-done | bytes 65568 | tf_op jit(solution)/shard_map/all_to_all | solution.py:85
  73.9 0.7 fusion.24
  75.2 3.3 %all-to-all-start.5 = ((bf16[4,1,32,128]{3,2,1,0:T(8,128)(2,1)}), bf16[4,1,32,128]{3,2,1,0:T(8,128)(2,1)S(1)}, u32[]{:S(2)}, u32[]{:S(2)}) async-start(bf16[4,1,32,128]{3,2,1,0:T(8,128)(2,1)} %broadcast_in_dim.50), calls=%async_computation.5 | async-start | bytes 65536 | tf_op jit(solution)/shard_map/all_to_all | solution.py:90
  78.4 0.7 subtract_convert_fusion
  79.2 4.9 %all-to-all-done.5.parts = bf16[4,1,32,128]{3,2,1,0:T(8,128)(2,1)S(1)} async-done(((bf16[4,1,32,128]{3,2,1,0:T(8,128)(2,1)}), bf16[4,1,32,128]{3,2,1,0:T(8,128)(2,1)S(1)}, u32[]{:S(2)}, u32[]{:S(2)}) %all-to-all-start.5) | async-done | bytes 32800 | tf_op jit(solution)/shard_map/all_to_all | solution.py:90
  84.1 0.6 broadcast_in_dim.55
  84.7 3.3 %all-to-all-start.13 = ((bf16[4,3,32,128]{3,2,1,0:T(8,128)(2,1)}), bf16[4,3,32,128]{3,2,1,0:T(8,128)(2,1)S(1)}, u32[]{:S(2)}, u32[]{:S(2)}) async-start(bf16[4,3,32,128]{3,2,1,0:T(8,128)(2,1)} %broadcast_in_dim.55), calls=%async_computation.13 | async-start | bytes 196608 | tf_op jit(solution)/shard_map/all_to_all | solution.py:90
  88.0 2.2 %copy-done.5 = bf16[1,1,32,256,256]{4,3,2,1,0:T(8,128)(2,1)S(1)} copy-done((bf16[1,1,32,256,256]{4,3,2,1,0:T(8,128)(2,1)S(1)}, bf16[1,1,32,256,256]{4,3,2,1,0:T(8,128)(2,1)}, u32[]{:S(2)}) %copy-start.5) | copy-done | bytes 4194328
  90.2 2.4 %image_1.1 = f32[8,1,16,128]{3,2,1,0:T(8,128)} custom-call(s32[1,1,32]{2,1,0:T(1,128)S(1)} %copy-done.12, s32[1,1,32]{2,1,0:T(1,128)S(1)} %copy-done.10, s32[1,1]{1,0:T(1,128)S(6)} %copy.31.count, bf16[32,256,256]{2,1,0:T(8,128)(2,1)S(1)} %bitcast.105, bf16[4,1,32,128]{3,2,1,0:T(8,128)(2,1)S(1)} %all-to-all-done.5.parts), custom_call_target="tpu_custom_call" | custom-call | flops 4194304 | bytes 4194304 | tf_op jit(solution)/shard_map/image_1/pallas_call | solution.py:67
  92.6 1.2 all-to-all-done.13.parts
  93.8 3.8 %all-to-all-start.6 = ((f32[8,1,16,128]{3,2,1,0:T(8,128)}), f32[8,1,16,128]{3,2,1,0:T(8,128)S(1)}, u32[]{:S(2)}, u32[]{:S(2)}) async-start(f32[8,1,16,128]{3,2,1,0:T(8,128)} %image_1.1), calls=%async_computation.6 | async-start | bytes 131072 | tf_op jit(solution)/shard_map/all_to_all | solution.py:85
  97.6 2.2 %copy-done.6 = bf16[1,1,32,256,256]{4,3,2,1,0:T(8,128)(2,1)S(1)} copy-done((bf16[1,1,32,256,256]{4,3,2,1,0:T(8,128)(2,1)S(1)}, bf16[1,1,32,256,256]{4,3,2,1,0:T(8,128)(2,1)}, u32[]{:S(2)}) %copy-start.6) | copy-done | bytes 4194328
  99.8 2.5 %image_saved.1 = f32[8,3,16,128]{3,2,1,0:T(8,128)} custom-call(s32[1,1,32]{2,1,0:T(1,128)S(1)} %copy-done.12, s32[1,1,32]{2,1,0:T(1,128)S(1)} %copy-done.10, s32[1,1]{1,0:T(1,128)S(6)} %copy.31.count, bf16[32,256,256]{2,1,0:T(8,128)(2,1)S(1)} %bitcast.106, bf16[4,3,32,128]{3,2,1,0:T(8,128)(2,1)S(1)} %all-to-all-done.13.parts), custom_call_target="tpu_custom_call" | custom-call | flops 12582912 | bytes 4194304 | tf_op jit(solution)/shard_map/image_saved/pallas_call | solution.py:67
  102.7 3.8 %all-to-all-start.14 = ((f32[8,3,16,128]{3,2,1,0:T(8,128)}), f32[8,3,16,128]{3,2,1,0:T(8,128)S(1)}, u32[]{:S(2)}, u32[]{:S(2)}) async-start(f32[8,3,16,128]{3,2,1,0:T(8,128)} %image_saved.1), calls=%async_computation.14 | async-start | bytes 393216 | tf_op jit(solution)/shard_map/all_to_all | solution.py:85
  106.5 6.2 %all-to-all-done.14 = f32[8,3,16,128]{3,2,1,0:T(8,128)S(1)} async-done(((f32[8,3,16,128]{3,2,1,0:T(8,128)}), f32[8,3,16,128]{3,2,1,0:T(8,128)S(1)}, u32[]{:S(2)}, u32[]{:S(2)}) %all-to-all-start.14) | async-done | bytes 196640 | tf_op jit(solution)/shard_map/all_to_all | solution.py:85
  112.8 1.3 fusion.11
  114.1 0.6 broadcast_in_dim.51
  114.7 3.3 %all-to-all-start.7 = ((bf16[8,1,16,128]{3,2,1,0:T(8,128)(2,1)}), bf16[8,1,16,128]{3,2,1,0:T(8,128)(2,1)S(1)}, u32[]{:S(2)}, u32[]{:S(2)}) async-start(bf16[8,1,16,128]{3,2,1,0:T(8,128)(2,1)} %broadcast_in_dim.51), calls=%async_computation.7 | async-start | bytes 65536 | tf_op jit(solution)/shard_map/all_to_all | solution.py:90
  119.9 2.9 %all-to-all-done.7.parts = bf16[8,1,16,128]{3,2,1,0:T(8,128)(2,1)S(1)} async-done(((bf16[8,1,16,128]{3,2,1,0:T(8,128)(2,1)}), bf16[8,1,16,128]{3,2,1,0:T(8,128)(2,1)S(1)}, u32[]{:S(2)}, u32[]{:S(2)}) %all-to-all-start.7) | async-done | bytes 32800 | tf_op jit(solution)/shard_map/all_to_all | solution.py:90
  122.8 2.2 %copy-done.7 = bf16[1,1,32,256,256]{4,3,2,1,0:T(8,128)(2,1)S(1)} copy-done((bf16[1,1,32,256,256]{4,3,2,1,0:T(8,128)(2,1)S(1)}, bf16[1,1,32,256,256]{4,3,2,1,0:T(8,128)(2,1)}, u32[]{:S(2)}) %copy-start.7) | copy-done | bytes 4194328
  125.0 1.8 back_0.1
  126.9 3.8 %all-to-all-start.8 = ((f32[4,1,32,128]{3,2,1,0:T(8,128)}), f32[4,1,32,128]{3,2,1,0:T(8,128)S(1)}, u32[]{:S(2)}, u32[]{:S(2)}) async-start(f32[4,1,32,128]{3,2,1,0:T(8,128)} %back_0.1), calls=%async_computation.8 | async-start | bytes 131072 | tf_op jit(solution)/shard_map/all_to_all | solution.py:85
  130.7 5.7 %all-to-all-done.8 = f32[4,1,32,128]{3,2,1,0:T(8,128)S(1)} async-done(((f32[4,1,32,128]{3,2,1,0:T(8,128)}), f32[4,1,32,128]{3,2,1,0:T(8,128)S(1)}, u32[]{:S(2)}, u32[]{:S(2)}) %all-to-all-start.8) | async-done | bytes 65568 | tf_op jit(solution)/shard_map/all_to_all | solution.py:85
  136.5 1.3 fusion.2
  140.2 3.3 %all-to-all-start.15 = ((f32[4,8,128]{2,1,0:T(8,128)}), f32[4,8,128]{2,1,0:T(8,128)S(1)}, u32[]{:S(2)}, u32[]{:S(2)}) async-start(f32[4,8,128]{2,1,0:T(8,128)} %broadcast_in_dim.58), calls=%async_computation.15 | async-start | bytes 32768 | tf_op jit(solution)/shard_map/all_to_all | solution.py:90
  143.5 0.7 fusion.31
  144.2 4.9 %all-to-all-done.15 = f32[4,8,128]{2,1,0:T(8,128)S(1)} async-done(((f32[4,8,128]{2,1,0:T(8,128)}), f32[4,8,128]{2,1,0:T(8,128)S(1)}, u32[]{:S(2)}, u32[]{:S(2)}) %all-to-all-start.15) | async-done | bytes 16416 | tf_op jit(solution)/shard_map/all_to_all | solution.py:90
  149.7 3.3 %all-to-all-start.10 = ((bf16[4,1,32,128]{3,2,1,0:T(8,128)(2,1)}), bf16[4,1,32,128]{3,2,1,0:T(8,128)(2,1)S(1)}, u32[]{:S(2)}, u32[]{:S(2)}) async-start(bf16[4,1,32,128]{3,2,1,0:T(8,128)(2,1)} %broadcast_in_dim.53), calls=%async_computation.10 | async-start | bytes 65536 | tf_op jit(solution)/shard_map/all_to_all | solution.py:90
  153.0 5.6 %all-to-all-done.10.parts = bf16[4,1,32,128]{3,2,1,0:T(8,128)(2,1)S(1)} async-done(((bf16[4,1,32,128]{3,2,1,0:T(8,128)(2,1)}), bf16[4,1,32,128]{3,2,1,0:T(8,128)(2,1)S(1)}, u32[]{:S(2)}, u32[]{:S(2)}) %all-to-all-start.10) | async-done | bytes 32800 | tf_op jit(solution)/shard_map/all_to_all | solution.py:90
  158.6 7.2 %all_to_all.85 = f32[8,8,128]{2,1,0:T(8,128)S(1)} all-to-all(f32[8,8,128]{2,1,0:T(8,128)S(1)} %broadcast_in_dim.59), channel_id=1, replica_groups=mesh['row'=4,'col'=8] {'col'}, dimensions={0} | all-to-all | bytes 65536 | tf_op jit(solution)/shard_map/all_to_all | solution.py:90
  165.8 0.6 broadcast_in_dim.52
  166.4 3.3 %all-to-all-start.9 = ((f32[4,32,128]{2,1,0:T(8,128)}), f32[4,32,128]{2,1,0:T(8,128)S(1)}, u32[]{:S(2)}, u32[]{:S(2)}) async-start(f32[4,32,128]{2,1,0:T(8,128)} %broadcast_in_dim.52), calls=%async_computation.9 | async-start | bytes 131072 | tf_op jit(solution)/shard_map/all_to_all | solution.py:90
  169.7 2.2 %copy-done.8 = bf16[1,1,32,256,256]{4,3,2,1,0:T(8,128)(2,1)S(1)} copy-done((bf16[1,1,32,256,256]{4,3,2,1,0:T(8,128)(2,1)S(1)}, bf16[1,1,32,256,256]{4,3,2,1,0:T(8,128)(2,1)}, u32[]{:S(2)}) %copy-start.8) | copy-done | bytes 4194328
  171.9 2.4 %image_0.1 = f32[8,1,16,128]{3,2,1,0:T(8,128)} custom-call(s32[1,1,32]{2,1,0:T(1,128)S(1)} %copy-done.12, s32[1,1,32]{2,1,0:T(1,128)S(1)} %copy-done.10, s32[1,1]{1,0:T(1,128)S(6)} %copy.31.count, bf16[32,256,256]{2,1,0:T(8,128)(2,1)S(1)} %bitcast.108, bf16[4,1,32,128]{3,2,1,0:T(8,128)(2,1)S(1)} %all-to-all-done.10.parts), custom_call_target="tpu_custom_call" | custom-call | flops 4194304 | bytes 4194304 | tf_op jit(solution)/shard_map/image_0/pallas_call | solution.py:67
  174.3 1.1 all-to-all-done.9
  175.4 3.3 %all-to-all-start.11 = ((f32[8,1,16,128]{3,2,1,0:T(8,128)}), f32[8,1,16,128]{3,2,1,0:T(8,128)S(1)}, u32[]{:S(2)}, u32[]{:S(2)}) async-start(f32[8,1,16,128]{3,2,1,0:T(8,128)} %image_0.1), calls=%async_computation.11 | async-start | bytes 131072 | tf_op jit(solution)/shard_map/all_to_all | solution.py:85
  179.3 4.4 %all-to-all-done.11 = f32[8,1,16,128]{3,2,1,0:T(8,128)S(1)} async-done(((f32[8,1,16,128]{3,2,1,0:T(8,128)}), f32[8,1,16,128]{3,2,1,0:T(8,128)S(1)}, u32[]{:S(2)}, u32[]{:S(2)}) %all-to-all-start.11) | async-done | bytes 65568 | tf_op jit(solution)/shard_map/all_to_all | solution.py:85
  183.7 2.0 %add_bitcast_fusion = f32[2048]{0:T(1024)} fusion(f32[16,128]{1,0:T(8,128)S(1)} %get-tuple-element.10, f32[16,128]{1,0:T(8,128)S(1)} %reduce_sum.149, f32[128,128]{1,0:T(8,128)} %bitcast.118, s32[]{:T(128)S(6)} %select_n.22, f32[]{:T(128)} %bitcast.11, f32[16,128]{1,0:T(8,128)S(1)} %get-tuple-element.17, f32[16,128]{1,0:T(8,128)S(1)} %reduce_sum.145, ...), kind=kLoop, calls=%fused_computation.49 | loop fusion | flops 24576 | bytes 65544 | tf_op jit(solution)/shard_map/reshape | solution.py:203
  185.7 0.6 copy.32
  (63 shorter events, 4.9 us)
Async XLA Ops:
  0.6 105.9 %copy-start = (f32[16384]{0:T(1024)S(1)}, f32[16384]{0:T(1024)}, u32[]{:S(2)}) copy-start(f32[16384]{0:T(1024)} %param.24) | copy-start | bytes 196612
  0.6 24.0 %copy-start.13 = (s32[3,16384]{1,0:T(4,128)S(1)}, s32[3,16384]{1,0:T(4,128)}, u32[]{:S(2)}) copy-start(s32[3,16384]{1,0:T(4,128)} %param.22) | copy-start | bytes 589828
  0.7 29.6 %copy-start.12 = (s32[1,1,32]{2,1,0:T(1,128)S(1)}, s32[1,1,32]{2,1,0:T(1,128)}, u32[]{:S(2)}) copy-start(s32[1,1,32]{2,1,0:T(1,128)} %in_index.15) | copy-start | bytes 388
  0.7 29.6 %copy-start.10 = (s32[1,1,32]{2,1,0:T(1,128)S(1)}, s32[1,1,32]{2,1,0:T(1,128)}, u32[]{:S(2)}) copy-start(s32[1,1,32]{2,1,0:T(1,128)} %out_index.15) | copy-start | bytes 388
  0.7 14.3 %copy-start.18 = (f32[2]{0:T(128)S(1)}, f32[2]{0:T(128)}, u32[]{:S(2)}) copy-start(f32[2]{0:T(128)} %param.26) | copy-start | bytes 28
  3.3 2.2 %copy-start.1 = (bf16[1,1,32,256,256]{4,3,2,1,0:T(8,128)(2,1)S(1)}, bf16[1,1,32,256,256]{4,3,2,1,0:T(8,128)(2,1)}, u32[]{:S(2)}) copy-start(bf16[1,1,32,256,256]{4,3,2,1,0:T(8,128)(2,1)} %param.15) | copy-start | bytes 12582916
  5.5 0.7 copy-start.9
  6.1 0.7 copy-start.11
  6.8 8.8 %copy-start.14 = (s32[3,16384]{1,0:T(4,128)S(1)}, s32[3,16384]{1,0:T(4,128)}, u32[]{:S(2)}) copy-start(s32[3,16384]{1,0:T(4,128)} %param.21) | copy-start | bytes 589828
  6.8 13.9 %copy-start.17 = (f32[16384]{0:T(1024)S(1)}, f32[16384]{0:T(1024)}, u32[]{:S(2)}) copy-start(f32[16384]{0:T(1024)} %param.27) | copy-start | bytes 196612
  6.8 42.2 %copy-start.16 = (f32[3,16384]{1,0:T(4,128)S(1)}, f32[3,16384]{1,0:T(4,128)}, u32[]{:S(2)}) copy-start(f32[3,16384]{1,0:T(4,128)} %param.20) | copy-start | bytes 589828
  8.6 12.1 %all-to-all-start = ((f32[4,1,32,128]{3,2,1,0:T(8,128)}), f32[4,1,32,128]{3,2,1,0:T(8,128)S(1)}, u32[]{:S(2)}, u32[]{:S(2)}) async-start(f32[4,1,32,128]{3,2,1,0:T(8,128)} %back_first.1), calls=%async_computation | async-start | bytes 131072 | tf_op jit(solution)/shard_map/all_to_all | solution.py:85
  21.4 8.9 %all-to-all-start.1 = ((bf16[4,1,32,128]{3,2,1,0:T(8,128)(2,1)}), bf16[4,1,32,128]{3,2,1,0:T(8,128)(2,1)S(1)}, u32[]{:S(2)}, u32[]{:S(2)}) async-start(bf16[4,1,32,128]{3,2,1,0:T(8,128)(2,1)} %broadcast_in_dim.48), calls=%async_computation.1 | async-start | bytes 65536 | tf_op jit(solution)/shard_map/all_to_all | solution.py:90
  30.3 2.2 %copy-start.2 = (bf16[1,1,32,256,256]{4,3,2,1,0:T(8,128)(2,1)S(1)}, bf16[1,1,32,256,256]{4,3,2,1,0:T(8,128)(2,1)}, u32[]{:S(2)}) copy-start(bf16[1,1,32,256,256]{4,3,2,1,0:T(8,128)(2,1)} %param.15) | copy-start | bytes 12582916
  32.5 24.7 %copy-start.15 = (f32[3,16384]{1,0:T(4,128)S(1)}, f32[3,16384]{1,0:T(4,128)}, u32[]{:S(2)}) copy-start(f32[3,16384]{1,0:T(4,128)} %param.19) | copy-start | bytes 589828
  34.9 8.7 %all-to-all-start.2 = ((f32[8,1,16,128]{3,2,1,0:T(8,128)}), f32[8,1,16,128]{3,2,1,0:T(8,128)S(1)}, u32[]{:S(2)}, u32[]{:S(2)}) async-start(f32[8,1,16,128]{3,2,1,0:T(8,128)} %image_2.1), calls=%async_computation.2 | async-start | bytes 131072 | tf_op jit(solution)/shard_map/all_to_all | solution.py:85
  45.6 8.1 %all-to-all-start.3 = ((bf16[8,1,16,128]{3,2,1,0:T(8,128)(2,1)}), bf16[8,1,16,128]{3,2,1,0:T(8,128)(2,1)S(1)}, u32[]{:S(2)}, u32[]{:S(2)}) async-start(bf16[8,1,16,128]{3,2,1,0:T(8,128)(2,1)} %broadcast_in_dim.49), calls=%async_computation.3 | async-start | bytes 65536 | tf_op jit(solution)/shard_map/all_to_all | solution.py:90
  49.1 2.2 %copy-start.3 = (bf16[1,1,32,256,256]{4,3,2,1,0:T(8,128)(2,1)S(1)}, bf16[1,1,32,256,256]{4,3,2,1,0:T(8,128)(2,1)}, u32[]{:S(2)}) copy-start(bf16[1,1,32,256,256]{4,3,2,1,0:T(8,128)(2,1)} %param.15) | copy-start | bytes 12582916
  53.8 11.1 %all-to-all-start.12 = ((f32[4,3,32,128]{3,2,1,0:T(8,128)}), f32[4,3,32,128]{3,2,1,0:T(8,128)S(1)}, u32[]{:S(2)}, u32[]{:S(2)}) async-start(f32[4,3,32,128]{3,2,1,0:T(8,128)} %back_saved.1), calls=%async_computation.12 | async-start | bytes 393216 | tf_op jit(solution)/shard_map/all_to_all | solution.py:85
  57.2 2.2 %copy-start.4 = (bf16[1,1,32,256,256]{4,3,2,1,0:T(8,128)(2,1)S(1)}, bf16[1,1,32,256,256]{4,3,2,1,0:T(8,128)(2,1)}, u32[]{:S(2)}) copy-start(bf16[1,1,32,256,256]{4,3,2,1,0:T(8,128)(2,1)} %param.15) | copy-start | bytes 12582916
  64.9 9.0 %all-to-all-start.4 = ((f32[4,1,32,128]{3,2,1,0:T(8,128)}), f32[4,1,32,128]{3,2,1,0:T(8,128)S(1)}, u32[]{:S(2)}, u32[]{:S(2)}) async-start(f32[4,1,32,128]{3,2,1,0:T(8,128)} %back_1.1), calls=%async_computation.4 | async-start | bytes 131072 | tf_op jit(solution)/shard_map/all_to_all | solution.py:85
  75.2 8.9 %all-to-all-start.5 = ((bf16[4,1,32,128]{3,2,1,0:T(8,128)(2,1)}), bf16[4,1,32,128]{3,2,1,0:T(8,128)(2,1)S(1)}, u32[]{:S(2)}, u32[]{:S(2)}) async-start(bf16[4,1,32,128]{3,2,1,0:T(8,128)(2,1)} %broadcast_in_dim.50), calls=%async_computation.5 | async-start | bytes 65536 | tf_op jit(solution)/shard_map/all_to_all | solution.py:90
  84.7 9.1 %all-to-all-start.13 = ((bf16[4,3,32,128]{3,2,1,0:T(8,128)(2,1)}), bf16[4,3,32,128]{3,2,1,0:T(8,128)(2,1)S(1)}, u32[]{:S(2)}, u32[]{:S(2)}) async-start(bf16[4,3,32,128]{3,2,1,0:T(8,128)(2,1)} %broadcast_in_dim.55), calls=%async_computation.13 | async-start | bytes 196608 | tf_op jit(solution)/shard_map/all_to_all | solution.py:90
  88.0 2.2 %copy-start.5 = (bf16[1,1,32,256,256]{4,3,2,1,0:T(8,128)(2,1)S(1)}, bf16[1,1,32,256,256]{4,3,2,1,0:T(8,128)(2,1)}, u32[]{:S(2)}) copy-start(bf16[1,1,32,256,256]{4,3,2,1,0:T(8,128)(2,1)} %param.15) | copy-start | bytes 12582916
  93.8 8.8 %all-to-all-start.6 = ((f32[8,1,16,128]{3,2,1,0:T(8,128)}), f32[8,1,16,128]{3,2,1,0:T(8,128)S(1)}, u32[]{:S(2)}, u32[]{:S(2)}) async-start(f32[8,1,16,128]{3,2,1,0:T(8,128)} %image_1.1), calls=%async_computation.6 | async-start | bytes 131072 | tf_op jit(solution)/shard_map/all_to_all | solution.py:85
  97.6 2.2 %copy-start.6 = (bf16[1,1,32,256,256]{4,3,2,1,0:T(8,128)(2,1)S(1)}, bf16[1,1,32,256,256]{4,3,2,1,0:T(8,128)(2,1)}, u32[]{:S(2)}) copy-start(bf16[1,1,32,256,256]{4,3,2,1,0:T(8,128)(2,1)} %param.15) | copy-start | bytes 12582916
  102.7 10.1 %all-to-all-start.14 = ((f32[8,3,16,128]{3,2,1,0:T(8,128)}), f32[8,3,16,128]{3,2,1,0:T(8,128)S(1)}, u32[]{:S(2)}, u32[]{:S(2)}) async-start(f32[8,3,16,128]{3,2,1,0:T(8,128)} %image_saved.1), calls=%async_computation.14 | async-start | bytes 393216 | tf_op jit(solution)/shard_map/all_to_all | solution.py:85
  114.7 8.1 %all-to-all-start.7 = ((bf16[8,1,16,128]{3,2,1,0:T(8,128)(2,1)}), bf16[8,1,16,128]{3,2,1,0:T(8,128)(2,1)S(1)}, u32[]{:S(2)}, u32[]{:S(2)}) async-start(bf16[8,1,16,128]{3,2,1,0:T(8,128)(2,1)} %broadcast_in_dim.51), calls=%async_computation.7 | async-start | bytes 65536 | tf_op jit(solution)/shard_map/all_to_all | solution.py:90
  122.8 2.2 %copy-start.7 = (bf16[1,1,32,256,256]{4,3,2,1,0:T(8,128)(2,1)S(1)}, bf16[1,1,32,256,256]{4,3,2,1,0:T(8,128)(2,1)}, u32[]{:S(2)}) copy-start(bf16[1,1,32,256,256]{4,3,2,1,0:T(8,128)(2,1)} %param.15) | copy-start | bytes 12582916
  125.0 53.8 %copy-start.19 = (f32[1,2]{1,0:T(1,128)S(1)}, f32[1,2]{1,0:T(1,128)}, u32[]{:S(2)}) copy-start(f32[1,2]{1,0:T(1,128)} %constant.14) | copy-start | bytes 28
  126.9 9.6 %all-to-all-start.8 = ((f32[4,1,32,128]{3,2,1,0:T(8,128)}), f32[4,1,32,128]{3,2,1,0:T(8,128)S(1)}, u32[]{:S(2)}, u32[]{:S(2)}) async-start(f32[4,1,32,128]{3,2,1,0:T(8,128)} %back_0.1), calls=%async_computation.8 | async-start | bytes 131072 | tf_op jit(solution)/shard_map/all_to_all | solution.py:85
  140.2 8.8 %all-to-all-start.15 = ((f32[4,8,128]{2,1,0:T(8,128)}), f32[4,8,128]{2,1,0:T(8,128)S(1)}, u32[]{:S(2)}, u32[]{:S(2)}) async-start(f32[4,8,128]{2,1,0:T(8,128)} %broadcast_in_dim.58), calls=%async_computation.15 | async-start | bytes 32768 | tf_op jit(solution)/shard_map/all_to_all | solution.py:90
  149.7 8.9 %all-to-all-start.10 = ((bf16[4,1,32,128]{3,2,1,0:T(8,128)(2,1)}), bf16[4,1,32,128]{3,2,1,0:T(8,128)(2,1)S(1)}, u32[]{:S(2)}, u32[]{:S(2)}) async-start(bf16[4,1,32,128]{3,2,1,0:T(8,128)(2,1)} %broadcast_in_dim.53), calls=%async_computation.10 | async-start | bytes 65536 | tf_op jit(solution)/shard_map/all_to_all | solution.py:90
  166.4 9.0 %all-to-all-start.9 = ((f32[4,32,128]{2,1,0:T(8,128)}), f32[4,32,128]{2,1,0:T(8,128)S(1)}, u32[]{:S(2)}, u32[]{:S(2)}) async-start(f32[4,32,128]{2,1,0:T(8,128)} %broadcast_in_dim.52), calls=%async_computation.9 | async-start | bytes 131072 | tf_op jit(solution)/shard_map/all_to_all | solution.py:90
  169.7 2.2 %copy-start.8 = (bf16[1,1,32,256,256]{4,3,2,1,0:T(8,128)(2,1)S(1)}, bf16[1,1,32,256,256]{4,3,2,1,0:T(8,128)(2,1)}, u32[]{:S(2)}) copy-start(bf16[1,1,32,256,256]{4,3,2,1,0:T(8,128)(2,1)} %param.15) | copy-start | bytes 12582916
  175.4 8.3 %all-to-all-start.11 = ((f32[8,1,16,128]{3,2,1,0:T(8,128)}), f32[8,1,16,128]{3,2,1,0:T(8,128)S(1)}, u32[]{:S(2)}, u32[]{:S(2)}) async-start(f32[8,1,16,128]{3,2,1,0:T(8,128)} %image_0.1), calls=%async_computation.11 | async-start | bytes 131072 | tf_op jit(solution)/shard_map/all_to_all | solution.py:85

commit v3 on v0

v3 whole, which is shorter than its diff:
```python
import functools
import math

import jax
import jax.numpy as jnp
from jax import lax
from jax.experimental import pallas as pl
from jax.experimental.pallas import tpu as pltpu
from jax.sharding import PartitionSpec as P

LANES = 128
EXTRA = 16
CHUNKS = 4
VMEM = pl.BlockSpec(memory_space=pltpu.VMEM)
SMEM = pl.BlockSpec(memory_space=pltpu.SMEM)
ANY = pl.BlockSpec(memory_space=pl.ANY)
GRANT = 32 * 1024 * 1024


def weight_of(step):
    return (step + 1.0) / (step + 2.0)


def tree_sum(parts):
    while len(parts) > 1:
        parts = [parts[i] + parts[i + 1] for i in range(0, len(parts), 2)]
    return parts[0]


def fold(lines):
    return lines.reshape(-1, 8, LANES).sum(axis=0)


def rounded(values):
    return values.astype(jnp.bfloat16).astype(jnp.float32)


def add_products(transpose, in_index, out_index, count, tiles, slots, source, total):
    per_block = tiles.shape[-1] // LANES
    several = len(total.shape) == 3
    live_count = count[0, 0]
    for slot in slots:
        start = in_index[0, 0, slot] * per_block
        place = out_index[0, 0, slot] * per_block
        live = (live_count > slot).astype(jnp.float32)
        halves = []
        for half in range(per_block):
            if not several:
                halves.append(source[pl.ds(start + half, 1), :])
                continue
            vectors = source.shape[0]
            rows = -(-vectors // 8) * 8
            which = lax.broadcasted_iota(jnp.int32, (rows, LANES), 0)
            stacked = jnp.zeros((rows, LANES), jnp.float32)
            for vector in range(vectors):
                line = source[vector, pl.ds(start + half, 1), :]
                stacked = jnp.where(which == vector, line, stacked)
            halves.append(stacked)
        block = (jnp.concatenate(halves, axis=1) * live).astype(jnp.bfloat16)
        contract = ((1,), (0,)) if transpose else ((1,), (1,))
        product = lax.dot_general(
            block, tiles[slot], (contract, ((), ())), preferred_element_type=jnp.float32
        )
        for half in range(per_block):
            at = pl.ds(place + half, 1)
            lanes = slice(half * LANES, (half + 1) * LANES)
            if several:
                for vector in range(total.shape[0]):
                    total[vector, at, :] += product[vector : vector + 1, lanes]
            else:
                total[at, :] += product[:, lanes]


def first_body(
    step, rows, columns, count, tile_data, mask, cotangent, tiles, term, anchor, out, source, arrived
):
    slots = tiles.shape[0]
    chunk = slots // CHUNKS

    def fetch(part):
        span = pl.ds(part * chunk, chunk)
        return pltpu.make_async_copy(tile_data.at[0, 0, span], tiles.at[span], arrived.at[part])

    for part in range(CHUNKS):
        fetch(part).start()
    weight = weight_of(step)
    adjoint = cotangent[...]
    anchor[...] = (1.0 - weight) * adjoint
    value = mask[:, step, :].astype(jnp.float32) * weight * adjoint
    term[...] = value
    source[...] = rounded(value)
    out[...] = jnp.zeros_like(out)
    for part in range(CHUNKS):
        fetch(part).wait()
        span = range(part * chunk, (part + 1) * chunk)
        add_products(True, rows, columns, count, tiles, span, source, out)


def dual_body(step, n_col, rows, columns, count, sizes, tiles, mask, parts, before, anchor, *refs):
    last = step == 0
    if last:
        demand, images, terms, term, anchor_out, out, source = refs
    else:
        term, anchor_out, out, source = refs
    weight = weight_of(step)
    image = tree_sum([part[...] for part in parts])
    adjoint = before[...] + sizes[0] * image
    anchor_out[...] = anchor[...] + (1.0 - weight) * adjoint
    value = mask[:, step, :].astype(jnp.float32) * weight * adjoint
    term[...] = value
    source[...] = rounded(value)
    lines = source.shape[0]
    total = out.at[pl.ds(0, lines)] if last else out
    total[...] = jnp.zeros(total.shape, jnp.float32)
    add_products(True, rows, columns, count, tiles, range(tiles.shape[0]), source, total)
    if last:
        share = demand[...] * (1.0 / n_col)
        found = value * (share - images[0])
        for other, earlier in enumerate(terms):
            found += earlier[...] * (share - images[other + 1])
        out[lines : lines + 8, :] = fold(found)
        out[lines + 8 : lines + 16, :] = jnp.zeros((8, LANES), jnp.float32)


def primal_body(step, n_col, rows, columns, count, sizes, tiles, mask, parts, before, anchor, *refs):
    last = step == 0
    if last:
        place, reduced, terms, final, mine, other, source, out = refs
    else:
        term, adjoint_out, anchor_out, out, source = refs
    sigma = sizes[1]
    weight = weight_of(step)
    lines = source.shape[0]
    back = tree_sum([part[...] for part in parts])
    if last:
        sums = back[lines : lines + 8]
        back = back[:lines]
    adjoint = before[...]
    anchored = (1.0 - weight) * adjoint
    if anchor is not None:
        anchored = anchor[...] + anchored
    value = mask[:, step, :].astype(jnp.float32) * (weight * adjoint - 2.0 * sigma * back)
    after = value + sigma * back
    if last:
        final[...] = after + anchored
    else:
        term[...] = value
        adjoint_out[...] = after
        anchor_out[...] = anchored
    source[...] = rounded(value)
    out[...] = jnp.zeros_like(out)
    add_products(False, columns, rows, count, tiles, range(tiles.shape[0]), source, out)
    if last:
        found = value * reduced[0]
        for other_step, later in enumerate(terms):
            found += later[...] * reduced[other_step + 1]
        tail = jnp.concatenate([sums, -fold(found)], axis=0)
        share = out.shape[0] // n_col
        core = place[0] % 2
        for chip in range(n_col // 2):
            span = slice(chip * share, (chip + 1) * share)
            mine[span, :] = out[pl.ds((2 * chip + core) * share, share), :]
            other[span, :] = out[pl.ds((2 * chip + 1 - core) * share, share), :]
        mine[n_col // 2 * share :, :] = tail
        other[n_col // 2 * share :, :] = tail


def split_body(n_chip, place, mine, received, *outs):
    share = (mine.shape[0] - EXTRA) // n_chip
    chip = place[0] // 2
    tail = mine[n_chip * share :, :] + received[n_chip * share :, :]
    for part, out in enumerate(outs):
        at = pl.ds((chip ^ part) * share, share)
        out[:share, :] = mine[at, :] + received[at, :]
        out[share:, :] = tail


def last_body(scales, place, sizes, parts, term, anchor, adjoint, gradients):
    share = adjoint.shape[0]
    total = tree_sum([part[...] for part in parts])
    at = pl.ds(place[0] * share, share)
    adjoint[...] = term[at, :] + sizes[0] * total[:share] + anchor[at, :]
    gradients[0] = jnp.sum(total[share + 8 : share + 16]) * scales[0]
    gradients[1] = jnp.sum(total[share : share + 8]) * scales[1]


def saved_back_body(rows, columns, count, place, tiles, saved, *refs):
    outs, (source, total) = refs[:-2], refs[-2:]
    for step in range(source.shape[0]):
        source[step] = rounded(saved[:, step, :])
    total[...] = jnp.zeros_like(total)
    add_products(True, rows, columns, count, tiles, range(tiles.shape[0]), source, total)
    share = total.shape[1] // len(outs)
    for part, out in enumerate(outs):
        out[...] = total[:, pl.ds((place[0] ^ part) * share, share), :]


def saved_image_body(
    rows, columns, count, place, sizes, tiles, parts, cost, upper, primal, reduced, images, source
):
    share = parts[0].shape[1]
    for part, held in enumerate(parts):
        at = pl.ds((place[0] ^ part) * share, share)
        reduced[:, at, :] = cost[at, :][None] - held[...]
    for step in range(source.shape[0]):
        saved = primal[:, step, :]
        half = jnp.minimum(jnp.maximum(saved - sizes[0] * reduced[step], 0.0), upper[...])
        source[step] = rounded(2.0 * half - saved)
    images[...] = jnp.zeros_like(images)
    add_products(False, columns, rows, count, tiles, range(tiles.shape[0]), source, images)


def run(body, out_shape, groups, scratch, name, cost=None):
    flat, specs, widths = [], [], []
    for spec, value in groups:
        if value is None:
            widths.append(None)
            continue
        many = isinstance(value, (list, tuple))
        widths.append(len(value) if many else 0)
        for array in value if many else [value]:
            flat.append(array)
            specs.append(spec)

    def kernel(*refs):
        given = list(refs)
        taken = []
        for width in widths:
            if width is None:
                taken.append(None)
            elif width == 0:
                taken.append(given.pop(0))
            else:
                taken.append([given.pop(0) for _ in range(width)])
        body(*taken, *given)

    in_smem = [isinstance(shape, tuple) for shape in out_shape]
    shapes = [shape[1] if isinstance(shape, tuple) else shape for shape in out_shape]
    return pl.pallas_call(
        kernel,
        out_shape=shapes,
        in_specs=specs,
        out_specs=[SMEM if smem else VMEM for smem in in_smem],
        scratch_shapes=scratch,
        compiler_params=pltpu.CompilerParams(vmem_limit_bytes=GRANT),
        cost_estimate=cost,
        name=name,
    )(*flat)


def exchange(parts, axis, stride=1):
    size = lax.axis_size(axis)
    return [parts[0]] + [
        lax.ppermute(parts[k], axis, [(i, i ^ (k * stride)) for i in range(size)])
        for k in range(1, size // stride)
    ]


def local(
    tile_data,
    tile_row_block,
    tile_column_block,
    tile_count,
    saved_primal,
    saved_dual,
    primal_mask,
    dual_mask,
    cost_vector,
    demand,
    upper_bound,
    step_sizes,
    primal_cotangent,
    dual_cotangent,
):
    slots, width = tile_data.shape[2], tile_data.shape[-1]
    iterations, row_length = saved_dual.shape
    column_length = saved_primal.shape[1]
    n_row, n_col = lax.axis_size("row"), lax.axis_size("col")
    n_chip = n_col // 2
    at_row = lax.axis_index("row").reshape(1).astype(jnp.int32)
    at_col = lax.axis_index("col").reshape(1).astype(jnp.int32)
    lines_y, lines_x = row_length // LANES, column_length // LANES
    share_y, share_x = lines_y // n_col, lines_x // n_row
    last = iterations - 1
    cost = pl.CostEstimate(
        flops=2 * tile_data.size, bytes_accessed=2 * tile_data.size, transcendentals=0
    )

    def lines(array):
        if array.ndim == 1:
            return array.reshape(-1, LANES)
        return array.reshape(iterations, -1, LANES).transpose(1, 0, 2)

    def f32(*shape):
        return jax.ShapeDtypeStruct(shape, jnp.float32)

    def scratch(*shape):
        return pltpu.VMEM(shape, jnp.float32)

    mask_x, mask_y = lines(primal_mask), lines(dual_mask)
    full_x, full_y = f32(lines_x, LANES), f32(lines_y, LANES)
    where = [(SMEM, tile_row_block), (SMEM, tile_column_block), (SMEM, tile_count)]

    tiles, term_y, anchor_y, partial = run(
        functools.partial(first_body, last),
        [pltpu.VMEM((slots, width, width), jnp.bfloat16), full_y, full_y, full_x],
        where + [(ANY, tile_data), (VMEM, mask_y), (VMEM, lines(dual_cotangent))],
        [scratch(lines_y, LANES), pltpu.SemaphoreType.DMA((CHUNKS,))],
        "first",
        cost,
    )
    common = where + [(SMEM, step_sizes), (VMEM, tiles)]
    adjoint_x, anchor_x = lines(primal_cotangent), None
    terms_x, terms_y = [], [term_y]
    reduced = images = None
    for step in reversed(range(iterations)):
        parts = exchange([partial] * n_row, "row")
        if reduced is None:
            saved_parts = run(
                saved_back_body,
                [f32(iterations, share_x, LANES)] * n_row,
                where + [(SMEM, at_row), (VMEM, tiles), (VMEM, lines(saved_dual))],
                [scratch(iterations, lines_y, LANES), scratch(iterations, lines_x, LANES)],
                "saved_back",
                cost,
            )
        body = functools.partial(primal_body, step, n_col)
        groups = common + [(VMEM, mask_x), (VMEM, parts), (VMEM, adjoint_x), (VMEM, anchor_x)]
        if step > 0:
            term_x, adjoint_x, anchor_x, partial = run(
                body,
                [full_x, full_x, full_x, full_y],
                groups,
                [scratch(lines_x, LANES)],
                f"primal_{step}",
                cost,
            )
            terms_x.insert(0, term_x)
            partial = sum_pair(partial)
            if reduced is None:
                summed = tree_sum(exchange(saved_parts, "row"))
                gathered = exchange([summed] * n_row, "row")
                reduced, images = run(
                    saved_image_body,
                    [f32(iterations, lines_x, LANES), f32(iterations, lines_y, LANES)],
                    where
                    + [(SMEM, at_row), (SMEM, step_sizes), (VMEM, tiles), (VMEM, gathered)]
                    + [(VMEM, lines(cost_vector)), (VMEM, lines(upper_bound))]
                    + [(VMEM, lines(saved_primal))],
                    [scratch(iterations, lines_x, LANES)],
                    "saved_image",
                    cost,
                )
            parts = exchange([partial] * n_chip, "col", 2)
            final_step = step == 1
            groups = common + [(VMEM, mask_y), (VMEM, parts), (VMEM, term_y), (VMEM, anchor_y)]
            if final_step:
                groups += [(VMEM, lines(demand)), (VMEM, images), (VMEM, list(terms_y))]
            term_y, anchor_y, partial = run(
                functools.partial(dual_body, step - 1, n_col),
                [full_y, full_y, f32(lines_x + (EXTRA if final_step else 0), LANES)],
                groups,
                [scratch(lines_y, LANES)],
                f"dual_{step - 1}",
                cost,
            )
            terms_y.insert(0, term_y)
    half_y = f32(n_chip * share_y + EXTRA, LANES)
    primal_adjoint, mine, other = run(
        body,
        [full_x, half_y, half_y],
        groups + [(SMEM, at_col), (VMEM, reduced), (VMEM, terms_x)],
        [scratch(lines_x, LANES), scratch(lines_y, LANES)],
        "primal_0",
        cost,
    )
    received = lax.ppermute(other, "col", [(i, i ^ 1) for i in range(n_col)])
    parts = run(
        functools.partial(split_body, n_chip),
        [f32(share_y + EXTRA, LANES)] * n_chip,
        [(SMEM, at_col), (VMEM, mine), (VMEM, received)],
        [],
        "split",
    )
    parts = exchange(parts, "col", 2)
    scales = (1.0 / math.sqrt(column_length * n_col), 1.0 / math.sqrt(row_length * n_row))
    dual_adjoint, gradients = run(
        functools.partial(last_body, scales),
        [f32(share_y, LANES), ("smem", f32(2))],
        [(SMEM, at_col), (SMEM, step_sizes), (VMEM, parts), (VMEM, term_y), (VMEM, anchor_y)],
        [],
        "last",
    )
    return (primal_adjoint.reshape(-1), dual_adjoint.reshape(-1), gradients)


def sum_pair(partial):
    size = lax.axis_size("col")
    return partial + lax.ppermute(partial, "col", [(i, i ^ 1) for i in range(size)])


def solution(mesh):
    placed = (
        P("row", "col", None, None, None),
        P("row", "col", None),
        P("row", "col", None),
        P("row", "col"),
        P(None, "col"),
        P(None, "row"),
        P(None, "col"),
        P(None, "row"),
        P("col"),
        P("row"),
        P("col"),
        P(),
        P("col"),
        P("row"),
    )
    return jax.shard_map(
        local,
        mesh=mesh,
        in_specs=placed,
        out_specs=(P("col"), P(("row", "col")), P()),
        check_vma=False,
    )
```

time: 378 us -> 84.8 us (0.22)
  waiting for transfers between devices: 255 us -> 25.1 us
  blocking collectives: 39.2 us -> 0 us
  starting transfers between devices: 0.25 us -> 32.9 us
  matrix products: 27.4 us -> 0 us
  other arithmetic: 22.1 us -> 0.03 us
  between operations: 20.9 us -> 1.51 us
  Pallas kernels: 0 us -> 15.3 us
    psum x6 -> x0, waiting for transfers between devices: 255 us -> none  [the longest x3 154 us: local(): image_rows = lax.psum(image, 'col')[0]]
    psum x1 -> x0, blocking collectives: 39.2 us -> none  [local(): tau_total, sigma_total = lax.psum((tau_local, sigma_local), ('row', 'col'))]
    ppermute x0 -> x27, starting transfers between devices: none -> 32.9 us  [the longest x24 32.8 us: exchange(): lax.ppermute(parts[k], axis, [(i, i ^ k * stride) for i in range(size)])]
    dot_general x16 -> x0, matrix products: 27.4 us -> none  [the longest x8 24.9 us: block_terms(): jnp.einsum(einsum_form, tile_part, picked, preferred_element_type=jnp.flo...]
    ppermute x0 -> x27, waiting for transfers between devices: none -> 25.1 us  [the longest x24 22.6 us: exchange(): lax.ppermute(parts[k], axis, [(i, i ^ k * stride) for i in range(size)])]
    pallas_call x0 -> x10, Pallas kernels: none -> 15.3 us  [run(): pl.pallas_call(kernel, out_shape=shapes, in_specs=specs, out_specs=[SMEM...]
    mul x7 -> x0, other arithmetic: 9.44 us -> none  [the longest x3 4.66 us: local(): adjoint_x = primal_term + sigma * back]
    gather x8 -> x0, local copies, waits for them, and re-layouts: 5.01 us -> none  [block_terms(): picked = jnp.take(blocks, in_part, axis=1)]
  transfers between devices with their start and end apart: 6 -> 27, of which waited for: 6 -> 17; matrix products, arithmetic and copies ran while one was open for 2% -> 0% of each run, Pallas kernels for 0% -> 6%
where the time goes in v3:
time: 84.8 us; the launch traced here: 84.5 us
  starting transfers between devices  32.9 us (39%)
  waiting for transfers between devices  25.1 us (30%)
  Pallas kernels  15.3 us (18%)
  local copies, waits for them, and re-layouts  9.71 us (11%)
  between operations  1.51 us (2%)
    ppermute x24, starting transfers between devices, exchange(): lax.ppermute(parts[k], axis, [(i, i ^ k * stride) for i in range(size)])  32.8 us
    ppermute x24, waiting for transfers between devices, exchange(): lax.ppermute(parts[k], axis, [(i, i ^ k * stride) for i in range(size)])  22.6 us
    pallas_call x10, Pallas kernels, run(): pl.pallas_call(kernel, out_shape=shapes, in_specs=specs, out_specs=[SMEM...  15.3 us
    unnamed x40, local copies, waits for them, and re-layouts  9.71 us
  transfers between devices with their start and end apart: 27, of which 17 were waited for; matrix products, arithmetic and copies ran while one was open for 0% of the time, Pallas kernels for 6%

profile of v3, /device:TPU:0, one launch (start us, length us, event | category | flops | bytes accessed | tf_op | source)
XLA Modules:
  0.0 84.5 jit_solution(2062178658937992553)
XLA Ops:
  1.3 2.2 %copy-done.4 = bf16[1,1,32,256,256]{4,3,2,1,0:T(8,128)(2,1)S(1)} copy-done((bf16[1,1,32,256,256]{4,3,2,1,0:T(8,128)(2,1)S(1)}, bf16[1,1,32,256,256]{4,3,2,1,0:T(8,128)(2,1)}, u32[]{:S(2)}) %copy-start.4) | copy-done | bytes 4194328
  3.5 0.9 %copy-done.6 = s32[3,16384]{1,0:T(4,128)S(1)} copy-done((s32[3,16384]{1,0:T(4,128)S(1)}, s32[3,16384]{1,0:T(4,128)}, u32[]{:S(2)}) %copy-start.6) | copy-done | bytes 196632
  4.4 0.8 copy-done.10
  5.3 0.7 copy-done.15
  5.9 0.7 copy-done.17
  6.6 2.0 %first.1 = (bf16[32,256,256]{2,1,0:T(8,128)(2,1)S(1)}, f32[128,128]{1,0:T(8,128)S(1)}, f32[128,128]{1,0:T(8,128)S(1)}, f32[128,128]{1,0:T(8,128)S(1)}) custom-call(s32[1,1,32]{2,1,0:T(1,128)S(1)} %copy-done.15, s32[1,1,32]{2,1,0:T(1,128)S(1)} %copy-done.17, s32[1,1]{1,0:T(1,128)S(6)} %copy.17.refs_2_, bf16[1,1,32,256,256]{4,3,2,1,0:T(8,128)(2,1)S(1)} %copy-done.4, ...), custom_call_target="tpu_custom_call" | custom-call | flops 4194304 | bytes 4194304 | tf_op jit(solution)/shard_map/first/pallas_call | solution.py:239
  8.6 5.1 %collective-permute-start.2 = (f32[128,128]{1,0:T(8,128)S(1)}, f32[128,128]{1,0:T(8,128)S(1)}, u32[]{:S(2)}, u32[]{:S(2)}) collective-permute-start(f32[128,128]{1,0:T(8,128)S(1)} %get-tuple-element.37.refs_6_), channel_id=1, source_target_pairs={{0,24},{8,16},{16,8},{24,0},{1,25},{9,17},{17,9},{25,1},{2,26},{10... | collective-permute-start | bytes 196616 | tf_op jit(solution)/shard_map/ppermute | solution.py:254
  13.7 0.6 collective-permute-start
  14.3 1.9 %collective-permute-done.2.refs_9_ = f32[128,128]{1,0:T(8,128)S(1)} collective-permute-done((f32[128,128]{1,0:T(8,128)S(1)}, f32[128,128]{1,0:T(8,128)S(1)}, u32[]{:S(2)}, u32[]{:S(2)}) %collective-permute-start.2) | collective-permute-done | bytes 65568 | tf_op jit(solution)/shard_map/ppermute | solution.py:254
  16.3 3.0 %collective-permute-done.1.refs_8_ = f32[128,128]{1,0:T(8,128)S(1)} collective-permute-done((f32[128,128]{1,0:T(8,128)S(1)}, f32[128,128]{1,0:T(8,128)S(1)}, u32[]{:S(2)}, u32[]{:S(2)}) %collective-permute-start.1) | collective-permute-done | bytes 65568 | tf_op jit(solution)/shard_map/ppermute | solution.py:254
  19.3 0.0 collective-permute-done.refs_7_
  19.3 0.0 copy-start.8
  19.3 0.0 copy-start.16
  19.3 0.0 copy-start.18
  19.4 1.8 %primal_2.1 = (f32[128,128]{1,0:T(8,128)S(1)}, f32[128,128]{1,0:T(8,128)S(1)}, f32[128,128]{1,0:T(8,128)S(1)}, f32[128,128]{1,0:T(8,128)S(1)}) custom-call(s32[1,1,32]{2,1,0:T(1,128)S(1)} %copy-done.15, s32[1,1,32]{2,1,0:T(1,128)S(1)} %copy-done.17, s32[1,1]{1,0:T(1,128)S(6)} %copy.17.refs_2_, f32[2]{0:T(128)S(1)} %copy-done.19, ...), custom_call_target="tpu_custom_call" | custom-call | flops 4194304 | bytes 4194304 | tf_op jit(solution)/shard_map/primal_2/pallas_call | solution.py:239
  21.2 0.0 collective-permute-start.3
  21.2 1.2 %collective-permute-done.3 = f32[128,128]{1,0:T(8,128)S(1)} collective-permute-done((f32[128,128]{1,0:T(8,128)S(1)}, f32[128,128]{1,0:T(8,128)S(1)}, u32[]{:S(2)}, u32[]{:S(2)}) %collective-permute-start.3) | collective-permute-done | bytes 65568 | tf_op jit(solution)/shard_map/ppermute | solution.py:399
  22.5 2.5 %collective-permute-start.6 = (f32[128,128]{1,0:T(8,128)S(1)}, f32[128,128]{1,0:T(8,128)S(1)}, u32[]{:S(2)}, u32[]{:S(2)}) collective-permute-start(f32[128,128]{1,0:T(8,128)S(1)} %add.15.refs_6_), channel_id=1, source_target_pairs={{0,6},{1,7},{2,4},{3,5},{4,2},{5,3},{6,0},{7,1},{8,14},{9,15},{10,... | collective-permute-start | bytes 196616 | tf_op jit(solution)/shard_map/ppermute | solution.py:254
  25.0 0.5 collective-permute-start.5
  25.5 0.5 collective-permute-start.4
  26.0 1.7 %collective-permute-done.6.refs_9_ = f32[128,128]{1,0:T(8,128)S(1)} collective-permute-done((f32[128,128]{1,0:T(8,128)S(1)}, f32[128,128]{1,0:T(8,128)S(1)}, u32[]{:S(2)}, u32[]{:S(2)}) %collective-permute-start.6) | collective-permute-done | bytes 65568 | tf_op jit(solution)/shard_map/ppermute | solution.py:254
  27.7 1.5 %collective-permute-done.5.refs_8_ = f32[128,128]{1,0:T(8,128)S(1)} collective-permute-done((f32[128,128]{1,0:T(8,128)S(1)}, f32[128,128]{1,0:T(8,128)S(1)}, u32[]{:S(2)}, u32[]{:S(2)}) %collective-permute-start.5) | collective-permute-done | bytes 65568 | tf_op jit(solution)/shard_map/ppermute | solution.py:254
  29.3 0.5 collective-permute-done.4.refs_7_
  29.8 1.3 %dual_1.1 = (f32[128,128]{1,0:T(8,128)S(1)}, f32[128,128]{1,0:T(8,128)S(1)}, f32[128,128]{1,0:T(8,128)S(1)}) custom-call(s32[1,1,32]{2,1,0:T(1,128)S(1)} %copy-done.15, s32[1,1,32]{2,1,0:T(1,128)S(1)} %copy-done.17, s32[1,1]{1,0:T(1,128)S(6)} %copy.17.refs_2_, f32[2]{0:T(128)S(1)} %copy-done.19, bf16[32,256,256]{2,1,0:T(8,128)(2,1)S(1)} %get-tuple-element.36.refs_4_.refs_5_, ...), custom_call_target="tpu_custom_call" | custom-call | flops 4194304 | bytes 4194304 | tf_op jit(solution)/shard_map/dual_1/pallas_call | solution.py:239
  31.1 2.8 %collective-permute-start.9 = (f32[128,128]{1,0:T(8,128)S(1)}, f32[128,128]{1,0:T(8,128)S(1)}, u32[]{:S(2)}, u32[]{:S(2)}) collective-permute-start(f32[128,128]{1,0:T(8,128)S(1)} %get-tuple-element.41.refs_6_), channel_id=1, source_target_pairs={{0,24},{8,16},{16,8},{24,0},{1,25},{9,17},{17,9},{25,1},{2,26},{10... | collective-permute-start | bytes 196616 | tf_op jit(solution)/shard_map/ppermute | solution.py:254
  33.9 0.0 collective-permute-start.8
  33.9 1.7 %collective-permute-start.7 = (f32[128,128]{1,0:T(8,128)S(1)}, f32[128,128]{1,0:T(8,128)S(1)}, u32[]{:S(2)}, u32[]{:S(2)}) collective-permute-start(f32[128,128]{1,0:T(8,128)S(1)} %get-tuple-element.41.refs_6_), channel_id=1, source_target_pairs={{0,8},{8,0},{16,24},{24,16},{1,9},{9,1},{17,25},{25,17},{2,10},{10... | collective-permute-start | bytes 196616 | tf_op jit(solution)/shard_map/ppermute | solution.py:254
  35.6 2.2 %copy-done.1 = bf16[32,256,256]{2,1,0:T(8,128)(2,1)S(1)} copy-done((bf16[32,256,256]{2,1,0:T(8,128)(2,1)S(1)}, bf16[32,256,256]{2,1,0:T(8,128)(2,1)}, u32[]{:S(2)}) %copy-start.1) | copy-done | bytes 4194328
  37.7 1.5 %saved_back.1 = (f32[3,32,128]{2,1,0:T(8,128)S(1)}, f32[3,32,128]{2,1,0:T(8,128)S(1)}, f32[3,32,128]{2,1,0:T(8,128)S(1)}, f32[3,32,128]{2,1,0:T(8,128)S(1)}) custom-call(s32[1,1,32]{2,1,0:T(1,128)S(1)} %copy-done.16, s32[1,1,32]{2,1,0:T(1,128)S(1)} %copy-done.18, s32[1,1]{1,0:T(1,128)S(6)} %copy.17.refs_2_, s32[1]{0:T(128)} %bitcast.9.refs_3_, ...), custom_call_target="tpu_custom_call" | custom-call | flops 4194304 | bytes 4194304 | tf_op jit(solution)/shard_map/saved_back/pallas_call | solution.py:239
  39.3 0.4 collective-permute-start.14
  39.7 2.9 %collective-permute-start.15 = (f32[3,32,128]{2,1,0:T(8,128)S(1)}, f32[3,32,128]{2,1,0:T(8,128)S(1)}, u32[]{:S(2)}, u32[]{:S(2)}) collective-permute-start(f32[3,32,128]{2,1,0:T(8,128)S(1)} %get-tuple-element.49), channel_id=1, source_target_pairs={{0,16},{8,24},{16,0},{24,8},{1,17},{9,25},{17,1},{25,9},{2,18},{10... | collective-permute-start | bytes 147464 | tf_op jit(solution)/shard_map/ppermute | solution.py:254
  42.6 0.0 collective-permute-done.9.refs_9_
  42.6 1.1 %collective-permute-start.16 = (f32[3,32,128]{2,1,0:T(8,128)S(1)}, f32[3,32,128]{2,1,0:T(8,128)S(1)}, u32[]{:S(2)}, u32[]{:S(2)}) collective-permute-start(f32[3,32,128]{2,1,0:T(8,128)S(1)} %get-tuple-element.50), channel_id=1, source_target_pairs={{0,24},{8,16},{16,8},{24,0},{1,25},{9,17},{17,9},{25,1},{2,26},{10... | collective-permute-start | bytes 147464 | tf_op jit(solution)/shard_map/ppermute | solution.py:254
  43.8 0.0 copy-start.14
  43.8 1.8 %primal_1.1 = (f32[128,128]{1,0:T(8,128)S(1)}, f32[128,128]{1,0:T(8,128)S(1)}, f32[128,128]{1,0:T(8,128)S(1)}, f32[128,128]{1,0:T(8,128)S(1)}) custom-call(s32[1,1,32]{2,1,0:T(1,128)S(1)} %copy-done.16, s32[1,1,32]{2,1,0:T(1,128)S(1)} %copy-done.18, s32[1,1]{1,0:T(1,128)S(6)} %copy.17.refs_2_, f32[2]{0:T(128)S(1)} %copy-done.19, ...), custom_call_target="tpu_custom_call" | custom-call | flops 4194304 | bytes 4194304 | tf_op jit(solution)/shard_map/primal_1/pallas_call | solution.py:239
  45.6 0.0 collective-permute-start.10
  45.7 3.0 %collective-permute-done.16 = f32[3,32,128]{2,1,0:T(8,128)S(1)} collective-permute-done((f32[3,32,128]{2,1,0:T(8,128)S(1)}, f32[3,32,128]{2,1,0:T(8,128)S(1)}, u32[]{:S(2)}, u32[]{:S(2)}) %collective-permute-start.16) | collective-permute-done | bytes 49184 | tf_op jit(solution)/shard_map/ppermute | solution.py:254
  48.7 1.1 %collective-permute-start.19 = (f32[3,32,128]{2,1,0:T(8,128)S(1)}, f32[3,32,128]{2,1,0:T(8,128)S(1)}, u32[]{:S(2)}, u32[]{:S(2)}) collective-permute-start(f32[3,32,128]{2,1,0:T(8,128)S(1)} %add_add_fusion.refs_6_), channel_id=1, source_target_pairs={{0,24},{8,16},{16,8},{24,0},{1,25},{9,17},{17,9},{25,1},{2,26},{10... | collective-permute-start | bytes 147464 | tf_op jit(solution)/shard_map/ppermute | solution.py:254
  49.7 1.6 %collective-permute-start.13 = (f32[128,128]{1,0:T(8,128)S(1)}, f32[128,128]{1,0:T(8,128)S(1)}, u32[]{:S(2)}, u32[]{:S(2)}) collective-permute-start(f32[128,128]{1,0:T(8,128)S(1)} %add.16.refs_6_), channel_id=1, source_target_pairs={{0,6},{1,7},{2,4},{3,5},{4,2},{5,3},{6,0},{7,1},{8,14},{9,15},{10,... | collective-permute-start | bytes 196616 | tf_op jit(solution)/shard_map/ppermute | solution.py:254
  51.3 0.8 collective-permute-start.12
  52.1 1.2 %collective-permute-start.11 = (f32[128,128]{1,0:T(8,128)S(1)}, f32[128,128]{1,0:T(8,128)S(1)}, u32[]{:S(2)}, u32[]{:S(2)}) collective-permute-start(f32[128,128]{1,0:T(8,128)S(1)} %add.16.refs_6_), channel_id=1, source_target_pairs={{0,2},{1,3},{2,0},{3,1},{4,6},{5,7},{6,4},{7,5},{8,10},{9,11},{10,... | collective-permute-start | bytes 196616 | tf_op jit(solution)/shard_map/ppermute | solution.py:254
  53.3 1.4 %collective-permute-done.19.refs_9_ = f32[3,32,128]{2,1,0:T(8,128)S(1)} collective-permute-done((f32[3,32,128]{2,1,0:T(8,128)S(1)}, f32[3,32,128]{2,1,0:T(8,128)S(1)}, u32[]{:S(2)}, u32[]{:S(2)}) %collective-permute-start.19) | collective-permute-done | bytes 49184 | tf_op jit(solution)/shard_map/ppermute | solution.py:254
  54.7 2.0 %collective-permute-start.17 = (f32[3,32,128]{2,1,0:T(8,128)S(1)}, f32[3,32,128]{2,1,0:T(8,128)S(1)}, u32[]{:S(2)}, u32[]{:S(2)}) collective-permute-start(f32[3,32,128]{2,1,0:T(8,128)S(1)} %add_add_fusion.refs_6_), channel_id=1, source_target_pairs={{0,8},{8,0},{16,24},{24,16},{1,9},{9,1},{17,25},{25,17},{2,10},{10... | collective-permute-start | bytes 147464 | tf_op jit(solution)/shard_map/ppermute | solution.py:254
  56.7 2.1 %collective-permute-done.18.refs_8_ = f32[3,32,128]{2,1,0:T(8,128)S(1)} collective-permute-done((f32[3,32,128]{2,1,0:T(8,128)S(1)}, f32[3,32,128]{2,1,0:T(8,128)S(1)}, u32[]{:S(2)}, u32[]{:S(2)}) %collective-permute-start.18) | collective-permute-done | bytes 49184 | tf_op jit(solution)/shard_map/ppermute | solution.py:254
  58.8 0.5 collective-permute-done.17.refs_7_
  59.2 1.9 %saved_image.1 = (f32[3,128,128]{2,1,0:T(8,128)S(1)}, f32[3,128,128]{2,1,0:T(8,128)S(1)}) custom-call(s32[1,1,32]{2,1,0:T(1,128)S(1)} %copy-done.16, s32[1,1,32]{2,1,0:T(1,128)S(1)} %copy-done.18, s32[1,1]{1,0:T(1,128)S(6)} %copy.17.refs_2_, s32[1]{0:T(128)} %bitcast.9.refs_3_, f32[2]{0:T(128)S(1)} %copy-done.19, bf16[32,256,256]{2,1,0:T(8,128)(2,1)S(1)} %copy-done.1, ...), custom_call_target="tpu_custom_call" | custom-call | flops 4194304 | bytes 4194304 | tf_op jit(solution)/shard_map/saved_image/pallas_call | solution.py:239
  61.1 0.0 collective-permute-done.13.refs_9_
  61.2 1.4 %dual_0.1 = (f32[128,128]{1,0:T(8,128)S(1)}, f32[128,128]{1,0:T(8,128)S(1)}, f32[144,128]{1,0:T(8,128)S(1)}) custom-call(s32[1,1,32]{2,1,0:T(1,128)S(1)} %copy-done.16, s32[1,1,32]{2,1,0:T(1,128)S(1)} %copy-done.18, s32[1,1]{1,0:T(1,128)S(6)} %copy.17.refs_2_, f32[2]{0:T(128)S(1)} %copy-done.19, bf16[32,256,256]{2,1,0:T(8,128)(2,1)S(1)} %copy-done.2, ...), custom_call_target="tpu_custom_call" | custom-call | flops 4194304 | bytes 4194304 | tf_op jit(solution)/shard_map/dual_0/pallas_call | solution.py:239
  62.6 1.9 %collective-permute-start.22 = (f32[144,128]{1,0:T(8,128)S(1)}, f32[144,128]{1,0:T(8,128)S(1)}, u32[]{:S(2)}, u32[]{:S(2)}) collective-permute-start(f32[144,128]{1,0:T(8,128)S(1)} %get-tuple-element.52.refs_6_), channel_id=1, source_target_pairs={{0,24},{8,16},{16,8},{24,0},{1,25},{9,17},{17,9},{25,1},{2,26},{10... | collective-permute-start | bytes 221192 | tf_op jit(solution)/shard_map/ppermute | solution.py:254
  64.5 1.1 %collective-permute-start.21 = (f32[144,128]{1,0:T(8,128)S(1)}, f32[144,128]{1,0:T(8,128)S(1)}, u32[]{:S(2)}, u32[]{:S(2)}) collective-permute-start(f32[144,128]{1,0:T(8,128)S(1)} %get-tuple-element.52.refs_6_), channel_id=1, source_target_pairs={{0,16},{8,24},{16,0},{24,8},{1,17},{9,25},{17,1},{25,9},{2,18},{10... | collective-permute-start | bytes 221192 | tf_op jit(solution)/shard_map/ppermute | solution.py:254
  65.6 1.4 %collective-permute-start.20 = (f32[144,128]{1,0:T(8,128)S(1)}, f32[144,128]{1,0:T(8,128)S(1)}, u32[]{:S(2)}, u32[]{:S(2)}) collective-permute-start(f32[144,128]{1,0:T(8,128)S(1)} %get-tuple-element.52.refs_6_), channel_id=1, source_target_pairs={{0,8},{8,0},{16,24},{24,16},{1,9},{9,1},{17,25},{25,17},{2,10},{10... | collective-permute-start | bytes 221192 | tf_op jit(solution)/shard_map/ppermute | solution.py:254
  67.0 1.8 %collective-permute-done.22.refs_9_ = f32[144,128]{1,0:T(8,128)S(1)} collective-permute-done((f32[144,128]{1,0:T(8,128)S(1)}, f32[144,128]{1,0:T(8,128)S(1)}, u32[]{:S(2)}, u32[]{:S(2)}) %collective-permute-start.22) | collective-permute-done | bytes 73760 | tf_op jit(solution)/shard_map/ppermute | solution.py:254
  68.8 1.7 %collective-permute-done.21.refs_8_ = f32[144,128]{1,0:T(8,128)S(1)} collective-permute-done((f32[144,128]{1,0:T(8,128)S(1)}, f32[144,128]{1,0:T(8,128)S(1)}, u32[]{:S(2)}, u32[]{:S(2)}) %collective-permute-start.21) | collective-permute-done | bytes 73760 | tf_op jit(solution)/shard_map/ppermute | solution.py:254
  70.5 0.3 collective-permute-done.20.refs_7_
  70.8 2.2 %copy-done.3 = bf16[32,256,256]{2,1,0:T(8,128)(2,1)S(1)} copy-done((bf16[32,256,256]{2,1,0:T(8,128)(2,1)S(1)}, bf16[32,256,256]{2,1,0:T(8,128)(2,1)}, u32[]{:S(2)}) %copy-start.3) | copy-done | bytes 4194328
  72.9 2.3 %primal_0.1 = (f32[128,128]{1,0:T(8,128)}, f32[80,128]{1,0:T(8,128)S(1)}, f32[80,128]{1,0:T(8,128)S(1)}) custom-call(s32[1,1,32]{2,1,0:T(1,128)S(1)} %copy-done.16, s32[1,1,32]{2,1,0:T(1,128)S(1)} %copy-done.18, s32[1,1]{1,0:T(1,128)S(6)} %copy.17.refs_2_, f32[2]{0:T(128)S(1)} %copy-done.19, bf16[32,256,256]{2,1,0:T(8,128)(2,1)S(1)} %copy-done.3, ...), custom_call_target="tpu_custom_call" | custom-call | flops 4194304 | bytes 4194304 | tf_op jit(solution)/shard_map/primal_0/pallas_call | solution.py:239
  75.3 1.2 %collective-permute-done.23.refs_2_ = f32[80,128]{1,0:T(8,128)S(1)} collective-permute-done((f32[80,128]{1,0:T(8,128)S(1)}, f32[80,128]{1,0:T(8,128)S(1)}, u32[]{:S(2)}, u32[]{:S(2)}) %collective-permute-start.23) | collective-permute-done | bytes 40992 | tf_op jit(solution)/shard_map/ppermute | solution.py:377
  76.5 0.9 %collective-permute-start.24 = (f32[32,128]{1,0:T(8,128)S(1)}, f32[32,128]{1,0:T(8,128)S(1)}, u32[]{:S(2)}, u32[]{:S(2)}) collective-permute-start(f32[32,128]{1,0:T(8,128)S(1)} %get-tuple-element.62), channel_id=1, source_target_pairs={{0,2},{1,3},{2,0},{3,1},{4,6},{5,7},{6,4},{7,5},{8,10},{9,11},{10,... | collective-permute-start | bytes 49160 | tf_op jit(solution)/shard_map/ppermute | solution.py:254
  77.4 1.3 %collective-permute-start.25 = (f32[32,128]{1,0:T(8,128)S(1)}, f32[32,128]{1,0:T(8,128)S(1)}, u32[]{:S(2)}, u32[]{:S(2)}) collective-permute-start(f32[32,128]{1,0:T(8,128)S(1)} %get-tuple-element.63), channel_id=1, source_target_pairs={{0,4},{1,5},{2,6},{3,7},{4,0},{5,1},{6,2},{7,3},{8,12},{9,13},{10,... | collective-permute-start | bytes 49160 | tf_op jit(solution)/shard_map/ppermute | solution.py:254
  78.6 1.4 %collective-permute-start.26 = (f32[32,128]{1,0:T(8,128)S(1)}, f32[32,128]{1,0:T(8,128)S(1)}, u32[]{:S(2)}, u32[]{:S(2)}) collective-permute-start(f32[32,128]{1,0:T(8,128)S(1)} %get-tuple-element.64), channel_id=1, source_target_pairs={{0,6},{1,7},{2,4},{3,5},{4,2},{5,3},{6,0},{7,1},{8,14},{9,15},{10,... | collective-permute-start | bytes 49160 | tf_op jit(solution)/shard_map/ppermute | solution.py:254
  80.1 0.2 collective-permute-done.24.refs_3_
  80.3 0.8 collective-permute-done.25.refs_4_
  81.1 2.2 %collective-permute-done.26.refs_5_ = f32[32,128]{1,0:T(8,128)S(1)} collective-permute-done((f32[32,128]{1,0:T(8,128)S(1)}, f32[32,128]{1,0:T(8,128)S(1)}, u32[]{:S(2)}, u32[]{:S(2)}) %collective-permute-start.26) | collective-permute-done | bytes 16416 | tf_op jit(solution)/shard_map/ppermute | solution.py:254
  83.3 1.2 %last.1 = (f32[16,128]{1,0:T(8,128)}, f32[2]{0:T(128)}) custom-call(s32[1]{0:T(128)} %bitcast.16.refs_12_.refs_0_, f32[2]{0:T(128)S(1)} %copy-done.19, f32[32,128]{1,0:T(8,128)S(1)} %get-tuple-element.61.refs_2_, f32[32,128]{1,0:T(8,128)S(1)} %collective-permute-done.24.refs_3_, f32[32,128]{1,0:T(8,128)S(1)} %collective-permute-done.25.refs_4_, ...), custom_call_target="tpu_custom_call" | custom-call | tf_op jit(solution)/shard_map/last/pallas_call | solution.py:239
  (43 shorter events, 0.1 us)
Async XLA Ops:
  0.6 18.7 %copy-start.19 = (f32[2]{0:T(128)S(1)}, f32[2]{0:T(128)}, u32[]{:S(2)}) copy-start(f32[2]{0:T(128)} %refs_1_.17) | copy-start | bytes 28
  1.3 2.2 %copy-start.4 = (bf16[1,1,32,256,256]{4,3,2,1,0:T(8,128)(2,1)S(1)}, bf16[1,1,32,256,256]{4,3,2,1,0:T(8,128)(2,1)}, u32[]{:S(2)}) copy-start(bf16[1,1,32,256,256]{4,3,2,1,0:T(8,128)(2,1)} %refs_3_.6) | copy-start | bytes 12582916
  3.5 0.9 %copy-start.6 = (s32[3,16384]{1,0:T(4,128)S(1)}, s32[3,16384]{1,0:T(4,128)}, u32[]{:S(2)}) copy-start(s32[3,16384]{1,0:T(4,128)} %param.21) | copy-start | bytes 589828
  4.4 0.8 copy-start.10
  5.3 0.7 copy-start.15
  5.9 0.7 copy-start.17
  6.6 12.7 %copy-start.5 = (s32[3,16384]{1,0:T(4,128)S(1)}, s32[3,16384]{1,0:T(4,128)}, u32[]{:S(2)}) copy-start(s32[3,16384]{1,0:T(4,128)} %param.20) | copy-start | bytes 589828
  6.6 12.7 %copy-start.11 = (f32[16384]{0:T(1024)S(1)}, f32[16384]{0:T(1024)}, u32[]{:S(2)}) copy-start(f32[16384]{0:T(1024)} %param.26) | copy-start | bytes 196612
  6.6 23.2 %copy-start.7 = (s32[3,16384]{1,0:T(4,128)S(1)}, s32[3,16384]{1,0:T(4,128)}, u32[]{:S(2)}) copy-start(s32[3,16384]{1,0:T(4,128)} %param.21) | copy-start | bytes 589828
  8.6 22.5 %copy-start = (bf16[32,256,256]{2,1,0:T(8,128)(2,1)}, bf16[32,256,256]{2,1,0:T(8,128)(2,1)S(1)}, u32[]{:S(2)}) copy-start(bf16[32,256,256]{2,1,0:T(8,128)(2,1)S(1)} %get-tuple-element.36.refs_4_.refs_5_) | copy-start | bytes 12582916
  8.6 7.7 %collective-permute-start.2 = (f32[128,128]{1,0:T(8,128)S(1)}, f32[128,128]{1,0:T(8,128)S(1)}, u32[]{:S(2)}, u32[]{:S(2)}) collective-permute-start(f32[128,128]{1,0:T(8,128)S(1)} %get-tuple-element.37.refs_6_), channel_id=1, source_target_pairs={{0,24},{8,16},{16,8},{24,0},{1,25},{9,17},{17,9},{25,1},{2,26},{10... | collective-permute-start | bytes 196616 | tf_op jit(solution)/shard_map/ppermute | solution.py:254
  13.7 5.6 %collective-permute-start.1 = (f32[128,128]{1,0:T(8,128)S(1)}, f32[128,128]{1,0:T(8,128)S(1)}, u32[]{:S(2)}, u32[]{:S(2)}) collective-permute-start(f32[128,128]{1,0:T(8,128)S(1)} %get-tuple-element.37.refs_6_), channel_id=1, source_target_pairs={{0,16},{8,24},{16,0},{24,8},{1,17},{9,25},{17,1},{25,9},{2,18},{10... | collective-permute-start | bytes 196616 | tf_op jit(solution)/shard_map/ppermute | solution.py:254
  13.7 5.6 %collective-permute-start = (f32[128,128]{1,0:T(8,128)S(1)}, f32[128,128]{1,0:T(8,128)S(1)}, u32[]{:S(2)}, u32[]{:S(2)}) collective-permute-start(f32[128,128]{1,0:T(8,128)S(1)} %get-tuple-element.37.refs_6_), channel_id=1, source_target_pairs={{0,8},{8,0},{16,24},{24,16},{1,9},{9,1},{17,25},{25,17},{2,10},{10... | collective-permute-start | bytes 196616 | tf_op jit(solution)/shard_map/ppermute | solution.py:254
  19.3 16.2 %copy-start.8 = (f32[3,16384]{1,0:T(4,128)S(1)}, f32[3,16384]{1,0:T(4,128)}, u32[]{:S(2)}) copy-start(f32[3,16384]{1,0:T(4,128)} %param.19) | copy-start | bytes 589828
  19.3 16.2 %copy-start.16 = (s32[1,1,32]{2,1,0:T(1,128)S(1)}, s32[1,1,32]{2,1,0:T(1,128)}, u32[]{:S(2)}) copy-start(s32[1,1,32]{2,1,0:T(1,128)} %refs_0_.15) | copy-start | bytes 388
  19.3 16.2 %copy-start.18 = (s32[1,1,32]{2,1,0:T(1,128)S(1)}, s32[1,1,32]{2,1,0:T(1,128)}, u32[]{:S(2)}) copy-start(s32[1,1,32]{2,1,0:T(1,128)} %refs_1_.16) | copy-start | bytes 388
  21.2 1.3 %collective-permute-start.3 = (f32[128,128]{1,0:T(8,128)S(1)}, f32[128,128]{1,0:T(8,128)S(1)}, u32[]{:S(2)}, u32[]{:S(2)}) collective-permute-start(f32[128,128]{1,0:T(8,128)S(1)} %get-tuple-element.38), channel_id=1, source_target_pairs={{0,1},{1,0},{2,3},{3,2},{4,5},{5,4},{6,7},{7,6},{8,9},{9,8},{10,11... | collective-permute-start | bytes 196616 | tf_op jit(solution)/shard_map/ppermute | solution.py:399
  22.5 5.3 %collective-permute-start.6 = (f32[128,128]{1,0:T(8,128)S(1)}, f32[128,128]{1,0:T(8,128)S(1)}, u32[]{:S(2)}, u32[]{:S(2)}) collective-permute-start(f32[128,128]{1,0:T(8,128)S(1)} %add.15.refs_6_), channel_id=1, source_target_pairs={{0,6},{1,7},{2,4},{3,5},{4,2},{5,3},{6,0},{7,1},{8,14},{9,15},{10,... | collective-permute-start | bytes 196616 | tf_op jit(solution)/shard_map/ppermute | solution.py:254
  25.0 4.3 %collective-permute-start.5 = (f32[128,128]{1,0:T(8,128)S(1)}, f32[128,128]{1,0:T(8,128)S(1)}, u32[]{:S(2)}, u32[]{:S(2)}) collective-permute-start(f32[128,128]{1,0:T(8,128)S(1)} %add.15.refs_6_), channel_id=1, source_target_pairs={{0,4},{1,5},{2,6},{3,7},{4,0},{5,1},{6,2},{7,3},{8,12},{9,13},{10,... | collective-permute-start | bytes 196616 | tf_op jit(solution)/shard_map/ppermute | solution.py:254
  25.5 4.3 %collective-permute-start.4 = (f32[128,128]{1,0:T(8,128)S(1)}, f32[128,128]{1,0:T(8,128)S(1)}, u32[]{:S(2)}, u32[]{:S(2)}) collective-permute-start(f32[128,128]{1,0:T(8,128)S(1)} %add.15.refs_6_), channel_id=1, source_target_pairs={{0,2},{1,3},{2,0},{3,1},{4,6},{5,7},{6,4},{7,5},{8,10},{9,11},{10,... | collective-permute-start | bytes 196616 | tf_op jit(solution)/shard_map/ppermute | solution.py:254
  31.1 11.5 %collective-permute-start.9 = (f32[128,128]{1,0:T(8,128)S(1)}, f32[128,128]{1,0:T(8,128)S(1)}, u32[]{:S(2)}, u32[]{:S(2)}) collective-permute-start(f32[128,128]{1,0:T(8,128)S(1)} %get-tuple-element.41.refs_6_), channel_id=1, source_target_pairs={{0,24},{8,16},{16,8},{24,0},{1,25},{9,17},{17,9},{25,1},{2,26},{10... | collective-permute-start | bytes 196616 | tf_op jit(solution)/shard_map/ppermute | solution.py:254
  33.9 9.9 %collective-permute-start.8 = (f32[128,128]{1,0:T(8,128)S(1)}, f32[128,128]{1,0:T(8,128)S(1)}, u32[]{:S(2)}, u32[]{:S(2)}) collective-permute-start(f32[128,128]{1,0:T(8,128)S(1)} %get-tuple-element.41.refs_6_), channel_id=1, source_target_pairs={{0,16},{8,24},{16,0},{24,8},{1,17},{9,25},{17,1},{25,9},{2,18},{10... | collective-permute-start | bytes 196616 | tf_op jit(solution)/shard_map/ppermute | solution.py:254
  33.9 9.9 %collective-permute-start.7 = (f32[128,128]{1,0:T(8,128)S(1)}, f32[128,128]{1,0:T(8,128)S(1)}, u32[]{:S(2)}, u32[]{:S(2)}) collective-permute-start(f32[128,128]{1,0:T(8,128)S(1)} %get-tuple-element.41.refs_6_), channel_id=1, source_target_pairs={{0,8},{8,0},{16,24},{24,16},{1,9},{9,1},{17,25},{25,17},{2,10},{10... | collective-permute-start | bytes 196616 | tf_op jit(solution)/shard_map/ppermute | solution.py:254
  35.5 2.2 %copy-start.1 = (bf16[32,256,256]{2,1,0:T(8,128)(2,1)S(1)}, bf16[32,256,256]{2,1,0:T(8,128)(2,1)}, u32[]{:S(2)}) copy-start(bf16[32,256,256]{2,1,0:T(8,128)(2,1)} %copy-done) | copy-start | bytes 12582916
  37.7 21.5 %copy-start.9 = (f32[3,16384]{1,0:T(4,128)S(1)}, f32[3,16384]{1,0:T(4,128)}, u32[]{:S(2)}) copy-start(f32[3,16384]{1,0:T(4,128)} %param.18) | copy-start | bytes 589828
  37.7 21.5 %copy-start.12 = (f32[16384]{0:T(1024)S(1)}, f32[16384]{0:T(1024)}, u32[]{:S(2)}) copy-start(f32[16384]{0:T(1024)} %param.22) | copy-start | bytes 196612
  37.7 21.5 %copy-start.13 = (f32[16384]{0:T(1024)S(1)}, f32[16384]{0:T(1024)}, u32[]{:S(2)}) copy-start(f32[16384]{0:T(1024)} %param.24) | copy-start | bytes 196612
  39.3 6.3 %collective-permute-start.14 = (f32[3,32,128]{2,1,0:T(8,128)S(1)}, f32[3,32,128]{2,1,0:T(8,128)S(1)}, u32[]{:S(2)}, u32[]{:S(2)}) collective-permute-start(f32[3,32,128]{2,1,0:T(8,128)S(1)} %get-tuple-element.48), channel_id=1, source_target_pairs={{0,8},{8,0},{16,24},{24,16},{1,9},{9,1},{17,25},{25,17},{2,10},{10... | collective-permute-start | bytes 147464 | tf_op jit(solution)/shard_map/ppermute | solution.py:254
  39.7 5.9 %collective-permute-start.15 = (f32[3,32,128]{2,1,0:T(8,128)S(1)}, f32[3,32,128]{2,1,0:T(8,128)S(1)}, u32[]{:S(2)}, u32[]{:S(2)}) collective-permute-start(f32[3,32,128]{2,1,0:T(8,128)S(1)} %get-tuple-element.49), channel_id=1, source_target_pairs={{0,16},{8,24},{16,0},{24,8},{1,17},{9,25},{17,1},{25,9},{2,18},{10... | collective-permute-start | bytes 147464 | tf_op jit(solution)/shard_map/ppermute | solution.py:254
  42.6 6.0 %collective-permute-start.16 = (f32[3,32,128]{2,1,0:T(8,128)S(1)}, f32[3,32,128]{2,1,0:T(8,128)S(1)}, u32[]{:S(2)}, u32[]{:S(2)}) collective-permute-start(f32[3,32,128]{2,1,0:T(8,128)S(1)} %get-tuple-element.50), channel_id=1, source_target_pairs={{0,24},{8,16},{16,8},{24,0},{1,25},{9,17},{17,9},{25,1},{2,26},{10... | collective-permute-start | bytes 147464 | tf_op jit(solution)/shard_map/ppermute | solution.py:254
  43.8 17.4 %copy-start.2 = (bf16[32,256,256]{2,1,0:T(8,128)(2,1)S(1)}, bf16[32,256,256]{2,1,0:T(8,128)(2,1)}, u32[]{:S(2)}) copy-start(bf16[32,256,256]{2,1,0:T(8,128)(2,1)} %copy-done) | copy-start | bytes 12582916
  43.8 17.4 %copy-start.14 = (f32[16384]{0:T(1024)S(1)}, f32[16384]{0:T(1024)}, u32[]{:S(2)}) copy-start(f32[16384]{0:T(1024)} %param.23) | copy-start | bytes 196612
  45.6 4.1 %collective-permute-start.10 = (f32[128,128]{1,0:T(8,128)S(1)}, f32[128,128]{1,0:T(8,128)S(1)}, u32[]{:S(2)}, u32[]{:S(2)}) collective-permute-start(f32[128,128]{1,0:T(8,128)S(1)} %get-tuple-element.44), channel_id=1, source_target_pairs={{0,1},{1,0},{2,3},{3,2},{4,5},{5,4},{6,7},{7,6},{8,9},{9,8},{10,11... | collective-permute-start | bytes 196616 | tf_op jit(solution)/shard_map/ppermute | solution.py:399
  48.7 6.1 %collective-permute-start.19 = (f32[3,32,128]{2,1,0:T(8,128)S(1)}, f32[3,32,128]{2,1,0:T(8,128)S(1)}, u32[]{:S(2)}, u32[]{:S(2)}) collective-permute-start(f32[3,32,128]{2,1,0:T(8,128)S(1)} %add_add_fusion.refs_6_), channel_id=1, source_target_pairs={{0,24},{8,16},{16,8},{24,0},{1,25},{9,17},{17,9},{25,1},{2,26},{10... | collective-permute-start | bytes 147464 | tf_op jit(solution)/shard_map/ppermute | solution.py:254
  49.7 11.4 %collective-permute-start.13 = (f32[128,128]{1,0:T(8,128)S(1)}, f32[128,128]{1,0:T(8,128)S(1)}, u32[]{:S(2)}, u32[]{:S(2)}) collective-permute-start(f32[128,128]{1,0:T(8,128)S(1)} %add.16.refs_6_), channel_id=1, source_target_pairs={{0,6},{1,7},{2,4},{3,5},{4,2},{5,3},{6,0},{7,1},{8,14},{9,15},{10,... | collective-permute-start | bytes 196616 | tf_op jit(solution)/shard_map/ppermute | solution.py:254
  51.3 9.9 %collective-permute-start.12 = (f32[128,128]{1,0:T(8,128)S(1)}, f32[128,128]{1,0:T(8,128)S(1)}, u32[]{:S(2)}, u32[]{:S(2)}) collective-permute-start(f32[128,128]{1,0:T(8,128)S(1)} %add.16.refs_6_), channel_id=1, source_target_pairs={{0,4},{1,5},{2,6},{3,7},{4,0},{5,1},{6,2},{7,3},{8,12},{9,13},{10,... | collective-permute-start | bytes 196616 | tf_op jit(solution)/shard_map/ppermute | solution.py:254
  52.1 9.1 %collective-permute-start.11 = (f32[128,128]{1,0:T(8,128)S(1)}, f32[128,128]{1,0:T(8,128)S(1)}, u32[]{:S(2)}, u32[]{:S(2)}) collective-permute-start(f32[128,128]{1,0:T(8,128)S(1)} %add.16.refs_6_), channel_id=1, source_target_pairs={{0,2},{1,3},{2,0},{3,1},{4,6},{5,7},{6,4},{7,5},{8,10},{9,11},{10,... | collective-permute-start | bytes 196616 | tf_op jit(solution)/shard_map/ppermute | solution.py:254
  53.3 5.5 %collective-permute-start.18 = (f32[3,32,128]{2,1,0:T(8,128)S(1)}, f32[3,32,128]{2,1,0:T(8,128)S(1)}, u32[]{:S(2)}, u32[]{:S(2)}) collective-permute-start(f32[3,32,128]{2,1,0:T(8,128)S(1)} %add_add_fusion.refs_6_), channel_id=1, source_target_pairs={{0,16},{8,24},{16,0},{24,8},{1,17},{9,25},{17,1},{25,9},{2,18},{10... | collective-permute-start | bytes 147464 | tf_op jit(solution)/shard_map/ppermute | solution.py:254
  54.7 4.5 %collective-permute-start.17 = (f32[3,32,128]{2,1,0:T(8,128)S(1)}, f32[3,32,128]{2,1,0:T(8,128)S(1)}, u32[]{:S(2)}, u32[]{:S(2)}) collective-permute-start(f32[3,32,128]{2,1,0:T(8,128)S(1)} %add_add_fusion.refs_6_), channel_id=1, source_target_pairs={{0,8},{8,0},{16,24},{24,16},{1,9},{9,1},{17,25},{25,17},{2,10},{10... | collective-permute-start | bytes 147464 | tf_op jit(solution)/shard_map/ppermute | solution.py:254
  62.6 6.2 %collective-permute-start.22 = (f32[144,128]{1,0:T(8,128)S(1)}, f32[144,128]{1,0:T(8,128)S(1)}, u32[]{:S(2)}, u32[]{:S(2)}) collective-permute-start(f32[144,128]{1,0:T(8,128)S(1)} %get-tuple-element.52.refs_6_), channel_id=1, source_target_pairs={{0,24},{8,16},{16,8},{24,0},{1,25},{9,17},{17,9},{25,1},{2,26},{10... | collective-permute-start | bytes 221192 | tf_op jit(solution)/shard_map/ppermute | solution.py:254
  64.5 6.0 %collective-permute-start.21 = (f32[144,128]{1,0:T(8,128)S(1)}, f32[144,128]{1,0:T(8,128)S(1)}, u32[]{:S(2)}, u32[]{:S(2)}) collective-permute-start(f32[144,128]{1,0:T(8,128)S(1)} %get-tuple-element.52.refs_6_), channel_id=1, source_target_pairs={{0,16},{8,24},{16,0},{24,8},{1,17},{9,25},{17,1},{25,9},{2,18},{10... | collective-permute-start | bytes 221192 | tf_op jit(solution)/shard_map/ppermute | solution.py:254
  65.6 5.1 %collective-permute-start.20 = (f32[144,128]{1,0:T(8,128)S(1)}, f32[144,128]{1,0:T(8,128)S(1)}, u32[]{:S(2)}, u32[]{:S(2)}) collective-permute-start(f32[144,128]{1,0:T(8,128)S(1)} %get-tuple-element.52.refs_6_), channel_id=1, source_target_pairs={{0,8},{8,0},{16,24},{24,16},{1,9},{9,1},{17,25},{25,17},{2,10},{10... | collective-permute-start | bytes 221192 | tf_op jit(solution)/shard_map/ppermute | solution.py:254
  70.8 2.2 %copy-start.3 = (bf16[32,256,256]{2,1,0:T(8,128)(2,1)S(1)}, bf16[32,256,256]{2,1,0:T(8,128)(2,1)}, u32[]{:S(2)}) copy-start(bf16[32,256,256]{2,1,0:T(8,128)(2,1)} %copy-done) | copy-start | bytes 12582916
  75.3 1.2 %collective-permute-start.23 = (f32[80,128]{1,0:T(8,128)S(1)}, f32[80,128]{1,0:T(8,128)S(1)}, u32[]{:S(2)}, u32[]{:S(2)}) collective-permute-start(f32[80,128]{1,0:T(8,128)S(1)} %get-tuple-element.60), channel_id=1, source_target_pairs={{0,1},{1,0},{2,3},{3,2},{4,5},{5,4},{6,7},{7,6},{8,9},{9,8},{10,11... | collective-permute-start | bytes 122888 | tf_op jit(solution)/shard_map/ppermute | solution.py:377
  76.5 3.8 %collective-permute-start.24 = (f32[32,128]{1,0:T(8,128)S(1)}, f32[32,128]{1,0:T(8,128)S(1)}, u32[]{:S(2)}, u32[]{:S(2)}) collective-permute-start(f32[32,128]{1,0:T(8,128)S(1)} %get-tuple-element.62), channel_id=1, source_target_pairs={{0,2},{1,3},{2,0},{3,1},{4,6},{5,7},{6,4},{7,5},{8,10},{9,11},{10,... | collective-permute-start | bytes 49160 | tf_op jit(solution)/shard_map/ppermute | solution.py:254
  77.4 3.7 %collective-permute-start.25 = (f32[32,128]{1,0:T(8,128)S(1)}, f32[32,128]{1,0:T(8,128)S(1)}, u32[]{:S(2)}, u32[]{:S(2)}) collective-permute-start(f32[32,128]{1,0:T(8,128)S(1)} %get-tuple-element.63), channel_id=1, source_target_pairs={{0,4},{1,5},{2,6},{3,7},{4,0},{5,1},{6,2},{7,3},{8,12},{9,13},{10,... | collective-permute-start | bytes 49160 | tf_op jit(solution)/shard_map/ppermute | solution.py:254
  78.6 4.6 %collective-permute-start.26 = (f32[32,128]{1,0:T(8,128)S(1)}, f32[32,128]{1,0:T(8,128)S(1)}, u32[]{:S(2)}, u32[]{:S(2)}) collective-permute-start(f32[32,128]{1,0:T(8,128)S(1)} %get-tuple-element.64), channel_id=1, source_target_pairs={{0,6},{1,7},{2,4},{3,5},{4,2},{5,3},{6,0},{7,1},{8,14},{9,15},{10,... | collective-permute-start | bytes 49160 | tf_op jit(solution)/shard_map/ppermute | solution.py:254

commit v4 on v3

--- a/solution.py
+++ b/solution.py
@@ -72,10 +72,19 @@
 
 
 def first_body(
-    step, rows, columns, count, tile_data, mask, cotangent, tiles, term, anchor, out, source, arrived
+    step, rows_far, columns_far, count, tile_data, mask_far, cotangent_far,
+    tiles, term, anchor, out, source, rows, columns, mask, cotangent, arrived, ready,
 ):
     slots = tiles.shape[0]
     chunk = slots // CHUNKS
+    small = [
+        pltpu.make_async_copy(far, near, ready.at[spot])
+        for spot, (far, near) in enumerate(
+            [(mask_far, mask), (cotangent_far, cotangent), (rows_far, rows), (columns_far, columns)]
+        )
+    ]
+    for copy in small:
+        copy.start()
 
     def fetch(part):
         span = pl.ds(part * chunk, chunk)
@@ -83,13 +92,15 @@
 
     for part in range(CHUNKS):
         fetch(part).start()
+    out[...] = jnp.zeros_like(out)
+    for copy in small:
+        copy.wait()
     weight = weight_of(step)
     adjoint = cotangent[...]
     anchor[...] = (1.0 - weight) * adjoint
     value = mask[:, step, :].astype(jnp.float32) * weight * adjoint
     term[...] = value
     source[...] = rounded(value)
-    out[...] = jnp.zeros_like(out)
     for part in range(CHUNKS):
         fetch(part).wait()
         span = range(part * chunk, (part + 1) * chunk)
@@ -208,6 +219,10 @@
         source[step] = rounded(2.0 * half - saved)
     images[...] = jnp.zeros_like(images)
     add_products(False, columns, rows, count, tiles, range(tiles.shape[0]), source, images)
+
+
+def far(array):
+    return pltpu.with_memory_space_constraint(array, pltpu.HBM)
 
 
 def run(body, out_shape, groups, scratch, name, cost=None):
@@ -304,11 +319,21 @@
     tiles, term_y, anchor_y, partial = run(
         functools.partial(first_body, last),
         [pltpu.VMEM((slots, width, width), jnp.bfloat16), full_y, full_y, full_x],
-        where + [(ANY, tile_data), (VMEM, mask_y), (VMEM, lines(dual_cotangent))],
-        [scratch(lines_y, LANES), pltpu.SemaphoreType.DMA((CHUNKS,))],
+        [(ANY, far(tile_row_block)), (ANY, far(tile_column_block)), (SMEM, tile_count)]
+        + [(ANY, far(tile_data)), (ANY, far(mask_y)), (ANY, far(lines(dual_cotangent)))],
+        [
+            scratch(lines_y, LANES),
+            pltpu.SMEM(tile_row_block.shape, jnp.int32),
+            pltpu.SMEM(tile_row_block.shape, jnp.int32),
+            pltpu.VMEM(mask_y.shape, jnp.int32),
+            scratch(lines_y, LANES),
+            pltpu.SemaphoreType.DMA((CHUNKS,)),
+            pltpu.SemaphoreType.DMA((4,)),
+        ],
         "first",
         cost,
     )
+    tiles = pltpu.with_memory_space_constraint(tiles, pltpu.VMEM)
     common = where + [(SMEM, step_sizes), (VMEM, tiles)]
     adjoint_x, anchor_x = lines(primal_cotangent), None
     terms_x, terms_y = [], [term_y]

time: 84.8 us -> 80.1 us (0.945)
  local copies, waits for them, and re-layouts: 9.71 us -> 4.43 us
    unnamed x40 -> x30, local copies, waits for them, and re-layouts: 9.71 us -> 4.43 us
  transfers between devices with their start and end apart: 27 -> 27, of which waited for: 17 -> 17; matrix products, arithmetic and copies ran while one was open for 0% -> 0% of each run, Pallas kernels for 6% -> 7%
where the time goes in v4:
time: 80.1 us; the launch traced here: 79.9 us
  starting transfers between devices  32.8 us (41%)
  waiting for transfers between devices  25.1 us (31%)
  Pallas kernels  15.9 us (20%)
  local copies, waits for them, and re-layouts  4.43 us (6%)
  between operations  1.56 us (2%)
    ppermute x24, starting transfers between devices, exchange(): lax.ppermute(parts[k], axis, [(i, i ^ k * stride) for i in range(size)])  32.8 us
    ppermute x24, waiting for transfers between devices, exchange(): lax.ppermute(parts[k], axis, [(i, i ^ k * stride) for i in range(size)])  22.6 us
    pallas_call x10, Pallas kernels, run(): pl.pallas_call(kernel, out_shape=shapes, in_specs=specs, out_specs=[SMEM...  15.9 us
    unnamed x30, local copies, waits for them, and re-layouts  4.43 us
  transfers between devices with their start and end apart: 27, of which 17 were waited for; matrix products, arithmetic and copies ran while one was open for 0% of the time, Pallas kernels for 7%

profile of v4, /device:TPU:0, one launch (start us, length us, event | category | flops | bytes accessed | tf_op | source)
XLA Modules:
  0.0 79.9 jit_solution(11979455066020468743)
XLA Ops:
  1.4 2.6 %first.1 = (bf16[32,256,256]{2,1,0:T(8,128)(2,1)S(1)}, f32[128,128]{1,0:T(8,128)S(1)}, f32[128,128]{1,0:T(8,128)S(1)}, f32[128,128]{1,0:T(8,128)S(1)}) custom-call(s32[1,1,32]{2,1,0:T(1,128)} %refs_0_.15, s32[1,1,32]{2,1,0:T(1,128)} %refs_1_.16, s32[1,1]{1,0:T(1,128)S(6)} %copy.17.refs_2_, bf16[1,1,32,256,256]{4,3,2,1,0:T(8,128)(2,1)} %refs_3_.6, ...), custom_call_target="tpu_custom_call" | custom-call | flops 4194304 | bytes 4194304 | tf_op jit(solution)/shard_map/first/pallas_call | solution.py:254
  4.0 5.1 %collective-permute-start.2 = (f32[128,128]{1,0:T(8,128)S(1)}, f32[128,128]{1,0:T(8,128)S(1)}, u32[]{:S(2)}, u32[]{:S(2)}) collective-permute-start(f32[128,128]{1,0:T(8,128)S(1)} %get-tuple-element.37.refs_6_), channel_id=1, source_target_pairs={{0,24},{8,16},{16,8},{24,0},{1,25},{9,17},{17,9},{25,1},{2,26},{10... | collective-permute-start | bytes 196616 | tf_op jit(solution)/shard_map/ppermute | solution.py:269
  9.1 0.0 collective-permute-start.1
  9.1 0.6 collective-permute-start
  9.8 1.9 %collective-permute-done.2.refs_9_ = f32[128,128]{1,0:T(8,128)S(1)} collective-permute-done((f32[128,128]{1,0:T(8,128)S(1)}, f32[128,128]{1,0:T(8,128)S(1)}, u32[]{:S(2)}, u32[]{:S(2)}) %collective-permute-start.2) | collective-permute-done | bytes 65568 | tf_op jit(solution)/shard_map/ppermute | solution.py:269
  11.7 3.0 %collective-permute-done.1.refs_8_ = f32[128,128]{1,0:T(8,128)S(1)} collective-permute-done((f32[128,128]{1,0:T(8,128)S(1)}, f32[128,128]{1,0:T(8,128)S(1)}, u32[]{:S(2)}, u32[]{:S(2)}) %collective-permute-start.1) | collective-permute-done | bytes 65568 | tf_op jit(solution)/shard_map/ppermute | solution.py:269
  14.7 0.0 collective-permute-done.refs_7_
  14.8 0.0 copy-start.6
  14.8 1.8 %primal_2.1 = (f32[128,128]{1,0:T(8,128)S(1)}, f32[128,128]{1,0:T(8,128)S(1)}, f32[128,128]{1,0:T(8,128)S(1)}, f32[128,128]{1,0:T(8,128)S(1)}) custom-call(s32[1,1,32]{2,1,0:T(1,128)S(1)} %copy-done.12, s32[1,1,32]{2,1,0:T(1,128)S(1)} %copy-done.13, s32[1,1]{1,0:T(1,128)S(6)} %copy.17.refs_2_, f32[2]{0:T(128)S(1)} %copy-done.14, ...), custom_call_target="tpu_custom_call" | custom-call | flops 4194304 | bytes 4194304 | tf_op jit(solution)/shard_map/primal_2/pallas_call | solution.py:254
  16.6 0.0 collective-permute-start.3
  16.7 1.2 %collective-permute-done.3 = f32[128,128]{1,0:T(8,128)S(1)} collective-permute-done((f32[128,128]{1,0:T(8,128)S(1)}, f32[128,128]{1,0:T(8,128)S(1)}, u32[]{:S(2)}, u32[]{:S(2)}) %collective-permute-start.3) | collective-permute-done | bytes 65568 | tf_op jit(solution)/shard_map/ppermute | solution.py:424
  17.9 2.5 %collective-permute-start.6 = (f32[128,128]{1,0:T(8,128)S(1)}, f32[128,128]{1,0:T(8,128)S(1)}, u32[]{:S(2)}, u32[]{:S(2)}) collective-permute-start(f32[128,128]{1,0:T(8,128)S(1)} %add.15.refs_6_), channel_id=1, source_target_pairs={{0,6},{1,7},{2,4},{3,5},{4,2},{5,3},{6,0},{7,1},{8,14},{9,15},{10,... | collective-permute-start | bytes 196616 | tf_op jit(solution)/shard_map/ppermute | solution.py:269
  20.4 0.5 collective-permute-start.5
  20.9 0.5 collective-permute-start.4
  21.5 1.7 %collective-permute-done.6.refs_9_ = f32[128,128]{1,0:T(8,128)S(1)} collective-permute-done((f32[128,128]{1,0:T(8,128)S(1)}, f32[128,128]{1,0:T(8,128)S(1)}, u32[]{:S(2)}, u32[]{:S(2)}) %collective-permute-start.6) | collective-permute-done | bytes 65568 | tf_op jit(solution)/shard_map/ppermute | solution.py:269
  23.2 1.5 %collective-permute-done.5.refs_8_ = f32[128,128]{1,0:T(8,128)S(1)} collective-permute-done((f32[128,128]{1,0:T(8,128)S(1)}, f32[128,128]{1,0:T(8,128)S(1)}, u32[]{:S(2)}, u32[]{:S(2)}) %collective-permute-start.5) | collective-permute-done | bytes 65568 | tf_op jit(solution)/shard_map/ppermute | solution.py:269
  24.7 0.5 collective-permute-done.4.refs_7_
  25.2 1.3 %dual_1.1 = (f32[128,128]{1,0:T(8,128)S(1)}, f32[128,128]{1,0:T(8,128)S(1)}, f32[128,128]{1,0:T(8,128)S(1)}) custom-call(s32[1,1,32]{2,1,0:T(1,128)S(1)} %copy-done.12, s32[1,1,32]{2,1,0:T(1,128)S(1)} %copy-done.13, s32[1,1]{1,0:T(1,128)S(6)} %copy.17.refs_2_, f32[2]{0:T(128)S(1)} %copy-done.14, bf16[32,256,256]{2,1,0:T(8,128)(2,1)S(1)} %get-tuple-element.36.refs_4_.refs_5_, ...), custom_call_target="tpu_custom_call" | custom-call | flops 4194304 | bytes 4194304 | tf_op jit(solution)/shard_map/dual_1/pallas_call | solution.py:254
  26.5 2.8 %collective-permute-start.9 = (f32[128,128]{1,0:T(8,128)S(1)}, f32[128,128]{1,0:T(8,128)S(1)}, u32[]{:S(2)}, u32[]{:S(2)}) collective-permute-start(f32[128,128]{1,0:T(8,128)S(1)} %get-tuple-element.41.refs_6_), channel_id=1, source_target_pairs={{0,24},{8,16},{16,8},{24,0},{1,25},{9,17},{17,9},{25,1},{2,26},{10... | collective-permute-start | bytes 196616 | tf_op jit(solution)/shard_map/ppermute | solution.py:269
  29.3 0.0 collective-permute-start.8
  29.3 1.7 %collective-permute-start.7 = (f32[128,128]{1,0:T(8,128)S(1)}, f32[128,128]{1,0:T(8,128)S(1)}, u32[]{:S(2)}, u32[]{:S(2)}) collective-permute-start(f32[128,128]{1,0:T(8,128)S(1)} %get-tuple-element.41.refs_6_), channel_id=1, source_target_pairs={{0,8},{8,0},{16,24},{24,16},{1,9},{9,1},{17,25},{25,17},{2,10},{10... | collective-permute-start | bytes 196616 | tf_op jit(solution)/shard_map/ppermute | solution.py:269
  31.0 2.2 %copy-done.1 = bf16[32,256,256]{2,1,0:T(8,128)(2,1)S(1)} copy-done((bf16[32,256,256]{2,1,0:T(8,128)(2,1)S(1)}, bf16[32,256,256]{2,1,0:T(8,128)(2,1)}, u32[]{:S(2)}) %copy-start.1) | copy-done | bytes 4194328
  33.2 1.5 %saved_back.1 = (f32[3,32,128]{2,1,0:T(8,128)S(1)}, f32[3,32,128]{2,1,0:T(8,128)S(1)}, f32[3,32,128]{2,1,0:T(8,128)S(1)}, f32[3,32,128]{2,1,0:T(8,128)S(1)}) custom-call(s32[1,1,32]{2,1,0:T(1,128)S(1)} %copy-done.12, s32[1,1,32]{2,1,0:T(1,128)S(1)} %copy-done.13, s32[1,1]{1,0:T(1,128)S(6)} %copy.17.refs_2_, s32[1]{0:T(128)} %bitcast.9.refs_3_, ...), custom_call_target="tpu_custom_call" | custom-call | flops 4194304 | bytes 4194304 | tf_op jit(solution)/shard_map/saved_back/pallas_call | solution.py:254
  34.7 0.4 collective-permute-start.14
  35.1 2.9 %collective-permute-start.15 = (f32[3,32,128]{2,1,0:T(8,128)S(1)}, f32[3,32,128]{2,1,0:T(8,128)S(1)}, u32[]{:S(2)}, u32[]{:S(2)}) collective-permute-start(f32[3,32,128]{2,1,0:T(8,128)S(1)} %get-tuple-element.49), channel_id=1, source_target_pairs={{0,16},{8,24},{16,0},{24,8},{1,17},{9,25},{17,1},{25,9},{2,18},{10... | collective-permute-start | bytes 147464 | tf_op jit(solution)/shard_map/ppermute | solution.py:269
  38.1 0.0 collective-permute-done.9.refs_9_
  38.1 1.1 %collective-permute-start.16 = (f32[3,32,128]{2,1,0:T(8,128)S(1)}, f32[3,32,128]{2,1,0:T(8,128)S(1)}, u32[]{:S(2)}, u32[]{:S(2)}) collective-permute-start(f32[3,32,128]{2,1,0:T(8,128)S(1)} %get-tuple-element.50), channel_id=1, source_target_pairs={{0,24},{8,16},{16,8},{24,0},{1,25},{9,17},{17,9},{25,1},{2,26},{10... | collective-permute-start | bytes 147464 | tf_op jit(solution)/shard_map/ppermute | solution.py:269
  39.2 0.0 collective-permute-done.8.refs_8_
  39.2 0.0 collective-permute-done.7.refs_7_
  39.2 0.0 copy-start.11
  39.2 1.8 %primal_1.1 = (f32[128,128]{1,0:T(8,128)S(1)}, f32[128,128]{1,0:T(8,128)S(1)}, f32[128,128]{1,0:T(8,128)S(1)}, f32[128,128]{1,0:T(8,128)S(1)}) custom-call(s32[1,1,32]{2,1,0:T(1,128)S(1)} %copy-done.12, s32[1,1,32]{2,1,0:T(1,128)S(1)} %copy-done.13, s32[1,1]{1,0:T(1,128)S(6)} %copy.17.refs_2_, f32[2]{0:T(128)S(1)} %copy-done.14, ...), custom_call_target="tpu_custom_call" | custom-call | flops 4194304 | bytes 4194304 | tf_op jit(solution)/shard_map/primal_1/pallas_call | solution.py:254
  41.0 0.0 collective-permute-start.10
  41.1 0.0 collective-permute-done.14
  41.1 0.0 collective-permute-done.15
  41.1 3.0 %collective-permute-done.16 = f32[3,32,128]{2,1,0:T(8,128)S(1)} collective-permute-done((f32[3,32,128]{2,1,0:T(8,128)S(1)}, f32[3,32,128]{2,1,0:T(8,128)S(1)}, u32[]{:S(2)}, u32[]{:S(2)}) %collective-permute-start.16) | collective-permute-done | bytes 49184 | tf_op jit(solution)/shard_map/ppermute | solution.py:269
  44.1 1.1 %collective-permute-start.19 = (f32[3,32,128]{2,1,0:T(8,128)S(1)}, f32[3,32,128]{2,1,0:T(8,128)S(1)}, u32[]{:S(2)}, u32[]{:S(2)}) collective-permute-start(f32[3,32,128]{2,1,0:T(8,128)S(1)} %add_add_fusion.refs_6_), channel_id=1, source_target_pairs={{0,24},{8,16},{16,8},{24,0},{1,25},{9,17},{17,9},{25,1},{2,26},{10... | collective-permute-start | bytes 147464 | tf_op jit(solution)/shard_map/ppermute | solution.py:269
  45.2 1.5 %collective-permute-start.13 = (f32[128,128]{1,0:T(8,128)S(1)}, f32[128,128]{1,0:T(8,128)S(1)}, u32[]{:S(2)}, u32[]{:S(2)}) collective-permute-start(f32[128,128]{1,0:T(8,128)S(1)} %add.16.refs_6_), channel_id=1, source_target_pairs={{0,6},{1,7},{2,4},{3,5},{4,2},{5,3},{6,0},{7,1},{8,14},{9,15},{10,... | collective-permute-start | bytes 196616 | tf_op jit(solution)/shard_map/ppermute | solution.py:269
  46.7 0.8 collective-permute-start.12
  47.5 1.2 %collective-permute-start.11 = (f32[128,128]{1,0:T(8,128)S(1)}, f32[128,128]{1,0:T(8,128)S(1)}, u32[]{:S(2)}, u32[]{:S(2)}) collective-permute-start(f32[128,128]{1,0:T(8,128)S(1)} %add.16.refs_6_), channel_id=1, source_target_pairs={{0,2},{1,3},{2,0},{3,1},{4,6},{5,7},{6,4},{7,5},{8,10},{9,11},{10,... | collective-permute-start | bytes 196616 | tf_op jit(solution)/shard_map/ppermute | solution.py:269
  48.7 1.4 %collective-permute-done.19.refs_9_ = f32[3,32,128]{2,1,0:T(8,128)S(1)} collective-permute-done((f32[3,32,128]{2,1,0:T(8,128)S(1)}, f32[3,32,128]{2,1,0:T(8,128)S(1)}, u32[]{:S(2)}, u32[]{:S(2)}) %collective-permute-start.19) | collective-permute-done | bytes 49184 | tf_op jit(solution)/shard_map/ppermute | solution.py:269
  50.1 2.0 %collective-permute-start.17 = (f32[3,32,128]{2,1,0:T(8,128)S(1)}, f32[3,32,128]{2,1,0:T(8,128)S(1)}, u32[]{:S(2)}, u32[]{:S(2)}) collective-permute-start(f32[3,32,128]{2,1,0:T(8,128)S(1)} %add_add_fusion.refs_6_), channel_id=1, source_target_pairs={{0,8},{8,0},{16,24},{24,16},{1,9},{9,1},{17,25},{25,17},{2,10},{10... | collective-permute-start | bytes 147464 | tf_op jit(solution)/shard_map/ppermute | solution.py:269
  52.1 2.1 %collective-permute-done.18.refs_8_ = f32[3,32,128]{2,1,0:T(8,128)S(1)} collective-permute-done((f32[3,32,128]{2,1,0:T(8,128)S(1)}, f32[3,32,128]{2,1,0:T(8,128)S(1)}, u32[]{:S(2)}, u32[]{:S(2)}) %collective-permute-start.18) | collective-permute-done | bytes 49184 | tf_op jit(solution)/shard_map/ppermute | solution.py:269
  54.2 0.5 collective-permute-done.17.refs_7_
  54.7 1.9 %saved_image.1 = (f32[3,128,128]{2,1,0:T(8,128)S(1)}, f32[3,128,128]{2,1,0:T(8,128)S(1)}) custom-call(s32[1,1,32]{2,1,0:T(1,128)S(1)} %copy-done.12, s32[1,1,32]{2,1,0:T(1,128)S(1)} %copy-done.13, s32[1,1]{1,0:T(1,128)S(6)} %copy.17.refs_2_, s32[1]{0:T(128)} %bitcast.9.refs_3_, f32[2]{0:T(128)S(1)} %copy-done.14, bf16[32,256,256]{2,1,0:T(8,128)(2,1)S(1)} %copy-done.1, ...), custom_call_target="tpu_custom_call" | custom-call | flops 4194304 | bytes 4194304 | tf_op jit(solution)/shard_map/saved_image/pallas_call | solution.py:254
  56.6 0.0 collective-permute-done.13.refs_9_
  56.6 0.0 collective-permute-done.12.refs_8_
  56.6 0.0 collective-permute-done.11.refs_7_
  56.6 1.4 %dual_0.1 = (f32[128,128]{1,0:T(8,128)S(1)}, f32[128,128]{1,0:T(8,128)S(1)}, f32[144,128]{1,0:T(8,128)S(1)}) custom-call(s32[1,1,32]{2,1,0:T(1,128)S(1)} %copy-done.12, s32[1,1,32]{2,1,0:T(1,128)S(1)} %copy-done.13, s32[1,1]{1,0:T(1,128)S(6)} %copy.17.refs_2_, f32[2]{0:T(128)S(1)} %copy-done.14, bf16[32,256,256]{2,1,0:T(8,128)(2,1)S(1)} %copy-done.2, ...), custom_call_target="tpu_custom_call" | custom-call | flops 4194304 | bytes 4194304 | tf_op jit(solution)/shard_map/dual_0/pallas_call | solution.py:254
  58.0 1.9 %collective-permute-start.22 = (f32[144,128]{1,0:T(8,128)S(1)}, f32[144,128]{1,0:T(8,128)S(1)}, u32[]{:S(2)}, u32[]{:S(2)}) collective-permute-start(f32[144,128]{1,0:T(8,128)S(1)} %get-tuple-element.52.refs_6_), channel_id=1, source_target_pairs={{0,24},{8,16},{16,8},{24,0},{1,25},{9,17},{17,9},{25,1},{2,26},{10... | collective-permute-start | bytes 221192 | tf_op jit(solution)/shard_map/ppermute | solution.py:269
  59.9 1.1 %collective-permute-start.21 = (f32[144,128]{1,0:T(8,128)S(1)}, f32[144,128]{1,0:T(8,128)S(1)}, u32[]{:S(2)}, u32[]{:S(2)}) collective-permute-start(f32[144,128]{1,0:T(8,128)S(1)} %get-tuple-element.52.refs_6_), channel_id=1, source_target_pairs={{0,16},{8,24},{16,0},{24,8},{1,17},{9,25},{17,1},{25,9},{2,18},{10... | collective-permute-start | bytes 221192 | tf_op jit(solution)/shard_map/ppermute | solution.py:269
  61.1 1.4 %collective-permute-start.20 = (f32[144,128]{1,0:T(8,128)S(1)}, f32[144,128]{1,0:T(8,128)S(1)}, u32[]{:S(2)}, u32[]{:S(2)}) collective-permute-start(f32[144,128]{1,0:T(8,128)S(1)} %get-tuple-element.52.refs_6_), channel_id=1, source_target_pairs={{0,8},{8,0},{16,24},{24,16},{1,9},{9,1},{17,25},{25,17},{2,10},{10... | collective-permute-start | bytes 221192 | tf_op jit(solution)/shard_map/ppermute | solution.py:269
  62.4 1.8 %collective-permute-done.22.refs_9_ = f32[144,128]{1,0:T(8,128)S(1)} collective-permute-done((f32[144,128]{1,0:T(8,128)S(1)}, f32[144,128]{1,0:T(8,128)S(1)}, u32[]{:S(2)}, u32[]{:S(2)}) %collective-permute-start.22) | collective-permute-done | bytes 73760 | tf_op jit(solution)/shard_map/ppermute | solution.py:269
  64.2 1.7 %collective-permute-done.21.refs_8_ = f32[144,128]{1,0:T(8,128)S(1)} collective-permute-done((f32[144,128]{1,0:T(8,128)S(1)}, f32[144,128]{1,0:T(8,128)S(1)}, u32[]{:S(2)}, u32[]{:S(2)}) %collective-permute-start.21) | collective-permute-done | bytes 73760 | tf_op jit(solution)/shard_map/ppermute | solution.py:269
  65.9 0.3 collective-permute-done.20.refs_7_
  66.2 2.2 %copy-done.3 = bf16[32,256,256]{2,1,0:T(8,128)(2,1)S(1)} copy-done((bf16[32,256,256]{2,1,0:T(8,128)(2,1)S(1)}, bf16[32,256,256]{2,1,0:T(8,128)(2,1)}, u32[]{:S(2)}) %copy-start.3) | copy-done | bytes 4194328
  68.4 2.3 %primal_0.1 = (f32[128,128]{1,0:T(8,128)}, f32[80,128]{1,0:T(8,128)S(1)}, f32[80,128]{1,0:T(8,128)S(1)}) custom-call(s32[1,1,32]{2,1,0:T(1,128)S(1)} %copy-done.12, s32[1,1,32]{2,1,0:T(1,128)S(1)} %copy-done.13, s32[1,1]{1,0:T(1,128)S(6)} %copy.17.refs_2_, f32[2]{0:T(128)S(1)} %copy-done.14, bf16[32,256,256]{2,1,0:T(8,128)(2,1)S(1)} %copy-done.3, ...), custom_call_target="tpu_custom_call" | custom-call | flops 4194304 | bytes 4194304 | tf_op jit(solution)/shard_map/primal_0/pallas_call | solution.py:254
  70.7 1.2 %collective-permute-done.23.refs_2_ = f32[80,128]{1,0:T(8,128)S(1)} collective-permute-done((f32[80,128]{1,0:T(8,128)S(1)}, f32[80,128]{1,0:T(8,128)S(1)}, u32[]{:S(2)}, u32[]{:S(2)}) %collective-permute-start.23) | collective-permute-done | bytes 40992 | tf_op jit(solution)/shard_map/ppermute | solution.py:402
  72.0 0.8 %collective-permute-start.24 = (f32[32,128]{1,0:T(8,128)S(1)}, f32[32,128]{1,0:T(8,128)S(1)}, u32[]{:S(2)}, u32[]{:S(2)}) collective-permute-start(f32[32,128]{1,0:T(8,128)S(1)} %get-tuple-element.62), channel_id=1, source_target_pairs={{0,2},{1,3},{2,0},{3,1},{4,6},{5,7},{6,4},{7,5},{8,10},{9,11},{10,... | collective-permute-start | bytes 49160 | tf_op jit(solution)/shard_map/ppermute | solution.py:269
  72.8 1.3 %collective-permute-start.25 = (f32[32,128]{1,0:T(8,128)S(1)}, f32[32,128]{1,0:T(8,128)S(1)}, u32[]{:S(2)}, u32[]{:S(2)}) collective-permute-start(f32[32,128]{1,0:T(8,128)S(1)} %get-tuple-element.63), channel_id=1, source_target_pairs={{0,4},{1,5},{2,6},{3,7},{4,0},{5,1},{6,2},{7,3},{8,12},{9,13},{10,... | collective-permute-start | bytes 49160 | tf_op jit(solution)/shard_map/ppermute | solution.py:269
  74.1 1.4 %collective-permute-start.26 = (f32[32,128]{1,0:T(8,128)S(1)}, f32[32,128]{1,0:T(8,128)S(1)}, u32[]{:S(2)}, u32[]{:S(2)}) collective-permute-start(f32[32,128]{1,0:T(8,128)S(1)} %get-tuple-element.64), channel_id=1, source_target_pairs={{0,6},{1,7},{2,4},{3,5},{4,2},{5,3},{6,0},{7,1},{8,14},{9,15},{10,... | collective-permute-start | bytes 49160 | tf_op jit(solution)/shard_map/ppermute | solution.py:269
  75.5 0.2 collective-permute-done.24.refs_3_
  75.8 0.8 collective-permute-done.25.refs_4_
  76.5 2.2 %collective-permute-done.26.refs_5_ = f32[32,128]{1,0:T(8,128)S(1)} collective-permute-done((f32[32,128]{1,0:T(8,128)S(1)}, f32[32,128]{1,0:T(8,128)S(1)}, u32[]{:S(2)}, u32[]{:S(2)}) %collective-permute-start.26) | collective-permute-done | bytes 16416 | tf_op jit(solution)/shard_map/ppermute | solution.py:269
  78.7 1.2 %last.1 = (f32[16,128]{1,0:T(8,128)}, f32[2]{0:T(128)}) custom-call(s32[1]{0:T(128)} %bitcast.16.refs_12_.refs_0_, f32[2]{0:T(128)S(1)} %copy-done.14, f32[32,128]{1,0:T(8,128)S(1)} %get-tuple-element.61.refs_2_, f32[32,128]{1,0:T(8,128)S(1)} %collective-permute-done.24.refs_3_, f32[32,128]{1,0:T(8,128)S(1)} %collective-permute-done.25.refs_4_, ...), custom_call_target="tpu_custom_call" | custom-call | tf_op jit(solution)/shard_map/last/pallas_call | solution.py:254
  (33 shorter events, 0.1 us)
Async XLA Ops:
  0.6 14.1 %copy-start.13 = (s32[1,1,32]{2,1,0:T(1,128)S(1)}, s32[1,1,32]{2,1,0:T(1,128)}, u32[]{:S(2)}) copy-start(s32[1,1,32]{2,1,0:T(1,128)} %refs_1_.16) | copy-start | bytes 388
  0.6 14.1 %copy-start.12 = (s32[1,1,32]{2,1,0:T(1,128)S(1)}, s32[1,1,32]{2,1,0:T(1,128)}, u32[]{:S(2)}) copy-start(s32[1,1,32]{2,1,0:T(1,128)} %refs_0_.15) | copy-start | bytes 388
  0.7 14.1 %copy-start.14 = (f32[2]{0:T(128)S(1)}, f32[2]{0:T(128)}, u32[]{:S(2)}) copy-start(f32[2]{0:T(128)} %refs_1_.17) | copy-start | bytes 28
  0.7 14.1 %copy-start.8 = (f32[16384]{0:T(1024)S(1)}, f32[16384]{0:T(1024)}, u32[]{:S(2)}) copy-start(f32[16384]{0:T(1024)} %param.26) | copy-start | bytes 196612
  0.7 14.1 %copy-start.4 = (s32[3,16384]{1,0:T(4,128)S(1)}, s32[3,16384]{1,0:T(4,128)}, u32[]{:S(2)}) copy-start(s32[3,16384]{1,0:T(4,128)} %param.20) | copy-start | bytes 589828
  1.4 23.8 %copy-start.5 = (s32[3,16384]{1,0:T(4,128)S(1)}, s32[3,16384]{1,0:T(4,128)}, u32[]{:S(2)}) copy-start(s32[3,16384]{1,0:T(4,128)} %param.21) | copy-start | bytes 589828
  4.0 22.5 %copy-start = (bf16[32,256,256]{2,1,0:T(8,128)(2,1)}, bf16[32,256,256]{2,1,0:T(8,128)(2,1)S(1)}, u32[]{:S(2)}) copy-start(bf16[32,256,256]{2,1,0:T(8,128)(2,1)S(1)} %get-tuple-element.36.refs_4_.refs_5_) | copy-start | bytes 12582916
  4.0 7.7 %collective-permute-start.2 = (f32[128,128]{1,0:T(8,128)S(1)}, f32[128,128]{1,0:T(8,128)S(1)}, u32[]{:S(2)}, u32[]{:S(2)}) collective-permute-start(f32[128,128]{1,0:T(8,128)S(1)} %get-tuple-element.37.refs_6_), channel_id=1, source_target_pairs={{0,24},{8,16},{16,8},{24,0},{1,25},{9,17},{17,9},{25,1},{2,26},{10... | collective-permute-start | bytes 196616 | tf_op jit(solution)/shard_map/ppermute | solution.py:269
  9.1 5.6 %collective-permute-start.1 = (f32[128,128]{1,0:T(8,128)S(1)}, f32[128,128]{1,0:T(8,128)S(1)}, u32[]{:S(2)}, u32[]{:S(2)}) collective-permute-start(f32[128,128]{1,0:T(8,128)S(1)} %get-tuple-element.37.refs_6_), channel_id=1, source_target_pairs={{0,16},{8,24},{16,0},{24,8},{1,17},{9,25},{17,1},{25,9},{2,18},{10... | collective-permute-start | bytes 196616 | tf_op jit(solution)/shard_map/ppermute | solution.py:269
  9.1 5.6 %collective-permute-start = (f32[128,128]{1,0:T(8,128)S(1)}, f32[128,128]{1,0:T(8,128)S(1)}, u32[]{:S(2)}, u32[]{:S(2)}) collective-permute-start(f32[128,128]{1,0:T(8,128)S(1)} %get-tuple-element.37.refs_6_), channel_id=1, source_target_pairs={{0,8},{8,0},{16,24},{24,16},{1,9},{9,1},{17,25},{25,17},{2,10},{10... | collective-permute-start | bytes 196616 | tf_op jit(solution)/shard_map/ppermute | solution.py:269
  14.8 16.2 %copy-start.6 = (f32[3,16384]{1,0:T(4,128)S(1)}, f32[3,16384]{1,0:T(4,128)}, u32[]{:S(2)}) copy-start(f32[3,16384]{1,0:T(4,128)} %param.19) | copy-start | bytes 589828
  16.6 1.3 %collective-permute-start.3 = (f32[128,128]{1,0:T(8,128)S(1)}, f32[128,128]{1,0:T(8,128)S(1)}, u32[]{:S(2)}, u32[]{:S(2)}) collective-permute-start(f32[128,128]{1,0:T(8,128)S(1)} %get-tuple-element.38), channel_id=1, source_target_pairs={{0,1},{1,0},{2,3},{3,2},{4,5},{5,4},{6,7},{7,6},{8,9},{9,8},{10,11... | collective-permute-start | bytes 196616 | tf_op jit(solution)/shard_map/ppermute | solution.py:424
  17.9 5.3 %collective-permute-start.6 = (f32[128,128]{1,0:T(8,128)S(1)}, f32[128,128]{1,0:T(8,128)S(1)}, u32[]{:S(2)}, u32[]{:S(2)}) collective-permute-start(f32[128,128]{1,0:T(8,128)S(1)} %add.15.refs_6_), channel_id=1, source_target_pairs={{0,6},{1,7},{2,4},{3,5},{4,2},{5,3},{6,0},{7,1},{8,14},{9,15},{10,... | collective-permute-start | bytes 196616 | tf_op jit(solution)/shard_map/ppermute | solution.py:269
  20.4 4.3 %collective-permute-start.5 = (f32[128,128]{1,0:T(8,128)S(1)}, f32[128,128]{1,0:T(8,128)S(1)}, u32[]{:S(2)}, u32[]{:S(2)}) collective-permute-start(f32[128,128]{1,0:T(8,128)S(1)} %add.15.refs_6_), channel_id=1, source_target_pairs={{0,4},{1,5},{2,6},{3,7},{4,0},{5,1},{6,2},{7,3},{8,12},{9,13},{10,... | collective-permute-start | bytes 196616 | tf_op jit(solution)/shard_map/ppermute | solution.py:269
  20.9 4.3 %collective-permute-start.4 = (f32[128,128]{1,0:T(8,128)S(1)}, f32[128,128]{1,0:T(8,128)S(1)}, u32[]{:S(2)}, u32[]{:S(2)}) collective-permute-start(f32[128,128]{1,0:T(8,128)S(1)} %add.15.refs_6_), channel_id=1, source_target_pairs={{0,2},{1,3},{2,0},{3,1},{4,6},{5,7},{6,4},{7,5},{8,10},{9,11},{10,... | collective-permute-start | bytes 196616 | tf_op jit(solution)/shard_map/ppermute | solution.py:269
  26.5 11.5 %collective-permute-start.9 = (f32[128,128]{1,0:T(8,128)S(1)}, f32[128,128]{1,0:T(8,128)S(1)}, u32[]{:S(2)}, u32[]{:S(2)}) collective-permute-start(f32[128,128]{1,0:T(8,128)S(1)} %get-tuple-element.41.refs_6_), channel_id=1, source_target_pairs={{0,24},{8,16},{16,8},{24,0},{1,25},{9,17},{17,9},{25,1},{2,26},{10... | collective-permute-start | bytes 196616 | tf_op jit(solution)/shard_map/ppermute | solution.py:269
  29.3 9.9 %collective-permute-start.8 = (f32[128,128]{1,0:T(8,128)S(1)}, f32[128,128]{1,0:T(8,128)S(1)}, u32[]{:S(2)}, u32[]{:S(2)}) collective-permute-start(f32[128,128]{1,0:T(8,128)S(1)} %get-tuple-element.41.refs_6_), channel_id=1, source_target_pairs={{0,16},{8,24},{16,0},{24,8},{1,17},{9,25},{17,1},{25,9},{2,18},{10... | collective-permute-start | bytes 196616 | tf_op jit(solution)/shard_map/ppermute | solution.py:269
  29.3 9.9 %collective-permute-start.7 = (f32[128,128]{1,0:T(8,128)S(1)}, f32[128,128]{1,0:T(8,128)S(1)}, u32[]{:S(2)}, u32[]{:S(2)}) collective-permute-start(f32[128,128]{1,0:T(8,128)S(1)} %get-tuple-element.41.refs_6_), channel_id=1, source_target_pairs={{0,8},{8,0},{16,24},{24,16},{1,9},{9,1},{17,25},{25,17},{2,10},{10... | collective-permute-start | bytes 196616 | tf_op jit(solution)/shard_map/ppermute | solution.py:269
  31.0 2.2 %copy-start.1 = (bf16[32,256,256]{2,1,0:T(8,128)(2,1)S(1)}, bf16[32,256,256]{2,1,0:T(8,128)(2,1)}, u32[]{:S(2)}) copy-start(bf16[32,256,256]{2,1,0:T(8,128)(2,1)} %copy-done) | copy-start | bytes 12582916
  33.2 21.5 %copy-start.7 = (f32[3,16384]{1,0:T(4,128)S(1)}, f32[3,16384]{1,0:T(4,128)}, u32[]{:S(2)}) copy-start(f32[3,16384]{1,0:T(4,128)} %param.18) | copy-start | bytes 589828
  33.2 21.5 %copy-start.9 = (f32[16384]{0:T(1024)S(1)}, f32[16384]{0:T(1024)}, u32[]{:S(2)}) copy-start(f32[16384]{0:T(1024)} %param.22) | copy-start | bytes 196612
  33.2 21.5 %copy-start.10 = (f32[16384]{0:T(1024)S(1)}, f32[16384]{0:T(1024)}, u32[]{:S(2)}) copy-start(f32[16384]{0:T(1024)} %param.24) | copy-start | bytes 196612
  34.7 6.3 %collective-permute-start.14 = (f32[3,32,128]{2,1,0:T(8,128)S(1)}, f32[3,32,128]{2,1,0:T(8,128)S(1)}, u32[]{:S(2)}, u32[]{:S(2)}) collective-permute-start(f32[3,32,128]{2,1,0:T(8,128)S(1)} %get-tuple-element.48), channel_id=1, source_target_pairs={{0,8},{8,0},{16,24},{24,16},{1,9},{9,1},{17,25},{25,17},{2,10},{10... | collective-permute-start | bytes 147464 | tf_op jit(solution)/shard_map/ppermute | solution.py:269
  35.1 5.9 %collective-permute-start.15 = (f32[3,32,128]{2,1,0:T(8,128)S(1)}, f32[3,32,128]{2,1,0:T(8,128)S(1)}, u32[]{:S(2)}, u32[]{:S(2)}) collective-permute-start(f32[3,32,128]{2,1,0:T(8,128)S(1)} %get-tuple-element.49), channel_id=1, source_target_pairs={{0,16},{8,24},{16,0},{24,8},{1,17},{9,25},{17,1},{25,9},{2,18},{10... | collective-permute-start | bytes 147464 | tf_op jit(solution)/shard_map/ppermute | solution.py:269
  38.1 6.0 %collective-permute-start.16 = (f32[3,32,128]{2,1,0:T(8,128)S(1)}, f32[3,32,128]{2,1,0:T(8,128)S(1)}, u32[]{:S(2)}, u32[]{:S(2)}) collective-permute-start(f32[3,32,128]{2,1,0:T(8,128)S(1)} %get-tuple-element.50), channel_id=1, source_target_pairs={{0,24},{8,16},{16,8},{24,0},{1,25},{9,17},{17,9},{25,1},{2,26},{10... | collective-permute-start | bytes 147464 | tf_op jit(solution)/shard_map/ppermute | solution.py:269
  39.2 17.4 %copy-start.2 = (bf16[32,256,256]{2,1,0:T(8,128)(2,1)S(1)}, bf16[32,256,256]{2,1,0:T(8,128)(2,1)}, u32[]{:S(2)}) copy-start(bf16[32,256,256]{2,1,0:T(8,128)(2,1)} %copy-done) | copy-start | bytes 12582916
  39.2 17.4 %copy-start.11 = (f32[16384]{0:T(1024)S(1)}, f32[16384]{0:T(1024)}, u32[]{:S(2)}) copy-start(f32[16384]{0:T(1024)} %param.23) | copy-start | bytes 196612
  41.0 4.1 %collective-permute-start.10 = (f32[128,128]{1,0:T(8,128)S(1)}, f32[128,128]{1,0:T(8,128)S(1)}, u32[]{:S(2)}, u32[]{:S(2)}) collective-permute-start(f32[128,128]{1,0:T(8,128)S(1)} %get-tuple-element.44), channel_id=1, source_target_pairs={{0,1},{1,0},{2,3},{3,2},{4,5},{5,4},{6,7},{7,6},{8,9},{9,8},{10,11... | collective-permute-start | bytes 196616 | tf_op jit(solution)/shard_map/ppermute | solution.py:424
  44.1 6.1 %collective-permute-start.19 = (f32[3,32,128]{2,1,0:T(8,128)S(1)}, f32[3,32,128]{2,1,0:T(8,128)S(1)}, u32[]{:S(2)}, u32[]{:S(2)}) collective-permute-start(f32[3,32,128]{2,1,0:T(8,128)S(1)} %add_add_fusion.refs_6_), channel_id=1, source_target_pairs={{0,24},{8,16},{16,8},{24,0},{1,25},{9,17},{17,9},{25,1},{2,26},{10... | collective-permute-start | bytes 147464 | tf_op jit(solution)/shard_map/ppermute | solution.py:269
  45.2 11.4 %collective-permute-start.13 = (f32[128,128]{1,0:T(8,128)S(1)}, f32[128,128]{1,0:T(8,128)S(1)}, u32[]{:S(2)}, u32[]{:S(2)}) collective-permute-start(f32[128,128]{1,0:T(8,128)S(1)} %add.16.refs_6_), channel_id=1, source_target_pairs={{0,6},{1,7},{2,4},{3,5},{4,2},{5,3},{6,0},{7,1},{8,14},{9,15},{10,... | collective-permute-start | bytes 196616 | tf_op jit(solution)/shard_map/ppermute | solution.py:269
  46.7 9.9 %collective-permute-start.12 = (f32[128,128]{1,0:T(8,128)S(1)}, f32[128,128]{1,0:T(8,128)S(1)}, u32[]{:S(2)}, u32[]{:S(2)}) collective-permute-start(f32[128,128]{1,0:T(8,128)S(1)} %add.16.refs_6_), channel_id=1, source_target_pairs={{0,4},{1,5},{2,6},{3,7},{4,0},{5,1},{6,2},{7,3},{8,12},{9,13},{10,... | collective-permute-start | bytes 196616 | tf_op jit(solution)/shard_map/ppermute | solution.py:269
  47.5 9.1 %collective-permute-start.11 = (f32[128,128]{1,0:T(8,128)S(1)}, f32[128,128]{1,0:T(8,128)S(1)}, u32[]{:S(2)}, u32[]{:S(2)}) collective-permute-start(f32[128,128]{1,0:T(8,128)S(1)} %add.16.refs_6_), channel_id=1, source_target_pairs={{0,2},{1,3},{2,0},{3,1},{4,6},{5,7},{6,4},{7,5},{8,10},{9,11},{10,... | collective-permute-start | bytes 196616 | tf_op jit(solution)/shard_map/ppermute | solution.py:269
  48.7 5.5 %collective-permute-start.18 = (f32[3,32,128]{2,1,0:T(8,128)S(1)}, f32[3,32,128]{2,1,0:T(8,128)S(1)}, u32[]{:S(2)}, u32[]{:S(2)}) collective-permute-start(f32[3,32,128]{2,1,0:T(8,128)S(1)} %add_add_fusion.refs_6_), channel_id=1, source_target_pairs={{0,16},{8,24},{16,0},{24,8},{1,17},{9,25},{17,1},{25,9},{2,18},{10... | collective-permute-start | bytes 147464 | tf_op jit(solution)/shard_map/ppermute | solution.py:269
  50.1 4.5 %collective-permute-start.17 = (f32[3,32,128]{2,1,0:T(8,128)S(1)}, f32[3,32,128]{2,1,0:T(8,128)S(1)}, u32[]{:S(2)}, u32[]{:S(2)}) collective-permute-start(f32[3,32,128]{2,1,0:T(8,128)S(1)} %add_add_fusion.refs_6_), channel_id=1, source_target_pairs={{0,8},{8,0},{16,24},{24,16},{1,9},{9,1},{17,25},{25,17},{2,10},{10... | collective-permute-start | bytes 147464 | tf_op jit(solution)/shard_map/ppermute | solution.py:269
  58.0 6.2 %collective-permute-start.22 = (f32[144,128]{1,0:T(8,128)S(1)}, f32[144,128]{1,0:T(8,128)S(1)}, u32[]{:S(2)}, u32[]{:S(2)}) collective-permute-start(f32[144,128]{1,0:T(8,128)S(1)} %get-tuple-element.52.refs_6_), channel_id=1, source_target_pairs={{0,24},{8,16},{16,8},{24,0},{1,25},{9,17},{17,9},{25,1},{2,26},{10... | collective-permute-start | bytes 221192 | tf_op jit(solution)/shard_map/ppermute | solution.py:269
  59.9 6.0 %collective-permute-start.21 = (f32[144,128]{1,0:T(8,128)S(1)}, f32[144,128]{1,0:T(8,128)S(1)}, u32[]{:S(2)}, u32[]{:S(2)}) collective-permute-start(f32[144,128]{1,0:T(8,128)S(1)} %get-tuple-element.52.refs_6_), channel_id=1, source_target_pairs={{0,16},{8,24},{16,0},{24,8},{1,17},{9,25},{17,1},{25,9},{2,18},{10... | collective-permute-start | bytes 221192 | tf_op jit(solution)/shard_map/ppermute | solution.py:269
  61.1 5.1 %collective-permute-start.20 = (f32[144,128]{1,0:T(8,128)S(1)}, f32[144,128]{1,0:T(8,128)S(1)}, u32[]{:S(2)}, u32[]{:S(2)}) collective-permute-start(f32[144,128]{1,0:T(8,128)S(1)} %get-tuple-element.52.refs_6_), channel_id=1, source_target_pairs={{0,8},{8,0},{16,24},{24,16},{1,9},{9,1},{17,25},{25,17},{2,10},{10... | collective-permute-start | bytes 221192 | tf_op jit(solution)/shard_map/ppermute | solution.py:269
  66.2 2.2 %copy-start.3 = (bf16[32,256,256]{2,1,0:T(8,128)(2,1)S(1)}, bf16[32,256,256]{2,1,0:T(8,128)(2,1)}, u32[]{:S(2)}) copy-start(bf16[32,256,256]{2,1,0:T(8,128)(2,1)} %copy-done) | copy-start | bytes 12582916
  70.7 1.2 %collective-permute-start.23 = (f32[80,128]{1,0:T(8,128)S(1)}, f32[80,128]{1,0:T(8,128)S(1)}, u32[]{:S(2)}, u32[]{:S(2)}) collective-permute-start(f32[80,128]{1,0:T(8,128)S(1)} %get-tuple-element.60), channel_id=1, source_target_pairs={{0,1},{1,0},{2,3},{3,2},{4,5},{5,4},{6,7},{7,6},{8,9},{9,8},{10,11... | collective-permute-start | bytes 122888 | tf_op jit(solution)/shard_map/ppermute | solution.py:402
  72.0 3.8 %collective-permute-start.24 = (f32[32,128]{1,0:T(8,128)S(1)}, f32[32,128]{1,0:T(8,128)S(1)}, u32[]{:S(2)}, u32[]{:S(2)}) collective-permute-start(f32[32,128]{1,0:T(8,128)S(1)} %get-tuple-element.62), channel_id=1, source_target_pairs={{0,2},{1,3},{2,0},{3,1},{4,6},{5,7},{6,4},{7,5},{8,10},{9,11},{10,... | collective-permute-start | bytes 49160 | tf_op jit(solution)/shard_map/ppermute | solution.py:269
  72.8 3.7 %collective-permute-start.25 = (f32[32,128]{1,0:T(8,128)S(1)}, f32[32,128]{1,0:T(8,128)S(1)}, u32[]{:S(2)}, u32[]{:S(2)}) collective-permute-start(f32[32,128]{1,0:T(8,128)S(1)} %get-tuple-element.63), channel_id=1, source_target_pairs={{0,4},{1,5},{2,6},{3,7},{4,0},{5,1},{6,2},{7,3},{8,12},{9,13},{10,... | collective-permute-start | bytes 49160 | tf_op jit(solution)/shard_map/ppermute | solution.py:269
  74.1 4.6 %collective-permute-start.26 = (f32[32,128]{1,0:T(8,128)S(1)}, f32[32,128]{1,0:T(8,128)S(1)}, u32[]{:S(2)}, u32[]{:S(2)}) collective-permute-start(f32[32,128]{1,0:T(8,128)S(1)} %get-tuple-element.64), channel_id=1, source_target_pairs={{0,6},{1,7},{2,4},{3,5},{4,2},{5,3},{6,0},{7,1},{8,14},{9,15},{10,... | collective-permute-start | bytes 49160 | tf_op jit(solution)/shard_map/ppermute | solution.py:269

commit v5 on v4

v5 whole, which is shorter than its diff:
```python
import functools
import math

import jax
import jax.numpy as jnp
from jax import lax
from jax.experimental import pallas as pl
from jax.experimental.pallas import tpu as pltpu
from jax.sharding import PartitionSpec as P

LANES = 128
EXTRA = 16
CHUNKS = 4
SCALES = 16
STEPS = 64.0
LIMIT = 32760.0
FINE = 65000.0
LN2 = math.log(2.0)
VMEM = pl.BlockSpec(memory_space=pltpu.VMEM)
SMEM = pl.BlockSpec(memory_space=pltpu.SMEM)
ANY = pl.BlockSpec(memory_space=pl.ANY)
GRANT = 16 * 1024 * 1024


def weight_of(step):
    return (step + 1.0) / (step + 2.0)


def tree_sum(parts):
    while len(parts) > 1:
        parts = [parts[i] + parts[i + 1] for i in range(0, len(parts), 2)]
    return parts[0]


def fold(lines):
    return lines.reshape(-1, 8, LANES).sum(axis=0)


def rounded(values):
    return values.astype(jnp.bfloat16).astype(jnp.float32)


def add_products(transpose, in_index, out_index, count, tiles, slots, source, total):
    per_block = tiles.shape[-1] // LANES
    several = len(total.shape) == 3
    live_count = count[0, 0]
    for slot in slots:
        start = in_index[0, 0, slot] * per_block
        place = out_index[0, 0, slot] * per_block
        live = (live_count > slot).astype(jnp.float32)
        halves = []
        for half in range(per_block):
            if not several:
                halves.append(source[pl.ds(start + half, 1), :])
                continue
            vectors = source.shape[0]
            rows = -(-vectors // 8) * 8
            which = lax.broadcasted_iota(jnp.int32, (rows, LANES), 0)
            stacked = jnp.zeros((rows, LANES), jnp.float32)
            for vector in range(vectors):
                line = source[vector, pl.ds(start + half, 1), :]
                stacked = jnp.where(which == vector, line, stacked)
            halves.append(stacked)
        block = (jnp.concatenate(halves, axis=1) * live).astype(jnp.bfloat16)
        contract = ((1,), (0,)) if transpose else ((1,), (1,))
        product = lax.dot_general(
            block, tiles[slot], (contract, ((), ())), preferred_element_type=jnp.float32
        )
        for half in range(per_block):
            at = pl.ds(place + half, 1)
            lanes = slice(half * LANES, (half + 1) * LANES)
            if several:
                for vector in range(total.shape[0]):
                    total[vector, at, :] += product[vector : vector + 1, lanes]
            else:
                total[at, :] += product[:, lanes]


def whole_scale(lines):
    largest = jnp.maximum(jnp.max(jnp.abs(lines), axis=0, keepdims=True), 1e-30)
    return jnp.floor(jnp.log(largest) * (STEPS / LN2) + 1.0)


def to_units(code):
    return jnp.exp(code * (-LN2 / STEPS)) * LIMIT


def from_units(code):
    return jnp.exp(code * (LN2 / STEPS)) * (1.0 / LIMIT)


def nearest(values):
    return jnp.floor(values + 0.5)


def short(values):
    return values.astype(jnp.int32).astype(jnp.int16)


def long(values):
    return values.astype(jnp.int32).astype(jnp.float32)


def encode(lines):
    code = whole_scale(lines)
    return nearest(lines * to_units(code)), code


def encode_fine(lines):
    code = whole_scale(lines)
    units = lines * to_units(code)
    coarse = nearest(units)
    return coarse, nearest((units - coarse) * FINE), code


def scale_rows(codes):
    which = lax.broadcasted_iota(jnp.int32, (SCALES, LANES), 0)
    rows = jnp.zeros((SCALES, LANES), jnp.float32)
    for spot, code in enumerate(codes):
        rows = jnp.where(which == spot, code, rows)
    return short(rows)


def scales_of(part):
    codes = long(part[part.shape[0] - SCALES :, :])
    return [from_units(codes[spot : spot + 1]) for spot in range(2)]


def first_body(
    step, n_row, rows_far, columns_far, count, tile_data, mask_far, cotangent_far, saved_far,
    tiles, term, anchor, *refs
):
    outs = refs[:n_row]
    source, total, rows, columns, mask, cotangent, saved, arrived, ready = refs[n_row:]
    slots = tiles.shape[0]
    chunk = slots // CHUNKS
    pairs = [(mask_far, mask), (cotangent_far, cotangent), (saved_far, saved)]
    pairs += [(rows_far, rows), (columns_far, columns)]
    small = [
        pltpu.make_async_copy(far_ref, near, ready.at[spot])
        for spot, (far_ref, near) in enumerate(pairs)
    ]
    for copy in small:
        copy.start()

    def fetch(part):
        span = pl.ds(part * chunk, chunk)
        return pltpu.make_async_copy(tile_data.at[0, 0, span], tiles.at[span], arrived.at[part])

    for part in range(CHUNKS):
        fetch(part).start()
    total[...] = jnp.zeros_like(total)
    for copy in small:
        copy.wait()
    weight = weight_of(step)
    adjoint = cotangent[...]
    anchor[...] = (1.0 - weight) * adjoint
    value = mask[:, step, :].astype(jnp.float32) * weight * adjoint
    term[...] = value
    source[0] = rounded(value)
    iterations = source.shape[0] - 1
    for vector in range(iterations):
        source[vector + 1] = rounded(saved[:, vector, :])
    for part in range(CHUNKS):
        fetch(part).wait()
        span = range(part * chunk, (part + 1) * chunk)
        add_products(True, rows, columns, count, tiles, span, source, total)
    lines = total.shape[1]
    share = lines // n_row
    me = lax.axis_index("row")
    units, code = encode(total[0])
    units = short(units)
    for part, out in enumerate(outs):
        at = pl.ds(pl.multiple_of((me ^ part) * share, share), share)
        out[:lines, :] = units
        saved_units, saved_code = encode(total[1:, at, :].reshape(iterations * share, LANES))
        out[lines : lines + iterations * share, :] = short(saved_units)
        out[lines + iterations * share :, :] = scale_rows([code, saved_code])


def dual_body(step, n_col, rows, columns, count, sizes, tiles, mask, parts, before, anchor, *refs):
    last = step == 0
    if last:
        demand, images, terms, term, anchor_out, out, _, source, total = refs
    else:
        saved, term, anchor_out, out, _, source, total = refs
    weight = weight_of(step)
    image = tree_sum([part[...] for part in parts])
    adjoint = before[...] + sizes[0] * image
    anchor_out[...] = anchor[...] + (1.0 - weight) * adjoint
    value = mask[:, step, :].astype(jnp.float32) * weight * adjoint
    term[...] = value
    source[...] = rounded(value)
    total[...] = jnp.zeros_like(total)
    add_products(True, rows, columns, count, tiles, range(tiles.shape[0]), source, total)
    lines = total.shape[0]
    units, code = encode(total[...])
    out[:lines, :] = short(units)
    if last:
        share = demand[...] * (1.0 / n_col)
        found = value * (share - images[0])
        for other, earlier in enumerate(terms):
            found += earlier[...] * (share - images[other + 1])
        coarse, fine, found_code = encode_fine(fold(found))
        out[lines : lines + EXTRA, :] = short(jnp.concatenate([coarse, fine], axis=0))
        out[lines + EXTRA :, :] = scale_rows([code, found_code])
    elif saved is None:
        out[lines:, :] = scale_rows([code])
    else:
        size = saved.shape[0]
        coarse, fine, saved_code = encode_fine(saved[...])
        out[lines : lines + size, :] = short(coarse)
        out[lines + size : lines + 2 * size, :] = short(fine)
        out[lines + 2 * size :, :] = scale_rows([code, saved_code])


def primal_body(kind, step, n_row, n_col, rows, columns, count, sizes, tiles, mask, parts, before, anchor, *refs):
    last = kind == "last"
    if last:
        reduced, terms, final, mine, other, _, source, out = refs
    elif kind == "sums":
        term, adjoint_out, anchor_out, out, saved, _, source = refs
    elif kind == "shares":
        cost, upper, primal, term, adjoint_out, anchor_out, out, reduced, images, _, source, total = refs
    else:
        term, adjoint_out, anchor_out, out, _, source = refs
    sigma = sizes[1]
    weight = weight_of(step)
    lines = mask.shape[0]
    scales = [scales_of(part) for part in parts]
    back = tree_sum([long(part[:lines, :]) * scale[0] for part, scale in zip(parts, scales)])
    adjoint = before[...]
    anchored = (1.0 - weight) * adjoint
    if anchor is not None:
        anchored = anchor[...] + anchored
    value = mask[:, step, :].astype(jnp.float32) * (weight * adjoint - 2.0 * sigma * back)
    after = value + sigma * back
    if last:
        final[...] = after + anchored
    else:
        term[...] = value
        adjoint_out[...] = after
        anchor_out[...] = anchored
    all_slots = range(tiles.shape[0])
    if kind == "shares":
        iterations = reduced.shape[0]
        share = lines // n_row
        size = iterations * share
        me = lax.axis_index("row")
        for part, (held, scale) in enumerate(zip(parts, scales)):
            at = pl.ds(pl.multiple_of((me ^ part) * share, share), share)
            units = long(held[lines : lines + size, :])
            units += long(held[lines + size : lines + 2 * size, :]) * (1.0 / FINE)
            sums = (units * scale[1]).reshape(iterations, share, LANES)
            reduced[:, at, :] = cost[at, :][None] - sums
        source[0] = rounded(value)
        for vector in range(iterations):
            saved = primal[:, vector, :]
            half = jnp.minimum(jnp.maximum(saved - sizes[0] * reduced[vector], 0.0), upper[...])
            source[vector + 1] = rounded(2.0 * half - saved)
        total[...] = jnp.zeros_like(total)
        add_products(False, columns, rows, count, tiles, all_slots, source, total)
        out[...] = total[0]
        images[...] = total[1:]
        return
    source[...] = rounded(value)
    out[...] = jnp.zeros_like(out)
    add_products(False, columns, rows, count, tiles, all_slots, source, out)
    if kind == "sums":
        size = saved.shape[0]
        saved[...] = tree_sum(
            [long(part[lines : lines + size, :]) * scale[1] for part, scale in zip(parts, scales)]
        )
    if last:
        sums = 0.0
        for part, scale in zip(parts, scales):
            units = long(part[lines : lines + EXTRA, :])
            sums += (units[:8] + units[8:] * (1.0 / FINE)) * scale[1]
        found = value * reduced[0]
        for other_step, later in enumerate(terms):
            found += later[...] * reduced[other_step + 1]
        tail = jnp.concatenate([sums, -fold(found)], axis=0)
        share = out.shape[0] // n_col
        core = lax.axis_index("col") % 2
        for chip in range(n_col // 2):
            span = slice(chip * share, (chip + 1) * share)
            mine[span, :] = out[pl.ds((2 * chip + core) * share, share), :]
            other[span, :] = out[pl.ds((2 * chip + 1 - core) * share, share), :]
        mine[n_col // 2 * share :, :] = tail
        other[n_col // 2 * share :, :] = tail


def split_body(n_chip, mine, received, *outs):
    share = (mine.shape[0] - EXTRA) // n_chip
    chip = lax.axis_index("col") // 2
    tail = mine[n_chip * share :, :] + received[n_chip * share :, :]
    for part, out in enumerate(outs):
        at = pl.ds((chip ^ part) * share, share)
        out[:share, :] = mine[at, :] + received[at, :]
        out[share:, :] = tail


def last_body(scales, sizes, parts, term, anchor, adjoint, gradients):
    share = adjoint.shape[0]
    total = tree_sum([part[...] for part in parts])
    at = pl.ds(lax.axis_index("col") * share, share)
    adjoint[...] = term[at, :] + sizes[0] * total[:share] + anchor[at, :]
    gradients[0] = jnp.sum(total[share + 8 : share + 16]) * scales[0]
    gradients[1] = jnp.sum(total[share : share + 8]) * scales[1]


def far(array):
    return pltpu.with_memory_space_constraint(array, pltpu.HBM)


def run(body, out_shape, groups, scratch, name, cost=None, tiles=None):
    flat, specs, widths, aliases = [], [], [], {}
    for spec, value in groups:
        if value is None:
            widths.append(None)
            continue
        many = isinstance(value, (list, tuple))
        widths.append(len(value) if many else 0)
        for array in value if many else [value]:
            if array is tiles:
                aliases[len(flat)] = len(out_shape)
                array = pltpu.with_memory_space_constraint(array, pltpu.VMEM)
            flat.append(array)
            specs.append(spec)

    def kernel(*refs):
        given = list(refs)
        taken = []
        for width in widths:
            if width is None:
                taken.append(None)
            elif width == 0:
                taken.append(given.pop(0))
            else:
                taken.append([given.pop(0) for _ in range(width)])
        body(*taken, *given)

    in_smem = [isinstance(shape, tuple) for shape in out_shape]
    shapes = [shape[1] if isinstance(shape, tuple) else shape for shape in out_shape]
    if tiles is not None:
        shapes.append(pltpu.VMEM(tiles.shape, tiles.dtype))
        in_smem.append(False)
    return pl.pallas_call(
        kernel,
        out_shape=shapes,
        in_specs=specs,
        out_specs=[SMEM if smem else VMEM for smem in in_smem],
        scratch_shapes=scratch,
        input_output_aliases=aliases,
        compiler_params=pltpu.CompilerParams(vmem_limit_bytes=GRANT),
        cost_estimate=cost,
        name=name,
    )(*flat)


def exchange(parts, axis, stride=1):
    size = lax.axis_size(axis)
    return [parts[0]] + [
        lax.ppermute(parts[k], axis, [(i, i ^ (k * stride)) for i in range(size)])
        for k in range(1, size // stride)
    ]


def local(
    tile_data,
    tile_row_block,
    tile_column_block,
    tile_count,
    saved_primal,
    saved_dual,
    primal_mask,
    dual_mask,
    cost_vector,
    demand,
    upper_bound,
    step_sizes,
    primal_cotangent,
    dual_cotangent,
):
    slots, width = tile_data.shape[2], tile_data.shape[-1]
    iterations, row_length = saved_dual.shape
    column_length = saved_primal.shape[1]
    n_row, n_col = lax.axis_size("row"), lax.axis_size("col")
    n_chip = n_col // 2
    lines_y, lines_x = row_length // LANES, column_length // LANES
    share_y, share_x = lines_y // n_col, lines_x // n_row
    saved_lines = iterations * share_x
    last = iterations - 1
    cost = pl.CostEstimate(
        flops=2 * tile_data.size, bytes_accessed=2 * tile_data.size, transcendentals=0
    )

    def lines(array):
        if array.ndim == 1:
            return array.reshape(-1, LANES)
        return array.reshape(iterations, -1, LANES).transpose(1, 0, 2)

    def f32(*shape):
        return jax.ShapeDtypeStruct(shape, jnp.float32)

    def row_part(more):
        return jax.ShapeDtypeStruct((lines_x + more + SCALES, LANES), jnp.int16)

    def scratch(*shape):
        return pltpu.VMEM(shape, jnp.float32)

    mask_x, mask_y = lines(primal_mask), lines(dual_mask)
    full_x, full_y = f32(lines_x, LANES), f32(lines_y, LANES)
    where = [(SMEM, tile_row_block), (SMEM, tile_column_block), (SMEM, tile_count)]
    saved = lines(saved_dual)
    tiles, term_y, anchor_y, *parts = run(
        functools.partial(first_body, last, n_row),
        [pltpu.VMEM((slots, width, width), jnp.bfloat16), full_y, full_y]
        + [row_part(saved_lines)] * n_row,
        [(ANY, far(tile_row_block)), (ANY, far(tile_column_block)), (SMEM, tile_count)]
        + [(ANY, far(tile_data)), (ANY, far(mask_y)), (ANY, far(lines(dual_cotangent)))]
        + [(ANY, far(saved))],
        [
            scratch(iterations + 1, lines_y, LANES),
            scratch(iterations + 1, lines_x, LANES),
            pltpu.SMEM(tile_row_block.shape, jnp.int32),
            pltpu.SMEM(tile_row_block.shape, jnp.int32),
            pltpu.VMEM(mask_y.shape, jnp.int32),
            scratch(lines_y, LANES),
            scratch(*saved.shape),
            pltpu.SemaphoreType.DMA((CHUNKS,)),
            pltpu.SemaphoreType.DMA((5,)),
        ],
        "first",
        cost,
    )
    adjoint_x, anchor_x = lines(primal_cotangent), None
    terms_x, terms_y = [], [term_y]
    reduced = images = saved_sums = None
    for step in reversed(range(iterations)):
        parts = exchange(parts, "row")
        kind = {0: "last", last: "sums", last - 1: "shares"}.get(step, "plain")
        groups = where + [(SMEM, step_sizes), (VMEM, tiles), (VMEM, mask_x), (VMEM, parts)]
        groups += [(VMEM, adjoint_x), (VMEM, anchor_x)]
        body = functools.partial(primal_body, kind, step, n_row, n_col)
        if step == 0:
            break
        outs = [full_x, full_x, full_x, full_y]
        extra = [scratch(lines_x, LANES)]
        if kind == "sums":
            outs.append(f32(saved_lines, LANES))
        if kind == "shares":
            outs += [f32(iterations, lines_x, LANES), f32(iterations, lines_y, LANES)]
            groups += [(VMEM, lines(cost_vector)), (VMEM, lines(upper_bound))]
            groups += [(VMEM, lines(saved_primal))]
            extra = [
                scratch(iterations + 1, lines_x, LANES),
                scratch(iterations + 1, lines_y, LANES),
            ]
        term_x, adjoint_x, anchor_x, partial, *more, tiles = run(
            body, outs, groups, extra, f"primal_{step}", cost, tiles
        )
        if kind == "sums":
            (saved_sums,) = more
        elif kind == "shares":
            reduced, images = more
            saved_sums = None
        terms_x.insert(0, term_x)
        partial = sum_pair(partial)
        parts = exchange([partial] * n_chip, "col", 2)
        groups = where + [(SMEM, step_sizes), (VMEM, tiles), (VMEM, mask_y), (VMEM, parts)]
        groups += [(VMEM, term_y), (VMEM, anchor_y)]
        if step == 1:
            groups += [(VMEM, lines(demand)), (VMEM, images), (VMEM, list(terms_y))]
            out = row_part(EXTRA)
        else:
            groups += [(VMEM, saved_sums)]
            out = row_part(2 * saved_lines if saved_sums is not None else 0)
        term_y, anchor_y, part, tiles = run(
            functools.partial(dual_body, step - 1, n_col),
            [full_y, full_y, out],
            groups,
            [scratch(lines_y, LANES), scratch(lines_x, LANES)],
            f"dual_{step - 1}",
            cost,
            tiles,
        )
        parts = [part] * n_row
        terms_y.insert(0, term_y)
    half_y = f32(n_chip * share_y + EXTRA, LANES)
    primal_adjoint, mine, other, tiles = run(
        body,
        [full_x, half_y, half_y],
        groups + [(VMEM, reduced), (VMEM, terms_x)],
        [scratch(lines_x, LANES), scratch(lines_y, LANES)],
        "primal_0",
        cost,
        tiles,
    )
    received = lax.ppermute(other, "col", [(i, i ^ 1) for i in range(n_col)])
    parts = run(
        functools.partial(split_body, n_chip),
        [f32(share_y + EXTRA, LANES)] * n_chip,
        [(VMEM, mine), (VMEM, received)],
        [],
        "split",
    )
    parts = exchange(parts, "col", 2)
    scales = (1.0 / math.sqrt(column_length * n_col), 1.0 / math.sqrt(row_length * n_row))
    dual_adjoint, gradients = run(
        functools.partial(last_body, scales),
        [f32(share_y, LANES), ("smem", f32(2))],
        [(SMEM, step_sizes), (VMEM, parts), (VMEM, term_y), (VMEM, anchor_y)],
        [],
        "last",
    )
    return (primal_adjoint.reshape(-1), dual_adjoint.reshape(-1), gradients)


def sum_pair(partial):
    size = lax.axis_size("col")
    return partial + lax.ppermute(partial, "col", [(i, i ^ 1) for i in range(size)])


def solution(mesh):
    placed = (
        P("row", "col", None, None, None),
        P("row", "col", None),
        P("row", "col", None),
        P("row", "col"),
        P(None, "col"),
        P(None, "row"),
        P(None, "col"),
        P(None, "row"),
        P("col"),
        P("row"),
        P("col"),
        P(),
        P("col"),
        P("row"),
    )
    return jax.shard_map(
        local,
        mesh=mesh,
        in_specs=placed,
        out_specs=(P("col"), P(("row", "col")), P()),
        check_vma=False,
    )
```

time: 80.1 us -> 68.3 us (0.85)
  starting transfers between devices: 32.8 us -> 25.4 us
  local copies, waits for them, and re-layouts: 4.43 us -> 0.05 us
  waiting for transfers between devices: 25.1 us -> 28.1 us
  Pallas kernels: 15.9 us -> 13.2 us
    ppermute x24 -> x18, starting transfers between devices: 32.8 us -> 25.2 us  [exchange(): lax.ppermute(parts[k], axis, [(i, i ^ k * stride) for i in range(size)])]
    unnamed x30 -> x20, local copies, waits for them, and re-layouts: 4.43 us -> 0.05 us
    pallas_call x10 -> x8, Pallas kernels: 15.9 us -> 13.2 us  [run(): pl.pallas_call(kernel, out_shape=shapes, in_specs=specs, out_specs=[SMEM...]
    ppermute x24 -> x18, waiting for transfers between devices: 22.6 us -> 24.4 us  [exchange(): lax.ppermute(parts[k], axis, [(i, i ^ k * stride) for i in range(size)])]
    ppermute x2, waiting for transfers between devices: 1.24 us -> 2.48 us  [sum_pair(): lax.ppermute(partial, 'col', [(i, i ^ 1) for i in range(size)])]
  transfers between devices with their start and end apart: 27 -> 21, of which waited for: 17 -> 18; matrix products, arithmetic and copies ran while one was open for 0% -> 0% of each run, Pallas kernels for 7% -> 0%
where the time goes in v5:
time: 68.3 us; the launch traced here: 68.2 us
  waiting for transfers between devices  28.1 us (41%)
  starting transfers between devices  25.4 us (37%)
  Pallas kernels  13.2 us (19%)
  between operations  1.51 us (2%)
    ppermute x18, starting transfers between devices, exchange(): lax.ppermute(parts[k], axis, [(i, i ^ k * stride) for i in range(size)])  25.2 us
    ppermute x18, waiting for transfers between devices, exchange(): lax.ppermute(parts[k], axis, [(i, i ^ k * stride) for i in range(size)])  24.4 us
    pallas_call x8, Pallas kernels, run(): pl.pallas_call(kernel, out_shape=shapes, in_specs=specs, out_specs=[SMEM...  13.2 us
    ppermute x2, waiting for transfers between devices, sum_pair(): lax.ppermute(partial, 'col', [(i, i ^ 1) for i in range(size)])  2.48 us
  transfers between devices with their start and end apart: 21, of which 18 were waited for; matrix products, arithmetic and copies ran while one was open for 0% of the time, Pallas kernels for 0%

profile of v5, /device:TPU:0, one launch (start us, length us, event | category | flops | bytes accessed | tf_op | source)
XLA Modules:
  0.0 68.2 jit_solution(5340402529957827931)
XLA Ops:
  0.6 0.0 copy-start.8
  0.6 0.0 copy-start.7
  0.7 0.0 copy-start.9
  0.7 0.0 copy-start.3
  0.7 0.0 copy-start.1
  1.4 0.0 copy-start
  1.4 2.9 %first.1 = (bf16[32,256,256]{2,1,0:T(8,128)(2,1)S(1)}, f32[128,128]{1,0:T(8,128)S(1)}, f32[128,128]{1,0:T(8,128)S(1)}, s16[240,128]{1,0:T(8,128)(2,1)S(1)}, s16[...) custom-call(s32[1,1,32]{2,1,0:T(1,128)} %refs_0_.12, s32[1,1,32]{2,1,0:T(1,128)} %refs_1_.11, ...), custom_call_target="tpu_custom_call" | custom-call | flops 4194304 | bytes 4194304 | tf_op jit(solution)/shard_map/first/pallas_call | solution.py:348
  4.3 3.1 %collective-permute-start = (s16[240,128]{1,0:T(8,128)(2,1)S(1)}, s16[240,128]{1,0:T(8,128)(2,1)S(1)}, u32[]{:S(2)}, u32[]{:S(2)}) collective-permute-start(s16[240,128]{1,0:T(8,128)(2,1)S(1)} %get-tuple-element.42), channel_id=1, source_target_pairs={{0,8},{8,0},{16,24},{24,16},{1,9},{9,1},{17,25},{25,17},{2,10},{10... | collective-permute-start | bytes 184328 | tf_op jit(solution)/shard_map/ppermute | solution.py:364
  7.4 2.6 %collective-permute-start.1 = (s16[240,128]{1,0:T(8,128)(2,1)S(1)}, s16[240,128]{1,0:T(8,128)(2,1)S(1)}, u32[]{:S(2)}, u32[]{:S(2)}) collective-permute-start(s16[240,128]{1,0:T(8,128)(2,1)S(1)} %get-tuple-element.43), channel_id=1, source_target_pairs={{0,16},{8,24},{16,0},{24,8},{1,17},{9,25},{17,1},{25,9},{2,18},{10... | collective-permute-start | bytes 184328 | tf_op jit(solution)/shard_map/ppermute | solution.py:364
  10.0 0.0 collective-permute-start.2
  10.0 0.0 collective-permute-done.refs_7_
  10.0 3.8 %collective-permute-done.1.refs_8_ = s16[240,128]{1,0:T(8,128)(2,1)S(1)} collective-permute-done((s16[240,128]{1,0:T(8,128)(2,1)S(1)}, s16[240,128]{1,0:T(8,128)(2,1)S(1)}, u32[]{:S(2)}, u32[]{:S(2)}) %collective-permute-start.1) | collective-permute-done | bytes 61472 | tf_op jit(solution)/shard_map/ppermute | solution.py:364
  13.8 2.3 %collective-permute-done.2.refs_9_ = s16[240,128]{1,0:T(8,128)(2,1)S(1)} collective-permute-done((s16[240,128]{1,0:T(8,128)(2,1)S(1)}, s16[240,128]{1,0:T(8,128)(2,1)S(1)}, u32[]{:S(2)}, u32[]{:S(2)}) %collective-permute-start.2) | collective-permute-done | bytes 61472 | tf_op jit(solution)/shard_map/ppermute | solution.py:364
  16.0 0.0 copy-done.8
  16.0 0.0 copy-done.7
  16.0 0.0 copy-done.3
  16.0 0.0 copy-done.1
  16.0 0.0 copy-start.2
  16.1 0.0 copy-start.4
  16.1 0.0 copy-start.5
  16.1 1.9 %primal_2.1 = (f32[128,128]{1,0:T(8,128)S(1)}, f32[128,128]{1,0:T(8,128)S(1)}, f32[128,128]{1,0:T(8,128)S(1)}, f32[128,128]{1,0:T(8,128)S(1)}, f32[96,128]{1,0:T(8,128)S(1)}, /*index=5*/bf16[32,256,256]{2,1,0:T(8,128)(2,1)S(1)}) custom-call(s32[1,1,32]{2,1,0:T(1,128)S(1)} %copy-done.7, s32[1,1,32]{2,1,0:T(1,128)S(1)} %copy-done.8, ...), custom_call_target="tpu_custom_call", output_to_operand_aliasing={{5}: (4, {})} | custom-call | flops 4194304 | bytes 4194304 | tf_op jit(solution)/shard_map/primal_2/pallas_call | solution.py:348
  18.0 0.0 collective-permute-start.3
  18.0 1.2 %collective-permute-done.3 = f32[128,128]{1,0:T(8,128)S(1)} collective-permute-done((f32[128,128]{1,0:T(8,128)S(1)}, f32[128,128]{1,0:T(8,128)S(1)}, u32[]{:S(2)}, u32[]{:S(2)}) %collective-permute-start.3) | collective-permute-done | bytes 65568 | tf_op jit(solution)/shard_map/ppermute | solution.py:522
  19.2 2.5 %collective-permute-start.6 = (f32[128,128]{1,0:T(8,128)S(1)}, f32[128,128]{1,0:T(8,128)S(1)}, u32[]{:S(2)}, u32[]{:S(2)}) collective-permute-start(f32[128,128]{1,0:T(8,128)S(1)} %add.6.refs_6_), channel_id=1, source_target_pairs={{0,6},{1,7},{2,4},{3,5},{4,2},{5,3},{6,0},{7,1},{8,14},{9,15},{10,... | collective-permute-start | bytes 196616 | tf_op jit(solution)/shard_map/ppermute | solution.py:364
  21.8 0.5 collective-permute-start.5
  22.3 0.5 collective-permute-start.4
  22.8 1.7 %collective-permute-done.6.refs_9_ = f32[128,128]{1,0:T(8,128)S(1)} collective-permute-done((f32[128,128]{1,0:T(8,128)S(1)}, f32[128,128]{1,0:T(8,128)S(1)}, u32[]{:S(2)}, u32[]{:S(2)}) %collective-permute-start.6) | collective-permute-done | bytes 65568 | tf_op jit(solution)/shard_map/ppermute | solution.py:364
  24.5 1.5 %collective-permute-done.5.refs_8_ = f32[128,128]{1,0:T(8,128)S(1)} collective-permute-done((f32[128,128]{1,0:T(8,128)S(1)}, f32[128,128]{1,0:T(8,128)S(1)}, u32[]{:S(2)}, u32[]{:S(2)}) %collective-permute-start.5) | collective-permute-done | bytes 65568 | tf_op jit(solution)/shard_map/ppermute | solution.py:364
  26.0 0.5 collective-permute-done.4.refs_7_
  26.5 1.4 %dual_1.1 = (f32[128,128]{1,0:T(8,128)S(1)}, f32[128,128]{1,0:T(8,128)S(1)}, s16[336,128]{1,0:T(8,128)(2,1)S(1)}, bf16[32,256,256]{2,1,0:T(8,128)(2,1)S(1)}) custom-call(s32[1,1,32]{2,1,0:T(1,128)S(1)} %copy-done.7, s32[1,1,32]{2,1,0:T(1,128)S(1)} %copy-done.8, s32[1,1]{1,0:T(1,128)S(6)} %copy.27.refs_2_, ...), custom_call_target="tpu_custom_call", output_to_operand_aliasing={{3}: (4, {})} | custom-call | flops 4194304 | bytes 4194304 | tf_op jit(solution)/shard_map/dual_1/pallas_call | solution.py:348
  27.9 1.6 %collective-permute-start.9 = (s16[336,128]{1,0:T(8,128)(2,1)S(1)}, s16[336,128]{1,0:T(8,128)(2,1)S(1)}, u32[]{:S(2)}, u32[]{:S(2)}) collective-permute-start(s16[336,128]{1,0:T(8,128)(2,1)S(1)} %get-tuple-element.51.refs_6_), channel_id=1, source_target_pairs={{0,24},{8,16},{16,8},{24,0},{1,25},{9,17},{17,9},{25,1},{2,26},{10... | collective-permute-start | bytes 258056 | tf_op jit(solution)/shard_map/ppermute | solution.py:364
  29.5 0.0 collective-permute-start.8
  29.5 2.9 %collective-permute-start.7 = (s16[336,128]{1,0:T(8,128)(2,1)S(1)}, s16[336,128]{1,0:T(8,128)(2,1)S(1)}, u32[]{:S(2)}, u32[]{:S(2)}) collective-permute-start(s16[336,128]{1,0:T(8,128)(2,1)S(1)} %get-tuple-element.51.refs_6_), channel_id=1, source_target_pairs={{0,8},{8,0},{16,24},{24,16},{1,9},{9,1},{17,25},{25,17},{2,10},{10... | collective-permute-start | bytes 258056 | tf_op jit(solution)/shard_map/ppermute | solution.py:364
  32.4 2.4 %collective-permute-done.9.refs_9_ = s16[336,128]{1,0:T(8,128)(2,1)S(1)} collective-permute-done((s16[336,128]{1,0:T(8,128)(2,1)S(1)}, s16[336,128]{1,0:T(8,128)(2,1)S(1)}, u32[]{:S(2)}, u32[]{:S(2)}) %collective-permute-start.9) | collective-permute-done | bytes 86048 | tf_op jit(solution)/shard_map/ppermute | solution.py:364
  34.8 2.5 %collective-permute-done.8.refs_8_ = s16[336,128]{1,0:T(8,128)(2,1)S(1)} collective-permute-done((s16[336,128]{1,0:T(8,128)(2,1)S(1)}, s16[336,128]{1,0:T(8,128)(2,1)S(1)}, u32[]{:S(2)}, u32[]{:S(2)}) %collective-permute-start.8) | collective-permute-done | bytes 86048 | tf_op jit(solution)/shard_map/ppermute | solution.py:364
  37.3 0.0 collective-permute-done.7.refs_7_
  37.3 0.0 copy-done.5
  37.3 2.1 %primal_1.1 = (f32[128,128]{1,0:T(8,128)S(1)}, f32[128,128]{1,0:T(8,128)S(1)}, f32[128,128]{1,0:T(8,128)S(1)}, f32[128,128]{1,0:T(8,128)S(1)}, f32[3,128,128]{2,...) custom-call(s32[1,1,32]{2,1,0:T(1,128)S(1)} %copy-done.7, ...), custom_call_target="tpu_custom_call", output_to_operand_aliasing={{6}: (4, {})} | custom-call | flops 4194304 | bytes 4194304 | tf_op jit(solution)/shard_map/primal_1/pallas_call | solution.py:348
  39.4 0.1 collective-permute-start.10
  39.5 1.2 %collective-permute-done.10 = f32[128,128]{1,0:T(8,128)S(1)} collective-permute-done((f32[128,128]{1,0:T(8,128)S(1)}, f32[128,128]{1,0:T(8,128)S(1)}, u32[]{:S(2)}, u32[]{:S(2)}) %collective-permute-start.10) | collective-permute-done | bytes 65568 | tf_op jit(solution)/shard_map/ppermute | solution.py:522
  40.7 1.6 %collective-permute-start.13 = (f32[128,128]{1,0:T(8,128)S(1)}, f32[128,128]{1,0:T(8,128)S(1)}, u32[]{:S(2)}, u32[]{:S(2)}) collective-permute-start(f32[128,128]{1,0:T(8,128)S(1)} %add.7.refs_6_), channel_id=1, source_target_pairs={{0,6},{1,7},{2,4},{3,5},{4,2},{5,3},{6,0},{7,1},{8,14},{9,15},{10,... | collective-permute-start | bytes 196616 | tf_op jit(solution)/shard_map/ppermute | solution.py:364
  42.3 1.3 %collective-permute-start.12 = (f32[128,128]{1,0:T(8,128)S(1)}, f32[128,128]{1,0:T(8,128)S(1)}, u32[]{:S(2)}, u32[]{:S(2)}) collective-permute-start(f32[128,128]{1,0:T(8,128)S(1)} %add.7.refs_6_), channel_id=1, source_target_pairs={{0,4},{1,5},{2,6},{3,7},{4,0},{5,1},{6,2},{7,3},{8,12},{9,13},{10,... | collective-permute-start | bytes 196616 | tf_op jit(solution)/shard_map/ppermute | solution.py:364
  43.6 0.7 %collective-permute-start.11 = (f32[128,128]{1,0:T(8,128)S(1)}, f32[128,128]{1,0:T(8,128)S(1)}, u32[]{:S(2)}, u32[]{:S(2)}) collective-permute-start(f32[128,128]{1,0:T(8,128)S(1)} %add.7.refs_6_), channel_id=1, source_target_pairs={{0,2},{1,3},{2,0},{3,1},{4,6},{5,7},{6,4},{7,5},{8,10},{9,11},{10,... | collective-permute-start | bytes 196616 | tf_op jit(solution)/shard_map/ppermute | solution.py:364
  44.3 1.7 %collective-permute-done.13.refs_9_ = f32[128,128]{1,0:T(8,128)S(1)} collective-permute-done((f32[128,128]{1,0:T(8,128)S(1)}, f32[128,128]{1,0:T(8,128)S(1)}, u32[]{:S(2)}, u32[]{:S(2)}) %collective-permute-start.13) | collective-permute-done | bytes 65568 | tf_op jit(solution)/shard_map/ppermute | solution.py:364
  46.0 1.2 %collective-permute-done.12.refs_8_ = f32[128,128]{1,0:T(8,128)S(1)} collective-permute-done((f32[128,128]{1,0:T(8,128)S(1)}, f32[128,128]{1,0:T(8,128)S(1)}, u32[]{:S(2)}, u32[]{:S(2)}) %collective-permute-start.12) | collective-permute-done | bytes 65568 | tf_op jit(solution)/shard_map/ppermute | solution.py:364
  47.3 0.6 collective-permute-done.11.refs_7_
  47.9 0.0 copy-done.6
  47.9 1.4 %dual_0.1 = (f32[128,128]{1,0:T(8,128)S(1)}, f32[128,128]{1,0:T(8,128)S(1)}, s16[160,128]{1,0:T(8,128)(2,1)S(1)}, bf16[32,256,256]{2,1,0:T(8,128)(2,1)S(1)}) custom-call(s32[1,1,32]{2,1,0:T(1,128)S(1)} %copy-done.7, s32[1,1,32]{2,1,0:T(1,128)S(1)} %copy-done.8, s32[1,1]{1,0:T(1,128)S(6)} %copy.27.refs_2_, ...), custom_call_target="tpu_custom_call", output_to_operand_aliasing={{3}: (4, {})} | custom-call | flops 4194304 | bytes 4194304 | tf_op jit(solution)/shard_map/dual_0/pallas_call | solution.py:348
  49.3 2.4 %collective-permute-start.16 = (s16[160,128]{1,0:T(8,128)(2,1)S(1)}, s16[160,128]{1,0:T(8,128)(2,1)S(1)}, u32[]{:S(2)}, u32[]{:S(2)}) collective-permute-start(s16[160,128]{1,0:T(8,128)(2,1)S(1)} %get-tuple-element.60.refs_6_), channel_id=1, source_target_pairs={{0,24},{8,16},{16,8},{24,0},{1,25},{9,17},{17,9},{25,1},{2,26},{10... | collective-permute-start | bytes 122888 | tf_op jit(solution)/shard_map/ppermute | solution.py:364
  51.7 0.0 collective-permute-start.15
  51.7 2.0 %collective-permute-start.14 = (s16[160,128]{1,0:T(8,128)(2,1)S(1)}, s16[160,128]{1,0:T(8,128)(2,1)S(1)}, u32[]{:S(2)}, u32[]{:S(2)}) collective-permute-start(s16[160,128]{1,0:T(8,128)(2,1)S(1)} %get-tuple-element.60.refs_6_), channel_id=1, source_target_pairs={{0,8},{8,0},{16,24},{24,16},{1,9},{9,1},{17,25},{25,17},{2,10},{10... | collective-permute-start | bytes 122888 | tf_op jit(solution)/shard_map/ppermute | solution.py:364
  53.7 1.7 %collective-permute-done.16.refs_9_ = s16[160,128]{1,0:T(8,128)(2,1)S(1)} collective-permute-done((s16[160,128]{1,0:T(8,128)(2,1)S(1)}, s16[160,128]{1,0:T(8,128)(2,1)S(1)}, u32[]{:S(2)}, u32[]{:S(2)}) %collective-permute-start.16) | collective-permute-done | bytes 40992 | tf_op jit(solution)/shard_map/ppermute | solution.py:364
  55.4 1.2 %collective-permute-done.15.refs_8_ = s16[160,128]{1,0:T(8,128)(2,1)S(1)} collective-permute-done((s16[160,128]{1,0:T(8,128)(2,1)S(1)}, s16[160,128]{1,0:T(8,128)(2,1)S(1)}, u32[]{:S(2)}, u32[]{:S(2)}) %collective-permute-start.15) | collective-permute-done | bytes 40992 | tf_op jit(solution)/shard_map/ppermute | solution.py:364
  56.6 0.0 collective-permute-done.14.refs_7_
  56.6 2.3 %primal_0.1 = (f32[128,128]{1,0:T(8,128)}, f32[80,128]{1,0:T(8,128)S(1)}, f32[80,128]{1,0:T(8,128)S(1)}, bf16[32,256,256]{2,1,0:T(8,128)(2,1)S(1)}) custom-call(s32[1,1,32]{2,1,0:T(1,128)S(1)} %copy-done.7, s32[1,1,32]{2,1,0:T(1,128)S(1)} %copy-done.8, s32[1,1]{1,0:T(1,128)S(6)} %copy.27.refs_2_, f32[2]{0:T(128)S(1)} %copy-done.9, ...), custom_call_target="tpu_custom_call", output_to_operand_aliasing={{3}: (4, {})} | custom-call | flops 4194304 | bytes 4194304 | tf_op jit(solution)/shard_map/primal_0/pallas_call | solution.py:348
  58.9 0.0 collective-permute-start.17
  58.9 1.2 %collective-permute-done.17.refs_1_ = f32[80,128]{1,0:T(8,128)S(1)} collective-permute-done((f32[80,128]{1,0:T(8,128)S(1)}, f32[80,128]{1,0:T(8,128)S(1)}, u32[]{:S(2)}, u32[]{:S(2)}) %collective-permute-start.17) | collective-permute-done | bytes 40992 | tf_op jit(solution)/shard_map/ppermute | solution.py:500
  60.2 0.8 %collective-permute-start.18 = (f32[32,128]{1,0:T(8,128)S(1)}, f32[32,128]{1,0:T(8,128)S(1)}, u32[]{:S(2)}, u32[]{:S(2)}) collective-permute-start(f32[32,128]{1,0:T(8,128)S(1)} %get-tuple-element.70), channel_id=1, source_target_pairs={{0,2},{1,3},{2,0},{3,1},{4,6},{5,7},{6,4},{7,5},{8,10},{9,11},{10,... | collective-permute-start | bytes 49160 | tf_op jit(solution)/shard_map/ppermute | solution.py:364
  61.0 1.4 %collective-permute-start.19 = (f32[32,128]{1,0:T(8,128)S(1)}, f32[32,128]{1,0:T(8,128)S(1)}, u32[]{:S(2)}, u32[]{:S(2)}) collective-permute-start(f32[32,128]{1,0:T(8,128)S(1)} %get-tuple-element.71), channel_id=1, source_target_pairs={{0,4},{1,5},{2,6},{3,7},{4,0},{5,1},{6,2},{7,3},{8,12},{9,13},{10,... | collective-permute-start | bytes 49160 | tf_op jit(solution)/shard_map/ppermute | solution.py:364
  62.4 1.4 %collective-permute-start.20 = (f32[32,128]{1,0:T(8,128)S(1)}, f32[32,128]{1,0:T(8,128)S(1)}, u32[]{:S(2)}, u32[]{:S(2)}) collective-permute-start(f32[32,128]{1,0:T(8,128)S(1)} %get-tuple-element.72), channel_id=1, source_target_pairs={{0,6},{1,7},{2,4},{3,5},{4,2},{5,3},{6,0},{7,1},{8,14},{9,15},{10,... | collective-permute-start | bytes 49160 | tf_op jit(solution)/shard_map/ppermute | solution.py:364
  63.7 0.2 collective-permute-done.18.refs_2_
  64.0 0.7 %collective-permute-done.19.refs_3_ = f32[32,128]{1,0:T(8,128)S(1)} collective-permute-done((f32[32,128]{1,0:T(8,128)S(1)}, f32[32,128]{1,0:T(8,128)S(1)}, u32[]{:S(2)}, u32[]{:S(2)}) %collective-permute-start.19) | collective-permute-done | bytes 16416 | tf_op jit(solution)/shard_map/ppermute | solution.py:364
  64.7 2.3 %collective-permute-done.20.refs_4_ = f32[32,128]{1,0:T(8,128)S(1)} collective-permute-done((f32[32,128]{1,0:T(8,128)S(1)}, f32[32,128]{1,0:T(8,128)S(1)}, u32[]{:S(2)}, u32[]{:S(2)}) %collective-permute-start.20) | collective-permute-done | bytes 16416 | tf_op jit(solution)/shard_map/ppermute | solution.py:364
  67.0 1.2 %last.1 = (f32[16,128]{1,0:T(8,128)}, f32[2]{0:T(128)}) custom-call(f32[2]{0:T(128)S(1)} %copy-done.9, f32[32,128]{1,0:T(8,128)S(1)} %get-tuple-element.69.refs_1_, f32[32,128]{1,0:T(8,128)S(1)} %collective-permute-done.18.refs_2_, f32[32,128]{1,0:T(8,128)S(1)} %collective-permute-done.19.refs_3_, f32[32,128]{1,0:T(8,128)S(1)} %collective-permute-done.20.refs_4_, ...), custom_call_target="tpu_custom_call" | custom-call | tf_op jit(solution)/shard_map/last/pallas_call | solution.py:348
  (8 shorter events, 0.0 us)
Async XLA Ops:
  0.6 15.4 %copy-start.8 = (s32[1,1,32]{2,1,0:T(1,128)S(1)}, s32[1,1,32]{2,1,0:T(1,128)}, u32[]{:S(2)}) copy-start(s32[1,1,32]{2,1,0:T(1,128)} %refs_1_.11) | copy-start | bytes 388
  0.6 15.4 %copy-start.7 = (s32[1,1,32]{2,1,0:T(1,128)S(1)}, s32[1,1,32]{2,1,0:T(1,128)}, u32[]{:S(2)}) copy-start(s32[1,1,32]{2,1,0:T(1,128)} %refs_0_.12) | copy-start | bytes 388
  0.7 15.4 %copy-start.9 = (f32[2]{0:T(128)S(1)}, f32[2]{0:T(128)}, u32[]{:S(2)}) copy-start(f32[2]{0:T(128)} %refs_0_.13) | copy-start | bytes 28
  0.7 15.4 %copy-start.3 = (f32[16384]{0:T(1024)S(1)}, f32[16384]{0:T(1024)}, u32[]{:S(2)}) copy-start(f32[16384]{0:T(1024)} %param.26) | copy-start | bytes 196612
  0.7 15.4 %copy-start.1 = (s32[3,16384]{1,0:T(4,128)S(1)}, s32[3,16384]{1,0:T(4,128)}, u32[]{:S(2)}) copy-start(s32[3,16384]{1,0:T(4,128)} %param.20) | copy-start | bytes 589828
  1.4 25.2 %copy-start = (s32[3,16384]{1,0:T(4,128)S(1)}, s32[3,16384]{1,0:T(4,128)}, u32[]{:S(2)}) copy-start(s32[3,16384]{1,0:T(4,128)} %param.21) | copy-start | bytes 589828
  4.3 5.7 %collective-permute-start = (s16[240,128]{1,0:T(8,128)(2,1)S(1)}, s16[240,128]{1,0:T(8,128)(2,1)S(1)}, u32[]{:S(2)}, u32[]{:S(2)}) collective-permute-start(s16[240,128]{1,0:T(8,128)(2,1)S(1)} %get-tuple-element.42), channel_id=1, source_target_pairs={{0,8},{8,0},{16,24},{24,16},{1,9},{9,1},{17,25},{25,17},{2,10},{10... | collective-permute-start | bytes 184328 | tf_op jit(solution)/shard_map/ppermute | solution.py:364
  7.4 6.3 %collective-permute-start.1 = (s16[240,128]{1,0:T(8,128)(2,1)S(1)}, s16[240,128]{1,0:T(8,128)(2,1)S(1)}, u32[]{:S(2)}, u32[]{:S(2)}) collective-permute-start(s16[240,128]{1,0:T(8,128)(2,1)S(1)} %get-tuple-element.43), channel_id=1, source_target_pairs={{0,16},{8,24},{16,0},{24,8},{1,17},{9,25},{17,1},{25,9},{2,18},{10... | collective-permute-start | bytes 184328 | tf_op jit(solution)/shard_map/ppermute | solution.py:364
  10.0 6.0 %collective-permute-start.2 = (s16[240,128]{1,0:T(8,128)(2,1)S(1)}, s16[240,128]{1,0:T(8,128)(2,1)S(1)}, u32[]{:S(2)}, u32[]{:S(2)}) collective-permute-start(s16[240,128]{1,0:T(8,128)(2,1)S(1)} %get-tuple-element.44), channel_id=1, source_target_pairs={{0,24},{8,16},{16,8},{24,0},{1,25},{9,17},{17,9},{25,1},{2,26},{10... | collective-permute-start | bytes 184328 | tf_op jit(solution)/shard_map/ppermute | solution.py:364
  16.0 21.2 %copy-start.2 = (f32[3,16384]{1,0:T(4,128)S(1)}, f32[3,16384]{1,0:T(4,128)}, u32[]{:S(2)}) copy-start(f32[3,16384]{1,0:T(4,128)} %param.18) | copy-start | bytes 589828
  16.1 21.2 %copy-start.4 = (f32[16384]{0:T(1024)S(1)}, f32[16384]{0:T(1024)}, u32[]{:S(2)}) copy-start(f32[16384]{0:T(1024)} %param.22) | copy-start | bytes 196612
  16.1 21.2 %copy-start.5 = (f32[16384]{0:T(1024)S(1)}, f32[16384]{0:T(1024)}, u32[]{:S(2)}) copy-start(f32[16384]{0:T(1024)} %param.24) | copy-start | bytes 196612
  18.0 1.3 %collective-permute-start.3 = (f32[128,128]{1,0:T(8,128)S(1)}, f32[128,128]{1,0:T(8,128)S(1)}, u32[]{:S(2)}, u32[]{:S(2)}) collective-permute-start(f32[128,128]{1,0:T(8,128)S(1)} %get-tuple-element.46), channel_id=1, source_target_pairs={{0,1},{1,0},{2,3},{3,2},{4,5},{5,4},{6,7},{7,6},{8,9},{9,8},{10,11... | collective-permute-start | bytes 196616 | tf_op jit(solution)/shard_map/ppermute | solution.py:522
  19.2 5.3 %collective-permute-start.6 = (f32[128,128]{1,0:T(8,128)S(1)}, f32[128,128]{1,0:T(8,128)S(1)}, u32[]{:S(2)}, u32[]{:S(2)}) collective-permute-start(f32[128,128]{1,0:T(8,128)S(1)} %add.6.refs_6_), channel_id=1, source_target_pairs={{0,6},{1,7},{2,4},{3,5},{4,2},{5,3},{6,0},{7,1},{8,14},{9,15},{10,... | collective-permute-start | bytes 196616 | tf_op jit(solution)/shard_map/ppermute | solution.py:364
  21.8 4.3 %collective-permute-start.5 = (f32[128,128]{1,0:T(8,128)S(1)}, f32[128,128]{1,0:T(8,128)S(1)}, u32[]{:S(2)}, u32[]{:S(2)}) collective-permute-start(f32[128,128]{1,0:T(8,128)S(1)} %add.6.refs_6_), channel_id=1, source_target_pairs={{0,4},{1,5},{2,6},{3,7},{4,0},{5,1},{6,2},{7,3},{8,12},{9,13},{10,... | collective-permute-start | bytes 196616 | tf_op jit(solution)/shard_map/ppermute | solution.py:364
  22.3 4.3 %collective-permute-start.4 = (f32[128,128]{1,0:T(8,128)S(1)}, f32[128,128]{1,0:T(8,128)S(1)}, u32[]{:S(2)}, u32[]{:S(2)}) collective-permute-start(f32[128,128]{1,0:T(8,128)S(1)} %add.6.refs_6_), channel_id=1, source_target_pairs={{0,2},{1,3},{2,0},{3,1},{4,6},{5,7},{6,4},{7,5},{8,10},{9,11},{10,... | collective-permute-start | bytes 196616 | tf_op jit(solution)/shard_map/ppermute | solution.py:364
  26.5 21.3 %copy-start.6 = (f32[16384]{0:T(1024)S(1)}, f32[16384]{0:T(1024)}, u32[]{:S(2)}) copy-start(f32[16384]{0:T(1024)} %param.23) | copy-start | bytes 196612
  27.9 6.9 %collective-permute-start.9 = (s16[336,128]{1,0:T(8,128)(2,1)S(1)}, s16[336,128]{1,0:T(8,128)(2,1)S(1)}, u32[]{:S(2)}, u32[]{:S(2)}) collective-permute-start(s16[336,128]{1,0:T(8,128)(2,1)S(1)} %get-tuple-element.51.refs_6_), channel_id=1, source_target_pairs={{0,24},{8,16},{16,8},{24,0},{1,25},{9,17},{17,9},{25,1},{2,26},{10... | collective-permute-start | bytes 258056 | tf_op jit(solution)/shard_map/ppermute | solution.py:364
  29.5 7.7 %collective-permute-start.8 = (s16[336,128]{1,0:T(8,128)(2,1)S(1)}, s16[336,128]{1,0:T(8,128)(2,1)S(1)}, u32[]{:S(2)}, u32[]{:S(2)}) collective-permute-start(s16[336,128]{1,0:T(8,128)(2,1)S(1)} %get-tuple-element.51.refs_6_), channel_id=1, source_target_pairs={{0,16},{8,24},{16,0},{24,8},{1,17},{9,25},{17,1},{25,9},{2,18},{10... | collective-permute-start | bytes 258056 | tf_op jit(solution)/shard_map/ppermute | solution.py:364
  29.5 7.7 %collective-permute-start.7 = (s16[336,128]{1,0:T(8,128)(2,1)S(1)}, s16[336,128]{1,0:T(8,128)(2,1)S(1)}, u32[]{:S(2)}, u32[]{:S(2)}) collective-permute-start(s16[336,128]{1,0:T(8,128)(2,1)S(1)} %get-tuple-element.51.refs_6_), channel_id=1, source_target_pairs={{0,8},{8,0},{16,24},{24,16},{1,9},{9,1},{17,25},{25,17},{2,10},{10... | collective-permute-start | bytes 258056 | tf_op jit(solution)/shard_map/ppermute | solution.py:364
  39.4 1.3 %collective-permute-start.10 = (f32[128,128]{1,0:T(8,128)S(1)}, f32[128,128]{1,0:T(8,128)S(1)}, u32[]{:S(2)}, u32[]{:S(2)}) collective-permute-start(f32[128,128]{1,0:T(8,128)S(1)} %get-tuple-element.55), channel_id=1, source_target_pairs={{0,1},{1,0},{2,3},{3,2},{4,5},{5,4},{6,7},{7,6},{8,9},{9,8},{10,11... | collective-permute-start | bytes 196616 | tf_op jit(solution)/shard_map/ppermute | solution.py:522
  40.7 5.3 %collective-permute-start.13 = (f32[128,128]{1,0:T(8,128)S(1)}, f32[128,128]{1,0:T(8,128)S(1)}, u32[]{:S(2)}, u32[]{:S(2)}) collective-permute-start(f32[128,128]{1,0:T(8,128)S(1)} %add.7.refs_6_), channel_id=1, source_target_pairs={{0,6},{1,7},{2,4},{3,5},{4,2},{5,3},{6,0},{7,1},{8,14},{9,15},{10,... | collective-permute-start | bytes 196616 | tf_op jit(solution)/shard_map/ppermute | solution.py:364
  42.3 5.0 %collective-permute-start.12 = (f32[128,128]{1,0:T(8,128)S(1)}, f32[128,128]{1,0:T(8,128)S(1)}, u32[]{:S(2)}, u32[]{:S(2)}) collective-permute-start(f32[128,128]{1,0:T(8,128)S(1)} %add.7.refs_6_), channel_id=1, source_target_pairs={{0,4},{1,5},{2,6},{3,7},{4,0},{5,1},{6,2},{7,3},{8,12},{9,13},{10,... | collective-permute-start | bytes 196616 | tf_op jit(solution)/shard_map/ppermute | solution.py:364
  43.6 4.3 %collective-permute-start.11 = (f32[128,128]{1,0:T(8,128)S(1)}, f32[128,128]{1,0:T(8,128)S(1)}, u32[]{:S(2)}, u32[]{:S(2)}) collective-permute-start(f32[128,128]{1,0:T(8,128)S(1)} %add.7.refs_6_), channel_id=1, source_target_pairs={{0,2},{1,3},{2,0},{3,1},{4,6},{5,7},{6,4},{7,5},{8,10},{9,11},{10,... | collective-permute-start | bytes 196616 | tf_op jit(solution)/shard_map/ppermute | solution.py:364
  49.3 6.1 %collective-permute-start.16 = (s16[160,128]{1,0:T(8,128)(2,1)S(1)}, s16[160,128]{1,0:T(8,128)(2,1)S(1)}, u32[]{:S(2)}, u32[]{:S(2)}) collective-permute-start(s16[160,128]{1,0:T(8,128)(2,1)S(1)} %get-tuple-element.60.refs_6_), channel_id=1, source_target_pairs={{0,24},{8,16},{16,8},{24,0},{1,25},{9,17},{17,9},{25,1},{2,26},{10... | collective-permute-start | bytes 122888 | tf_op jit(solution)/shard_map/ppermute | solution.py:364
  51.7 4.9 %collective-permute-start.15 = (s16[160,128]{1,0:T(8,128)(2,1)S(1)}, s16[160,128]{1,0:T(8,128)(2,1)S(1)}, u32[]{:S(2)}, u32[]{:S(2)}) collective-permute-start(s16[160,128]{1,0:T(8,128)(2,1)S(1)} %get-tuple-element.60.refs_6_), channel_id=1, source_target_pairs={{0,16},{8,24},{16,0},{24,8},{1,17},{9,25},{17,1},{25,9},{2,18},{10... | collective-permute-start | bytes 122888 | tf_op jit(solution)/shard_map/ppermute | solution.py:364
  51.7 4.9 %collective-permute-start.14 = (s16[160,128]{1,0:T(8,128)(2,1)S(1)}, s16[160,128]{1,0:T(8,128)(2,1)S(1)}, u32[]{:S(2)}, u32[]{:S(2)}) collective-permute-start(s16[160,128]{1,0:T(8,128)(2,1)S(1)} %get-tuple-element.60.refs_6_), channel_id=1, source_target_pairs={{0,8},{8,0},{16,24},{24,16},{1,9},{9,1},{17,25},{25,17},{2,10},{10... | collective-permute-start | bytes 122888 | tf_op jit(solution)/shard_map/ppermute | solution.py:364
  58.9 1.2 %collective-permute-start.17 = (f32[80,128]{1,0:T(8,128)S(1)}, f32[80,128]{1,0:T(8,128)S(1)}, u32[]{:S(2)}, u32[]{:S(2)}) collective-permute-start(f32[80,128]{1,0:T(8,128)S(1)} %get-tuple-element.68), channel_id=1, source_target_pairs={{0,1},{1,0},{2,3},{3,2},{4,5},{5,4},{6,7},{7,6},{8,9},{9,8},{10,11... | collective-permute-start | bytes 122888 | tf_op jit(solution)/shard_map/ppermute | solution.py:500
  60.2 3.8 %collective-permute-start.18 = (f32[32,128]{1,0:T(8,128)S(1)}, f32[32,128]{1,0:T(8,128)S(1)}, u32[]{:S(2)}, u32[]{:S(2)}) collective-permute-start(f32[32,128]{1,0:T(8,128)S(1)} %get-tuple-element.70), channel_id=1, source_target_pairs={{0,2},{1,3},{2,0},{3,1},{4,6},{5,7},{6,4},{7,5},{8,10},{9,11},{10,... | collective-permute-start | bytes 49160 | tf_op jit(solution)/shard_map/ppermute | solution.py:364
  61.0 3.7 %collective-permute-start.19 = (f32[32,128]{1,0:T(8,128)S(1)}, f32[32,128]{1,0:T(8,128)S(1)}, u32[]{:S(2)}, u32[]{:S(2)}) collective-permute-start(f32[32,128]{1,0:T(8,128)S(1)} %get-tuple-element.71), channel_id=1, source_target_pairs={{0,4},{1,5},{2,6},{3,7},{4,0},{5,1},{6,2},{7,3},{8,12},{9,13},{10,... | collective-permute-start | bytes 49160 | tf_op jit(solution)/shard_map/ppermute | solution.py:364
  62.4 4.6 %collective-permute-start.20 = (f32[32,128]{1,0:T(8,128)S(1)}, f32[32,128]{1,0:T(8,128)S(1)}, u32[]{:S(2)}, u32[]{:S(2)}) collective-permute-start(f32[32,128]{1,0:T(8,128)S(1)} %get-tuple-element.72), channel_id=1, source_target_pairs={{0,6},{1,7},{2,4},{3,5},{4,2},{5,3},{6,0},{7,1},{8,14},{9,15},{10,... | collective-permute-start | bytes 49160 | tf_op jit(solution)/shard_map/ppermute | solution.py:364

commit v6 on v5

--- a/solution.py
+++ b/solution.py
@@ -121,17 +121,91 @@
     return short(rows)
 
 
-def scales_of(part):
-    codes = long(part[part.shape[0] - SCALES :, :])
-    return [from_units(codes[spot : spot + 1]) for spot in range(2)]
+def codes_of(part):
+    return long(part[part.shape[0] - SCALES :, :])
+
+
+def group(part, lines, size, spot):
+    return part[lines + spot * size : lines + (spot + 1) * size, :]
+
+
+def both(lines, mine, received):
+    ours, theirs = codes_of(mine)[:1], codes_of(received)[:1]
+    return long(mine[:lines, :]) * from_units(ours) + long(received[:lines, :]) * from_units(theirs)
+
+
+def both_fine(lines, mine, received):
+    sums = 0.0
+    for part in (mine, received):
+        units = long(group(part, lines, EXTRA, 0))
+        sums += (units[:8] + units[8:] * (1.0 / FINE)) * from_units(codes_of(part)[1:2])
+    return sums
+
+
+def write_payload(out, lines, main, groups):
+    units, code = encode(main)
+    out[:lines, :] = short(units)
+    codes = [code]
+    row = lines
+    for units, code in groups:
+        out[row : row + units.shape[0], :] = units
+        row += units.shape[0]
+        codes.append(code)
+    out[row:, :] = scale_rows(codes)
+
+
+def coded(lines):
+    units, code = encode(lines)
+    return short(units), code
+
+
+def coded_fine(lines):
+    coarse, fine, code = encode_fine(lines)
+    return short(jnp.concatenate([coarse, fine], axis=0)), code
+
+
+def middle_body(kind, lines, size, mine, received, kept, *outs):
+    main = both(lines, mine, received)
+    groups = []
+    if kind == "scatter":
+        out, keep = outs
+        codes = codes_of(received)
+        for spot in range(kept.shape[0]):
+            units = long(group(received, lines, size, spot))
+            sums = kept[spot] + units * from_units(codes[spot + 1 : spot + 2])
+            if spot % 2:
+                groups.append(coded(sums))
+            else:
+                keep[spot // 2] = sums
+    elif kind == "gather":
+        (out,) = outs
+        count = (mine.shape[0] - lines - SCALES) // size
+        for part in (mine, received):
+            codes = codes_of(part)
+            for spot in range(count):
+                groups.append((group(part, lines, size, spot), codes[spot + 1 : spot + 2]))
+    elif kind == "sums":
+        (out,) = outs
+        groups.append(coded_fine(both_fine(lines, mine, received)))
+    else:
+        (out,) = outs
+    write_payload(out, lines, main, groups)
+
+
+def halve_body(kept, received, keep, send):
+    count = kept.shape[0] - 1
+    tail = kept[count] + received[count]
+    for spot in range(count):
+        (send if spot % 2 else keep)[spot // 2] = kept[spot] + received[spot]
+    keep[count // 2] = tail
+    send[count // 2] = tail
 
 
 def first_body(
     step, n_row, rows_far, columns_far, count, tile_data, mask_far, cotangent_far, saved_far,
     tiles, term, anchor, *refs
 ):
-    outs = refs[:n_row]
-    source, total, rows, columns, mask, cotangent, saved, arrived, ready = refs[n_row:]
+    out, keep, source, total, rows, columns, mask, cotangent, saved, arrived, ready = refs
     slots = tiles.shape[0]
     chunk = slots // CHUNKS
     pairs = [(mask_far, mask), (cotangent_far, cotangent), (saved_far, saved)]
@@ -168,25 +242,27 @@
     lines = total.shape[1]
     share = lines // n_row
     me = lax.axis_index("row")
-    units, code = encode(total[0])
-    units = short(units)
-    for part, out in enumerate(outs):
+    groups = []
+    for part in range(n_row):
         at = pl.ds(pl.multiple_of((me ^ part) * share, share), share)
-        out[:lines, :] = units
-        saved_units, saved_code = encode(total[1:, at, :].reshape(iterations * share, LANES))
-        out[lines : lines + iterations * share, :] = short(saved_units)
-        out[lines + iterations * share :, :] = scale_rows([code, saved_code])
-
-
-def dual_body(step, n_col, rows, columns, count, sizes, tiles, mask, parts, before, anchor, *refs):
+        sums = total[1:, at, :].reshape(iterations * share, LANES)
+        if part % 2:
+            groups.append(coded(sums))
+        else:
+            keep[part // 2] = sums
+    write_payload(out, lines, total[0], groups)
+
+
+def dual_body(
+    step, n_col, rows, columns, count, sizes, tiles, mask, image, received, before, anchor, *refs
+):
     last = step == 0
     if last:
         demand, images, terms, term, anchor_out, out, _, source, total = refs
     else:
         saved, term, anchor_out, out, _, source, total = refs
     weight = weight_of(step)
-    image = tree_sum([part[...] for part in parts])
-    adjoint = before[...] + sizes[0] * image
+    adjoint = before[...] + sizes[0] * (image[...] + received[...])
     anchor_out[...] = anchor[...] + (1.0 - weight) * adjoint
     value = mask[:, step, :].astype(jnp.float32) * weight * adjoint
     term[...] = value
@@ -194,41 +270,35 @@
     total[...] = jnp.zeros_like(total)
     add_products(True, rows, columns, count, tiles, range(tiles.shape[0]), source, total)
     lines = total.shape[0]
-    units, code = encode(total[...])
-    out[:lines, :] = short(units)
+    groups = []
     if last:
         share = demand[...] * (1.0 / n_col)
         found = value * (share - images[0])
         for other, earlier in enumerate(terms):
             found += earlier[...] * (share - images[other + 1])
-        coarse, fine, found_code = encode_fine(fold(found))
-        out[lines : lines + EXTRA, :] = short(jnp.concatenate([coarse, fine], axis=0))
-        out[lines + EXTRA :, :] = scale_rows([code, found_code])
-    elif saved is None:
-        out[lines:, :] = scale_rows([code])
-    else:
-        size = saved.shape[0]
-        coarse, fine, saved_code = encode_fine(saved[...])
-        out[lines : lines + size, :] = short(coarse)
-        out[lines + size : lines + 2 * size, :] = short(fine)
-        out[lines + 2 * size :, :] = scale_rows([code, saved_code])
-
-
-def primal_body(kind, step, n_row, n_col, rows, columns, count, sizes, tiles, mask, parts, before, anchor, *refs):
-    last = kind == "last"
+        groups.append(coded_fine(fold(found)))
+    elif saved is not None:
+        groups.append(coded(saved[...]))
+    write_payload(out, lines, total[...], groups)
+
+
+def primal_body(
+    kind, step, n_row, n_col,
+    rows, columns, count, sizes, tiles, mask, mine, received, before, anchor, *refs
+):
+    last = kind == "sums"
     if last:
-        reduced, terms, final, mine, other, _, source, out = refs
-    elif kind == "sums":
-        term, adjoint_out, anchor_out, out, saved, _, source = refs
-    elif kind == "shares":
+        reduced, terms, final, keep, send, _, source, out = refs
+    elif kind == "scatter":
+        kept, term, adjoint_out, anchor_out, out, saved, _, source = refs
+    elif kind == "gather":
         cost, upper, primal, term, adjoint_out, anchor_out, out, reduced, images, _, source, total = refs
     else:
         term, adjoint_out, anchor_out, out, _, source = refs
     sigma = sizes[1]
     weight = weight_of(step)
     lines = mask.shape[0]
-    scales = [scales_of(part) for part in parts]
-    back = tree_sum([long(part[:lines, :]) * scale[0] for part, scale in zip(parts, scales)])
+    back = both(lines, mine, received)
     adjoint = before[...]
     anchored = (1.0 - weight) * adjoint
     if anchor is not None:
@@ -242,17 +312,20 @@
         adjoint_out[...] = after
         anchor_out[...] = anchored
     all_slots = range(tiles.shape[0])
-    if kind == "shares":
+    if kind == "gather":
         iterations = reduced.shape[0]
         share = lines // n_row
         size = iterations * share
         me = lax.axis_index("row")
-        for part, (held, scale) in enumerate(zip(parts, scales)):
-            at = pl.ds(pl.multiple_of((me ^ part) * share, share), share)
-            units = long(held[lines : lines + size, :])
-            units += long(held[lines + size : lines + 2 * size, :]) * (1.0 / FINE)
-            sums = (units * scale[1]).reshape(iterations, share, LANES)
-            reduced[:, at, :] = cost[at, :][None] - sums
+        owners = gather_order(n_row)
+        held = n_row // 2
+        codes = [codes_of(mine), codes_of(received)]
+        for spot, owner in enumerate(owners):
+            part, where = (mine, received)[spot // held], spot % held
+            at = pl.ds(pl.multiple_of((me ^ owner) * share, share), share)
+            code = codes[spot // held][where + 1 : where + 2]
+            sums = long(group(part, lines, size, where)) * from_units(code)
+            reduced[:, at, :] = cost[at, :][None] - sums.reshape(iterations, share, LANES)
         source[0] = rounded(value)
         for vector in range(iterations):
             saved = primal[:, vector, :]
@@ -266,47 +339,33 @@
     source[...] = rounded(value)
     out[...] = jnp.zeros_like(out)
     add_products(False, columns, rows, count, tiles, all_slots, source, out)
-    if kind == "sums":
+    if kind == "scatter":
         size = saved.shape[0]
-        saved[...] = tree_sum(
-            [long(part[lines : lines + size, :]) * scale[1] for part, scale in zip(parts, scales)]
-        )
+        code = codes_of(received)[1:2]
+        saved[...] = kept[0] + long(group(received, lines, size, 0)) * from_units(code)
     if last:
-        sums = 0.0
-        for part, scale in zip(parts, scales):
-            units = long(part[lines : lines + EXTRA, :])
-            sums += (units[:8] + units[8:] * (1.0 / FINE)) * scale[1]
+        sums = both_fine(lines, mine, received)
         found = value * reduced[0]
         for other_step, later in enumerate(terms):
             found += later[...] * reduced[other_step + 1]
         tail = jnp.concatenate([sums, -fold(found)], axis=0)
         share = out.shape[0] // n_col
-        core = lax.axis_index("col") % 2
-        for chip in range(n_col // 2):
-            span = slice(chip * share, (chip + 1) * share)
-            mine[span, :] = out[pl.ds((2 * chip + core) * share, share), :]
-            other[span, :] = out[pl.ds((2 * chip + 1 - core) * share, share), :]
-        mine[n_col // 2 * share :, :] = tail
-        other[n_col // 2 * share :, :] = tail
-
-
-def split_body(n_chip, mine, received, *outs):
-    share = (mine.shape[0] - EXTRA) // n_chip
-    chip = lax.axis_index("col") // 2
-    tail = mine[n_chip * share :, :] + received[n_chip * share :, :]
-    for part, out in enumerate(outs):
-        at = pl.ds((chip ^ part) * share, share)
-        out[:share, :] = mine[at, :] + received[at, :]
-        out[share:, :] = tail
-
-
-def last_body(scales, sizes, parts, term, anchor, adjoint, gradients):
+        me = lax.axis_index("col")
+        for part in range(n_col):
+            at = pl.ds((me ^ part) * share, share)
+            (send if part % 2 else keep)[part // 2, :share, :] = out[at, :]
+        for half in (keep, send):
+            half[n_col // 2, :EXTRA, :] = tail
+
+
+def last_body(scales, sizes, kept, received, term, anchor, adjoint, gradients):
     share = adjoint.shape[0]
-    total = tree_sum([part[...] for part in parts])
+    image = kept[0, :share, :] + received[0, :share, :]
+    sums = kept[1, :EXTRA, :] + received[1, :EXTRA, :]
     at = pl.ds(lax.axis_index("col") * share, share)
-    adjoint[...] = term[at, :] + sizes[0] * total[:share] + anchor[at, :]
-    gradients[0] = jnp.sum(total[share + 8 : share + 16]) * scales[0]
-    gradients[1] = jnp.sum(total[share : share + 8]) * scales[1]
+    adjoint[...] = term[at, :] + sizes[0] * image + anchor[at, :]
+    gradients[0] = jnp.sum(sums[8:]) * scales[0]
+    gradients[1] = jnp.sum(sums[:8]) * scales[1]
 
 
 def far(array):
@@ -358,12 +417,21 @@
     )(*flat)
 
 
-def exchange(parts, axis, stride=1):
+def gather_order(size):
+    order, stride = [0], size // 2
+    while stride:
+        order += [owner ^ stride for owner in order]
+        stride //= 2
+    return order
+
+
+def swap(array, axis, stride):
     size = lax.axis_size(axis)
-    return [parts[0]] + [
-        lax.ppermute(parts[k], axis, [(i, i ^ (k * stride)) for i in range(size)])
-        for k in range(1, size // stride)
-    ]
+    return lax.ppermute(array, axis, [(i, i ^ stride) for i in range(size)])
+
+
+def strides(size):
+    return [1 << bit for bit in range(size.bit_length() - 1)]
 
 
 def local(
@@ -386,7 +454,6 @@
     iterations, row_length = saved_dual.shape
     column_length = saved_primal.shape[1]
     n_row, n_col = lax.axis_size("row"), lax.axis_size("col")
-    n_chip = n_col // 2
     lines_y, lines_x = row_length // LANES, column_length // LANES
     share_y, share_x = lines_y // n_col, lines_x // n_row
     saved_lines = iterations * share_x
@@ -403,8 +470,40 @@
     def f32(*shape):
         return jax.ShapeDtypeStruct(shape, jnp.float32)
 
-    def row_part(more):
-        return jax.ShapeDtypeStruct((lines_x + more + SCALES, LANES), jnp.int16)
+    def payload(size, count):
+        return jax.ShapeDtypeStruct((lines_x + size * count + SCALES, LANES), jnp.int16)
+
+    def row_rounds(kind, part, size, kept):
+        order = strides(n_row)
+        if kind == "gather":
+            order = order[::-1]
+        for spot, stride in enumerate(order):
+            received = swap(part, "row", stride)
+            if spot == len(order) - 1:
+                return part, received, kept
+            outs, count = [], 1
+            if kind == "scatter":
+                count = kept.shape[0] // 2
+                outs = [f32(count, size, LANES)]
+            elif kind == "gather":
+                count = 2 << spot
+            elif kind == "plain":
+                count = 0
+            part, *more = run(
+                functools.partial(middle_body, kind, lines_x, size),
+                [payload(size, count)] + outs,
+                [(VMEM, part), (VMEM, received), (VMEM, kept)],
+                [],
+                f"{kind}_{spot}",
+            )
+            if kind == "scatter":
+                (kept,) = more
+
+    def col_rounds(part):
+        order = strides(n_col)
+        for stride in order[:-1]:
+            part = part + swap(part, "col", stride)
+        return part, swap(part, "col", order[-1])
 
     def scratch(*shape):
         return pltpu.VMEM(shape, jnp.float32)
@@ -413,10 +512,10 @@
     full_x, full_y = f32(lines_x, LANES), f32(lines_y, LANES)
     where = [(SMEM, tile_row_block), (SMEM, tile_column_block), (SMEM, tile_count)]
     saved = lines(saved_dual)
-    tiles, term_y, anchor_y, *parts = run(
+    tiles, term_y, anchor_y, part, kept = run(
         functools.partial(first_body, last, n_row),
         [pltpu.VMEM((slots, width, width), jnp.bfloat16), full_y, full_y]
-        + [row_part(saved_lines)] * n_row,
+        + [payload(saved_lines, n_row // 2), f32(n_row // 2, saved_lines, LANES)],
         [(ANY, far(tile_row_block)), (ANY, far(tile_column_block)), (SMEM, tile_count)]
         + [(ANY, far(tile_data)), (ANY, far(mask_y)), (ANY, far(lines(dual_cotangent)))]
         + [(ANY, far(saved))],
@@ -438,18 +537,20 @@
     terms_x, terms_y = [], [term_y]
     reduced = images = saved_sums = None
     for step in reversed(range(iterations)):
-        parts = exchange(parts, "row")
-        kind = {0: "last", last: "sums", last - 1: "shares"}.get(step, "plain")
-        groups = where + [(SMEM, step_sizes), (VMEM, tiles), (VMEM, mask_x), (VMEM, parts)]
-        groups += [(VMEM, adjoint_x), (VMEM, anchor_x)]
+        kind = {0: "sums", last: "scatter", last - 1: "gather"}.get(step, "plain")
+        size = EXTRA if kind == "sums" else saved_lines
+        mine, received, kept = row_rounds(kind, part, size, kept)
+        groups = where + [(SMEM, step_sizes), (VMEM, tiles), (VMEM, mask_x)]
+        groups += [(VMEM, mine), (VMEM, received), (VMEM, adjoint_x), (VMEM, anchor_x)]
         body = functools.partial(primal_body, kind, step, n_row, n_col)
         if step == 0:
             break
         outs = [full_x, full_x, full_x, full_y]
         extra = [scratch(lines_x, LANES)]
-        if kind == "sums":
+        if kind == "scatter":
+            groups += [(VMEM, kept)]
             outs.append(f32(saved_lines, LANES))
-        if kind == "shares":
+        if kind == "gather":
             outs += [f32(iterations, lines_x, LANES), f32(iterations, lines_y, LANES)]
             groups += [(VMEM, lines(cost_vector)), (VMEM, lines(upper_bound))]
             groups += [(VMEM, lines(saved_primal))]
@@ -460,22 +561,21 @@
         term_x, adjoint_x, anchor_x, partial, *more, tiles = run(
             body, outs, groups, extra, f"primal_{step}", cost, tiles
         )
-        if kind == "sums":
+        kept = saved_sums = None
+        if kind == "scatter":
             (saved_sums,) = more
-        elif kind == "shares":
+        elif kind == "gather":
             reduced, images = more
-            saved_sums = None
         terms_x.insert(0, term_x)
-        partial = sum_pair(partial)
-        parts = exchange([partial] * n_chip, "col", 2)
-        groups = where + [(SMEM, step_sizes), (VMEM, tiles), (VMEM, mask_y), (VMEM, parts)]
-        groups += [(VMEM, term_y), (VMEM, anchor_y)]
+        image, received = col_rounds(partial)
+        groups = where + [(SMEM, step_sizes), (VMEM, tiles), (VMEM, mask_y)]
+        groups += [(VMEM, image), (VMEM, received), (VMEM, term_y), (VMEM, anchor_y)]
         if step == 1:
             groups += [(VMEM, lines(demand)), (VMEM, images), (VMEM, list(terms_y))]
-            out = row_part(EXTRA)
+            out = payload(EXTRA, 1)
         else:
             groups += [(VMEM, saved_sums)]
-            out = row_part(2 * saved_lines if saved_sums is not None else 0)
+            out = payload(saved_lines, 0 if saved_sums is None else 1)
         term_y, anchor_y, part, tiles = run(
             functools.partial(dual_body, step - 1, n_col),
             [full_y, full_y, out],
@@ -485,41 +585,36 @@
             cost,
             tiles,
         )
-        parts = [part] * n_row
         terms_y.insert(0, term_y)
-    half_y = f32(n_chip * share_y + EXTRA, LANES)
-    primal_adjoint, mine, other, tiles = run(
+
+    def halves(count):
+        return [f32(count + 1, max(share_y, EXTRA), LANES)] * 2
+
+    primal_adjoint, kept, sent, tiles = run(
         body,
-        [full_x, half_y, half_y],
+        [full_x] + halves(n_col // 2),
         groups + [(VMEM, reduced), (VMEM, terms_x)],
         [scratch(lines_x, LANES), scratch(lines_y, LANES)],
         "primal_0",
         cost,
         tiles,
     )
-    received = lax.ppermute(other, "col", [(i, i ^ 1) for i in range(n_col)])
-    parts = run(
-        functools.partial(split_body, n_chip),
-        [f32(share_y + EXTRA, LANES)] * n_chip,
-        [(VMEM, mine), (VMEM, received)],
-        [],
-        "split",
-    )
-    parts = exchange(parts, "col", 2)
+    for stride in strides(n_col):
+        received = swap(sent, "col", stride)
+        count = kept.shape[0] - 1
+        if count > 1:
+            kept, sent = run(
+                halve_body, halves(count // 2), [(VMEM, kept), (VMEM, received)], [], f"halve_{count}"
+            )
     scales = (1.0 / math.sqrt(column_length * n_col), 1.0 / math.sqrt(row_length * n_row))
     dual_adjoint, gradients = run(
         functools.partial(last_body, scales),
         [f32(share_y, LANES), ("smem", f32(2))],
-        [(SMEM, step_sizes), (VMEM, parts), (VMEM, term_y), (VMEM, anchor_y)],
+        [(SMEM, step_sizes), (VMEM, kept), (VMEM, received), (VMEM, term_y), (VMEM, anchor_y)],
         [],
         "last",
     )
     return (primal_adjoint.reshape(-1), dual_adjoint.reshape(-1), gradients)
-
-
-def sum_pair(partial):
-    size = lax.axis_size("col")
-    return partial + lax.ppermute(partial, "col", [(i, i ^ 1) for i in range(size)])
 
 
 def solution(mesh):

time: 68.3 us -> 74.1 us (1.085)
  waiting for transfers between devices: 28.1 us -> 31.5 us
  starting transfers between devices: 25.4 us -> 27.5 us
    ppermute x21 -> x15, waiting for transfers between devices: 28.1 us -> 31.5 us  [swap(): return lax.ppermute(array, axis, [(i, i ^ stride) for i in range(size)])]
    ppermute x21 -> x15, starting transfers between devices: 25.4 us -> 27.5 us  [swap(): return lax.ppermute(array, axis, [(i, i ^ stride) for i in range(size)])]
    pallas_call x8 -> x12, Pallas kernels: 13.2 us -> 13.3 us  [run(): pl.pallas_call(kernel, out_shape=shapes, in_specs=specs, out_specs=[SMEM...]
  transfers between devices with their start and end apart: 21 -> 15, of which waited for: 18 -> 15; matrix products, arithmetic and copies ran while one was open for 0% -> 0% of each run, Pallas kernels for 0% -> 0%
where the time goes in v6:
time: 74.1 us; the launch traced here: 73.9 us
  waiting for transfers between devices  31.5 us (43%)
  starting transfers between devices  27.5 us (37%)
  Pallas kernels  13.3 us (18%)
  between operations  1.53 us (2%)
    ppermute x15, waiting for transfers between devices, swap(): return lax.ppermute(array, axis, [(i, i ^ stride) for i in range(size)])  31.5 us
    ppermute x15, starting transfers between devices, swap(): return lax.ppermute(array, axis, [(i, i ^ stride) for i in range(size)])  27.5 us
    pallas_call x12, Pallas kernels, run(): pl.pallas_call(kernel, out_shape=shapes, in_specs=specs, out_specs=[SMEM...  13.3 us
  transfers between devices with their start and end apart: 15, of which 15 were waited for; matrix products, arithmetic and copies ran while one was open for 0% of the time, Pallas kernels for 0%

profile of v6, /device:TPU:0, one launch (start us, length us, event | category | flops | bytes accessed | tf_op | source)
XLA Modules:
  0.0 73.9 jit_solution(12674830826336639829)
XLA Ops:
  0.6 0.0 copy-start.8
  0.6 0.0 copy-start.7
  0.7 0.0 copy-start.9
  0.7 0.0 copy-start.3
  0.7 0.0 copy-start.1
  1.4 0.0 copy-start
  1.4 2.9 %first.1 = (bf16[32,256,256]{2,1,0:T(8,128)(2,1)S(1)}, f32[128,128]{1,0:T(8,128)S(1)}, f32[128,128]{1,0:T(8,128)S(1)}, s16[336,128]{1,0:T(8,128)(2,1)S(1)}, f32[2,96,128]{2,1,0:T(8,128)S(1)}) custom-call(s32[1,1,32]{2,1,0:T(1,128)} %refs_0_.12, s32[1,1,32]{2,1,0:T(1,128)} %refs_1_.11, s32[1,1]{1,0:T(1,128)S(6)} %copy.27.refs_2_, ...), custom_call_target="tpu_custom_call" | custom-call | flops 4194304 | bytes 4194304 | tf_op jit(solution)/shard_map/first/pallas_call | solution.py:407
  4.3 3.1 %collective-permute-start = (s16[336,128]{1,0:T(8,128)(2,1)S(1)}, s16[336,128]{1,0:T(8,128)(2,1)S(1)}, u32[]{:S(2)}, u32[]{:S(2)}) collective-permute-start(s16[336,128]{1,0:T(8,128)(2,1)S(1)} %get-tuple-element.41.refs_0_), channel_id=1, source_target_pairs={{0,8},{8,0},{16,24},{24,16},{1,9},{9,1},{17,25},{25,17},{2,10},{10... | collective-permute-start | bytes 258056 | tf_op jit(solution)/shard_map/ppermute | solution.py:430
  7.4 2.5 %collective-permute-done.refs_1_ = s16[336,128]{1,0:T(8,128)(2,1)S(1)} collective-permute-done((s16[336,128]{1,0:T(8,128)(2,1)S(1)}, s16[336,128]{1,0:T(8,128)(2,1)S(1)}, u32[]{:S(2)}, u32[]{:S(2)}) %collective-permute-start) | collective-permute-done | bytes 86048 | tf_op jit(solution)/shard_map/ppermute | solution.py:430
  9.9 0.1 scatter_0.1
  10.0 3.0 %collective-permute-start.1 = (s16[240,128]{1,0:T(8,128)(2,1)S(1)}, s16[240,128]{1,0:T(8,128)(2,1)S(1)}, u32[]{:S(2)}, u32[]{:S(2)}) collective-permute-start(s16[240,128]{1,0:T(8,128)(2,1)S(1)} %get-tuple-element.43.refs_6_), channel_id=1, source_target_pairs={{0,16},{8,24},{16,0},{24,8},{1,17},{9,25},{17,1},{25,9},{2,18},{10... | collective-permute-start | bytes 184328 | tf_op jit(solution)/shard_map/ppermute | solution.py:430
  13.0 2.2 %collective-permute-done.1.refs_7_ = s16[240,128]{1,0:T(8,128)(2,1)S(1)} collective-permute-done((s16[240,128]{1,0:T(8,128)(2,1)S(1)}, s16[240,128]{1,0:T(8,128)(2,1)S(1)}, u32[]{:S(2)}, u32[]{:S(2)}) %collective-permute-start.1) | collective-permute-done | bytes 61472 | tf_op jit(solution)/shard_map/ppermute | solution.py:430
  15.2 0.0 copy-done.8
  15.2 0.0 copy-done.7
  15.2 0.0 copy-done.9
  15.2 0.0 copy-done.3
  15.3 0.0 copy-done.1
  15.3 0.0 copy-start.2
  15.3 0.0 copy-start.4
  15.3 0.0 copy-start.5
  15.3 1.8 %primal_2.1 = (f32[128,128]{1,0:T(8,128)S(1)}, f32[128,128]{1,0:T(8,128)S(1)}, f32[128,128]{1,0:T(8,128)S(1)}, f32[128,128]{1,0:T(8,128)S(1)}, f32[96,128]{1,0:T(8,128)S(1)}, /*index=5*/bf16[32,256,256]{2,1,0:T(8,128)(2,1)S(1)}) custom-call(s32[1,1,32]{2,1,0:T(1,128)S(1)} %copy-done.7, s32[1,1,32]{2,1,0:T(1,128)S(1)} %copy-done.8, ...), custom_call_target="tpu_custom_call", output_to_operand_aliasing={{5}: (4, {})} | custom-call | flops 4194304 | bytes 4194304 | tf_op jit(solution)/shard_map/primal_2/pallas_call | solution.py:407
  17.1 0.0 collective-permute-start.2
  17.2 1.2 %collective-permute-done.2 = f32[128,128]{1,0:T(8,128)S(1)} collective-permute-done((f32[128,128]{1,0:T(8,128)S(1)}, f32[128,128]{1,0:T(8,128)S(1)}, u32[]{:S(2)}, u32[]{:S(2)}) %collective-permute-start.2) | collective-permute-done | bytes 65568 | tf_op jit(solution)/shard_map/ppermute | solution.py:430
  18.4 1.9 %collective-permute-start.3 = (f32[128,128]{1,0:T(8,128)S(1)}, f32[128,128]{1,0:T(8,128)S(1)}, u32[]{:S(2)}, u32[]{:S(2)}) collective-permute-start(f32[128,128]{1,0:T(8,128)S(1)} %add.12), channel_id=1, source_target_pairs={{0,2},{1,3},{2,0},{3,1},{4,6},{5,7},{6,4},{7,5},{8,10},{9,11},{10,... | collective-permute-start | bytes 196616 | tf_op jit(solution)/shard_map/ppermute | solution.py:430
  20.3 2.4 %collective-permute-done.3 = f32[128,128]{1,0:T(8,128)S(1)} collective-permute-done((f32[128,128]{1,0:T(8,128)S(1)}, f32[128,128]{1,0:T(8,128)S(1)}, u32[]{:S(2)}, u32[]{:S(2)}) %collective-permute-start.3) | collective-permute-done | bytes 65568 | tf_op jit(solution)/shard_map/ppermute | solution.py:430
  22.8 1.9 %collective-permute-start.4 = (f32[128,128]{1,0:T(8,128)S(1)}, f32[128,128]{1,0:T(8,128)S(1)}, u32[]{:S(2)}, u32[]{:S(2)}) collective-permute-start(f32[128,128]{1,0:T(8,128)S(1)} %add.13.refs_6_), channel_id=1, source_target_pairs={{0,4},{1,5},{2,6},{3,7},{4,0},{5,1},{6,2},{7,3},{8,12},{9,13},{10,... | collective-permute-start | bytes 196616 | tf_op jit(solution)/shard_map/ppermute | solution.py:430
  24.7 2.4 %collective-permute-done.4.refs_7_ = f32[128,128]{1,0:T(8,128)S(1)} collective-permute-done((f32[128,128]{1,0:T(8,128)S(1)}, f32[128,128]{1,0:T(8,128)S(1)}, u32[]{:S(2)}, u32[]{:S(2)}) %collective-permute-start.4) | collective-permute-done | bytes 65568 | tf_op jit(solution)/shard_map/ppermute | solution.py:430
  27.1 0.0 copy-done
  27.1 0.0 copy-start.6
  27.1 1.4 %dual_1.1 = (f32[128,128]{1,0:T(8,128)S(1)}, f32[128,128]{1,0:T(8,128)S(1)}, s16[240,128]{1,0:T(8,128)(2,1)S(1)}, bf16[32,256,256]{2,1,0:T(8,128)(2,1)S(1)}) custom-call(s32[1,1,32]{2,1,0:T(1,128)S(1)} %copy-done.7, s32[1,1,32]{2,1,0:T(1,128)S(1)} %copy-done.8, s32[1,1]{1,0:T(1,128)S(6)} %copy.27.refs_2_, ...), custom_call_target="tpu_custom_call", output_to_operand_aliasing={{3}: (4, {})} | custom-call | flops 4194304 | bytes 4194304 | tf_op jit(solution)/shard_map/dual_1/pallas_call | solution.py:407
  28.5 3.0 %collective-permute-start.5 = (s16[240,128]{1,0:T(8,128)(2,1)S(1)}, s16[240,128]{1,0:T(8,128)(2,1)S(1)}, u32[]{:S(2)}, u32[]{:S(2)}) collective-permute-start(s16[240,128]{1,0:T(8,128)(2,1)S(1)} %get-tuple-element.51.refs_0_), channel_id=1, source_target_pairs={{0,16},{8,24},{16,0},{24,8},{1,17},{9,25},{17,1},{25,9},{2,18},{10... | collective-permute-start | bytes 184328 | tf_op jit(solution)/shard_map/ppermute | solution.py:430
  31.5 2.2 %collective-permute-done.5.refs_1_ = s16[240,128]{1,0:T(8,128)(2,1)S(1)} collective-permute-done((s16[240,128]{1,0:T(8,128)(2,1)S(1)}, s16[240,128]{1,0:T(8,128)(2,1)S(1)}, u32[]{:S(2)}, u32[]{:S(2)}) %collective-permute-start.5) | collective-permute-done | bytes 61472 | tf_op jit(solution)/shard_map/ppermute | solution.py:430
  33.7 0.1 gather_0.1.refs_6_
  33.8 2.1 %collective-permute-start.6 = (s16[336,128]{1,0:T(8,128)(2,1)S(1)}, s16[336,128]{1,0:T(8,128)(2,1)S(1)}, u32[]{:S(2)}, u32[]{:S(2)}) collective-permute-start(s16[336,128]{1,0:T(8,128)(2,1)S(1)} %gather_0.1.refs_6_), channel_id=1, source_target_pairs={{0,8},{8,0},{16,24},{24,16},{1,9},{9,1},{17,25},{25,17},{2,10},{10... | collective-permute-start | bytes 258056 | tf_op jit(solution)/shard_map/ppermute | solution.py:430
  35.9 2.5 %collective-permute-done.6.refs_7_ = s16[336,128]{1,0:T(8,128)(2,1)S(1)} collective-permute-done((s16[336,128]{1,0:T(8,128)(2,1)S(1)}, s16[336,128]{1,0:T(8,128)(2,1)S(1)}, u32[]{:S(2)}, u32[]{:S(2)}) %collective-permute-start.6) | collective-permute-done | bytes 86048 | tf_op jit(solution)/shard_map/ppermute | solution.py:430
  38.4 0.0 copy-done.2
  38.4 0.0 copy-done.4
  38.4 0.0 copy-done.5
  38.4 2.1 %primal_1.1 = (f32[128,128]{1,0:T(8,128)S(1)}, f32[128,128]{1,0:T(8,128)S(1)}, f32[128,128]{1,0:T(8,128)S(1)}, f32[128,128]{1,0:T(8,128)S(1)}, f32[3,128,128]{2,...) custom-call(s32[1,1,32]{2,1,0:T(1,128)S(1)} %copy-done.7, ...), custom_call_target="tpu_custom_call", output_to_operand_aliasing={{6}: (4, {})} | custom-call | flops 4194304 | bytes 4194304 | tf_op jit(solution)/shard_map/primal_1/pallas_call | solution.py:407
  40.5 0.1 collective-permute-start.7
  40.6 1.2 %collective-permute-done.7 = f32[128,128]{1,0:T(8,128)S(1)} collective-permute-done((f32[128,128]{1,0:T(8,128)S(1)}, f32[128,128]{1,0:T(8,128)S(1)}, u32[]{:S(2)}, u32[]{:S(2)}) %collective-permute-start.7) | collective-permute-done | bytes 65568 | tf_op jit(solution)/shard_map/ppermute | solution.py:430
  41.8 1.8 %collective-permute-start.8 = (f32[128,128]{1,0:T(8,128)S(1)}, f32[128,128]{1,0:T(8,128)S(1)}, u32[]{:S(2)}, u32[]{:S(2)}) collective-permute-start(f32[128,128]{1,0:T(8,128)S(1)} %add.14), channel_id=1, source_target_pairs={{0,2},{1,3},{2,0},{3,1},{4,6},{5,7},{6,4},{7,5},{8,10},{9,11},{10,... | collective-permute-start | bytes 196616 | tf_op jit(solution)/shard_map/ppermute | solution.py:430
  43.6 2.5 %collective-permute-done.8 = f32[128,128]{1,0:T(8,128)S(1)} collective-permute-done((f32[128,128]{1,0:T(8,128)S(1)}, f32[128,128]{1,0:T(8,128)S(1)}, u32[]{:S(2)}, u32[]{:S(2)}) %collective-permute-start.8) | collective-permute-done | bytes 65568 | tf_op jit(solution)/shard_map/ppermute | solution.py:430
  46.2 1.8 %collective-permute-start.9 = (f32[128,128]{1,0:T(8,128)S(1)}, f32[128,128]{1,0:T(8,128)S(1)}, u32[]{:S(2)}, u32[]{:S(2)}) collective-permute-start(f32[128,128]{1,0:T(8,128)S(1)} %add.15.refs_6_), channel_id=1, source_target_pairs={{0,4},{1,5},{2,6},{3,7},{4,0},{5,1},{6,2},{7,3},{8,12},{9,13},{10,... | collective-permute-start | bytes 196616 | tf_op jit(solution)/shard_map/ppermute | solution.py:430
  48.0 2.5 %collective-permute-done.9.refs_7_ = f32[128,128]{1,0:T(8,128)S(1)} collective-permute-done((f32[128,128]{1,0:T(8,128)S(1)}, f32[128,128]{1,0:T(8,128)S(1)}, u32[]{:S(2)}, u32[]{:S(2)}) %collective-permute-start.9) | collective-permute-done | bytes 65568 | tf_op jit(solution)/shard_map/ppermute | solution.py:430
  50.5 0.0 copy-done.6
  50.5 1.4 %dual_0.1 = (f32[128,128]{1,0:T(8,128)S(1)}, f32[128,128]{1,0:T(8,128)S(1)}, s16[160,128]{1,0:T(8,128)(2,1)S(1)}, bf16[32,256,256]{2,1,0:T(8,128)(2,1)S(1)}) custom-call(s32[1,1,32]{2,1,0:T(1,128)S(1)} %copy-done.7, s32[1,1,32]{2,1,0:T(1,128)S(1)} %copy-done.8, s32[1,1]{1,0:T(1,128)S(6)} %copy.27.refs_2_, ...), custom_call_target="tpu_custom_call", output_to_operand_aliasing={{3}: (4, {})} | custom-call | flops 4194304 | bytes 4194304 | tf_op jit(solution)/shard_map/dual_0/pallas_call | solution.py:407
  51.9 2.1 %collective-permute-start.10 = (s16[160,128]{1,0:T(8,128)(2,1)S(1)}, s16[160,128]{1,0:T(8,128)(2,1)S(1)}, u32[]{:S(2)}, u32[]{:S(2)}) collective-permute-start(s16[160,128]{1,0:T(8,128)(2,1)S(1)} %get-tuple-element.60.refs_0_), channel_id=1, source_target_pairs={{0,8},{8,0},{16,24},{24,16},{1,9},{9,1},{17,25},{25,17},{2,10},{10... | collective-permute-start | bytes 122888 | tf_op jit(solution)/shard_map/ppermute | solution.py:430
  54.0 2.0 %collective-permute-done.10.refs_1_ = s16[160,128]{1,0:T(8,128)(2,1)S(1)} collective-permute-done((s16[160,128]{1,0:T(8,128)(2,1)S(1)}, s16[160,128]{1,0:T(8,128)(2,1)S(1)}, u32[]{:S(2)}, u32[]{:S(2)}) %collective-permute-start.10) | collective-permute-done | bytes 40992 | tf_op jit(solution)/shard_map/ppermute | solution.py:430
  55.9 0.1 sums_0.1.refs_6_
  56.0 3.6 %collective-permute-start.11 = (s16[160,128]{1,0:T(8,128)(2,1)S(1)}, s16[160,128]{1,0:T(8,128)(2,1)S(1)}, u32[]{:S(2)}, u32[]{:S(2)}) collective-permute-start(s16[160,128]{1,0:T(8,128)(2,1)S(1)} %sums_0.1.refs_6_), channel_id=1, source_target_pairs={{0,16},{8,24},{16,0},{24,8},{1,17},{9,25},{17,1},{25,9},{2,18},{10... | collective-permute-start | bytes 122888 | tf_op jit(solution)/shard_map/ppermute | solution.py:430
  59.6 2.0 %collective-permute-done.11.refs_7_ = s16[160,128]{1,0:T(8,128)(2,1)S(1)} collective-permute-done((s16[160,128]{1,0:T(8,128)(2,1)S(1)}, s16[160,128]{1,0:T(8,128)(2,1)S(1)}, u32[]{:S(2)}, u32[]{:S(2)}) %collective-permute-start.11) | collective-permute-done | bytes 40992 | tf_op jit(solution)/shard_map/ppermute | solution.py:430
  61.6 2.3 %primal_0.1 = (f32[128,128]{1,0:T(8,128)}, f32[5,16,128]{2,1,0:T(8,128)S(1)}, f32[5,16,128]{2,1,0:T(8,128)S(1)}, bf16[32,256,256]{2,1,0:T(8,128)(2,1)S(1)}) custom-call(s32[1,1,32]{2,1,0:T(1,128)S(1)} %copy-done.7, s32[1,1,32]{2,1,0:T(1,128)S(1)} %copy-done.8, s32[1,1]{1,0:T(1,128)S(6)} %copy.27.refs_2_, ...), custom_call_target="tpu_custom_call", output_to_operand_aliasing={{3}: (4, {})} | custom-call | flops 4194304 | bytes 4194304 | tf_op jit(solution)/shard_map/primal_0/pallas_call | solution.py:407
  63.9 0.0 collective-permute-start.12
  63.9 1.2 %collective-permute-done.12.refs_1_ = f32[5,16,128]{2,1,0:T(8,128)S(1)} collective-permute-done((f32[5,16,128]{2,1,0:T(8,128)S(1)}, f32[5,16,128]{2,1,0:T(8,128)S(1)}, u32[]{:S(2)}, u32[]{:S(2)}) %collective-permute-start.12) | collective-permute-done | bytes 40992 | tf_op jit(solution)/shard_map/ppermute | solution.py:430
  65.1 1.5 %collective-permute-start.13 = (f32[3,16,128]{2,1,0:T(8,128)S(1)}, f32[3,16,128]{2,1,0:T(8,128)S(1)}, u32[]{:S(2)}, u32[]{:S(2)}) collective-permute-start(f32[3,16,128]{2,1,0:T(8,128)S(1)} %get-tuple-element.70), channel_id=1, source_target_pairs={{0,2},{1,3},{2,0},{3,1},{4,6},{5,7},{6,4},{7,5},{8,10},{9,11},{10,... | collective-permute-start | bytes 73736 | tf_op jit(solution)/shard_map/ppermute | solution.py:430
  66.6 2.3 %collective-permute-done.13.refs_1_ = f32[3,16,128]{2,1,0:T(8,128)S(1)} collective-permute-done((f32[3,16,128]{2,1,0:T(8,128)S(1)}, f32[3,16,128]{2,1,0:T(8,128)S(1)}, u32[]{:S(2)}, u32[]{:S(2)}) %collective-permute-start.13) | collective-permute-done | bytes 24608 | tf_op jit(solution)/shard_map/ppermute | solution.py:430
  69.0 1.5 %collective-permute-start.14 = (f32[2,16,128]{2,1,0:T(8,128)S(1)}, f32[2,16,128]{2,1,0:T(8,128)S(1)}, u32[]{:S(2)}, u32[]{:S(2)}) collective-permute-start(f32[2,16,128]{2,1,0:T(8,128)S(1)} %get-tuple-element.72), channel_id=1, source_target_pairs={{0,4},{1,5},{2,6},{3,7},{4,0},{5,1},{6,2},{7,3},{8,12},{9,13},{10,... | collective-permute-start | bytes 49160 | tf_op jit(solution)/shard_map/ppermute | solution.py:430
  70.5 2.2 %collective-permute-done.14.refs_2_ = f32[2,16,128]{2,1,0:T(8,128)S(1)} collective-permute-done((f32[2,16,128]{2,1,0:T(8,128)S(1)}, f32[2,16,128]{2,1,0:T(8,128)S(1)}, u32[]{:S(2)}, u32[]{:S(2)}) %collective-permute-start.14) | collective-permute-done | bytes 16416 | tf_op jit(solution)/shard_map/ppermute | solution.py:430
  72.7 1.2 %last.1 = (f32[16,128]{1,0:T(8,128)}, f32[2]{0:T(128)}) custom-call(f32[2]{0:T(128)S(1)} %copy-done.9, f32[2,16,128]{2,1,0:T(8,128)S(1)} %get-tuple-element.71.refs_1_, f32[2,16,128]{2,1,0:T(8,128)S(1)} %collective-permute-done.14.refs_2_, f32[128,128]{1,0:T(8,128)S(1)} %get-tuple-element.73.refs_3_, f32[128,128]{1,0:T(8,128)S(1)} %get-tuple-element.74.refs_4_), custom_call_target="tpu_custom_call" | custom-call | tf_op jit(solution)/shard_map/last/pallas_call | solution.py:407
  (6 shorter events, 0.0 us)
Async XLA Ops:
  0.6 14.6 %copy-start.8 = (s32[1,1,32]{2,1,0:T(1,128)S(1)}, s32[1,1,32]{2,1,0:T(1,128)}, u32[]{:S(2)}) copy-start(s32[1,1,32]{2,1,0:T(1,128)} %refs_1_.11) | copy-start | bytes 388
  0.6 14.6 %copy-start.7 = (s32[1,1,32]{2,1,0:T(1,128)S(1)}, s32[1,1,32]{2,1,0:T(1,128)}, u32[]{:S(2)}) copy-start(s32[1,1,32]{2,1,0:T(1,128)} %refs_0_.12) | copy-start | bytes 388
  0.7 14.6 %copy-start.9 = (f32[2]{0:T(128)S(1)}, f32[2]{0:T(128)}, u32[]{:S(2)}) copy-start(f32[2]{0:T(128)} %refs_0_.13) | copy-start | bytes 28
  0.7 14.6 %copy-start.3 = (f32[16384]{0:T(1024)S(1)}, f32[16384]{0:T(1024)}, u32[]{:S(2)}) copy-start(f32[16384]{0:T(1024)} %param.26) | copy-start | bytes 196612
  0.7 14.6 %copy-start.1 = (s32[3,16384]{1,0:T(4,128)S(1)}, s32[3,16384]{1,0:T(4,128)}, u32[]{:S(2)}) copy-start(s32[3,16384]{1,0:T(4,128)} %param.20) | copy-start | bytes 589828
  1.4 25.7 %copy-start = (s32[3,16384]{1,0:T(4,128)S(1)}, s32[3,16384]{1,0:T(4,128)}, u32[]{:S(2)}) copy-start(s32[3,16384]{1,0:T(4,128)} %param.21) | copy-start | bytes 589828
  4.3 5.6 %collective-permute-start = (s16[336,128]{1,0:T(8,128)(2,1)S(1)}, s16[336,128]{1,0:T(8,128)(2,1)S(1)}, u32[]{:S(2)}, u32[]{:S(2)}) collective-permute-start(s16[336,128]{1,0:T(8,128)(2,1)S(1)} %get-tuple-element.41.refs_0_), channel_id=1, source_target_pairs={{0,8},{8,0},{16,24},{24,16},{1,9},{9,1},{17,25},{25,17},{2,10},{10... | collective-permute-start | bytes 258056 | tf_op jit(solution)/shard_map/ppermute | solution.py:430
  10.0 5.2 %collective-permute-start.1 = (s16[240,128]{1,0:T(8,128)(2,1)S(1)}, s16[240,128]{1,0:T(8,128)(2,1)S(1)}, u32[]{:S(2)}, u32[]{:S(2)}) collective-permute-start(s16[240,128]{1,0:T(8,128)(2,1)S(1)} %get-tuple-element.43.refs_6_), channel_id=1, source_target_pairs={{0,16},{8,24},{16,0},{24,8},{1,17},{9,25},{17,1},{25,9},{2,18},{10... | collective-permute-start | bytes 184328 | tf_op jit(solution)/shard_map/ppermute | solution.py:430
  15.3 23.1 %copy-start.2 = (f32[3,16384]{1,0:T(4,128)S(1)}, f32[3,16384]{1,0:T(4,128)}, u32[]{:S(2)}) copy-start(f32[3,16384]{1,0:T(4,128)} %param.18) | copy-start | bytes 589828
  15.3 23.1 %copy-start.4 = (f32[16384]{0:T(1024)S(1)}, f32[16384]{0:T(1024)}, u32[]{:S(2)}) copy-start(f32[16384]{0:T(1024)} %param.22) | copy-start | bytes 196612
  15.3 23.1 %copy-start.5 = (f32[16384]{0:T(1024)S(1)}, f32[16384]{0:T(1024)}, u32[]{:S(2)}) copy-start(f32[16384]{0:T(1024)} %param.24) | copy-start | bytes 196612
  17.1 1.3 %collective-permute-start.2 = (f32[128,128]{1,0:T(8,128)S(1)}, f32[128,128]{1,0:T(8,128)S(1)}, u32[]{:S(2)}, u32[]{:S(2)}) collective-permute-start(f32[128,128]{1,0:T(8,128)S(1)} %get-tuple-element.46), channel_id=1, source_target_pairs={{0,1},{1,0},{2,3},{3,2},{4,5},{5,4},{6,7},{7,6},{8,9},{9,8},{10,11... | collective-permute-start | bytes 196616 | tf_op jit(solution)/shard_map/ppermute | solution.py:430
  18.4 4.3 %collective-permute-start.3 = (f32[128,128]{1,0:T(8,128)S(1)}, f32[128,128]{1,0:T(8,128)S(1)}, u32[]{:S(2)}, u32[]{:S(2)}) collective-permute-start(f32[128,128]{1,0:T(8,128)S(1)} %add.12), channel_id=1, source_target_pairs={{0,2},{1,3},{2,0},{3,1},{4,6},{5,7},{6,4},{7,5},{8,10},{9,11},{10,... | collective-permute-start | bytes 196616 | tf_op jit(solution)/shard_map/ppermute | solution.py:430
  22.8 4.3 %collective-permute-start.4 = (f32[128,128]{1,0:T(8,128)S(1)}, f32[128,128]{1,0:T(8,128)S(1)}, u32[]{:S(2)}, u32[]{:S(2)}) collective-permute-start(f32[128,128]{1,0:T(8,128)S(1)} %add.13.refs_6_), channel_id=1, source_target_pairs={{0,4},{1,5},{2,6},{3,7},{4,0},{5,1},{6,2},{7,3},{8,12},{9,13},{10,... | collective-permute-start | bytes 196616 | tf_op jit(solution)/shard_map/ppermute | solution.py:430
  27.1 23.4 %copy-start.6 = (f32[16384]{0:T(1024)S(1)}, f32[16384]{0:T(1024)}, u32[]{:S(2)}) copy-start(f32[16384]{0:T(1024)} %param.23) | copy-start | bytes 196612
  28.5 5.2 %collective-permute-start.5 = (s16[240,128]{1,0:T(8,128)(2,1)S(1)}, s16[240,128]{1,0:T(8,128)(2,1)S(1)}, u32[]{:S(2)}, u32[]{:S(2)}) collective-permute-start(s16[240,128]{1,0:T(8,128)(2,1)S(1)} %get-tuple-element.51.refs_0_), channel_id=1, source_target_pairs={{0,16},{8,24},{16,0},{24,8},{1,17},{9,25},{17,1},{25,9},{2,18},{10... | collective-permute-start | bytes 184328 | tf_op jit(solution)/shard_map/ppermute | solution.py:430
  33.8 4.6 %collective-permute-start.6 = (s16[336,128]{1,0:T(8,128)(2,1)S(1)}, s16[336,128]{1,0:T(8,128)(2,1)S(1)}, u32[]{:S(2)}, u32[]{:S(2)}) collective-permute-start(s16[336,128]{1,0:T(8,128)(2,1)S(1)} %gather_0.1.refs_6_), channel_id=1, source_target_pairs={{0,8},{8,0},{16,24},{24,16},{1,9},{9,1},{17,25},{25,17},{2,10},{10... | collective-permute-start | bytes 258056 | tf_op jit(solution)/shard_map/ppermute | solution.py:430
  40.5 1.3 %collective-permute-start.7 = (f32[128,128]{1,0:T(8,128)S(1)}, f32[128,128]{1,0:T(8,128)S(1)}, u32[]{:S(2)}, u32[]{:S(2)}) collective-permute-start(f32[128,128]{1,0:T(8,128)S(1)} %get-tuple-element.55), channel_id=1, source_target_pairs={{0,1},{1,0},{2,3},{3,2},{4,5},{5,4},{6,7},{7,6},{8,9},{9,8},{10,11... | collective-permute-start | bytes 196616 | tf_op jit(solution)/shard_map/ppermute | solution.py:430
  41.8 4.3 %collective-permute-start.8 = (f32[128,128]{1,0:T(8,128)S(1)}, f32[128,128]{1,0:T(8,128)S(1)}, u32[]{:S(2)}, u32[]{:S(2)}) collective-permute-start(f32[128,128]{1,0:T(8,128)S(1)} %add.14), channel_id=1, source_target_pairs={{0,2},{1,3},{2,0},{3,1},{4,6},{5,7},{6,4},{7,5},{8,10},{9,11},{10,... | collective-permute-start | bytes 196616 | tf_op jit(solution)/shard_map/ppermute | solution.py:430
  46.2 4.3 %collective-permute-start.9 = (f32[128,128]{1,0:T(8,128)S(1)}, f32[128,128]{1,0:T(8,128)S(1)}, u32[]{:S(2)}, u32[]{:S(2)}) collective-permute-start(f32[128,128]{1,0:T(8,128)S(1)} %add.15.refs_6_), channel_id=1, source_target_pairs={{0,4},{1,5},{2,6},{3,7},{4,0},{5,1},{6,2},{7,3},{8,12},{9,13},{10,... | collective-permute-start | bytes 196616 | tf_op jit(solution)/shard_map/ppermute | solution.py:430
  51.9 4.1 %collective-permute-start.10 = (s16[160,128]{1,0:T(8,128)(2,1)S(1)}, s16[160,128]{1,0:T(8,128)(2,1)S(1)}, u32[]{:S(2)}, u32[]{:S(2)}) collective-permute-start(s16[160,128]{1,0:T(8,128)(2,1)S(1)} %get-tuple-element.60.refs_0_), channel_id=1, source_target_pairs={{0,8},{8,0},{16,24},{24,16},{1,9},{9,1},{17,25},{25,17},{2,10},{10... | collective-permute-start | bytes 122888 | tf_op jit(solution)/shard_map/ppermute | solution.py:430
  56.0 5.6 %collective-permute-start.11 = (s16[160,128]{1,0:T(8,128)(2,1)S(1)}, s16[160,128]{1,0:T(8,128)(2,1)S(1)}, u32[]{:S(2)}, u32[]{:S(2)}) collective-permute-start(s16[160,128]{1,0:T(8,128)(2,1)S(1)} %sums_0.1.refs_6_), channel_id=1, source_target_pairs={{0,16},{8,24},{16,0},{24,8},{1,17},{9,25},{17,1},{25,9},{2,18},{10... | collective-permute-start | bytes 122888 | tf_op jit(solution)/shard_map/ppermute | solution.py:430
  63.9 1.2 %collective-permute-start.12 = (f32[5,16,128]{2,1,0:T(8,128)S(1)}, f32[5,16,128]{2,1,0:T(8,128)S(1)}, u32[]{:S(2)}, u32[]{:S(2)}) collective-permute-start(f32[5,16,128]{2,1,0:T(8,128)S(1)} %get-tuple-element.68), channel_id=1, source_target_pairs={{0,1},{1,0},{2,3},{3,2},{4,5},{5,4},{6,7},{7,6},{8,9},{9,8},{10,11... | collective-permute-start | bytes 122888 | tf_op jit(solution)/shard_map/ppermute | solution.py:430
  65.1 3.8 %collective-permute-start.13 = (f32[3,16,128]{2,1,0:T(8,128)S(1)}, f32[3,16,128]{2,1,0:T(8,128)S(1)}, u32[]{:S(2)}, u32[]{:S(2)}) collective-permute-start(f32[3,16,128]{2,1,0:T(8,128)S(1)} %get-tuple-element.70), channel_id=1, source_target_pairs={{0,2},{1,3},{2,0},{3,1},{4,6},{5,7},{6,4},{7,5},{8,10},{9,11},{10,... | collective-permute-start | bytes 73736 | tf_op jit(solution)/shard_map/ppermute | solution.py:430
  69.0 3.7 %collective-permute-start.14 = (f32[2,16,128]{2,1,0:T(8,128)S(1)}, f32[2,16,128]{2,1,0:T(8,128)S(1)}, u32[]{:S(2)}, u32[]{:S(2)}) collective-permute-start(f32[2,16,128]{2,1,0:T(8,128)S(1)} %get-tuple-element.72), channel_id=1, source_target_pairs={{0,4},{1,5},{2,6},{3,7},{4,0},{5,1},{6,2},{7,3},{8,12},{9,13},{10,... | collective-permute-start | bytes 49160 | tf_op jit(solution)/shard_map/ppermute | solution.py:430

commit v7 on v5

--- a/solution.py
+++ b/solution.py
@@ -10,7 +10,7 @@
 
 LANES = 128
 EXTRA = 16
-CHUNKS = 4
+CHUNKS = 8
 SCALES = 16
 STEPS = 64.0
 LIMIT = 32760.0
@@ -40,7 +40,7 @@
     return values.astype(jnp.bfloat16).astype(jnp.float32)
 
 
-def add_products(transpose, in_index, out_index, count, tiles, slots, source, total):
+def add_products(in_index, out_index, count, tiles, slots, source, total):
     per_block = tiles.shape[-1] // LANES
     several = len(total.shape) == 3
     live_count = count[0, 0]
@@ -62,10 +62,7 @@
                 stacked = jnp.where(which == vector, line, stacked)
             halves.append(stacked)
         block = (jnp.concatenate(halves, axis=1) * live).astype(jnp.bfloat16)
-        contract = ((1,), (0,)) if transpose else ((1,), (1,))
-        product = lax.dot_general(
-            block, tiles[slot], (contract, ((), ())), preferred_element_type=jnp.float32
-        )
+        product = jnp.dot(block, tiles[slot], preferred_element_type=jnp.float32)
         for half in range(per_block):
             at = pl.ds(place + half, 1)
             lanes = slice(half * LANES, (half + 1) * LANES)
@@ -164,7 +161,7 @@
     for part in range(CHUNKS):
         fetch(part).wait()
         span = range(part * chunk, (part + 1) * chunk)
-        add_products(True, rows, columns, count, tiles, span, source, total)
+        add_products(rows, columns, count, tiles, span, source, total)
     lines = total.shape[1]
     share = lines // n_row
     me = lax.axis_index("row")
@@ -178,6 +175,11 @@
         out[lines + iterations * share :, :] = scale_rows([code, saved_code])
 
 
+def turn_body(tiles, turned, _):
+    for slot in range(tiles.shape[0]):
+        turned[slot] = tiles[slot].T
+
+
 def dual_body(step, n_col, rows, columns, count, sizes, tiles, mask, parts, before, anchor, *refs):
     last = step == 0
     if last:
@@ -185,14 +187,15 @@
     else:
         saved, term, anchor_out, out, _, source, total = refs
     weight = weight_of(step)
-    image = tree_sum([part[...] for part in parts])
+    rows_y = before.shape[0]
+    image = tree_sum([long(part[:rows_y, :]) * scales_of(part)[0] for part in parts])
     adjoint = before[...] + sizes[0] * image
     anchor_out[...] = anchor[...] + (1.0 - weight) * adjoint
     value = mask[:, step, :].astype(jnp.float32) * weight * adjoint
     term[...] = value
     source[...] = rounded(value)
     total[...] = jnp.zeros_like(total)
-    add_products(True, rows, columns, count, tiles, range(tiles.shape[0]), source, total)
+    add_products(rows, columns, count, tiles, range(tiles.shape[0]), source, total)
     lines = total.shape[0]
     units, code = encode(total[...])
     out[:lines, :] = short(units)
@@ -208,10 +211,9 @@
         out[lines:, :] = scale_rows([code])
     else:
         size = saved.shape[0]
-        coarse, fine, saved_code = encode_fine(saved[...])
-        out[lines : lines + size, :] = short(coarse)
-        out[lines + size : lines + 2 * size, :] = short(fine)
-        out[lines + 2 * size :, :] = scale_rows([code, saved_code])
+        saved_units, saved_code = encode(saved[...])
+        out[lines : lines + size, :] = short(saved_units)
+        out[lines + size :, :] = scale_rows([code, saved_code])
 
 
 def primal_body(kind, step, n_row, n_col, rows, columns, count, sizes, tiles, mask, parts, before, anchor, *refs):
@@ -249,9 +251,7 @@
         me = lax.axis_index("row")
         for part, (held, scale) in enumerate(zip(parts, scales)):
             at = pl.ds(pl.multiple_of((me ^ part) * share, share), share)
-            units = long(held[lines : lines + size, :])
-            units += long(held[lines + size : lines + 2 * size, :]) * (1.0 / FINE)
-            sums = (units * scale[1]).reshape(iterations, share, LANES)
+            sums = (long(held[lines : lines + size, :]) * scale[1]).reshape(iterations, share, LANES)
             reduced[:, at, :] = cost[at, :][None] - sums
         source[0] = rounded(value)
         for vector in range(iterations):
@@ -259,13 +259,13 @@
             half = jnp.minimum(jnp.maximum(saved - sizes[0] * reduced[vector], 0.0), upper[...])
             source[vector + 1] = rounded(2.0 * half - saved)
         total[...] = jnp.zeros_like(total)
-        add_products(False, columns, rows, count, tiles, all_slots, source, total)
+        add_products(columns, rows, count, tiles, all_slots, source, total)
         out[...] = total[0]
         images[...] = total[1:]
         return
     source[...] = rounded(value)
     out[...] = jnp.zeros_like(out)
-    add_products(False, columns, rows, count, tiles, all_slots, source, out)
+    add_products(columns, rows, count, tiles, all_slots, source, out)
     if kind == "sums":
         size = saved.shape[0]
         saved[...] = tree_sum(
@@ -290,6 +290,13 @@
         other[n_col // 2 * share :, :] = tail
 
 
+def pair_body(mine, received, out):
+    lines = mine.shape[0]
+    units, code = encode(mine[...] + received[...])
+    out[:lines, :] = short(units)
+    out[lines:, :] = scale_rows([code])
+
+
 def split_body(n_chip, mine, received, *outs):
     share = (mine.shape[0] - EXTRA) // n_chip
     chip = lax.axis_index("col") // 2
@@ -358,12 +365,14 @@
     )(*flat)
 
 
+def swap(array, axis, stride):
+    size = lax.axis_size(axis)
+    return lax.ppermute(array, axis, [(i, i ^ stride) for i in range(size)])
+
+
 def exchange(parts, axis, stride=1):
-    size = lax.axis_size(axis)
-    return [parts[0]] + [
-        lax.ppermute(parts[k], axis, [(i, i ^ (k * stride)) for i in range(size)])
-        for k in range(1, size // stride)
-    ]
+    size = lax.axis_size(axis) // stride
+    return [parts[0]] + [swap(parts[k], axis, k * stride) for k in range(1, size)]
 
 
 def local(
@@ -434,13 +443,22 @@
         "first",
         cost,
     )
+    turned, tiles = run(
+        turn_body,
+        [pltpu.VMEM(tiles.shape, tiles.dtype)],
+        [(VMEM, tiles)],
+        [],
+        "turn",
+        cost,
+        tiles,
+    )
     adjoint_x, anchor_x = lines(primal_cotangent), None
     terms_x, terms_y = [], [term_y]
     reduced = images = saved_sums = None
     for step in reversed(range(iterations)):
         parts = exchange(parts, "row")
         kind = {0: "last", last: "sums", last - 1: "shares"}.get(step, "plain")
-        groups = where + [(SMEM, step_sizes), (VMEM, tiles), (VMEM, mask_x), (VMEM, parts)]
+        groups = where + [(SMEM, step_sizes), (VMEM, turned), (VMEM, mask_x), (VMEM, parts)]
         groups += [(VMEM, adjoint_x), (VMEM, anchor_x)]
         body = functools.partial(primal_body, kind, step, n_row, n_col)
         if step == 0:
@@ -457,8 +475,8 @@
                 scratch(iterations + 1, lines_x, LANES),
                 scratch(iterations + 1, lines_y, LANES),
             ]
-        term_x, adjoint_x, anchor_x, partial, *more, tiles = run(
-            body, outs, groups, extra, f"primal_{step}", cost, tiles
+        term_x, adjoint_x, anchor_x, partial, *more, turned = run(
+            body, outs, groups, extra, f"primal_{step}", cost, turned
         )
         if kind == "sums":
             (saved_sums,) = more
@@ -466,8 +484,14 @@
             reduced, images = more
             saved_sums = None
         terms_x.insert(0, term_x)
-        partial = sum_pair(partial)
-        parts = exchange([partial] * n_chip, "col", 2)
+        part = run(
+            pair_body,
+            [jax.ShapeDtypeStruct((lines_y + SCALES, LANES), jnp.int16)],
+            [(VMEM, partial), (VMEM, swap(partial, "col", 1))],
+            [],
+            f"pair_{step}",
+        )[0]
+        parts = exchange([part] * n_chip, "col", 2)
         groups = where + [(SMEM, step_sizes), (VMEM, tiles), (VMEM, mask_y), (VMEM, parts)]
         groups += [(VMEM, term_y), (VMEM, anchor_y)]
         if step == 1:
@@ -475,7 +499,7 @@
             out = row_part(EXTRA)
         else:
             groups += [(VMEM, saved_sums)]
-            out = row_part(2 * saved_lines if saved_sums is not None else 0)
+            out = row_part(saved_lines if saved_sums is not None else 0)
         term_y, anchor_y, part, tiles = run(
             functools.partial(dual_body, step - 1, n_col),
             [full_y, full_y, out],
@@ -488,16 +512,16 @@
         parts = [part] * n_row
         terms_y.insert(0, term_y)
     half_y = f32(n_chip * share_y + EXTRA, LANES)
-    primal_adjoint, mine, other, tiles = run(
+    primal_adjoint, mine, other, turned = run(
         body,
-        [full_x, half_y, half_y],
+        [pltpu.VMEM((lines_x, LANES), jnp.float32), half_y, half_y],
         groups + [(VMEM, reduced), (VMEM, terms_x)],
         [scratch(lines_x, LANES), scratch(lines_y, LANES)],
         "primal_0",
         cost,
-        tiles,
-    )
-    received = lax.ppermute(other, "col", [(i, i ^ 1) for i in range(n_col)])
+        turned,
+    )
+    received = swap(other, "col", 1)
     parts = run(
         functools.partial(split_body, n_chip),
         [f32(share_y + EXTRA, LANES)] * n_chip,
@@ -515,11 +539,6 @@
         "last",
     )
     return (primal_adjoint.reshape(-1), dual_adjoint.reshape(-1), gradients)
-
-
-def sum_pair(partial):
-    size = lax.axis_size("col")
-    return partial + lax.ppermute(partial, "col", [(i, i ^ 1) for i in range(size)])
 
 
 def solution(mesh):

time: 68.3 us -> 64.9 us (0.950)
  waiting for transfers between devices: 28.1 us -> 23.7 us
    ppermute x21, waiting for transfers between devices: 28.1 us -> 23.7 us  [swap(): return lax.ppermute(array, axis, [(i, i ^ stride) for i in range(size)])]
    pallas_call x8 -> x11, Pallas kernels: 13.2 us -> 13.4 us  [run(): pl.pallas_call(kernel, out_shape=shapes, in_specs=specs, out_specs=[SMEM...]
  transfers between devices with their start and end apart: 21 -> 21, of which waited for: 18 -> 17; matrix products, arithmetic and copies ran while one was open for 0% -> 1% of each run, Pallas kernels for 0% -> 2%
where the time goes in v7:
time: 64.9 us; the launch traced here: 64.7 us
  starting transfers between devices  25.4 us (39%)
  waiting for transfers between devices  23.7 us (37%)
  Pallas kernels  13.4 us (21%)
  between operations  1.49 us (2%)
  local copies, waits for them, and re-layouts  0.68 us (1%)
    ppermute x21, starting transfers between devices, swap(): return lax.ppermute(array, axis, [(i, i ^ stride) for i in range(size)])  25.4 us
    ppermute x21, waiting for transfers between devices, swap(): return lax.ppermute(array, axis, [(i, i ^ stride) for i in range(size)])  23.7 us
    pallas_call x11, Pallas kernels, run(): pl.pallas_call(kernel, out_shape=shapes, in_specs=specs, out_specs=[SMEM...  13.4 us
  transfers between devices with their start and end apart: 21, of which 17 were waited for; matrix products, arithmetic and copies ran while one was open for 1% of the time, Pallas kernels for 2%

profile of v7, /device:TPU:0, one launch (start us, length us, event | category | flops | bytes accessed | tf_op | source)
XLA Modules:
  0.0 64.7 jit_solution(1420781561951704934)
XLA Ops:
  1.3 0.0 copy-start.1
  1.3 0.0 copy-start.3
  1.3 0.0 copy-start.7
  1.3 0.0 copy-start.8
  1.3 0.0 copy-start.9
  1.3 3.9 %first.1 = (bf16[32,256,256]{2,1,0:T(8,128)(2,1)S(1)}, f32[128,128]{1,0:T(8,128)S(1)}, f32[128,128]{1,0:T(8,128)S(1)}, s16[240,128]{1,0:T(8,128)(2,1)S(1)}, s16[...) custom-call(s32[1,1,32]{2,1,0:T(1,128)} %refs_0_.12, s32[1,1,32]{2,1,0:T(1,128)} %refs_1_.11, ...), custom_call_target="tpu_custom_call" | custom-call | flops 4194304 | bytes 4194304 | tf_op jit(solution)/shard_map/first/pallas_call | solution.py:355
  5.2 3.1 %collective-permute-start = (s16[240,128]{1,0:T(8,128)(2,1)S(1)}, s16[240,128]{1,0:T(8,128)(2,1)S(1)}, u32[]{:S(2)}, u32[]{:S(2)}) collective-permute-start(s16[240,128]{1,0:T(8,128)(2,1)S(1)} %get-tuple-element.44), channel_id=1, source_target_pairs={{0,8},{8,0},{16,24},{24,16},{1,9},{9,1},{17,25},{25,17},{2,10},{10... | collective-permute-start | bytes 184328 | tf_op jit(solution)/shard_map/ppermute | solution.py:370
  8.3 2.6 %collective-permute-start.1 = (s16[240,128]{1,0:T(8,128)(2,1)S(1)}, s16[240,128]{1,0:T(8,128)(2,1)S(1)}, u32[]{:S(2)}, u32[]{:S(2)}) collective-permute-start(s16[240,128]{1,0:T(8,128)(2,1)S(1)} %get-tuple-element.45), channel_id=1, source_target_pairs={{0,16},{8,24},{16,0},{24,8},{1,17},{9,25},{17,1},{25,9},{2,18},{10... | collective-permute-start | bytes 184328 | tf_op jit(solution)/shard_map/ppermute | solution.py:370
  10.9 0.0 collective-permute-start.2
  10.9 1.1 %turn.1 = (bf16[32,256,256]{2,1,0:T(8,128)(2,1)S(1)}, bf16[32,256,256]{2,1,0:T(8,128)(2,1)S(1)}) custom-call(bf16[32,256,256]{2,1,0:T(8,128)(2,1)S(1)} %get-tuple-element.41.refs_0_), custom_call_target="tpu_custom_call", output_to_operand_aliasing={{1}: (0, {})} | custom-call | flops 4194304 | bytes 4194304 | tf_op jit(solution)/shard_map/turn/pallas_call | solution.py:355
  12.0 0.0 collective-permute-done.refs_7_
  12.0 2.6 %collective-permute-done.1.refs_8_ = s16[240,128]{1,0:T(8,128)(2,1)S(1)} collective-permute-done((s16[240,128]{1,0:T(8,128)(2,1)S(1)}, s16[240,128]{1,0:T(8,128)(2,1)S(1)}, u32[]{:S(2)}, u32[]{:S(2)}) %collective-permute-start.1) | collective-permute-done | bytes 61472 | tf_op jit(solution)/shard_map/ppermute | solution.py:370
  14.6 2.3 %collective-permute-done.2.refs_9_ = s16[240,128]{1,0:T(8,128)(2,1)S(1)} collective-permute-done((s16[240,128]{1,0:T(8,128)(2,1)S(1)}, s16[240,128]{1,0:T(8,128)(2,1)S(1)}, u32[]{:S(2)}, u32[]{:S(2)}) %collective-permute-start.2) | collective-permute-done | bytes 61472 | tf_op jit(solution)/shard_map/ppermute | solution.py:370
  16.9 0.0 copy-done.1
  16.9 0.0 copy-done.3
  16.9 0.0 copy-start.2
  16.9 0.0 copy-start.4
  17.0 0.0 copy-start.5
  17.0 1.4 %primal_2.1 = (f32[128,128]{1,0:T(8,128)S(1)}, f32[128,128]{1,0:T(8,128)S(1)}, f32[128,128]{1,0:T(8,128)S(1)}, f32[128,128]{1,0:T(8,128)S(1)}, f32[96,128]{1,0:T(8,128)S(1)}, /*index=5*/bf16[32,256,256]{2,1,0:T(8,128)(2,1)S(1)}) custom-call(s32[1,1,32]{2,1,0:T(1,128)S(1)} %copy-done.7, s32[1,1,32]{2,1,0:T(1,128)S(1)} %copy-done.8, ...), custom_call_target="tpu_custom_call", output_to_operand_aliasing={{5}: (4, {})} | custom-call | flops 4194304 | bytes 4194304 | tf_op jit(solution)/shard_map/primal_2/pallas_call | solution.py:355
  18.3 0.1 collective-permute-start.3
  18.4 1.2 %collective-permute-done.3.refs_1_ = f32[128,128]{1,0:T(8,128)S(1)} collective-permute-done((f32[128,128]{1,0:T(8,128)S(1)}, f32[128,128]{1,0:T(8,128)S(1)}, u32[]{:S(2)}, u32[]{:S(2)}) %collective-permute-start.3) | collective-permute-done | bytes 65568 | tf_op jit(solution)/shard_map/ppermute | solution.py:370
  19.7 2.5 %collective-permute-start.6 = (s16[144,128]{1,0:T(8,128)(2,1)S(1)}, s16[144,128]{1,0:T(8,128)(2,1)S(1)}, u32[]{:S(2)}, u32[]{:S(2)}) collective-permute-start(s16[144,128]{1,0:T(8,128)(2,1)S(1)} %pair_2.1.refs_6_), channel_id=1, source_target_pairs={{0,6},{1,7},{2,4},{3,5},{4,2},{5,3},{6,0},{7,1},{8,14},{9,15},{10,... | collective-permute-start | bytes 110600 | tf_op jit(solution)/shard_map/ppermute | solution.py:370
  22.2 0.5 collective-permute-start.5
  22.7 0.5 collective-permute-start.4
  23.3 1.4 %collective-permute-done.6.refs_9_ = s16[144,128]{1,0:T(8,128)(2,1)S(1)} collective-permute-done((s16[144,128]{1,0:T(8,128)(2,1)S(1)}, s16[144,128]{1,0:T(8,128)(2,1)S(1)}, u32[]{:S(2)}, u32[]{:S(2)}) %collective-permute-start.6) | collective-permute-done | bytes 36896 | tf_op jit(solution)/shard_map/ppermute | solution.py:370
  24.6 1.5 %collective-permute-done.5.refs_8_ = s16[144,128]{1,0:T(8,128)(2,1)S(1)} collective-permute-done((s16[144,128]{1,0:T(8,128)(2,1)S(1)}, s16[144,128]{1,0:T(8,128)(2,1)S(1)}, u32[]{:S(2)}, u32[]{:S(2)}) %collective-permute-start.5) | collective-permute-done | bytes 36896 | tf_op jit(solution)/shard_map/ppermute | solution.py:370
  26.2 0.5 collective-permute-done.4.refs_7_
  26.7 1.4 %dual_1.1 = (f32[128,128]{1,0:T(8,128)S(1)}, f32[128,128]{1,0:T(8,128)S(1)}, s16[240,128]{1,0:T(8,128)(2,1)S(1)}, bf16[32,256,256]{2,1,0:T(8,128)(2,1)S(1)}) custom-call(s32[1,1,32]{2,1,0:T(1,128)S(1)} %copy-done.7, s32[1,1,32]{2,1,0:T(1,128)S(1)} %copy-done.8, s32[1,1]{1,0:T(1,128)S(6)} %copy.30.refs_2_, ...), custom_call_target="tpu_custom_call", output_to_operand_aliasing={{3}: (4, {})} | custom-call | flops 4194304 | bytes 4194304 | tf_op jit(solution)/shard_map/dual_1/pallas_call | solution.py:355
  28.1 1.6 %collective-permute-start.9 = (s16[240,128]{1,0:T(8,128)(2,1)S(1)}, s16[240,128]{1,0:T(8,128)(2,1)S(1)}, u32[]{:S(2)}, u32[]{:S(2)}) collective-permute-start(s16[240,128]{1,0:T(8,128)(2,1)S(1)} %get-tuple-element.53.refs_6_), channel_id=1, source_target_pairs={{0,24},{8,16},{16,8},{24,0},{1,25},{9,17},{17,9},{25,1},{2,26},{10... | collective-permute-start | bytes 184328 | tf_op jit(solution)/shard_map/ppermute | solution.py:370
  29.7 0.0 collective-permute-start.8
  29.7 2.9 %collective-permute-start.7 = (s16[240,128]{1,0:T(8,128)(2,1)S(1)}, s16[240,128]{1,0:T(8,128)(2,1)S(1)}, u32[]{:S(2)}, u32[]{:S(2)}) collective-permute-start(s16[240,128]{1,0:T(8,128)(2,1)S(1)} %get-tuple-element.53.refs_6_), channel_id=1, source_target_pairs={{0,8},{8,0},{16,24},{24,16},{1,9},{9,1},{17,25},{25,17},{2,10},{10... | collective-permute-start | bytes 184328 | tf_op jit(solution)/shard_map/ppermute | solution.py:370
  32.6 1.8 %collective-permute-done.9.refs_9_ = s16[240,128]{1,0:T(8,128)(2,1)S(1)} collective-permute-done((s16[240,128]{1,0:T(8,128)(2,1)S(1)}, s16[240,128]{1,0:T(8,128)(2,1)S(1)}, u32[]{:S(2)}, u32[]{:S(2)}) %collective-permute-start.9) | collective-permute-done | bytes 61472 | tf_op jit(solution)/shard_map/ppermute | solution.py:370
  34.3 1.3 %collective-permute-done.8.refs_8_ = s16[240,128]{1,0:T(8,128)(2,1)S(1)} collective-permute-done((s16[240,128]{1,0:T(8,128)(2,1)S(1)}, s16[240,128]{1,0:T(8,128)(2,1)S(1)}, u32[]{:S(2)}, u32[]{:S(2)}) %collective-permute-start.8) | collective-permute-done | bytes 61472 | tf_op jit(solution)/shard_map/ppermute | solution.py:370
  35.6 0.0 collective-permute-done.7.refs_7_
  35.6 0.0 copy-done.2
  35.6 1.6 %primal_1.1 = (f32[128,128]{1,0:T(8,128)S(1)}, f32[128,128]{1,0:T(8,128)S(1)}, f32[128,128]{1,0:T(8,128)S(1)}, f32[128,128]{1,0:T(8,128)S(1)}, f32[3,128,128]{2,...) custom-call(s32[1,1,32]{2,1,0:T(1,128)S(1)} %copy-done.7, ...), custom_call_target="tpu_custom_call", output_to_operand_aliasing={{6}: (4, {})} | custom-call | flops 4194304 | bytes 4194304 | tf_op jit(solution)/shard_map/primal_1/pallas_call | solution.py:355
  37.2 0.1 collective-permute-start.10
  37.3 1.2 %collective-permute-done.10.refs_1_ = f32[128,128]{1,0:T(8,128)S(1)} collective-permute-done((f32[128,128]{1,0:T(8,128)S(1)}, f32[128,128]{1,0:T(8,128)S(1)}, u32[]{:S(2)}, u32[]{:S(2)}) %collective-permute-start.10) | collective-permute-done | bytes 65568 | tf_op jit(solution)/shard_map/ppermute | solution.py:370
  38.5 0.1 pair_1.1.refs_6_
  38.6 1.6 %collective-permute-start.13 = (s16[144,128]{1,0:T(8,128)(2,1)S(1)}, s16[144,128]{1,0:T(8,128)(2,1)S(1)}, u32[]{:S(2)}, u32[]{:S(2)}) collective-permute-start(s16[144,128]{1,0:T(8,128)(2,1)S(1)} %pair_1.1.refs_6_), channel_id=1, source_target_pairs={{0,6},{1,7},{2,4},{3,5},{4,2},{5,3},{6,0},{7,1},{8,14},{9,15},{10,... | collective-permute-start | bytes 110600 | tf_op jit(solution)/shard_map/ppermute | solution.py:370
  40.2 0.5 collective-permute-start.12
  40.7 1.5 %collective-permute-start.11 = (s16[144,128]{1,0:T(8,128)(2,1)S(1)}, s16[144,128]{1,0:T(8,128)(2,1)S(1)}, u32[]{:S(2)}, u32[]{:S(2)}) collective-permute-start(s16[144,128]{1,0:T(8,128)(2,1)S(1)} %pair_1.1.refs_6_), channel_id=1, source_target_pairs={{0,2},{1,3},{2,0},{3,1},{4,6},{5,7},{6,4},{7,5},{8,10},{9,11},{10,... | collective-permute-start | bytes 110600 | tf_op jit(solution)/shard_map/ppermute | solution.py:370
  42.1 1.4 %collective-permute-done.13.refs_9_ = s16[144,128]{1,0:T(8,128)(2,1)S(1)} collective-permute-done((s16[144,128]{1,0:T(8,128)(2,1)S(1)}, s16[144,128]{1,0:T(8,128)(2,1)S(1)}, u32[]{:S(2)}, u32[]{:S(2)}) %collective-permute-start.13) | collective-permute-done | bytes 36896 | tf_op jit(solution)/shard_map/ppermute | solution.py:370
  43.5 0.6 collective-permute-done.12.refs_8_
  44.1 0.5 collective-permute-done.11.refs_7_
  44.6 0.0 copy-done.6
  44.6 1.4 %dual_0.1 = (f32[128,128]{1,0:T(8,128)S(1)}, f32[128,128]{1,0:T(8,128)S(1)}, s16[160,128]{1,0:T(8,128)(2,1)S(1)}, bf16[32,256,256]{2,1,0:T(8,128)(2,1)S(1)}) custom-call(s32[1,1,32]{2,1,0:T(1,128)S(1)} %copy-done.7, s32[1,1,32]{2,1,0:T(1,128)S(1)} %copy-done.8, s32[1,1]{1,0:T(1,128)S(6)} %copy.30.refs_2_, ...), custom_call_target="tpu_custom_call", output_to_operand_aliasing={{3}: (4, {})} | custom-call | flops 4194304 | bytes 4194304 | tf_op jit(solution)/shard_map/dual_0/pallas_call | solution.py:355
  46.1 2.1 %collective-permute-start.16 = (s16[160,128]{1,0:T(8,128)(2,1)S(1)}, s16[160,128]{1,0:T(8,128)(2,1)S(1)}, u32[]{:S(2)}, u32[]{:S(2)}) collective-permute-start(s16[160,128]{1,0:T(8,128)(2,1)S(1)} %get-tuple-element.62.refs_6_), channel_id=1, source_target_pairs={{0,24},{8,16},{16,8},{24,0},{1,25},{9,17},{17,9},{25,1},{2,26},{10... | collective-permute-start | bytes 122888 | tf_op jit(solution)/shard_map/ppermute | solution.py:370
  48.2 0.5 collective-permute-start.15
  48.7 1.8 %collective-permute-start.14 = (s16[160,128]{1,0:T(8,128)(2,1)S(1)}, s16[160,128]{1,0:T(8,128)(2,1)S(1)}, u32[]{:S(2)}, u32[]{:S(2)}) collective-permute-start(s16[160,128]{1,0:T(8,128)(2,1)S(1)} %get-tuple-element.62.refs_6_), channel_id=1, source_target_pairs={{0,8},{8,0},{16,24},{24,16},{1,9},{9,1},{17,25},{25,17},{2,10},{10... | collective-permute-start | bytes 122888 | tf_op jit(solution)/shard_map/ppermute | solution.py:370
  50.5 1.8 %collective-permute-done.16.refs_9_ = s16[160,128]{1,0:T(8,128)(2,1)S(1)} collective-permute-done((s16[160,128]{1,0:T(8,128)(2,1)S(1)}, s16[160,128]{1,0:T(8,128)(2,1)S(1)}, u32[]{:S(2)}, u32[]{:S(2)}) %collective-permute-start.16) | collective-permute-done | bytes 40992 | tf_op jit(solution)/shard_map/ppermute | solution.py:370
  52.3 0.9 %collective-permute-done.15.refs_8_ = s16[160,128]{1,0:T(8,128)(2,1)S(1)} collective-permute-done((s16[160,128]{1,0:T(8,128)(2,1)S(1)}, s16[160,128]{1,0:T(8,128)(2,1)S(1)}, u32[]{:S(2)}, u32[]{:S(2)}) %collective-permute-start.15) | collective-permute-done | bytes 40992 | tf_op jit(solution)/shard_map/ppermute | solution.py:370
  53.2 0.0 collective-permute-done.14.refs_7_
  53.2 1.4 %primal_0.1 = (f32[128,128]{1,0:T(8,128)S(1)}, f32[80,128]{1,0:T(8,128)S(1)}, f32[80,128]{1,0:T(8,128)S(1)}, bf16[32,256,256]{2,1,0:T(8,128)(2,1)S(1)}) custom-call(s32[1,1,32]{2,1,0:T(1,128)S(1)} %copy-done.7, s32[1,1,32]{2,1,0:T(1,128)S(1)} %copy-done.8, s32[1,1]{1,0:T(1,128)S(6)} %copy.30.refs_2_, ...), custom_call_target="tpu_custom_call", output_to_operand_aliasing={{3}: (4, {})} | custom-call | flops 4194304 | bytes 4194304 | tf_op jit(solution)/shard_map/primal_0/pallas_call | solution.py:355
  54.5 0.1 collective-permute-start.17
  54.6 1.2 %collective-permute-done.17.refs_1_ = f32[80,128]{1,0:T(8,128)S(1)} collective-permute-done((f32[80,128]{1,0:T(8,128)S(1)}, f32[80,128]{1,0:T(8,128)S(1)}, u32[]{:S(2)}, u32[]{:S(2)}) %collective-permute-start.17) | collective-permute-done | bytes 40992 | tf_op jit(solution)/shard_map/ppermute | solution.py:370
  55.8 1.6 %collective-permute-start.18 = (f32[32,128]{1,0:T(8,128)S(1)}, f32[32,128]{1,0:T(8,128)S(1)}, u32[]{:S(2)}, u32[]{:S(2)}) collective-permute-start(f32[32,128]{1,0:T(8,128)S(1)} %get-tuple-element.72), channel_id=1, source_target_pairs={{0,2},{1,3},{2,0},{3,1},{4,6},{5,7},{6,4},{7,5},{8,10},{9,11},{10,... | collective-permute-start | bytes 49160 | tf_op jit(solution)/shard_map/ppermute | solution.py:370
  57.4 1.5 %collective-permute-start.19 = (f32[32,128]{1,0:T(8,128)S(1)}, f32[32,128]{1,0:T(8,128)S(1)}, u32[]{:S(2)}, u32[]{:S(2)}) collective-permute-start(f32[32,128]{1,0:T(8,128)S(1)} %get-tuple-element.73), channel_id=1, source_target_pairs={{0,4},{1,5},{2,6},{3,7},{4,0},{5,1},{6,2},{7,3},{8,12},{9,13},{10,... | collective-permute-start | bytes 49160 | tf_op jit(solution)/shard_map/ppermute | solution.py:370
  58.9 0.5 collective-permute-start.20
  59.4 0.6 copy.29
  60.0 0.0 collective-permute-done.18.refs_2_
  60.0 1.1 %collective-permute-done.19.refs_3_ = f32[32,128]{1,0:T(8,128)S(1)} collective-permute-done((f32[32,128]{1,0:T(8,128)S(1)}, f32[32,128]{1,0:T(8,128)S(1)}, u32[]{:S(2)}, u32[]{:S(2)}) %collective-permute-start.19) | collective-permute-done | bytes 16416 | tf_op jit(solution)/shard_map/ppermute | solution.py:370
  61.1 2.4 %collective-permute-done.20.refs_4_ = f32[32,128]{1,0:T(8,128)S(1)} collective-permute-done((f32[32,128]{1,0:T(8,128)S(1)}, f32[32,128]{1,0:T(8,128)S(1)}, u32[]{:S(2)}, u32[]{:S(2)}) %collective-permute-start.20) | collective-permute-done | bytes 16416 | tf_op jit(solution)/shard_map/ppermute | solution.py:370
  63.6 1.2 %last.1 = (f32[16,128]{1,0:T(8,128)}, f32[2]{0:T(128)}) custom-call(f32[2]{0:T(128)S(1)} %copy-done.9, f32[32,128]{1,0:T(8,128)S(1)} %get-tuple-element.71.refs_1_, f32[32,128]{1,0:T(8,128)S(1)} %collective-permute-done.18.refs_2_, f32[32,128]{1,0:T(8,128)S(1)} %collective-permute-done.19.refs_3_, f32[32,128]{1,0:T(8,128)S(1)} %collective-permute-done.20.refs_4_, ...), custom_call_target="tpu_custom_call" | custom-call | tf_op jit(solution)/shard_map/last/pallas_call | solution.py:355
  (10 shorter events, 0.1 us)
Async XLA Ops:
  1.3 15.6 %copy-start.1 = (s32[3,16384]{1,0:T(4,128)S(1)}, s32[3,16384]{1,0:T(4,128)}, u32[]{:S(2)}) copy-start(s32[3,16384]{1,0:T(4,128)} %param.20) | copy-start | bytes 589828
  1.3 15.6 %copy-start.3 = (f32[16384]{0:T(1024)S(1)}, f32[16384]{0:T(1024)}, u32[]{:S(2)}) copy-start(f32[16384]{0:T(1024)} %param.26) | copy-start | bytes 196612
  1.3 15.6 %copy-start.7 = (s32[1,1,32]{2,1,0:T(1,128)S(1)}, s32[1,1,32]{2,1,0:T(1,128)}, u32[]{:S(2)}) copy-start(s32[1,1,32]{2,1,0:T(1,128)} %refs_0_.12) | copy-start | bytes 388
  1.3 15.6 %copy-start.8 = (s32[1,1,32]{2,1,0:T(1,128)S(1)}, s32[1,1,32]{2,1,0:T(1,128)}, u32[]{:S(2)}) copy-start(s32[1,1,32]{2,1,0:T(1,128)} %refs_1_.11) | copy-start | bytes 388
  1.3 15.6 %copy-start.9 = (f32[2]{0:T(128)S(1)}, f32[2]{0:T(128)}, u32[]{:S(2)}) copy-start(f32[2]{0:T(128)} %refs_0_.13) | copy-start | bytes 28
  5.2 6.8 %collective-permute-start = (s16[240,128]{1,0:T(8,128)(2,1)S(1)}, s16[240,128]{1,0:T(8,128)(2,1)S(1)}, u32[]{:S(2)}, u32[]{:S(2)}) collective-permute-start(s16[240,128]{1,0:T(8,128)(2,1)S(1)} %get-tuple-element.44), channel_id=1, source_target_pairs={{0,8},{8,0},{16,24},{24,16},{1,9},{9,1},{17,25},{25,17},{2,10},{10... | collective-permute-start | bytes 184328 | tf_op jit(solution)/shard_map/ppermute | solution.py:370
  8.3 6.3 %collective-permute-start.1 = (s16[240,128]{1,0:T(8,128)(2,1)S(1)}, s16[240,128]{1,0:T(8,128)(2,1)S(1)}, u32[]{:S(2)}, u32[]{:S(2)}) collective-permute-start(s16[240,128]{1,0:T(8,128)(2,1)S(1)} %get-tuple-element.45), channel_id=1, source_target_pairs={{0,16},{8,24},{16,0},{24,8},{1,17},{9,25},{17,1},{25,9},{2,18},{10... | collective-permute-start | bytes 184328 | tf_op jit(solution)/shard_map/ppermute | solution.py:370
  10.9 6.0 %collective-permute-start.2 = (s16[240,128]{1,0:T(8,128)(2,1)S(1)}, s16[240,128]{1,0:T(8,128)(2,1)S(1)}, u32[]{:S(2)}, u32[]{:S(2)}) collective-permute-start(s16[240,128]{1,0:T(8,128)(2,1)S(1)} %get-tuple-element.46), channel_id=1, source_target_pairs={{0,24},{8,16},{16,8},{24,0},{1,25},{9,17},{17,9},{25,1},{2,26},{10... | collective-permute-start | bytes 184328 | tf_op jit(solution)/shard_map/ppermute | solution.py:370
  10.9 15.8 %copy-start = (s32[3,16384]{1,0:T(4,128)S(1)}, s32[3,16384]{1,0:T(4,128)}, u32[]{:S(2)}) copy-start(s32[3,16384]{1,0:T(4,128)} %param.21) | copy-start | bytes 589828
  16.9 18.7 %copy-start.2 = (f32[3,16384]{1,0:T(4,128)S(1)}, f32[3,16384]{1,0:T(4,128)}, u32[]{:S(2)}) copy-start(f32[3,16384]{1,0:T(4,128)} %param.18) | copy-start | bytes 589828
  16.9 18.7 %copy-start.4 = (f32[16384]{0:T(1024)S(1)}, f32[16384]{0:T(1024)}, u32[]{:S(2)}) copy-start(f32[16384]{0:T(1024)} %param.22) | copy-start | bytes 196612
  17.0 18.7 %copy-start.5 = (f32[16384]{0:T(1024)S(1)}, f32[16384]{0:T(1024)}, u32[]{:S(2)}) copy-start(f32[16384]{0:T(1024)} %param.24) | copy-start | bytes 196612
  18.3 1.3 %collective-permute-start.3 = (f32[128,128]{1,0:T(8,128)S(1)}, f32[128,128]{1,0:T(8,128)S(1)}, u32[]{:S(2)}, u32[]{:S(2)}) collective-permute-start(f32[128,128]{1,0:T(8,128)S(1)} %get-tuple-element.49.refs_0_), channel_id=1, source_target_pairs={{0,1},{1,0},{2,3},{3,2},{4,5},{5,4},{6,7},{7,6},{8,9},{9,8},{10,11... | collective-permute-start | bytes 196616 | tf_op jit(solution)/shard_map/ppermute | solution.py:370
  19.7 4.9 %collective-permute-start.6 = (s16[144,128]{1,0:T(8,128)(2,1)S(1)}, s16[144,128]{1,0:T(8,128)(2,1)S(1)}, u32[]{:S(2)}, u32[]{:S(2)}) collective-permute-start(s16[144,128]{1,0:T(8,128)(2,1)S(1)} %pair_2.1.refs_6_), channel_id=1, source_target_pairs={{0,6},{1,7},{2,4},{3,5},{4,2},{5,3},{6,0},{7,1},{8,14},{9,15},{10,... | collective-permute-start | bytes 110600 | tf_op jit(solution)/shard_map/ppermute | solution.py:370
  22.2 4.0 %collective-permute-start.5 = (s16[144,128]{1,0:T(8,128)(2,1)S(1)}, s16[144,128]{1,0:T(8,128)(2,1)S(1)}, u32[]{:S(2)}, u32[]{:S(2)}) collective-permute-start(s16[144,128]{1,0:T(8,128)(2,1)S(1)} %pair_2.1.refs_6_), channel_id=1, source_target_pairs={{0,4},{1,5},{2,6},{3,7},{4,0},{5,1},{6,2},{7,3},{8,12},{9,13},{10,... | collective-permute-start | bytes 110600 | tf_op jit(solution)/shard_map/ppermute | solution.py:370
  22.7 4.0 %collective-permute-start.4 = (s16[144,128]{1,0:T(8,128)(2,1)S(1)}, s16[144,128]{1,0:T(8,128)(2,1)S(1)}, u32[]{:S(2)}, u32[]{:S(2)}) collective-permute-start(s16[144,128]{1,0:T(8,128)(2,1)S(1)} %pair_2.1.refs_6_), channel_id=1, source_target_pairs={{0,2},{1,3},{2,0},{3,1},{4,6},{5,7},{6,4},{7,5},{8,10},{9,11},{10,... | collective-permute-start | bytes 110600 | tf_op jit(solution)/shard_map/ppermute | solution.py:370
  26.7 17.9 %copy-start.6 = (f32[16384]{0:T(1024)S(1)}, f32[16384]{0:T(1024)}, u32[]{:S(2)}) copy-start(f32[16384]{0:T(1024)} %param.23) | copy-start | bytes 196612
  28.1 6.2 %collective-permute-start.9 = (s16[240,128]{1,0:T(8,128)(2,1)S(1)}, s16[240,128]{1,0:T(8,128)(2,1)S(1)}, u32[]{:S(2)}, u32[]{:S(2)}) collective-permute-start(s16[240,128]{1,0:T(8,128)(2,1)S(1)} %get-tuple-element.53.refs_6_), channel_id=1, source_target_pairs={{0,24},{8,16},{16,8},{24,0},{1,25},{9,17},{17,9},{25,1},{2,26},{10... | collective-permute-start | bytes 184328 | tf_op jit(solution)/shard_map/ppermute | solution.py:370
  29.7 5.9 %collective-permute-start.8 = (s16[240,128]{1,0:T(8,128)(2,1)S(1)}, s16[240,128]{1,0:T(8,128)(2,1)S(1)}, u32[]{:S(2)}, u32[]{:S(2)}) collective-permute-start(s16[240,128]{1,0:T(8,128)(2,1)S(1)} %get-tuple-element.53.refs_6_), channel_id=1, source_target_pairs={{0,16},{8,24},{16,0},{24,8},{1,17},{9,25},{17,1},{25,9},{2,18},{10... | collective-permute-start | bytes 184328 | tf_op jit(solution)/shard_map/ppermute | solution.py:370
  29.7 5.9 %collective-permute-start.7 = (s16[240,128]{1,0:T(8,128)(2,1)S(1)}, s16[240,128]{1,0:T(8,128)(2,1)S(1)}, u32[]{:S(2)}, u32[]{:S(2)}) collective-permute-start(s16[240,128]{1,0:T(8,128)(2,1)S(1)} %get-tuple-element.53.refs_6_), channel_id=1, source_target_pairs={{0,8},{8,0},{16,24},{24,16},{1,9},{9,1},{17,25},{25,17},{2,10},{10... | collective-permute-start | bytes 184328 | tf_op jit(solution)/shard_map/ppermute | solution.py:370
  37.2 1.3 %collective-permute-start.10 = (f32[128,128]{1,0:T(8,128)S(1)}, f32[128,128]{1,0:T(8,128)S(1)}, u32[]{:S(2)}, u32[]{:S(2)}) collective-permute-start(f32[128,128]{1,0:T(8,128)S(1)} %get-tuple-element.58.refs_0_), channel_id=1, source_target_pairs={{0,1},{1,0},{2,3},{3,2},{4,5},{5,4},{6,7},{7,6},{8,9},{9,8},{10,11... | collective-permute-start | bytes 196616 | tf_op jit(solution)/shard_map/ppermute | solution.py:370
  38.6 4.9 %collective-permute-start.13 = (s16[144,128]{1,0:T(8,128)(2,1)S(1)}, s16[144,128]{1,0:T(8,128)(2,1)S(1)}, u32[]{:S(2)}, u32[]{:S(2)}) collective-permute-start(s16[144,128]{1,0:T(8,128)(2,1)S(1)} %pair_1.1.refs_6_), channel_id=1, source_target_pairs={{0,6},{1,7},{2,4},{3,5},{4,2},{5,3},{6,0},{7,1},{8,14},{9,15},{10,... | collective-permute-start | bytes 110600 | tf_op jit(solution)/shard_map/ppermute | solution.py:370
  40.2 4.0 %collective-permute-start.12 = (s16[144,128]{1,0:T(8,128)(2,1)S(1)}, s16[144,128]{1,0:T(8,128)(2,1)S(1)}, u32[]{:S(2)}, u32[]{:S(2)}) collective-permute-start(s16[144,128]{1,0:T(8,128)(2,1)S(1)} %pair_1.1.refs_6_), channel_id=1, source_target_pairs={{0,4},{1,5},{2,6},{3,7},{4,0},{5,1},{6,2},{7,3},{8,12},{9,13},{10,... | collective-permute-start | bytes 110600 | tf_op jit(solution)/shard_map/ppermute | solution.py:370
  40.7 4.0 %collective-permute-start.11 = (s16[144,128]{1,0:T(8,128)(2,1)S(1)}, s16[144,128]{1,0:T(8,128)(2,1)S(1)}, u32[]{:S(2)}, u32[]{:S(2)}) collective-permute-start(s16[144,128]{1,0:T(8,128)(2,1)S(1)} %pair_1.1.refs_6_), channel_id=1, source_target_pairs={{0,2},{1,3},{2,0},{3,1},{4,6},{5,7},{6,4},{7,5},{8,10},{9,11},{10,... | collective-permute-start | bytes 110600 | tf_op jit(solution)/shard_map/ppermute | solution.py:370
  46.1 6.2 %collective-permute-start.16 = (s16[160,128]{1,0:T(8,128)(2,1)S(1)}, s16[160,128]{1,0:T(8,128)(2,1)S(1)}, u32[]{:S(2)}, u32[]{:S(2)}) collective-permute-start(s16[160,128]{1,0:T(8,128)(2,1)S(1)} %get-tuple-element.62.refs_6_), channel_id=1, source_target_pairs={{0,24},{8,16},{16,8},{24,0},{1,25},{9,17},{17,9},{25,1},{2,26},{10... | collective-permute-start | bytes 122888 | tf_op jit(solution)/shard_map/ppermute | solution.py:370
  48.2 5.0 %collective-permute-start.15 = (s16[160,128]{1,0:T(8,128)(2,1)S(1)}, s16[160,128]{1,0:T(8,128)(2,1)S(1)}, u32[]{:S(2)}, u32[]{:S(2)}) collective-permute-start(s16[160,128]{1,0:T(8,128)(2,1)S(1)} %get-tuple-element.62.refs_6_), channel_id=1, source_target_pairs={{0,16},{8,24},{16,0},{24,8},{1,17},{9,25},{17,1},{25,9},{2,18},{10... | collective-permute-start | bytes 122888 | tf_op jit(solution)/shard_map/ppermute | solution.py:370
  48.7 4.4 %collective-permute-start.14 = (s16[160,128]{1,0:T(8,128)(2,1)S(1)}, s16[160,128]{1,0:T(8,128)(2,1)S(1)}, u32[]{:S(2)}, u32[]{:S(2)}) collective-permute-start(s16[160,128]{1,0:T(8,128)(2,1)S(1)} %get-tuple-element.62.refs_6_), channel_id=1, source_target_pairs={{0,8},{8,0},{16,24},{24,16},{1,9},{9,1},{17,25},{25,17},{2,10},{10... | collective-permute-start | bytes 122888 | tf_op jit(solution)/shard_map/ppermute | solution.py:370
  54.5 1.3 %collective-permute-start.17 = (f32[80,128]{1,0:T(8,128)S(1)}, f32[80,128]{1,0:T(8,128)S(1)}, u32[]{:S(2)}, u32[]{:S(2)}) collective-permute-start(f32[80,128]{1,0:T(8,128)S(1)} %get-tuple-element.70), channel_id=1, source_target_pairs={{0,1},{1,0},{2,3},{3,2},{4,5},{5,4},{6,7},{7,6},{8,9},{9,8},{10,11... | collective-permute-start | bytes 122888 | tf_op jit(solution)/shard_map/ppermute | solution.py:370
  55.8 4.2 %collective-permute-start.18 = (f32[32,128]{1,0:T(8,128)S(1)}, f32[32,128]{1,0:T(8,128)S(1)}, u32[]{:S(2)}, u32[]{:S(2)}) collective-permute-start(f32[32,128]{1,0:T(8,128)S(1)} %get-tuple-element.72), channel_id=1, source_target_pairs={{0,2},{1,3},{2,0},{3,1},{4,6},{5,7},{6,4},{7,5},{8,10},{9,11},{10,... | collective-permute-start | bytes 49160 | tf_op jit(solution)/shard_map/ppermute | solution.py:370
  57.4 3.7 %collective-permute-start.19 = (f32[32,128]{1,0:T(8,128)S(1)}, f32[32,128]{1,0:T(8,128)S(1)}, u32[]{:S(2)}, u32[]{:S(2)}) collective-permute-start(f32[32,128]{1,0:T(8,128)S(1)} %get-tuple-element.73), channel_id=1, source_target_pairs={{0,4},{1,5},{2,6},{3,7},{4,0},{5,1},{6,2},{7,3},{8,12},{9,13},{10,... | collective-permute-start | bytes 49160 | tf_op jit(solution)/shard_map/ppermute | solution.py:370
  58.9 4.6 %collective-permute-start.20 = (f32[32,128]{1,0:T(8,128)S(1)}, f32[32,128]{1,0:T(8,128)S(1)}, u32[]{:S(2)}, u32[]{:S(2)}) collective-permute-start(f32[32,128]{1,0:T(8,128)S(1)} %get-tuple-element.74), channel_id=1, source_target_pairs={{0,6},{1,7},{2,4},{3,5},{4,2},{5,3},{6,0},{7,1},{8,14},{9,15},{10,... | collective-permute-start | bytes 49160 | tf_op jit(solution)/shard_map/ppermute | solution.py:370

commit v8 on v7

--- a/solution.py
+++ b/solution.py
@@ -10,7 +10,7 @@
 
 LANES = 128
 EXTRA = 16
-CHUNKS = 8
+CHUNKS = 4
 SCALES = 16
 STEPS = 64.0
 LIMIT = 32760.0
@@ -145,7 +145,7 @@
         return pltpu.make_async_copy(tile_data.at[0, 0, span], tiles.at[span], arrived.at[part])
 
     for part in range(CHUNKS):
-        fetch(part).start()
+        fetch(part).start(priority=part % 2)
     total[...] = jnp.zeros_like(total)
     for copy in small:
         copy.wait()
@@ -307,13 +307,21 @@
         out[share:, :] = tail
 
 
-def last_body(scales, sizes, parts, term, anchor, adjoint, gradients):
+def last_body(
+    scales, sizes, parts, term, anchor, adjoint_far, gradients_far, adjoint, gradients, sent
+):
     share = adjoint.shape[0]
     total = tree_sum([part[...] for part in parts])
     at = pl.ds(lax.axis_index("col") * share, share)
     adjoint[...] = term[at, :] + sizes[0] * total[:share] + anchor[at, :]
+    first = pltpu.make_async_copy(adjoint, adjoint_far, sent.at[0])
+    first.start()
     gradients[0] = jnp.sum(total[share + 8 : share + 16]) * scales[0]
     gradients[1] = jnp.sum(total[share : share + 8]) * scales[1]
+    second = pltpu.make_async_copy(gradients, gradients_far, sent.at[1])
+    second.start()
+    first.wait()
+    second.wait()
 
 
 def far(array):
@@ -347,16 +355,16 @@
                 taken.append([given.pop(0) for _ in range(width)])
         body(*taken, *given)
 
-    in_smem = [isinstance(shape, tuple) for shape in out_shape]
+    out_specs = [shape[0] if isinstance(shape, tuple) else VMEM for shape in out_shape]
     shapes = [shape[1] if isinstance(shape, tuple) else shape for shape in out_shape]
     if tiles is not None:
         shapes.append(pltpu.VMEM(tiles.shape, tiles.dtype))
-        in_smem.append(False)
+        out_specs.append(VMEM)
     return pl.pallas_call(
         kernel,
         out_shape=shapes,
         in_specs=specs,
-        out_specs=[SMEM if smem else VMEM for smem in in_smem],
+        out_specs=out_specs,
         scratch_shapes=scratch,
         input_output_aliases=aliases,
         compiler_params=pltpu.CompilerParams(vmem_limit_bytes=GRANT),
@@ -533,9 +541,13 @@
     scales = (1.0 / math.sqrt(column_length * n_col), 1.0 / math.sqrt(row_length * n_row))
     dual_adjoint, gradients = run(
         functools.partial(last_body, scales),
-        [f32(share_y, LANES), ("smem", f32(2))],
+        [(ANY, f32(share_y, LANES)), (ANY, f32(2))],
         [(SMEM, step_sizes), (VMEM, parts), (VMEM, term_y), (VMEM, anchor_y)],
-        [],
+        [
+            scratch(share_y, LANES),
+            pltpu.SMEM((2,), jnp.float32),
+            pltpu.SemaphoreType.DMA((2,)),
+        ],
         "last",
     )
     return (primal_adjoint.reshape(-1), dual_adjoint.reshape(-1), gradients)

time: 64.9 us -> 64.1 us (0.988)
  Pallas kernels: 13.4 us -> 12.6 us
    pallas_call x11, Pallas kernels: 13.4 us -> 12.6 us  [run(): pl.pallas_call(kernel, out_shape=shapes, in_specs=specs, out_specs=out_sp...]
where the time goes in v8:
time: 64.1 us; the launch traced here: 63.9 us
  starting transfers between devices  25.4 us (40%)
  waiting for transfers between devices  23.7 us (37%)
  Pallas kernels  12.6 us (20%)
  between operations  1.49 us (2%)
  local copies, waits for them, and re-layouts  0.68 us (1%)
    ppermute x21, starting transfers between devices, swap(): return lax.ppermute(array, axis, [(i, i ^ stride) for i in range(size)])  25.4 us
    ppermute x21, waiting for transfers between devices, swap(): return lax.ppermute(array, axis, [(i, i ^ stride) for i in range(size)])  23.7 us
    pallas_call x11, Pallas kernels, run(): pl.pallas_call(kernel, out_shape=shapes, in_specs=specs, out_specs=out_sp...  12.6 us
  transfers between devices with their start and end apart: 21, of which 17 were waited for; matrix products, arithmetic and copies ran while one was open for 1% of the time, Pallas kernels for 2%

profile of v8, /device:TPU:0, one launch (start us, length us, event | category | flops | bytes accessed | tf_op | source)
XLA Modules:
  0.0 63.9 jit_solution(9409321265607239562)
XLA Ops:
  1.3 0.0 copy-start.1
  1.3 0.0 copy-start.3
  1.3 0.0 copy-start.7
  1.3 0.0 copy-start.8
  1.3 0.0 copy-start.9
  1.3 3.0 %first.1 = (bf16[32,256,256]{2,1,0:T(8,128)(2,1)S(1)}, f32[128,128]{1,0:T(8,128)S(1)}, f32[128,128]{1,0:T(8,128)S(1)}, s16[240,128]{1,0:T(8,128)(2,1)S(1)}, s16[...) custom-call(s32[1,1,32]{2,1,0:T(1,128)} %refs_0_.12, s32[1,1,32]{2,1,0:T(1,128)} %refs_1_.11, ...), custom_call_target="tpu_custom_call" | custom-call | flops 4194304 | bytes 4194304 | tf_op jit(solution)/shard_map/first/pallas_call | solution.py:363
  4.4 3.1 %collective-permute-start = (s16[240,128]{1,0:T(8,128)(2,1)S(1)}, s16[240,128]{1,0:T(8,128)(2,1)S(1)}, u32[]{:S(2)}, u32[]{:S(2)}) collective-permute-start(s16[240,128]{1,0:T(8,128)(2,1)S(1)} %get-tuple-element.44), channel_id=1, source_target_pairs={{0,8},{8,0},{16,24},{24,16},{1,9},{9,1},{17,25},{25,17},{2,10},{10... | collective-permute-start | bytes 184328 | tf_op jit(solution)/shard_map/ppermute | solution.py:378
  7.5 2.6 %collective-permute-start.1 = (s16[240,128]{1,0:T(8,128)(2,1)S(1)}, s16[240,128]{1,0:T(8,128)(2,1)S(1)}, u32[]{:S(2)}, u32[]{:S(2)}) collective-permute-start(s16[240,128]{1,0:T(8,128)(2,1)S(1)} %get-tuple-element.45), channel_id=1, source_target_pairs={{0,16},{8,24},{16,0},{24,8},{1,17},{9,25},{17,1},{25,9},{2,18},{10... | collective-permute-start | bytes 184328 | tf_op jit(solution)/shard_map/ppermute | solution.py:378
  10.1 0.0 collective-permute-start.2
  10.1 1.1 %turn.1 = (bf16[32,256,256]{2,1,0:T(8,128)(2,1)S(1)}, bf16[32,256,256]{2,1,0:T(8,128)(2,1)S(1)}) custom-call(bf16[32,256,256]{2,1,0:T(8,128)(2,1)S(1)} %get-tuple-element.41.refs_0_), custom_call_target="tpu_custom_call", output_to_operand_aliasing={{1}: (0, {})} | custom-call | flops 4194304 | bytes 4194304 | tf_op jit(solution)/shard_map/turn/pallas_call | solution.py:363
  11.2 0.0 collective-permute-done.refs_7_
  11.2 2.6 %collective-permute-done.1.refs_8_ = s16[240,128]{1,0:T(8,128)(2,1)S(1)} collective-permute-done((s16[240,128]{1,0:T(8,128)(2,1)S(1)}, s16[240,128]{1,0:T(8,128)(2,1)S(1)}, u32[]{:S(2)}, u32[]{:S(2)}) %collective-permute-start.1) | collective-permute-done | bytes 61472 | tf_op jit(solution)/shard_map/ppermute | solution.py:378
  13.8 2.3 %collective-permute-done.2.refs_9_ = s16[240,128]{1,0:T(8,128)(2,1)S(1)} collective-permute-done((s16[240,128]{1,0:T(8,128)(2,1)S(1)}, s16[240,128]{1,0:T(8,128)(2,1)S(1)}, u32[]{:S(2)}, u32[]{:S(2)}) %collective-permute-start.2) | collective-permute-done | bytes 61472 | tf_op jit(solution)/shard_map/ppermute | solution.py:378
  16.1 0.0 copy-done.1
  16.1 0.0 copy-done.8
  16.1 0.0 copy-done.9
  16.1 0.0 copy-start.2
  16.1 0.0 copy-start.4
  16.1 0.0 copy-start.5
  16.1 1.4 %primal_2.1 = (f32[128,128]{1,0:T(8,128)S(1)}, f32[128,128]{1,0:T(8,128)S(1)}, f32[128,128]{1,0:T(8,128)S(1)}, f32[128,128]{1,0:T(8,128)S(1)}, f32[96,128]{1,0:T(8,128)S(1)}, /*index=5*/bf16[32,256,256]{2,1,0:T(8,128)(2,1)S(1)}) custom-call(s32[1,1,32]{2,1,0:T(1,128)S(1)} %copy-done.7, s32[1,1,32]{2,1,0:T(1,128)S(1)} %copy-done.8, ...), custom_call_target="tpu_custom_call", output_to_operand_aliasing={{5}: (4, {})} | custom-call | flops 4194304 | bytes 4194304 | tf_op jit(solution)/shard_map/primal_2/pallas_call | solution.py:363
  17.5 0.1 collective-permute-start.3
  17.6 1.2 %collective-permute-done.3.refs_1_ = f32[128,128]{1,0:T(8,128)S(1)} collective-permute-done((f32[128,128]{1,0:T(8,128)S(1)}, f32[128,128]{1,0:T(8,128)S(1)}, u32[]{:S(2)}, u32[]{:S(2)}) %collective-permute-start.3) | collective-permute-done | bytes 65568 | tf_op jit(solution)/shard_map/ppermute | solution.py:378
  18.9 2.5 %collective-permute-start.6 = (s16[144,128]{1,0:T(8,128)(2,1)S(1)}, s16[144,128]{1,0:T(8,128)(2,1)S(1)}, u32[]{:S(2)}, u32[]{:S(2)}) collective-permute-start(s16[144,128]{1,0:T(8,128)(2,1)S(1)} %pair_2.1.refs_6_), channel_id=1, source_target_pairs={{0,6},{1,7},{2,4},{3,5},{4,2},{5,3},{6,0},{7,1},{8,14},{9,15},{10,... | collective-permute-start | bytes 110600 | tf_op jit(solution)/shard_map/ppermute | solution.py:378
  21.4 0.5 collective-permute-start.5
  21.9 0.5 collective-permute-start.4
  22.4 1.4 %collective-permute-done.6.refs_9_ = s16[144,128]{1,0:T(8,128)(2,1)S(1)} collective-permute-done((s16[144,128]{1,0:T(8,128)(2,1)S(1)}, s16[144,128]{1,0:T(8,128)(2,1)S(1)}, u32[]{:S(2)}, u32[]{:S(2)}) %collective-permute-start.6) | collective-permute-done | bytes 36896 | tf_op jit(solution)/shard_map/ppermute | solution.py:378
  23.8 1.5 %collective-permute-done.5.refs_8_ = s16[144,128]{1,0:T(8,128)(2,1)S(1)} collective-permute-done((s16[144,128]{1,0:T(8,128)(2,1)S(1)}, s16[144,128]{1,0:T(8,128)(2,1)S(1)}, u32[]{:S(2)}, u32[]{:S(2)}) %collective-permute-start.5) | collective-permute-done | bytes 36896 | tf_op jit(solution)/shard_map/ppermute | solution.py:378
  25.3 0.5 collective-permute-done.4.refs_7_
  25.9 1.4 %dual_1.1 = (f32[128,128]{1,0:T(8,128)S(1)}, f32[128,128]{1,0:T(8,128)S(1)}, s16[240,128]{1,0:T(8,128)(2,1)S(1)}, bf16[32,256,256]{2,1,0:T(8,128)(2,1)S(1)}) custom-call(s32[1,1,32]{2,1,0:T(1,128)S(1)} %copy-done.7, s32[1,1,32]{2,1,0:T(1,128)S(1)} %copy-done.8, s32[1,1]{1,0:T(1,128)S(6)} %copy.30.refs_2_, ...), custom_call_target="tpu_custom_call", output_to_operand_aliasing={{3}: (4, {})} | custom-call | flops 4194304 | bytes 4194304 | tf_op jit(solution)/shard_map/dual_1/pallas_call | solution.py:363
  27.3 1.6 %collective-permute-start.9 = (s16[240,128]{1,0:T(8,128)(2,1)S(1)}, s16[240,128]{1,0:T(8,128)(2,1)S(1)}, u32[]{:S(2)}, u32[]{:S(2)}) collective-permute-start(s16[240,128]{1,0:T(8,128)(2,1)S(1)} %get-tuple-element.53.refs_6_), channel_id=1, source_target_pairs={{0,24},{8,16},{16,8},{24,0},{1,25},{9,17},{17,9},{25,1},{2,26},{10... | collective-permute-start | bytes 184328 | tf_op jit(solution)/shard_map/ppermute | solution.py:378
  28.9 0.0 collective-permute-start.8
  28.9 2.9 %collective-permute-start.7 = (s16[240,128]{1,0:T(8,128)(2,1)S(1)}, s16[240,128]{1,0:T(8,128)(2,1)S(1)}, u32[]{:S(2)}, u32[]{:S(2)}) collective-permute-start(s16[240,128]{1,0:T(8,128)(2,1)S(1)} %get-tuple-element.53.refs_6_), channel_id=1, source_target_pairs={{0,8},{8,0},{16,24},{24,16},{1,9},{9,1},{17,25},{25,17},{2,10},{10... | collective-permute-start | bytes 184328 | tf_op jit(solution)/shard_map/ppermute | solution.py:378
  31.7 1.8 %collective-permute-done.9.refs_9_ = s16[240,128]{1,0:T(8,128)(2,1)S(1)} collective-permute-done((s16[240,128]{1,0:T(8,128)(2,1)S(1)}, s16[240,128]{1,0:T(8,128)(2,1)S(1)}, u32[]{:S(2)}, u32[]{:S(2)}) %collective-permute-start.9) | collective-permute-done | bytes 61472 | tf_op jit(solution)/shard_map/ppermute | solution.py:378
  33.5 1.3 %collective-permute-done.8.refs_8_ = s16[240,128]{1,0:T(8,128)(2,1)S(1)} collective-permute-done((s16[240,128]{1,0:T(8,128)(2,1)S(1)}, s16[240,128]{1,0:T(8,128)(2,1)S(1)}, u32[]{:S(2)}, u32[]{:S(2)}) %collective-permute-start.8) | collective-permute-done | bytes 61472 | tf_op jit(solution)/shard_map/ppermute | solution.py:378
  34.8 0.0 collective-permute-done.7.refs_7_
  34.8 0.0 copy-done.5
  34.8 1.6 %primal_1.1 = (f32[128,128]{1,0:T(8,128)S(1)}, f32[128,128]{1,0:T(8,128)S(1)}, f32[128,128]{1,0:T(8,128)S(1)}, f32[128,128]{1,0:T(8,128)S(1)}, f32[3,128,128]{2,...) custom-call(s32[1,1,32]{2,1,0:T(1,128)S(1)} %copy-done.7, ...), custom_call_target="tpu_custom_call", output_to_operand_aliasing={{6}: (4, {})} | custom-call | flops 4194304 | bytes 4194304 | tf_op jit(solution)/shard_map/primal_1/pallas_call | solution.py:363
  36.4 0.1 collective-permute-start.10
  36.5 1.2 %collective-permute-done.10.refs_1_ = f32[128,128]{1,0:T(8,128)S(1)} collective-permute-done((f32[128,128]{1,0:T(8,128)S(1)}, f32[128,128]{1,0:T(8,128)S(1)}, u32[]{:S(2)}, u32[]{:S(2)}) %collective-permute-start.10) | collective-permute-done | bytes 65568 | tf_op jit(solution)/shard_map/ppermute | solution.py:378
  37.7 0.1 pair_1.1.refs_6_
  37.8 1.5 %collective-permute-start.13 = (s16[144,128]{1,0:T(8,128)(2,1)S(1)}, s16[144,128]{1,0:T(8,128)(2,1)S(1)}, u32[]{:S(2)}, u32[]{:S(2)}) collective-permute-start(s16[144,128]{1,0:T(8,128)(2,1)S(1)} %pair_1.1.refs_6_), channel_id=1, source_target_pairs={{0,6},{1,7},{2,4},{3,5},{4,2},{5,3},{6,0},{7,1},{8,14},{9,15},{10,... | collective-permute-start | bytes 110600 | tf_op jit(solution)/shard_map/ppermute | solution.py:378
  39.3 0.5 collective-permute-start.12
  39.8 1.5 %collective-permute-start.11 = (s16[144,128]{1,0:T(8,128)(2,1)S(1)}, s16[144,128]{1,0:T(8,128)(2,1)S(1)}, u32[]{:S(2)}, u32[]{:S(2)}) collective-permute-start(s16[144,128]{1,0:T(8,128)(2,1)S(1)} %pair_1.1.refs_6_), channel_id=1, source_target_pairs={{0,2},{1,3},{2,0},{3,1},{4,6},{5,7},{6,4},{7,5},{8,10},{9,11},{10,... | collective-permute-start | bytes 110600 | tf_op jit(solution)/shard_map/ppermute | solution.py:378
  41.3 1.4 %collective-permute-done.13.refs_9_ = s16[144,128]{1,0:T(8,128)(2,1)S(1)} collective-permute-done((s16[144,128]{1,0:T(8,128)(2,1)S(1)}, s16[144,128]{1,0:T(8,128)(2,1)S(1)}, u32[]{:S(2)}, u32[]{:S(2)}) %collective-permute-start.13) | collective-permute-done | bytes 36896 | tf_op jit(solution)/shard_map/ppermute | solution.py:378
  42.7 0.6 collective-permute-done.12.refs_8_
  43.3 0.5 collective-permute-done.11.refs_7_
  43.8 1.4 %dual_0.1 = (f32[128,128]{1,0:T(8,128)S(1)}, f32[128,128]{1,0:T(8,128)S(1)}, s16[160,128]{1,0:T(8,128)(2,1)S(1)}, bf16[32,256,256]{2,1,0:T(8,128)(2,1)S(1)}) custom-call(s32[1,1,32]{2,1,0:T(1,128)S(1)} %copy-done.7, s32[1,1,32]{2,1,0:T(1,128)S(1)} %copy-done.8, s32[1,1]{1,0:T(1,128)S(6)} %copy.30.refs_2_, ...), custom_call_target="tpu_custom_call", output_to_operand_aliasing={{3}: (4, {})} | custom-call | flops 4194304 | bytes 4194304 | tf_op jit(solution)/shard_map/dual_0/pallas_call | solution.py:363
  45.2 2.1 %collective-permute-start.16 = (s16[160,128]{1,0:T(8,128)(2,1)S(1)}, s16[160,128]{1,0:T(8,128)(2,1)S(1)}, u32[]{:S(2)}, u32[]{:S(2)}) collective-permute-start(s16[160,128]{1,0:T(8,128)(2,1)S(1)} %get-tuple-element.62.refs_6_), channel_id=1, source_target_pairs={{0,24},{8,16},{16,8},{24,0},{1,25},{9,17},{17,9},{25,1},{2,26},{10... | collective-permute-start | bytes 122888 | tf_op jit(solution)/shard_map/ppermute | solution.py:378
  47.4 0.6 collective-permute-start.15
  47.9 1.8 %collective-permute-start.14 = (s16[160,128]{1,0:T(8,128)(2,1)S(1)}, s16[160,128]{1,0:T(8,128)(2,1)S(1)}, u32[]{:S(2)}, u32[]{:S(2)}) collective-permute-start(s16[160,128]{1,0:T(8,128)(2,1)S(1)} %get-tuple-element.62.refs_6_), channel_id=1, source_target_pairs={{0,8},{8,0},{16,24},{24,16},{1,9},{9,1},{17,25},{25,17},{2,10},{10... | collective-permute-start | bytes 122888 | tf_op jit(solution)/shard_map/ppermute | solution.py:378
  49.7 1.8 %collective-permute-done.16.refs_9_ = s16[160,128]{1,0:T(8,128)(2,1)S(1)} collective-permute-done((s16[160,128]{1,0:T(8,128)(2,1)S(1)}, s16[160,128]{1,0:T(8,128)(2,1)S(1)}, u32[]{:S(2)}, u32[]{:S(2)}) %collective-permute-start.16) | collective-permute-done | bytes 40992 | tf_op jit(solution)/shard_map/ppermute | solution.py:378
  51.5 0.9 %collective-permute-done.15.refs_8_ = s16[160,128]{1,0:T(8,128)(2,1)S(1)} collective-permute-done((s16[160,128]{1,0:T(8,128)(2,1)S(1)}, s16[160,128]{1,0:T(8,128)(2,1)S(1)}, u32[]{:S(2)}, u32[]{:S(2)}) %collective-permute-start.15) | collective-permute-done | bytes 40992 | tf_op jit(solution)/shard_map/ppermute | solution.py:378
  52.4 0.0 collective-permute-done.14.refs_7_
  52.4 1.4 %primal_0.1 = (f32[128,128]{1,0:T(8,128)S(1)}, f32[80,128]{1,0:T(8,128)S(1)}, f32[80,128]{1,0:T(8,128)S(1)}, bf16[32,256,256]{2,1,0:T(8,128)(2,1)S(1)}) custom-call(s32[1,1,32]{2,1,0:T(1,128)S(1)} %copy-done.7, s32[1,1,32]{2,1,0:T(1,128)S(1)} %copy-done.8, s32[1,1]{1,0:T(1,128)S(6)} %copy.30.refs_2_, ...), custom_call_target="tpu_custom_call", output_to_operand_aliasing={{3}: (4, {})} | custom-call | flops 4194304 | bytes 4194304 | tf_op jit(solution)/shard_map/primal_0/pallas_call | solution.py:363
  53.7 0.1 collective-permute-start.17
  53.8 1.2 %collective-permute-done.17.refs_1_ = f32[80,128]{1,0:T(8,128)S(1)} collective-permute-done((f32[80,128]{1,0:T(8,128)S(1)}, f32[80,128]{1,0:T(8,128)S(1)}, u32[]{:S(2)}, u32[]{:S(2)}) %collective-permute-start.17) | collective-permute-done | bytes 40992 | tf_op jit(solution)/shard_map/ppermute | solution.py:378
  55.0 1.6 %collective-permute-start.18 = (f32[32,128]{1,0:T(8,128)S(1)}, f32[32,128]{1,0:T(8,128)S(1)}, u32[]{:S(2)}, u32[]{:S(2)}) collective-permute-start(f32[32,128]{1,0:T(8,128)S(1)} %get-tuple-element.72), channel_id=1, source_target_pairs={{0,2},{1,3},{2,0},{3,1},{4,6},{5,7},{6,4},{7,5},{8,10},{9,11},{10,... | collective-permute-start | bytes 49160 | tf_op jit(solution)/shard_map/ppermute | solution.py:378
  56.6 1.5 %collective-permute-start.19 = (f32[32,128]{1,0:T(8,128)S(1)}, f32[32,128]{1,0:T(8,128)S(1)}, u32[]{:S(2)}, u32[]{:S(2)}) collective-permute-start(f32[32,128]{1,0:T(8,128)S(1)} %get-tuple-element.73), channel_id=1, source_target_pairs={{0,4},{1,5},{2,6},{3,7},{4,0},{5,1},{6,2},{7,3},{8,12},{9,13},{10,... | collective-permute-start | bytes 49160 | tf_op jit(solution)/shard_map/ppermute | solution.py:378
  58.1 0.5 collective-permute-start.20
  58.6 0.6 copy.29
  59.2 0.0 collective-permute-done.18.refs_2_
  59.2 1.1 %collective-permute-done.19.refs_3_ = f32[32,128]{1,0:T(8,128)S(1)} collective-permute-done((f32[32,128]{1,0:T(8,128)S(1)}, f32[32,128]{1,0:T(8,128)S(1)}, u32[]{:S(2)}, u32[]{:S(2)}) %collective-permute-start.19) | collective-permute-done | bytes 16416 | tf_op jit(solution)/shard_map/ppermute | solution.py:378
  60.3 2.4 %collective-permute-done.20.refs_4_ = f32[32,128]{1,0:T(8,128)S(1)} collective-permute-done((f32[32,128]{1,0:T(8,128)S(1)}, f32[32,128]{1,0:T(8,128)S(1)}, u32[]{:S(2)}, u32[]{:S(2)}) %collective-permute-start.20) | collective-permute-done | bytes 16416 | tf_op jit(solution)/shard_map/ppermute | solution.py:378
  62.7 1.2 %last.1 = (f32[16,128]{1,0:T(8,128)}, f32[2]{0:T(128)}) custom-call(f32[2]{0:T(128)S(1)} %copy-done.9, f32[32,128]{1,0:T(8,128)S(1)} %get-tuple-element.71.refs_1_, f32[32,128]{1,0:T(8,128)S(1)} %collective-permute-done.18.refs_2_, f32[32,128]{1,0:T(8,128)S(1)} %collective-permute-done.19.refs_3_, f32[32,128]{1,0:T(8,128)S(1)} %collective-permute-done.20.refs_4_, ...), custom_call_target="tpu_custom_call" | custom-call | tf_op jit(solution)/shard_map/last/pallas_call | solution.py:363
  (10 shorter events, 0.1 us)
Async XLA Ops:
  1.3 14.8 %copy-start.1 = (s32[3,16384]{1,0:T(4,128)S(1)}, s32[3,16384]{1,0:T(4,128)}, u32[]{:S(2)}) copy-start(s32[3,16384]{1,0:T(4,128)} %param.20) | copy-start | bytes 589828
  1.3 14.8 %copy-start.3 = (f32[16384]{0:T(1024)S(1)}, f32[16384]{0:T(1024)}, u32[]{:S(2)}) copy-start(f32[16384]{0:T(1024)} %param.26) | copy-start | bytes 196612
  1.3 14.8 %copy-start.7 = (s32[1,1,32]{2,1,0:T(1,128)S(1)}, s32[1,1,32]{2,1,0:T(1,128)}, u32[]{:S(2)}) copy-start(s32[1,1,32]{2,1,0:T(1,128)} %refs_0_.12) | copy-start | bytes 388
  1.3 14.8 %copy-start.8 = (s32[1,1,32]{2,1,0:T(1,128)S(1)}, s32[1,1,32]{2,1,0:T(1,128)}, u32[]{:S(2)}) copy-start(s32[1,1,32]{2,1,0:T(1,128)} %refs_1_.11) | copy-start | bytes 388
  1.3 14.8 %copy-start.9 = (f32[2]{0:T(128)S(1)}, f32[2]{0:T(128)}, u32[]{:S(2)}) copy-start(f32[2]{0:T(128)} %refs_0_.13) | copy-start | bytes 28
  4.4 6.8 %collective-permute-start = (s16[240,128]{1,0:T(8,128)(2,1)S(1)}, s16[240,128]{1,0:T(8,128)(2,1)S(1)}, u32[]{:S(2)}, u32[]{:S(2)}) collective-permute-start(s16[240,128]{1,0:T(8,128)(2,1)S(1)} %get-tuple-element.44), channel_id=1, source_target_pairs={{0,8},{8,0},{16,24},{24,16},{1,9},{9,1},{17,25},{25,17},{2,10},{10... | collective-permute-start | bytes 184328 | tf_op jit(solution)/shard_map/ppermute | solution.py:378
  7.5 6.3 %collective-permute-start.1 = (s16[240,128]{1,0:T(8,128)(2,1)S(1)}, s16[240,128]{1,0:T(8,128)(2,1)S(1)}, u32[]{:S(2)}, u32[]{:S(2)}) collective-permute-start(s16[240,128]{1,0:T(8,128)(2,1)S(1)} %get-tuple-element.45), channel_id=1, source_target_pairs={{0,16},{8,24},{16,0},{24,8},{1,17},{9,25},{17,1},{25,9},{2,18},{10... | collective-permute-start | bytes 184328 | tf_op jit(solution)/shard_map/ppermute | solution.py:378
  10.1 6.0 %collective-permute-start.2 = (s16[240,128]{1,0:T(8,128)(2,1)S(1)}, s16[240,128]{1,0:T(8,128)(2,1)S(1)}, u32[]{:S(2)}, u32[]{:S(2)}) collective-permute-start(s16[240,128]{1,0:T(8,128)(2,1)S(1)} %get-tuple-element.46), channel_id=1, source_target_pairs={{0,24},{8,16},{16,8},{24,0},{1,25},{9,17},{17,9},{25,1},{2,26},{10... | collective-permute-start | bytes 184328 | tf_op jit(solution)/shard_map/ppermute | solution.py:378
  10.1 15.8 %copy-start = (s32[3,16384]{1,0:T(4,128)S(1)}, s32[3,16384]{1,0:T(4,128)}, u32[]{:S(2)}) copy-start(s32[3,16384]{1,0:T(4,128)} %param.21) | copy-start | bytes 589828
  16.1 18.7 %copy-start.2 = (f32[3,16384]{1,0:T(4,128)S(1)}, f32[3,16384]{1,0:T(4,128)}, u32[]{:S(2)}) copy-start(f32[3,16384]{1,0:T(4,128)} %param.18) | copy-start | bytes 589828
  16.1 18.7 %copy-start.4 = (f32[16384]{0:T(1024)S(1)}, f32[16384]{0:T(1024)}, u32[]{:S(2)}) copy-start(f32[16384]{0:T(1024)} %param.22) | copy-start | bytes 196612
  16.1 18.7 %copy-start.5 = (f32[16384]{0:T(1024)S(1)}, f32[16384]{0:T(1024)}, u32[]{:S(2)}) copy-start(f32[16384]{0:T(1024)} %param.24) | copy-start | bytes 196612
  17.5 1.3 %collective-permute-start.3 = (f32[128,128]{1,0:T(8,128)S(1)}, f32[128,128]{1,0:T(8,128)S(1)}, u32[]{:S(2)}, u32[]{:S(2)}) collective-permute-start(f32[128,128]{1,0:T(8,128)S(1)} %get-tuple-element.49.refs_0_), channel_id=1, source_target_pairs={{0,1},{1,0},{2,3},{3,2},{4,5},{5,4},{6,7},{7,6},{8,9},{9,8},{10,11... | collective-permute-start | bytes 196616 | tf_op jit(solution)/shard_map/ppermute | solution.py:378
  18.9 4.9 %collective-permute-start.6 = (s16[144,128]{1,0:T(8,128)(2,1)S(1)}, s16[144,128]{1,0:T(8,128)(2,1)S(1)}, u32[]{:S(2)}, u32[]{:S(2)}) collective-permute-start(s16[144,128]{1,0:T(8,128)(2,1)S(1)} %pair_2.1.refs_6_), channel_id=1, source_target_pairs={{0,6},{1,7},{2,4},{3,5},{4,2},{5,3},{6,0},{7,1},{8,14},{9,15},{10,... | collective-permute-start | bytes 110600 | tf_op jit(solution)/shard_map/ppermute | solution.py:378
  21.4 4.0 %collective-permute-start.5 = (s16[144,128]{1,0:T(8,128)(2,1)S(1)}, s16[144,128]{1,0:T(8,128)(2,1)S(1)}, u32[]{:S(2)}, u32[]{:S(2)}) collective-permute-start(s16[144,128]{1,0:T(8,128)(2,1)S(1)} %pair_2.1.refs_6_), channel_id=1, source_target_pairs={{0,4},{1,5},{2,6},{3,7},{4,0},{5,1},{6,2},{7,3},{8,12},{9,13},{10,... | collective-permute-start | bytes 110600 | tf_op jit(solution)/shard_map/ppermute | solution.py:378
  21.9 4.0 %collective-permute-start.4 = (s16[144,128]{1,0:T(8,128)(2,1)S(1)}, s16[144,128]{1,0:T(8,128)(2,1)S(1)}, u32[]{:S(2)}, u32[]{:S(2)}) collective-permute-start(s16[144,128]{1,0:T(8,128)(2,1)S(1)} %pair_2.1.refs_6_), channel_id=1, source_target_pairs={{0,2},{1,3},{2,0},{3,1},{4,6},{5,7},{6,4},{7,5},{8,10},{9,11},{10,... | collective-permute-start | bytes 110600 | tf_op jit(solution)/shard_map/ppermute | solution.py:378
  25.9 17.9 %copy-start.6 = (f32[16384]{0:T(1024)S(1)}, f32[16384]{0:T(1024)}, u32[]{:S(2)}) copy-start(f32[16384]{0:T(1024)} %param.23) | copy-start | bytes 196612
  27.3 6.2 %collective-permute-start.9 = (s16[240,128]{1,0:T(8,128)(2,1)S(1)}, s16[240,128]{1,0:T(8,128)(2,1)S(1)}, u32[]{:S(2)}, u32[]{:S(2)}) collective-permute-start(s16[240,128]{1,0:T(8,128)(2,1)S(1)} %get-tuple-element.53.refs_6_), channel_id=1, source_target_pairs={{0,24},{8,16},{16,8},{24,0},{1,25},{9,17},{17,9},{25,1},{2,26},{10... | collective-permute-start | bytes 184328 | tf_op jit(solution)/shard_map/ppermute | solution.py:378
  28.9 5.9 %collective-permute-start.8 = (s16[240,128]{1,0:T(8,128)(2,1)S(1)}, s16[240,128]{1,0:T(8,128)(2,1)S(1)}, u32[]{:S(2)}, u32[]{:S(2)}) collective-permute-start(s16[240,128]{1,0:T(8,128)(2,1)S(1)} %get-tuple-element.53.refs_6_), channel_id=1, source_target_pairs={{0,16},{8,24},{16,0},{24,8},{1,17},{9,25},{17,1},{25,9},{2,18},{10... | collective-permute-start | bytes 184328 | tf_op jit(solution)/shard_map/ppermute | solution.py:378
  28.9 5.9 %collective-permute-start.7 = (s16[240,128]{1,0:T(8,128)(2,1)S(1)}, s16[240,128]{1,0:T(8,128)(2,1)S(1)}, u32[]{:S(2)}, u32[]{:S(2)}) collective-permute-start(s16[240,128]{1,0:T(8,128)(2,1)S(1)} %get-tuple-element.53.refs_6_), channel_id=1, source_target_pairs={{0,8},{8,0},{16,24},{24,16},{1,9},{9,1},{17,25},{25,17},{2,10},{10... | collective-permute-start | bytes 184328 | tf_op jit(solution)/shard_map/ppermute | solution.py:378
  36.4 1.3 %collective-permute-start.10 = (f32[128,128]{1,0:T(8,128)S(1)}, f32[128,128]{1,0:T(8,128)S(1)}, u32[]{:S(2)}, u32[]{:S(2)}) collective-permute-start(f32[128,128]{1,0:T(8,128)S(1)} %get-tuple-element.58.refs_0_), channel_id=1, source_target_pairs={{0,1},{1,0},{2,3},{3,2},{4,5},{5,4},{6,7},{7,6},{8,9},{9,8},{10,11... | collective-permute-start | bytes 196616 | tf_op jit(solution)/shard_map/ppermute | solution.py:378
  37.8 4.9 %collective-permute-start.13 = (s16[144,128]{1,0:T(8,128)(2,1)S(1)}, s16[144,128]{1,0:T(8,128)(2,1)S(1)}, u32[]{:S(2)}, u32[]{:S(2)}) collective-permute-start(s16[144,128]{1,0:T(8,128)(2,1)S(1)} %pair_1.1.refs_6_), channel_id=1, source_target_pairs={{0,6},{1,7},{2,4},{3,5},{4,2},{5,3},{6,0},{7,1},{8,14},{9,15},{10,... | collective-permute-start | bytes 110600 | tf_op jit(solution)/shard_map/ppermute | solution.py:378
  39.3 4.0 %collective-permute-start.12 = (s16[144,128]{1,0:T(8,128)(2,1)S(1)}, s16[144,128]{1,0:T(8,128)(2,1)S(1)}, u32[]{:S(2)}, u32[]{:S(2)}) collective-permute-start(s16[144,128]{1,0:T(8,128)(2,1)S(1)} %pair_1.1.refs_6_), channel_id=1, source_target_pairs={{0,4},{1,5},{2,6},{3,7},{4,0},{5,1},{6,2},{7,3},{8,12},{9,13},{10,... | collective-permute-start | bytes 110600 | tf_op jit(solution)/shard_map/ppermute | solution.py:378
  39.8 4.0 %collective-permute-start.11 = (s16[144,128]{1,0:T(8,128)(2,1)S(1)}, s16[144,128]{1,0:T(8,128)(2,1)S(1)}, u32[]{:S(2)}, u32[]{:S(2)}) collective-permute-start(s16[144,128]{1,0:T(8,128)(2,1)S(1)} %pair_1.1.refs_6_), channel_id=1, source_target_pairs={{0,2},{1,3},{2,0},{3,1},{4,6},{5,7},{6,4},{7,5},{8,10},{9,11},{10,... | collective-permute-start | bytes 110600 | tf_op jit(solution)/shard_map/ppermute | solution.py:378
  45.2 6.2 %collective-permute-start.16 = (s16[160,128]{1,0:T(8,128)(2,1)S(1)}, s16[160,128]{1,0:T(8,128)(2,1)S(1)}, u32[]{:S(2)}, u32[]{:S(2)}) collective-permute-start(s16[160,128]{1,0:T(8,128)(2,1)S(1)} %get-tuple-element.62.refs_6_), channel_id=1, source_target_pairs={{0,24},{8,16},{16,8},{24,0},{1,25},{9,17},{17,9},{25,1},{2,26},{10... | collective-permute-start | bytes 122888 | tf_op jit(solution)/shard_map/ppermute | solution.py:378
  47.4 5.0 %collective-permute-start.15 = (s16[160,128]{1,0:T(8,128)(2,1)S(1)}, s16[160,128]{1,0:T(8,128)(2,1)S(1)}, u32[]{:S(2)}, u32[]{:S(2)}) collective-permute-start(s16[160,128]{1,0:T(8,128)(2,1)S(1)} %get-tuple-element.62.refs_6_), channel_id=1, source_target_pairs={{0,16},{8,24},{16,0},{24,8},{1,17},{9,25},{17,1},{25,9},{2,18},{10... | collective-permute-start | bytes 122888 | tf_op jit(solution)/shard_map/ppermute | solution.py:378
  47.9 4.4 %collective-permute-start.14 = (s16[160,128]{1,0:T(8,128)(2,1)S(1)}, s16[160,128]{1,0:T(8,128)(2,1)S(1)}, u32[]{:S(2)}, u32[]{:S(2)}) collective-permute-start(s16[160,128]{1,0:T(8,128)(2,1)S(1)} %get-tuple-element.62.refs_6_), channel_id=1, source_target_pairs={{0,8},{8,0},{16,24},{24,16},{1,9},{9,1},{17,25},{25,17},{2,10},{10... | collective-permute-start | bytes 122888 | tf_op jit(solution)/shard_map/ppermute | solution.py:378
  53.7 1.3 %collective-permute-start.17 = (f32[80,128]{1,0:T(8,128)S(1)}, f32[80,128]{1,0:T(8,128)S(1)}, u32[]{:S(2)}, u32[]{:S(2)}) collective-permute-start(f32[80,128]{1,0:T(8,128)S(1)} %get-tuple-element.70), channel_id=1, source_target_pairs={{0,1},{1,0},{2,3},{3,2},{4,5},{5,4},{6,7},{7,6},{8,9},{9,8},{10,11... | collective-permute-start | bytes 122888 | tf_op jit(solution)/shard_map/ppermute | solution.py:378
  55.0 4.2 %collective-permute-start.18 = (f32[32,128]{1,0:T(8,128)S(1)}, f32[32,128]{1,0:T(8,128)S(1)}, u32[]{:S(2)}, u32[]{:S(2)}) collective-permute-start(f32[32,128]{1,0:T(8,128)S(1)} %get-tuple-element.72), channel_id=1, source_target_pairs={{0,2},{1,3},{2,0},{3,1},{4,6},{5,7},{6,4},{7,5},{8,10},{9,11},{10,... | collective-permute-start | bytes 49160 | tf_op jit(solution)/shard_map/ppermute | solution.py:378
  56.6 3.7 %collective-permute-start.19 = (f32[32,128]{1,0:T(8,128)S(1)}, f32[32,128]{1,0:T(8,128)S(1)}, u32[]{:S(2)}, u32[]{:S(2)}) collective-permute-start(f32[32,128]{1,0:T(8,128)S(1)} %get-tuple-element.73), channel_id=1, source_target_pairs={{0,4},{1,5},{2,6},{3,7},{4,0},{5,1},{6,2},{7,3},{8,12},{9,13},{10,... | collective-permute-start | bytes 49160 | tf_op jit(solution)/shard_map/ppermute | solution.py:378
  58.1 4.6 %collective-permute-start.20 = (f32[32,128]{1,0:T(8,128)S(1)}, f32[32,128]{1,0:T(8,128)S(1)}, u32[]{:S(2)}, u32[]{:S(2)}) collective-permute-start(f32[32,128]{1,0:T(8,128)S(1)} %get-tuple-element.74), channel_id=1, source_target_pairs={{0,6},{1,7},{2,4},{3,5},{4,2},{5,3},{6,0},{7,1},{8,14},{9,15},{10,... | collective-permute-start | bytes 49160 | tf_op jit(solution)/shard_map/ppermute | solution.py:378

commit v9 on v8

--- a/solution.py
+++ b/solution.py
@@ -118,17 +118,22 @@
     return short(rows)
 
 
+def write_payload(out, lines):
+    units, code = encode(lines)
+    out[: lines.shape[0], :] = short(units)
+    out[lines.shape[0] :, :] = scale_rows([code])
+
+
 def scales_of(part):
     codes = long(part[part.shape[0] - SCALES :, :])
     return [from_units(codes[spot : spot + 1]) for spot in range(2)]
 
 
 def first_body(
-    step, n_row, rows_far, columns_far, count, tile_data, mask_far, cotangent_far, saved_far,
+    step, rows_far, columns_far, count, tile_data, mask_far, cotangent_far, saved_far,
     tiles, term, anchor, *refs
 ):
-    outs = refs[:n_row]
-    source, total, rows, columns, mask, cotangent, saved, arrived, ready = refs[n_row:]
+    out, saved_out, source, total, rows, columns, mask, cotangent, saved, arrived, ready = refs
     slots = tiles.shape[0]
     chunk = slots // CHUNKS
     pairs = [(mask_far, mask), (cotangent_far, cotangent), (saved_far, saved)]
@@ -163,16 +168,8 @@
         span = range(part * chunk, (part + 1) * chunk)
         add_products(rows, columns, count, tiles, span, source, total)
     lines = total.shape[1]
-    share = lines // n_row
-    me = lax.axis_index("row")
-    units, code = encode(total[0])
-    units = short(units)
-    for part, out in enumerate(outs):
-        at = pl.ds(pl.multiple_of((me ^ part) * share, share), share)
-        out[:lines, :] = units
-        saved_units, saved_code = encode(total[1:, at, :].reshape(iterations * share, LANES))
-        out[lines : lines + iterations * share, :] = short(saved_units)
-        out[lines + iterations * share :, :] = scale_rows([code, saved_code])
+    write_payload(out, total[0])
+    saved_out[...] = total[1:].reshape(iterations * lines, LANES)
 
 
 def turn_body(tiles, turned, _):
@@ -185,7 +182,7 @@
     if last:
         demand, images, terms, term, anchor_out, out, _, source, total = refs
     else:
-        saved, term, anchor_out, out, _, source, total = refs
+        term, anchor_out, out, _, source, total = refs
     weight = weight_of(step)
     rows_y = before.shape[0]
     image = tree_sum([long(part[:rows_y, :]) * scales_of(part)[0] for part in parts])
@@ -207,23 +204,16 @@
         coarse, fine, found_code = encode_fine(fold(found))
         out[lines : lines + EXTRA, :] = short(jnp.concatenate([coarse, fine], axis=0))
         out[lines + EXTRA :, :] = scale_rows([code, found_code])
-    elif saved is None:
+    else:
         out[lines:, :] = scale_rows([code])
-    else:
-        size = saved.shape[0]
-        saved_units, saved_code = encode(saved[...])
-        out[lines : lines + size, :] = short(saved_units)
-        out[lines + size :, :] = scale_rows([code, saved_code])
 
 
 def primal_body(kind, step, n_row, n_col, rows, columns, count, sizes, tiles, mask, parts, before, anchor, *refs):
     last = kind == "last"
     if last:
         reduced, terms, final, mine, other, _, source, out = refs
-    elif kind == "sums":
-        term, adjoint_out, anchor_out, out, saved, _, source = refs
-    elif kind == "shares":
-        cost, upper, primal, term, adjoint_out, anchor_out, out, reduced, images, _, source, total = refs
+    elif kind == "saved":
+        gathered, cost, upper, primal, term, adjoint_out, anchor_out, out, reduced, images, _, source, total = refs
     else:
         term, adjoint_out, anchor_out, out, _, source = refs
     sigma = sizes[1]
@@ -244,15 +234,13 @@
         adjoint_out[...] = after
         anchor_out[...] = anchored
     all_slots = range(tiles.shape[0])
-    if kind == "shares":
+    if kind == "saved":
         iterations = reduced.shape[0]
-        share = lines // n_row
-        size = iterations * share
-        me = lax.axis_index("row")
-        for part, (held, scale) in enumerate(zip(parts, scales)):
-            at = pl.ds(pl.multiple_of((me ^ part) * share, share), share)
-            sums = (long(held[lines : lines + size, :]) * scale[1]).reshape(iterations, share, LANES)
-            reduced[:, at, :] = cost[at, :][None] - sums
+        size = iterations * lines
+        for vector in range(iterations):
+            at = slice(vector * lines, (vector + 1) * lines)
+            sums = [gathered[part, at, :] for part in range(n_row)]
+            reduced[vector] = cost[...] - tree_sum(sums)
         source[0] = rounded(value)
         for vector in range(iterations):
             saved = primal[:, vector, :]
@@ -266,11 +254,6 @@
     source[...] = rounded(value)
     out[...] = jnp.zeros_like(out)
     add_products(columns, rows, count, tiles, all_slots, source, out)
-    if kind == "sums":
-        size = saved.shape[0]
-        saved[...] = tree_sum(
-            [long(part[lines : lines + size, :]) * scale[1] for part, scale in zip(parts, scales)]
-        )
     if last:
         sums = 0.0
         for part, scale in zip(parts, scales):
@@ -405,8 +388,7 @@
     n_row, n_col = lax.axis_size("row"), lax.axis_size("col")
     n_chip = n_col // 2
     lines_y, lines_x = row_length // LANES, column_length // LANES
-    share_y, share_x = lines_y // n_col, lines_x // n_row
-    saved_lines = iterations * share_x
+    share_y = lines_y // n_col
     last = iterations - 1
     cost = pl.CostEstimate(
         flops=2 * tile_data.size, bytes_accessed=2 * tile_data.size, transcendentals=0
@@ -430,10 +412,10 @@
     full_x, full_y = f32(lines_x, LANES), f32(lines_y, LANES)
     where = [(SMEM, tile_row_block), (SMEM, tile_column_block), (SMEM, tile_count)]
     saved = lines(saved_dual)
-    tiles, term_y, anchor_y, *parts = run(
-        functools.partial(first_body, last, n_row),
+    tiles, term_y, anchor_y, part, saved_part = run(
+        functools.partial(first_body, last),
         [pltpu.VMEM((slots, width, width), jnp.bfloat16), full_y, full_y]
-        + [row_part(saved_lines)] * n_row,
+        + [row_part(0), scratch(iterations * lines_x, LANES)],
         [(ANY, far(tile_row_block)), (ANY, far(tile_column_block)), (SMEM, tile_count)]
         + [(ANY, far(tile_data)), (ANY, far(mask_y)), (ANY, far(lines(dual_cotangent)))]
         + [(ANY, far(saved))],
@@ -462,10 +444,12 @@
     )
     adjoint_x, anchor_x = lines(primal_cotangent), None
     terms_x, terms_y = [], [term_y]
-    reduced = images = saved_sums = None
+    parts = [part] * n_row
+    gathered = lax.all_gather(saved_part, "row")
+    reduced = images = None
     for step in reversed(range(iterations)):
         parts = exchange(parts, "row")
-        kind = {0: "last", last: "sums", last - 1: "shares"}.get(step, "plain")
+        kind = {0: "last", last - 1: "saved"}.get(step, "plain")
         groups = where + [(SMEM, step_sizes), (VMEM, turned), (VMEM, mask_x), (VMEM, parts)]
         groups += [(VMEM, adjoint_x), (VMEM, anchor_x)]
         body = functools.partial(primal_body, kind, step, n_row, n_col)
@@ -473,11 +457,9 @@
             break
         outs = [full_x, full_x, full_x, full_y]
         extra = [scratch(lines_x, LANES)]
-        if kind == "sums":
-            outs.append(f32(saved_lines, LANES))
-        if kind == "shares":
+        if kind == "saved":
             outs += [f32(iterations, lines_x, LANES), f32(iterations, lines_y, LANES)]
-            groups += [(VMEM, lines(cost_vector)), (VMEM, lines(upper_bound))]
+            groups += [(VMEM, gathered), (VMEM, lines(cost_vector)), (VMEM, lines(upper_bound))]
             groups += [(VMEM, lines(saved_primal))]
             extra = [
                 scratch(iterations + 1, lines_x, LANES),
@@ -486,11 +468,8 @@
         term_x, adjoint_x, anchor_x, partial, *more, turned = run(
             body, outs, groups, extra, f"primal_{step}", cost, turned
         )
-        if kind == "sums":
-            (saved_sums,) = more
-        elif kind == "shares":
+        if kind == "saved":
             reduced, images = more
-            saved_sums = None
         terms_x.insert(0, term_x)
         part = run(
             pair_body,
@@ -506,8 +485,7 @@
             groups += [(VMEM, lines(demand)), (VMEM, images), (VMEM, list(terms_y))]
             out = row_part(EXTRA)
         else:
-            groups += [(VMEM, saved_sums)]
-            out = row_part(saved_lines if saved_sums is not None else 0)
+            out = row_part(0)
         term_y, anchor_y, part, tiles = run(
             functools.partial(dual_body, step - 1, n_col),
             [full_y, full_y, out],

time: 64.1 us -> 76.8 us (1.20)
  blocking collectives: 0 us -> 17.7 us
  waiting for transfers between devices: 23.7 us -> 18.7 us
    all_gather x0 -> x1, blocking collectives: none -> 17.7 us  [local(): gathered = lax.all_gather(saved_part, 'row')]
    ppermute x21, waiting for transfers between devices: 23.7 us -> 18.7 us  [swap(): return lax.ppermute(array, axis, [(i, i ^ stride) for i in range(size)])]
  transfers between devices with their start and end apart: 21 -> 21, of which waited for: 17 -> 15; matrix products, arithmetic and copies ran while one was open for 1% -> 1% of each run, Pallas kernels for 2% -> 1%
where the time goes in v9:
time: 76.8 us; the launch traced here: 76.6 us
  starting transfers between devices  25.5 us (33%)
  waiting for transfers between devices  18.7 us (24%)
  blocking collectives  17.7 us (23%)
  Pallas kernels  12.6 us (16%)
  between operations  1.52 us (2%)
    ppermute x21, starting transfers between devices, swap(): return lax.ppermute(array, axis, [(i, i ^ stride) for i in range(size)])  25.5 us
    ppermute x21, waiting for transfers between devices, swap(): return lax.ppermute(array, axis, [(i, i ^ stride) for i in range(size)])  18.7 us
    all_gather x1, blocking collectives, local(): gathered = lax.all_gather(saved_part, 'row')  17.7 us
    pallas_call x11, Pallas kernels, run(): pl.pallas_call(kernel, out_shape=shapes, in_specs=specs, out_specs=out_sp...  12.6 us
  transfers between devices with their start and end apart: 21, of which 15 were waited for; matrix products, arithmetic and copies ran while one was open for 1% of the time, Pallas kernels for 1%

profile of v9, /device:TPU:0, one launch (start us, length us, event | category | flops | bytes accessed | tf_op | source)
XLA Modules:
  0.0 76.6 jit_solution(15811343509756959178)
XLA Ops:
  1.3 0.0 copy-start.1
  1.3 0.0 copy-start.3
  1.3 0.0 copy-start.7
  1.3 0.0 copy-start.8
  1.3 0.0 copy-start.9
  1.3 3.0 %first.1 = (bf16[32,256,256]{2,1,0:T(8,128)(2,1)S(1)}, f32[128,128]{1,0:T(8,128)S(1)}, f32[128,128]{1,0:T(8,128)S(1)}, s16[144,128]{1,0:T(8,128)(2,1)S(1)}, f32[384,128]{1,0:T(8,128)S(1)}) custom-call(s32[1,1,32]{2,1,0:T(1,128)} %refs_0_.12, s32[1,1,32]{2,1,0:T(1,128)} %refs_1_.11, s32[1,1]{1,0:T(1,128)S(6)} %copy.30.refs_2_, ...), custom_call_target="tpu_custom_call" | custom-call | flops 4194304 | bytes 4194304 | tf_op jit(solution)/shard_map/first/pallas_call | solution.py:346
  4.3 5.1 %collective-permute-start.2 = (s16[144,128]{1,0:T(8,128)(2,1)S(1)}, s16[144,128]{1,0:T(8,128)(2,1)S(1)}, u32[]{:S(2)}, u32[]{:S(2)}) collective-permute-start(s16[144,128]{1,0:T(8,128)(2,1)S(1)} %get-tuple-element.40.refs_6_), channel_id=1, source_target_pairs={{0,24},{8,16},{16,8},{24,0},{1,25},{9,17},{17,9},{25,1},{2,26},{10... | collective-permute-start | bytes 110600 | tf_op jit(solution)/shard_map/ppermute | solution.py:361
  9.5 0.0 collective-permute-start.1
  9.5 0.6 collective-permute-start
  10.1 1.1 %turn.1 = (bf16[32,256,256]{2,1,0:T(8,128)(2,1)S(1)}, bf16[32,256,256]{2,1,0:T(8,128)(2,1)S(1)}) custom-call(bf16[32,256,256]{2,1,0:T(8,128)(2,1)S(1)} %get-tuple-element.38.refs_0_), custom_call_target="tpu_custom_call", output_to_operand_aliasing={{1}: (0, {})} | custom-call | flops 4194304 | bytes 4194304 | tf_op jit(solution)/shard_map/turn/pallas_call | solution.py:346
  11.2 0.2 collective-permute-done.2.refs_9_
  11.4 2.9 %collective-permute-done.1.refs_8_ = s16[144,128]{1,0:T(8,128)(2,1)S(1)} collective-permute-done((s16[144,128]{1,0:T(8,128)(2,1)S(1)}, s16[144,128]{1,0:T(8,128)(2,1)S(1)}, u32[]{:S(2)}, u32[]{:S(2)}) %collective-permute-start.1) | collective-permute-done | bytes 36896 | tf_op jit(solution)/shard_map/ppermute | solution.py:361
  14.3 0.0 collective-permute-done.refs_7_
  14.4 0.0 copy-start.2
  14.4 0.0 copy-start.4
  14.4 0.0 copy-start.5
  14.4 1.3 %primal_2.1 = (f32[128,128]{1,0:T(8,128)S(1)}, f32[128,128]{1,0:T(8,128)S(1)}, f32[128,128]{1,0:T(8,128)S(1)}, f32[128,128]{1,0:T(8,128)S(1)}, bf16[32,256,256]{2,1,0:T(8,128)(2,1)S(1)}) custom-call(s32[1,1,32]{2,1,0:T(1,128)S(1)} %copy-done.7, s32[1,1,32]{2,1,0:T(1,128)S(1)} %copy-done.8, ...), custom_call_target="tpu_custom_call", output_to_operand_aliasing={{4}: (4, {})} | custom-call | flops 4194304 | bytes 4194304 | tf_op jit(solution)/shard_map/primal_2/pallas_call | solution.py:346
  15.7 0.1 collective-permute-start.3
  15.8 1.2 %collective-permute-done.3.refs_1_ = f32[128,128]{1,0:T(8,128)S(1)} collective-permute-done((f32[128,128]{1,0:T(8,128)S(1)}, f32[128,128]{1,0:T(8,128)S(1)}, u32[]{:S(2)}, u32[]{:S(2)}) %collective-permute-start.3) | collective-permute-done | bytes 65568 | tf_op jit(solution)/shard_map/ppermute | solution.py:361
  17.1 2.5 %collective-permute-start.6 = (s16[144,128]{1,0:T(8,128)(2,1)S(1)}, s16[144,128]{1,0:T(8,128)(2,1)S(1)}, u32[]{:S(2)}, u32[]{:S(2)}) collective-permute-start(s16[144,128]{1,0:T(8,128)(2,1)S(1)} %pair_2.1.refs_6_), channel_id=1, source_target_pairs={{0,6},{1,7},{2,4},{3,5},{4,2},{5,3},{6,0},{7,1},{8,14},{9,15},{10,... | collective-permute-start | bytes 110600 | tf_op jit(solution)/shard_map/ppermute | solution.py:361
  19.6 0.5 collective-permute-start.5
  20.1 0.5 collective-permute-start.4
  20.6 1.4 %collective-permute-done.6.refs_9_ = s16[144,128]{1,0:T(8,128)(2,1)S(1)} collective-permute-done((s16[144,128]{1,0:T(8,128)(2,1)S(1)}, s16[144,128]{1,0:T(8,128)(2,1)S(1)}, u32[]{:S(2)}, u32[]{:S(2)}) %collective-permute-start.6) | collective-permute-done | bytes 36896 | tf_op jit(solution)/shard_map/ppermute | solution.py:361
  22.0 1.6 %collective-permute-done.5.refs_8_ = s16[144,128]{1,0:T(8,128)(2,1)S(1)} collective-permute-done((s16[144,128]{1,0:T(8,128)(2,1)S(1)}, s16[144,128]{1,0:T(8,128)(2,1)S(1)}, u32[]{:S(2)}, u32[]{:S(2)}) %collective-permute-start.5) | collective-permute-done | bytes 36896 | tf_op jit(solution)/shard_map/ppermute | solution.py:361
  23.6 0.5 collective-permute-done.4.refs_7_
  24.1 1.4 %dual_1.1 = (f32[128,128]{1,0:T(8,128)S(1)}, f32[128,128]{1,0:T(8,128)S(1)}, s16[144,128]{1,0:T(8,128)(2,1)S(1)}, bf16[32,256,256]{2,1,0:T(8,128)(2,1)S(1)}) custom-call(s32[1,1,32]{2,1,0:T(1,128)S(1)} %copy-done.7, s32[1,1,32]{2,1,0:T(1,128)S(1)} %copy-done.8, s32[1,1]{1,0:T(1,128)S(6)} %copy.30.refs_2_, ...), custom_call_target="tpu_custom_call", output_to_operand_aliasing={{3}: (4, {})} | custom-call | flops 4194304 | bytes 4194304 | tf_op jit(solution)/shard_map/dual_1/pallas_call | solution.py:346
  25.5 0.0 copy-start.6
  25.5 1.5 %collective-permute-start.9 = (s16[144,128]{1,0:T(8,128)(2,1)S(1)}, s16[144,128]{1,0:T(8,128)(2,1)S(1)}, u32[]{:S(2)}, u32[]{:S(2)}) collective-permute-start(s16[144,128]{1,0:T(8,128)(2,1)S(1)} %get-tuple-element.46.refs_6_), channel_id=1, source_target_pairs={{0,24},{8,16},{16,8},{24,0},{1,25},{9,17},{17,9},{25,1},{2,26},{10... | collective-permute-start | bytes 110600 | tf_op jit(solution)/shard_map/ppermute | solution.py:361
  27.0 0.6 collective-permute-start.8
  27.7 2.3 %collective-permute-start.7 = (s16[144,128]{1,0:T(8,128)(2,1)S(1)}, s16[144,128]{1,0:T(8,128)(2,1)S(1)}, u32[]{:S(2)}, u32[]{:S(2)}) collective-permute-start(s16[144,128]{1,0:T(8,128)(2,1)S(1)} %get-tuple-element.46.refs_6_), channel_id=1, source_target_pairs={{0,8},{8,0},{16,24},{24,16},{1,9},{9,1},{17,25},{25,17},{2,10},{10... | collective-permute-start | bytes 110600 | tf_op jit(solution)/shard_map/ppermute | solution.py:361
  30.0 17.7 %all-gather = f32[1536,128]{1,0:T(8,128)S(1)} all-gather(f32[384,128]{1,0:T(8,128)S(1)} %get-tuple-element.49), channel_id=2, replica_groups=mesh['row'=4,'col'=8] {'row'}, dimensions={0}, use_global_device_ids=true | all-gather | bytes 983040 | tf_op jit(solution)/shard_map/all_gather | solution.py:448
  47.6 0.0 collective-permute-done.9.refs_9_
  47.6 0.0 collective-permute-done.8.refs_8_
  47.6 0.0 collective-permute-done.7.refs_7_
  47.7 0.0 copy-done.2
  47.7 0.0 copy-done.4
  47.7 0.0 copy-done.5
  47.7 1.6 %primal_1.1 = (f32[128,128]{1,0:T(8,128)S(1)}, f32[128,128]{1,0:T(8,128)S(1)}, f32[128,128]{1,0:T(8,128)S(1)}, f32[128,128]{1,0:T(8,128)S(1)}, f32[3,128,128]{2,...) custom-call(s32[1,1,32]{2,1,0:T(1,128)S(1)} %copy-done.7, ...), custom_call_target="tpu_custom_call", output_to_operand_aliasing={{6}: (4, {})} | custom-call | flops 4194304 | bytes 4194304 | tf_op jit(solution)/shard_map/primal_1/pallas_call | solution.py:346
  49.3 0.1 collective-permute-start.10
  49.4 1.2 %collective-permute-done.10.refs_1_ = f32[128,128]{1,0:T(8,128)S(1)} collective-permute-done((f32[128,128]{1,0:T(8,128)S(1)}, f32[128,128]{1,0:T(8,128)S(1)}, u32[]{:S(2)}, u32[]{:S(2)}) %collective-permute-start.10) | collective-permute-done | bytes 65568 | tf_op jit(solution)/shard_map/ppermute | solution.py:361
  50.7 1.6 %collective-permute-start.13 = (s16[144,128]{1,0:T(8,128)(2,1)S(1)}, s16[144,128]{1,0:T(8,128)(2,1)S(1)}, u32[]{:S(2)}, u32[]{:S(2)}) collective-permute-start(s16[144,128]{1,0:T(8,128)(2,1)S(1)} %pair_1.1.refs_6_), channel_id=1, source_target_pairs={{0,6},{1,7},{2,4},{3,5},{4,2},{5,3},{6,0},{7,1},{8,14},{9,15},{10,... | collective-permute-start | bytes 110600 | tf_op jit(solution)/shard_map/ppermute | solution.py:361
  52.3 0.5 collective-permute-start.12
  52.8 1.5 %collective-permute-start.11 = (s16[144,128]{1,0:T(8,128)(2,1)S(1)}, s16[144,128]{1,0:T(8,128)(2,1)S(1)}, u32[]{:S(2)}, u32[]{:S(2)}) collective-permute-start(s16[144,128]{1,0:T(8,128)(2,1)S(1)} %pair_1.1.refs_6_), channel_id=1, source_target_pairs={{0,2},{1,3},{2,0},{3,1},{4,6},{5,7},{6,4},{7,5},{8,10},{9,11},{10,... | collective-permute-start | bytes 110600 | tf_op jit(solution)/shard_map/ppermute | solution.py:361
  54.2 1.4 %collective-permute-done.13.refs_9_ = s16[144,128]{1,0:T(8,128)(2,1)S(1)} collective-permute-done((s16[144,128]{1,0:T(8,128)(2,1)S(1)}, s16[144,128]{1,0:T(8,128)(2,1)S(1)}, u32[]{:S(2)}, u32[]{:S(2)}) %collective-permute-start.13) | collective-permute-done | bytes 36896 | tf_op jit(solution)/shard_map/ppermute | solution.py:361
  55.6 0.6 collective-permute-done.12.refs_8_
  56.2 0.5 collective-permute-done.11.refs_7_
  56.7 1.4 %dual_0.1 = (f32[128,128]{1,0:T(8,128)S(1)}, f32[128,128]{1,0:T(8,128)S(1)}, s16[160,128]{1,0:T(8,128)(2,1)S(1)}, bf16[32,256,256]{2,1,0:T(8,128)(2,1)S(1)}) custom-call(s32[1,1,32]{2,1,0:T(1,128)S(1)} %copy-done.7, s32[1,1,32]{2,1,0:T(1,128)S(1)} %copy-done.8, s32[1,1]{1,0:T(1,128)S(6)} %copy.30.refs_2_, ...), custom_call_target="tpu_custom_call", output_to_operand_aliasing={{3}: (4, {})} | custom-call | flops 4194304 | bytes 4194304 | tf_op jit(solution)/shard_map/dual_0/pallas_call | solution.py:346
  58.2 1.9 %collective-permute-start.16 = (s16[160,128]{1,0:T(8,128)(2,1)S(1)}, s16[160,128]{1,0:T(8,128)(2,1)S(1)}, u32[]{:S(2)}, u32[]{:S(2)}) collective-permute-start(s16[160,128]{1,0:T(8,128)(2,1)S(1)} %get-tuple-element.56.refs_6_), channel_id=1, source_target_pairs={{0,24},{8,16},{16,8},{24,0},{1,25},{9,17},{17,9},{25,1},{2,26},{10... | collective-permute-start | bytes 122888 | tf_op jit(solution)/shard_map/ppermute | solution.py:361
  60.0 0.0 collective-permute-start.15
  60.0 2.6 %collective-permute-start.14 = (s16[160,128]{1,0:T(8,128)(2,1)S(1)}, s16[160,128]{1,0:T(8,128)(2,1)S(1)}, u32[]{:S(2)}, u32[]{:S(2)}) collective-permute-start(s16[160,128]{1,0:T(8,128)(2,1)S(1)} %get-tuple-element.56.refs_6_), channel_id=1, source_target_pairs={{0,8},{8,0},{16,24},{24,16},{1,9},{9,1},{17,25},{25,17},{2,10},{10... | collective-permute-start | bytes 122888 | tf_op jit(solution)/shard_map/ppermute | solution.py:361
  62.6 1.5 %collective-permute-done.16.refs_9_ = s16[160,128]{1,0:T(8,128)(2,1)S(1)} collective-permute-done((s16[160,128]{1,0:T(8,128)(2,1)S(1)}, s16[160,128]{1,0:T(8,128)(2,1)S(1)}, u32[]{:S(2)}, u32[]{:S(2)}) %collective-permute-start.16) | collective-permute-done | bytes 40992 | tf_op jit(solution)/shard_map/ppermute | solution.py:361
  64.1 0.9 %collective-permute-done.15.refs_8_ = s16[160,128]{1,0:T(8,128)(2,1)S(1)} collective-permute-done((s16[160,128]{1,0:T(8,128)(2,1)S(1)}, s16[160,128]{1,0:T(8,128)(2,1)S(1)}, u32[]{:S(2)}, u32[]{:S(2)}) %collective-permute-start.15) | collective-permute-done | bytes 40992 | tf_op jit(solution)/shard_map/ppermute | solution.py:361
  65.0 0.0 collective-permute-done.14.refs_7_
  65.0 1.4 %primal_0.1 = (f32[128,128]{1,0:T(8,128)S(1)}, f32[80,128]{1,0:T(8,128)S(1)}, f32[80,128]{1,0:T(8,128)S(1)}, bf16[32,256,256]{2,1,0:T(8,128)(2,1)S(1)}) custom-call(s32[1,1,32]{2,1,0:T(1,128)S(1)} %copy-done.7, s32[1,1,32]{2,1,0:T(1,128)S(1)} %copy-done.8, s32[1,1]{1,0:T(1,128)S(6)} %copy.30.refs_2_, ...), custom_call_target="tpu_custom_call", output_to_operand_aliasing={{3}: (4, {})} | custom-call | flops 4194304 | bytes 4194304 | tf_op jit(solution)/shard_map/primal_0/pallas_call | solution.py:346
  66.4 0.1 collective-permute-start.17
  66.5 1.2 %collective-permute-done.17.refs_1_ = f32[80,128]{1,0:T(8,128)S(1)} collective-permute-done((f32[80,128]{1,0:T(8,128)S(1)}, f32[80,128]{1,0:T(8,128)S(1)}, u32[]{:S(2)}, u32[]{:S(2)}) %collective-permute-start.17) | collective-permute-done | bytes 40992 | tf_op jit(solution)/shard_map/ppermute | solution.py:361
  67.7 1.5 %collective-permute-start.18 = (f32[32,128]{1,0:T(8,128)S(1)}, f32[32,128]{1,0:T(8,128)S(1)}, u32[]{:S(2)}, u32[]{:S(2)}) collective-permute-start(f32[32,128]{1,0:T(8,128)S(1)} %get-tuple-element.66), channel_id=1, source_target_pairs={{0,2},{1,3},{2,0},{3,1},{4,6},{5,7},{6,4},{7,5},{8,10},{9,11},{10,... | collective-permute-start | bytes 49160 | tf_op jit(solution)/shard_map/ppermute | solution.py:361
  69.2 1.6 %collective-permute-start.19 = (f32[32,128]{1,0:T(8,128)S(1)}, f32[32,128]{1,0:T(8,128)S(1)}, u32[]{:S(2)}, u32[]{:S(2)}) collective-permute-start(f32[32,128]{1,0:T(8,128)S(1)} %get-tuple-element.67), channel_id=1, source_target_pairs={{0,4},{1,5},{2,6},{3,7},{4,0},{5,1},{6,2},{7,3},{8,12},{9,13},{10,... | collective-permute-start | bytes 49160 | tf_op jit(solution)/shard_map/ppermute | solution.py:361
  70.8 0.4 collective-permute-start.20
  71.2 0.6 copy.29
  71.9 0.0 collective-permute-done.18.refs_2_
  71.9 1.1 %collective-permute-done.19.refs_3_ = f32[32,128]{1,0:T(8,128)S(1)} collective-permute-done((f32[32,128]{1,0:T(8,128)S(1)}, f32[32,128]{1,0:T(8,128)S(1)}, u32[]{:S(2)}, u32[]{:S(2)}) %collective-permute-start.19) | collective-permute-done | bytes 16416 | tf_op jit(solution)/shard_map/ppermute | solution.py:361
  73.0 2.5 %collective-permute-done.20.refs_4_ = f32[32,128]{1,0:T(8,128)S(1)} collective-permute-done((f32[32,128]{1,0:T(8,128)S(1)}, f32[32,128]{1,0:T(8,128)S(1)}, u32[]{:S(2)}, u32[]{:S(2)}) %collective-permute-start.20) | collective-permute-done | bytes 16416 | tf_op jit(solution)/shard_map/ppermute | solution.py:361
  75.4 1.2 %last.1 = (f32[16,128]{1,0:T(8,128)}, f32[2]{0:T(128)}) custom-call(f32[2]{0:T(128)S(1)} %copy-done.9, f32[32,128]{1,0:T(8,128)S(1)} %get-tuple-element.65.refs_1_, f32[32,128]{1,0:T(8,128)S(1)} %collective-permute-done.18.refs_2_, f32[32,128]{1,0:T(8,128)S(1)} %collective-permute-done.19.refs_3_, f32[32,128]{1,0:T(8,128)S(1)} %collective-permute-done.20.refs_4_, ...), custom_call_target="tpu_custom_call" | custom-call | tf_op jit(solution)/shard_map/last/pallas_call | solution.py:346
  (11 shorter events, 0.1 us)
Async XLA Ops:
  1.3 13.0 %copy-start.1 = (s32[3,16384]{1,0:T(4,128)S(1)}, s32[3,16384]{1,0:T(4,128)}, u32[]{:S(2)}) copy-start(s32[3,16384]{1,0:T(4,128)} %param.20) | copy-start | bytes 589828
  1.3 13.0 %copy-start.3 = (f32[16384]{0:T(1024)S(1)}, f32[16384]{0:T(1024)}, u32[]{:S(2)}) copy-start(f32[16384]{0:T(1024)} %param.26) | copy-start | bytes 196612
  1.3 13.0 %copy-start.7 = (s32[1,1,32]{2,1,0:T(1,128)S(1)}, s32[1,1,32]{2,1,0:T(1,128)}, u32[]{:S(2)}) copy-start(s32[1,1,32]{2,1,0:T(1,128)} %refs_0_.12) | copy-start | bytes 388
  1.3 13.0 %copy-start.8 = (s32[1,1,32]{2,1,0:T(1,128)S(1)}, s32[1,1,32]{2,1,0:T(1,128)}, u32[]{:S(2)}) copy-start(s32[1,1,32]{2,1,0:T(1,128)} %refs_1_.11) | copy-start | bytes 388
  1.3 13.0 %copy-start.9 = (f32[2]{0:T(128)S(1)}, f32[2]{0:T(128)}, u32[]{:S(2)}) copy-start(f32[2]{0:T(128)} %refs_0_.13) | copy-start | bytes 28
  4.3 7.1 %collective-permute-start.2 = (s16[144,128]{1,0:T(8,128)(2,1)S(1)}, s16[144,128]{1,0:T(8,128)(2,1)S(1)}, u32[]{:S(2)}, u32[]{:S(2)}) collective-permute-start(s16[144,128]{1,0:T(8,128)(2,1)S(1)} %get-tuple-element.40.refs_6_), channel_id=1, source_target_pairs={{0,24},{8,16},{16,8},{24,0},{1,25},{9,17},{17,9},{25,1},{2,26},{10... | collective-permute-start | bytes 110600 | tf_op jit(solution)/shard_map/ppermute | solution.py:361
  9.5 4.9 %collective-permute-start.1 = (s16[144,128]{1,0:T(8,128)(2,1)S(1)}, s16[144,128]{1,0:T(8,128)(2,1)S(1)}, u32[]{:S(2)}, u32[]{:S(2)}) collective-permute-start(s16[144,128]{1,0:T(8,128)(2,1)S(1)} %get-tuple-element.40.refs_6_), channel_id=1, source_target_pairs={{0,16},{8,24},{16,0},{24,8},{1,17},{9,25},{17,1},{25,9},{2,18},{10... | collective-permute-start | bytes 110600 | tf_op jit(solution)/shard_map/ppermute | solution.py:361
  9.5 4.9 %collective-permute-start = (s16[144,128]{1,0:T(8,128)(2,1)S(1)}, s16[144,128]{1,0:T(8,128)(2,1)S(1)}, u32[]{:S(2)}, u32[]{:S(2)}) collective-permute-start(s16[144,128]{1,0:T(8,128)(2,1)S(1)} %get-tuple-element.40.refs_6_), channel_id=1, source_target_pairs={{0,8},{8,0},{16,24},{24,16},{1,9},{9,1},{17,25},{25,17},{2,10},{10... | collective-permute-start | bytes 110600 | tf_op jit(solution)/shard_map/ppermute | solution.py:361
  10.1 14.0 %copy-start = (s32[3,16384]{1,0:T(4,128)S(1)}, s32[3,16384]{1,0:T(4,128)}, u32[]{:S(2)}) copy-start(s32[3,16384]{1,0:T(4,128)} %param.21) | copy-start | bytes 589828
  14.4 33.3 %copy-start.2 = (f32[3,16384]{1,0:T(4,128)S(1)}, f32[3,16384]{1,0:T(4,128)}, u32[]{:S(2)}) copy-start(f32[3,16384]{1,0:T(4,128)} %param.18) | copy-start | bytes 589828
  14.4 33.3 %copy-start.4 = (f32[16384]{0:T(1024)S(1)}, f32[16384]{0:T(1024)}, u32[]{:S(2)}) copy-start(f32[16384]{0:T(1024)} %param.22) | copy-start | bytes 196612
  14.4 33.3 %copy-start.5 = (f32[16384]{0:T(1024)S(1)}, f32[16384]{0:T(1024)}, u32[]{:S(2)}) copy-start(f32[16384]{0:T(1024)} %param.24) | copy-start | bytes 196612
  15.7 1.3 %collective-permute-start.3 = (f32[128,128]{1,0:T(8,128)S(1)}, f32[128,128]{1,0:T(8,128)S(1)}, u32[]{:S(2)}, u32[]{:S(2)}) collective-permute-start(f32[128,128]{1,0:T(8,128)S(1)} %get-tuple-element.43.refs_0_), channel_id=1, source_target_pairs={{0,1},{1,0},{2,3},{3,2},{4,5},{5,4},{6,7},{7,6},{8,9},{9,8},{10,11... | collective-permute-start | bytes 196616 | tf_op jit(solution)/shard_map/ppermute | solution.py:361
  17.1 4.9 %collective-permute-start.6 = (s16[144,128]{1,0:T(8,128)(2,1)S(1)}, s16[144,128]{1,0:T(8,128)(2,1)S(1)}, u32[]{:S(2)}, u32[]{:S(2)}) collective-permute-start(s16[144,128]{1,0:T(8,128)(2,1)S(1)} %pair_2.1.refs_6_), channel_id=1, source_target_pairs={{0,6},{1,7},{2,4},{3,5},{4,2},{5,3},{6,0},{7,1},{8,14},{9,15},{10,... | collective-permute-start | bytes 110600 | tf_op jit(solution)/shard_map/ppermute | solution.py:361
  19.6 4.0 %collective-permute-start.5 = (s16[144,128]{1,0:T(8,128)(2,1)S(1)}, s16[144,128]{1,0:T(8,128)(2,1)S(1)}, u32[]{:S(2)}, u32[]{:S(2)}) collective-permute-start(s16[144,128]{1,0:T(8,128)(2,1)S(1)} %pair_2.1.refs_6_), channel_id=1, source_target_pairs={{0,4},{1,5},{2,6},{3,7},{4,0},{5,1},{6,2},{7,3},{8,12},{9,13},{10,... | collective-permute-start | bytes 110600 | tf_op jit(solution)/shard_map/ppermute | solution.py:361
  20.1 4.0 %collective-permute-start.4 = (s16[144,128]{1,0:T(8,128)(2,1)S(1)}, s16[144,128]{1,0:T(8,128)(2,1)S(1)}, u32[]{:S(2)}, u32[]{:S(2)}) collective-permute-start(s16[144,128]{1,0:T(8,128)(2,1)S(1)} %pair_2.1.refs_6_), channel_id=1, source_target_pairs={{0,2},{1,3},{2,0},{3,1},{4,6},{5,7},{6,4},{7,5},{8,10},{9,11},{10,... | collective-permute-start | bytes 110600 | tf_op jit(solution)/shard_map/ppermute | solution.py:361
  25.5 31.2 %copy-start.6 = (f32[16384]{0:T(1024)S(1)}, f32[16384]{0:T(1024)}, u32[]{:S(2)}) copy-start(f32[16384]{0:T(1024)} %param.23) | copy-start | bytes 196612
  25.5 22.1 %collective-permute-start.9 = (s16[144,128]{1,0:T(8,128)(2,1)S(1)}, s16[144,128]{1,0:T(8,128)(2,1)S(1)}, u32[]{:S(2)}, u32[]{:S(2)}) collective-permute-start(s16[144,128]{1,0:T(8,128)(2,1)S(1)} %get-tuple-element.46.refs_6_), channel_id=1, source_target_pairs={{0,24},{8,16},{16,8},{24,0},{1,25},{9,17},{17,9},{25,1},{2,26},{10... | collective-permute-start | bytes 110600 | tf_op jit(solution)/shard_map/ppermute | solution.py:361
  27.0 20.6 %collective-permute-start.8 = (s16[144,128]{1,0:T(8,128)(2,1)S(1)}, s16[144,128]{1,0:T(8,128)(2,1)S(1)}, u32[]{:S(2)}, u32[]{:S(2)}) collective-permute-start(s16[144,128]{1,0:T(8,128)(2,1)S(1)} %get-tuple-element.46.refs_6_), channel_id=1, source_target_pairs={{0,16},{8,24},{16,0},{24,8},{1,17},{9,25},{17,1},{25,9},{2,18},{10... | collective-permute-start | bytes 110600 | tf_op jit(solution)/shard_map/ppermute | solution.py:361
  27.7 20.0 %collective-permute-start.7 = (s16[144,128]{1,0:T(8,128)(2,1)S(1)}, s16[144,128]{1,0:T(8,128)(2,1)S(1)}, u32[]{:S(2)}, u32[]{:S(2)}) collective-permute-start(s16[144,128]{1,0:T(8,128)(2,1)S(1)} %get-tuple-element.46.refs_6_), channel_id=1, source_target_pairs={{0,8},{8,0},{16,24},{24,16},{1,9},{9,1},{17,25},{25,17},{2,10},{10... | collective-permute-start | bytes 110600 | tf_op jit(solution)/shard_map/ppermute | solution.py:361
  49.3 1.3 %collective-permute-start.10 = (f32[128,128]{1,0:T(8,128)S(1)}, f32[128,128]{1,0:T(8,128)S(1)}, u32[]{:S(2)}, u32[]{:S(2)}) collective-permute-start(f32[128,128]{1,0:T(8,128)S(1)} %get-tuple-element.52.refs_0_), channel_id=1, source_target_pairs={{0,1},{1,0},{2,3},{3,2},{4,5},{5,4},{6,7},{7,6},{8,9},{9,8},{10,11... | collective-permute-start | bytes 196616 | tf_op jit(solution)/shard_map/ppermute | solution.py:361
  50.7 4.9 %collective-permute-start.13 = (s16[144,128]{1,0:T(8,128)(2,1)S(1)}, s16[144,128]{1,0:T(8,128)(2,1)S(1)}, u32[]{:S(2)}, u32[]{:S(2)}) collective-permute-start(s16[144,128]{1,0:T(8,128)(2,1)S(1)} %pair_1.1.refs_6_), channel_id=1, source_target_pairs={{0,6},{1,7},{2,4},{3,5},{4,2},{5,3},{6,0},{7,1},{8,14},{9,15},{10,... | collective-permute-start | bytes 110600 | tf_op jit(solution)/shard_map/ppermute | solution.py:361
  52.3 4.0 %collective-permute-start.12 = (s16[144,128]{1,0:T(8,128)(2,1)S(1)}, s16[144,128]{1,0:T(8,128)(2,1)S(1)}, u32[]{:S(2)}, u32[]{:S(2)}) collective-permute-start(s16[144,128]{1,0:T(8,128)(2,1)S(1)} %pair_1.1.refs_6_), channel_id=1, source_target_pairs={{0,4},{1,5},{2,6},{3,7},{4,0},{5,1},{6,2},{7,3},{8,12},{9,13},{10,... | collective-permute-start | bytes 110600 | tf_op jit(solution)/shard_map/ppermute | solution.py:361
  52.8 4.0 %collective-permute-start.11 = (s16[144,128]{1,0:T(8,128)(2,1)S(1)}, s16[144,128]{1,0:T(8,128)(2,1)S(1)}, u32[]{:S(2)}, u32[]{:S(2)}) collective-permute-start(s16[144,128]{1,0:T(8,128)(2,1)S(1)} %pair_1.1.refs_6_), channel_id=1, source_target_pairs={{0,2},{1,3},{2,0},{3,1},{4,6},{5,7},{6,4},{7,5},{8,10},{9,11},{10,... | collective-permute-start | bytes 110600 | tf_op jit(solution)/shard_map/ppermute | solution.py:361
  58.2 5.9 %collective-permute-start.16 = (s16[160,128]{1,0:T(8,128)(2,1)S(1)}, s16[160,128]{1,0:T(8,128)(2,1)S(1)}, u32[]{:S(2)}, u32[]{:S(2)}) collective-permute-start(s16[160,128]{1,0:T(8,128)(2,1)S(1)} %get-tuple-element.56.refs_6_), channel_id=1, source_target_pairs={{0,24},{8,16},{16,8},{24,0},{1,25},{9,17},{17,9},{25,1},{2,26},{10... | collective-permute-start | bytes 122888 | tf_op jit(solution)/shard_map/ppermute | solution.py:361
  60.0 5.0 %collective-permute-start.15 = (s16[160,128]{1,0:T(8,128)(2,1)S(1)}, s16[160,128]{1,0:T(8,128)(2,1)S(1)}, u32[]{:S(2)}, u32[]{:S(2)}) collective-permute-start(s16[160,128]{1,0:T(8,128)(2,1)S(1)} %get-tuple-element.56.refs_6_), channel_id=1, source_target_pairs={{0,16},{8,24},{16,0},{24,8},{1,17},{9,25},{17,1},{25,9},{2,18},{10... | collective-permute-start | bytes 122888 | tf_op jit(solution)/shard_map/ppermute | solution.py:361
  60.0 5.0 %collective-permute-start.14 = (s16[160,128]{1,0:T(8,128)(2,1)S(1)}, s16[160,128]{1,0:T(8,128)(2,1)S(1)}, u32[]{:S(2)}, u32[]{:S(2)}) collective-permute-start(s16[160,128]{1,0:T(8,128)(2,1)S(1)} %get-tuple-element.56.refs_6_), channel_id=1, source_target_pairs={{0,8},{8,0},{16,24},{24,16},{1,9},{9,1},{17,25},{25,17},{2,10},{10... | collective-permute-start | bytes 122888 | tf_op jit(solution)/shard_map/ppermute | solution.py:361
  66.4 1.3 %collective-permute-start.17 = (f32[80,128]{1,0:T(8,128)S(1)}, f32[80,128]{1,0:T(8,128)S(1)}, u32[]{:S(2)}, u32[]{:S(2)}) collective-permute-start(f32[80,128]{1,0:T(8,128)S(1)} %get-tuple-element.64), channel_id=1, source_target_pairs={{0,1},{1,0},{2,3},{3,2},{4,5},{5,4},{6,7},{7,6},{8,9},{9,8},{10,11... | collective-permute-start | bytes 122888 | tf_op jit(solution)/shard_map/ppermute | solution.py:361
  67.7 4.2 %collective-permute-start.18 = (f32[32,128]{1,0:T(8,128)S(1)}, f32[32,128]{1,0:T(8,128)S(1)}, u32[]{:S(2)}, u32[]{:S(2)}) collective-permute-start(f32[32,128]{1,0:T(8,128)S(1)} %get-tuple-element.66), channel_id=1, source_target_pairs={{0,2},{1,3},{2,0},{3,1},{4,6},{5,7},{6,4},{7,5},{8,10},{9,11},{10,... | collective-permute-start | bytes 49160 | tf_op jit(solution)/shard_map/ppermute | solution.py:361
  69.2 3.7 %collective-permute-start.19 = (f32[32,128]{1,0:T(8,128)S(1)}, f32[32,128]{1,0:T(8,128)S(1)}, u32[]{:S(2)}, u32[]{:S(2)}) collective-permute-start(f32[32,128]{1,0:T(8,128)S(1)} %get-tuple-element.67), channel_id=1, source_target_pairs={{0,4},{1,5},{2,6},{3,7},{4,0},{5,1},{6,2},{7,3},{8,12},{9,13},{10,... | collective-permute-start | bytes 49160 | tf_op jit(solution)/shard_map/ppermute | solution.py:361
  70.8 4.6 %collective-permute-start.20 = (f32[32,128]{1,0:T(8,128)S(1)}, f32[32,128]{1,0:T(8,128)S(1)}, u32[]{:S(2)}, u32[]{:S(2)}) collective-permute-start(f32[32,128]{1,0:T(8,128)S(1)} %get-tuple-element.68), channel_id=1, source_target_pairs={{0,6},{1,7},{2,4},{3,5},{4,2},{5,3},{6,0},{7,1},{8,14},{9,15},{10,... | collective-permute-start | bytes 49160 | tf_op jit(solution)/shard_map/ppermute | solution.py:361

commit v10 on v8

--- a/solution.py
+++ b/solution.py
@@ -10,7 +10,7 @@
 
 LANES = 128
 EXTRA = 16
-CHUNKS = 4
+BOUNDS = (0, 5, 11, 16)
 SCALES = 16
 STEPS = 64.0
 LIMIT = 32760.0
@@ -124,15 +124,16 @@
 
 
 def first_body(
-    step, n_row, rows_far, columns_far, count, tile_data, mask_far, cotangent_far, saved_far,
-    tiles, term, anchor, *refs
+    step, n_row, rows_far, columns_far, count, sizes_far, tile_data, mask_far, cotangent_far, saved_far,
+    tiles, term, anchor, rows, columns, count_out, sizes, *refs
 ):
     outs = refs[:n_row]
-    source, total, rows, columns, mask, cotangent, saved, arrived, ready = refs[n_row:]
+    source, total, mask, cotangent, saved, arrived, ready = refs[n_row:]
+    count_out[0, 0] = count[0, 0]
     slots = tiles.shape[0]
-    chunk = slots // CHUNKS
+    bounds = [slots * part // 16 for part in BOUNDS]
     pairs = [(mask_far, mask), (cotangent_far, cotangent), (saved_far, saved)]
-    pairs += [(rows_far, rows), (columns_far, columns)]
+    pairs += [(rows_far, rows), (columns_far, columns), (sizes_far, sizes)]
     small = [
         pltpu.make_async_copy(far_ref, near, ready.at[spot])
         for spot, (far_ref, near) in enumerate(pairs)
@@ -141,11 +142,11 @@
         copy.start()
 
     def fetch(part):
-        span = pl.ds(part * chunk, chunk)
+        span = pl.ds(bounds[part], bounds[part + 1] - bounds[part])
         return pltpu.make_async_copy(tile_data.at[0, 0, span], tiles.at[span], arrived.at[part])
 
-    for part in range(CHUNKS):
-        fetch(part).start(priority=part % 2)
+    for part in range(len(BOUNDS) - 1):
+        fetch(part).start()
     total[...] = jnp.zeros_like(total)
     for copy in small:
         copy.wait()
@@ -158,9 +159,9 @@
     iterations = source.shape[0] - 1
     for vector in range(iterations):
         source[vector + 1] = rounded(saved[:, vector, :])
-    for part in range(CHUNKS):
+    for part in range(len(BOUNDS) - 1):
         fetch(part).wait()
-        span = range(part * chunk, (part + 1) * chunk)
+        span = range(bounds[part], bounds[part + 1])
         add_products(rows, columns, count, tiles, span, source, total)
     lines = total.shape[1]
     share = lines // n_row
@@ -428,29 +429,32 @@
 
     mask_x, mask_y = lines(primal_mask), lines(dual_mask)
     full_x, full_y = f32(lines_x, LANES), f32(lines_y, LANES)
-    where = [(SMEM, tile_row_block), (SMEM, tile_column_block), (SMEM, tile_count)]
     saved = lines(saved_dual)
+    index = (SMEM, pltpu.SMEM(tile_row_block.shape, jnp.int32))
     tiles, term_y, anchor_y, *parts = run(
         functools.partial(first_body, last, n_row),
-        [pltpu.VMEM((slots, width, width), jnp.bfloat16), full_y, full_y]
+        [pltpu.VMEM((slots, width, width), jnp.bfloat16), full_y, full_y, index, index]
+        + [(SMEM, pltpu.SMEM((1, 1), jnp.int32)), (SMEM, pltpu.SMEM((2,), jnp.float32))]
         + [row_part(saved_lines)] * n_row,
         [(ANY, far(tile_row_block)), (ANY, far(tile_column_block)), (SMEM, tile_count)]
-        + [(ANY, far(tile_data)), (ANY, far(mask_y)), (ANY, far(lines(dual_cotangent)))]
+        + [(ANY, far(step_sizes)), (ANY, far(tile_data)), (ANY, far(mask_y)), (ANY, far(lines(dual_cotangent)))]
         + [(ANY, far(saved))],
         [
             scratch(iterations + 1, lines_y, LANES),
             scratch(iterations + 1, lines_x, LANES),
-            pltpu.SMEM(tile_row_block.shape, jnp.int32),
-            pltpu.SMEM(tile_row_block.shape, jnp.int32),
             pltpu.VMEM(mask_y.shape, jnp.int32),
             scratch(lines_y, LANES),
             scratch(*saved.shape),
-            pltpu.SemaphoreType.DMA((CHUNKS,)),
-            pltpu.SemaphoreType.DMA((5,)),
+            pltpu.SemaphoreType.DMA((len(BOUNDS) - 1,)),
+            pltpu.SemaphoreType.DMA((6,)),
         ],
         "first",
         cost,
     )
+    *where, sizes = [
+        (SMEM, pltpu.with_memory_space_constraint(held, pltpu.SMEM)) for held in parts[:4]
+    ]
+    parts = parts[4:]
     turned, tiles = run(
         turn_body,
         [pltpu.VMEM(tiles.shape, tiles.dtype)],
@@ -466,7 +470,7 @@
     for step in reversed(range(iterations)):
         parts = exchange(parts, "row")
         kind = {0: "last", last: "sums", last - 1: "shares"}.get(step, "plain")
-        groups = where + [(SMEM, step_sizes), (VMEM, turned), (VMEM, mask_x), (VMEM, parts)]
+        groups = where + [sizes, (VMEM, turned), (VMEM, mask_x), (VMEM, parts)]
         groups += [(VMEM, adjoint_x), (VMEM, anchor_x)]
         body = functools.partial(primal_body, kind, step, n_row, n_col)
         if step == 0:
@@ -500,7 +504,7 @@
             f"pair_{step}",
         )[0]
         parts = exchange([part] * n_chip, "col", 2)
-        groups = where + [(SMEM, step_sizes), (VMEM, tiles), (VMEM, mask_y), (VMEM, parts)]
+        groups = where + [sizes, (VMEM, tiles), (VMEM, mask_y), (VMEM, parts)]
         groups += [(VMEM, term_y), (VMEM, anchor_y)]
         if step == 1:
             groups += [(VMEM, lines(demand)), (VMEM, images), (VMEM, list(terms_y))]
@@ -542,7 +546,7 @@
     dual_adjoint, gradients = run(
         functools.partial(last_body, scales),
         [(ANY, f32(share_y, LANES)), (ANY, f32(2))],
-        [(SMEM, step_sizes), (VMEM, parts), (VMEM, term_y), (VMEM, anchor_y)],
+        [sizes, (VMEM, parts), (VMEM, term_y), (VMEM, anchor_y)],
         [
             scratch(share_y, LANES),
             pltpu.SMEM((2,), jnp.float32),

time: 64.1 us -> 60.5 us (0.944)
  Pallas kernels: 12.6 us -> 9.13 us
    pallas_call x11, Pallas kernels: 12.6 us -> 9.13 us  [run(): pl.pallas_call(kernel, out_shape=shapes, in_specs=specs, out_specs=out_sp...]
where the time goes in v10:
time: 60.5 us; the launch traced here: 60.4 us
  starting transfers between devices  25.4 us (42%)
  waiting for transfers between devices  23.7 us (39%)
  Pallas kernels  9.13 us (15%)
  between operations  1.44 us (2%)
  local copies, waits for them, and re-layouts  0.66 us (1%)
    ppermute x21, starting transfers between devices, swap(): return lax.ppermute(array, axis, [(i, i ^ stride) for i in range(size)])  25.4 us
    ppermute x21, waiting for transfers between devices, swap(): return lax.ppermute(array, axis, [(i, i ^ stride) for i in range(size)])  23.7 us
    pallas_call x11, Pallas kernels, run(): pl.pallas_call(kernel, out_shape=shapes, in_specs=specs, out_specs=out_sp...  9.13 us
  transfers between devices with their start and end apart: 21, of which 17 were waited for; matrix products, arithmetic and copies ran while one was open for 1% of the time, Pallas kernels for 2%

profile of v10, /device:TPU:0, one launch (start us, length us, event | category | flops | bytes accessed | tf_op | source)
XLA Modules:
  0.0 60.4 jit_solution(17273672841520057265)
XLA Ops:
  1.3 0.0 copy-start.1
  1.3 0.0 copy-start.3
  1.3 2.8 %first.1 = (bf16[32,256,256]{2,1,0:T(8,128)(2,1)S(1)}, f32[128,128]{1,0:T(8,128)S(1)}, f32[128,128]{1,0:T(8,128)S(1)}, s32[1,1,32]{2,1,0:T(1,128)S(4)}, s32[1,1,...) custom-call(s32[1,1,32]{2,1,0:T(1,128)} %refs_0_.1, ...), custom_call_target="tpu_custom_call" | custom-call | flops 4194304 | bytes 4194304 | tf_op jit(solution)/shard_map/first/pallas_call | solution.py:364
  4.2 3.1 %collective-permute-start = (s16[240,128]{1,0:T(8,128)(2,1)S(1)}, s16[240,128]{1,0:T(8,128)(2,1)S(1)}, u32[]{:S(2)}, u32[]{:S(2)}) collective-permute-start(s16[240,128]{1,0:T(8,128)(2,1)S(1)} %get-tuple-element.52), channel_id=1, source_target_pairs={{0,8},{8,0},{16,24},{24,16},{1,9},{9,1},{17,25},{25,17},{2,10},{10... | collective-permute-start | bytes 184328 | tf_op jit(solution)/shard_map/ppermute | solution.py:379
  7.2 2.6 %collective-permute-start.1 = (s16[240,128]{1,0:T(8,128)(2,1)S(1)}, s16[240,128]{1,0:T(8,128)(2,1)S(1)}, u32[]{:S(2)}, u32[]{:S(2)}) collective-permute-start(s16[240,128]{1,0:T(8,128)(2,1)S(1)} %get-tuple-element.53), channel_id=1, source_target_pairs={{0,16},{8,24},{16,0},{24,8},{1,17},{9,25},{17,1},{25,9},{2,18},{10... | collective-permute-start | bytes 184328 | tf_op jit(solution)/shard_map/ppermute | solution.py:379
  9.8 0.0 collective-permute-start.2
  9.8 0.0 copy-start
  9.8 1.1 %turn.1 = (bf16[32,256,256]{2,1,0:T(8,128)(2,1)S(1)}, bf16[32,256,256]{2,1,0:T(8,128)(2,1)S(1)}) custom-call(bf16[32,256,256]{2,1,0:T(8,128)(2,1)S(1)} %get-tuple-element.49.refs_0_), custom_call_target="tpu_custom_call", output_to_operand_aliasing={{1}: (0, {})} | custom-call | flops 4194304 | bytes 4194304 | tf_op jit(solution)/shard_map/turn/pallas_call | solution.py:364
  11.0 0.0 collective-permute-done.refs_7_
  11.0 2.6 %collective-permute-done.1.refs_8_ = s16[240,128]{1,0:T(8,128)(2,1)S(1)} collective-permute-done((s16[240,128]{1,0:T(8,128)(2,1)S(1)}, s16[240,128]{1,0:T(8,128)(2,1)S(1)}, u32[]{:S(2)}, u32[]{:S(2)}) %collective-permute-start.1) | collective-permute-done | bytes 61472 | tf_op jit(solution)/shard_map/ppermute | solution.py:379
  13.6 2.3 %collective-permute-done.2.refs_9_ = s16[240,128]{1,0:T(8,128)(2,1)S(1)} collective-permute-done((s16[240,128]{1,0:T(8,128)(2,1)S(1)}, s16[240,128]{1,0:T(8,128)(2,1)S(1)}, u32[]{:S(2)}, u32[]{:S(2)}) %collective-permute-start.2) | collective-permute-done | bytes 61472 | tf_op jit(solution)/shard_map/ppermute | solution.py:379
  15.9 0.0 copy-done.1
  15.9 0.0 copy-done.3
  15.9 0.0 copy-start.2
  15.9 0.0 copy-start.5
  15.9 0.8 %primal_2.1 = (f32[128,128]{1,0:T(8,128)S(1)}, f32[128,128]{1,0:T(8,128)S(1)}, f32[128,128]{1,0:T(8,128)S(1)}, f32[128,128]{1,0:T(8,128)S(1)}, f32[96,128]{1,0:T(8,128)S(1)}, /*index=5*/bf16[32,256,256]{2,1,0:T(8,128)(2,1)S(1)}) custom-call(s32[1,1,32]{2,1,0:T(1,128)S(4)} %get-tuple-element.45.refs_0_, ...), custom_call_target="tpu_custom_call", output_to_operand_aliasing={{5}: (4, {})} | custom-call | flops 4194304 | bytes 4194304 | tf_op jit(solution)/shard_map/primal_2/pallas_call | solution.py:364
  16.7 0.0 collective-permute-start.3
  16.7 1.2 %collective-permute-done.3.refs_1_ = f32[128,128]{1,0:T(8,128)S(1)} collective-permute-done((f32[128,128]{1,0:T(8,128)S(1)}, f32[128,128]{1,0:T(8,128)S(1)}, u32[]{:S(2)}, u32[]{:S(2)}) %collective-permute-start.3) | collective-permute-done | bytes 65568 | tf_op jit(solution)/shard_map/ppermute | solution.py:379
  18.0 2.5 %collective-permute-start.6 = (s16[144,128]{1,0:T(8,128)(2,1)S(1)}, s16[144,128]{1,0:T(8,128)(2,1)S(1)}, u32[]{:S(2)}, u32[]{:S(2)}) collective-permute-start(s16[144,128]{1,0:T(8,128)(2,1)S(1)} %pair_2.1.refs_6_), channel_id=1, source_target_pairs={{0,6},{1,7},{2,4},{3,5},{4,2},{5,3},{6,0},{7,1},{8,14},{9,15},{10,... | collective-permute-start | bytes 110600 | tf_op jit(solution)/shard_map/ppermute | solution.py:379
  20.6 0.5 collective-permute-start.5
  21.1 0.5 collective-permute-start.4
  21.6 1.4 %collective-permute-done.6.refs_9_ = s16[144,128]{1,0:T(8,128)(2,1)S(1)} collective-permute-done((s16[144,128]{1,0:T(8,128)(2,1)S(1)}, s16[144,128]{1,0:T(8,128)(2,1)S(1)}, u32[]{:S(2)}, u32[]{:S(2)}) %collective-permute-start.6) | collective-permute-done | bytes 36896 | tf_op jit(solution)/shard_map/ppermute | solution.py:379
  23.0 1.5 %collective-permute-done.5.refs_8_ = s16[144,128]{1,0:T(8,128)(2,1)S(1)} collective-permute-done((s16[144,128]{1,0:T(8,128)(2,1)S(1)}, s16[144,128]{1,0:T(8,128)(2,1)S(1)}, u32[]{:S(2)}, u32[]{:S(2)}) %collective-permute-start.5) | collective-permute-done | bytes 36896 | tf_op jit(solution)/shard_map/ppermute | solution.py:379
  24.5 0.5 collective-permute-done.4.refs_7_
  25.0 0.0 copy-done
  25.0 0.9 %dual_1.1 = (f32[128,128]{1,0:T(8,128)S(1)}, f32[128,128]{1,0:T(8,128)S(1)}, s16[240,128]{1,0:T(8,128)(2,1)S(1)}, bf16[32,256,256]{2,1,0:T(8,128)(2,1)S(1)}) custom-call(s32[1,1,32]{2,1,0:T(1,128)S(4)} %get-tuple-element.45.refs_0_, s32[1,1,32]{2,1,0:T(1,128)S(4)} %get-tuple-element.46.refs_1_, ...), custom_call_target="tpu_custom_call", output_to_operand_aliasing={{3}: (4, {})} | custom-call | flops 4194304 | bytes 4194304 | tf_op jit(solution)/shard_map/dual_1/pallas_call | solution.py:364
  25.9 1.6 %collective-permute-start.9 = (s16[240,128]{1,0:T(8,128)(2,1)S(1)}, s16[240,128]{1,0:T(8,128)(2,1)S(1)}, u32[]{:S(2)}, u32[]{:S(2)}) collective-permute-start(s16[240,128]{1,0:T(8,128)(2,1)S(1)} %get-tuple-element.61.refs_6_), channel_id=1, source_target_pairs={{0,24},{8,16},{16,8},{24,0},{1,25},{9,17},{17,9},{25,1},{2,26},{10... | collective-permute-start | bytes 184328 | tf_op jit(solution)/shard_map/ppermute | solution.py:379
  27.5 0.0 collective-permute-start.8
  27.5 2.8 %collective-permute-start.7 = (s16[240,128]{1,0:T(8,128)(2,1)S(1)}, s16[240,128]{1,0:T(8,128)(2,1)S(1)}, u32[]{:S(2)}, u32[]{:S(2)}) collective-permute-start(s16[240,128]{1,0:T(8,128)(2,1)S(1)} %get-tuple-element.61.refs_6_), channel_id=1, source_target_pairs={{0,8},{8,0},{16,24},{24,16},{1,9},{9,1},{17,25},{25,17},{2,10},{10... | collective-permute-start | bytes 184328 | tf_op jit(solution)/shard_map/ppermute | solution.py:379
  30.4 1.7 %collective-permute-done.9.refs_9_ = s16[240,128]{1,0:T(8,128)(2,1)S(1)} collective-permute-done((s16[240,128]{1,0:T(8,128)(2,1)S(1)}, s16[240,128]{1,0:T(8,128)(2,1)S(1)}, u32[]{:S(2)}, u32[]{:S(2)}) %collective-permute-start.9) | collective-permute-done | bytes 61472 | tf_op jit(solution)/shard_map/ppermute | solution.py:379
  32.1 1.3 %collective-permute-done.8.refs_8_ = s16[240,128]{1,0:T(8,128)(2,1)S(1)} collective-permute-done((s16[240,128]{1,0:T(8,128)(2,1)S(1)}, s16[240,128]{1,0:T(8,128)(2,1)S(1)}, u32[]{:S(2)}, u32[]{:S(2)}) %collective-permute-start.8) | collective-permute-done | bytes 61472 | tf_op jit(solution)/shard_map/ppermute | solution.py:379
  33.4 0.0 collective-permute-done.7.refs_7_
  33.4 0.0 copy-done.2
  33.4 0.0 copy-done.4
  33.4 0.0 copy-done.5
  33.4 1.0 %primal_1.1 = (f32[128,128]{1,0:T(8,128)S(1)}, f32[128,128]{1,0:T(8,128)S(1)}, f32[128,128]{1,0:T(8,128)S(1)}, f32[128,128]{1,0:T(8,128)S(1)}, f32[3,128,128]{2,...) custom-call(s32[1,1,32]{2,1,0:T(1,128)S(4)} %get-tuple-element.45.re, ...), custom_call_target="tpu_custom_call", output_to_operand_aliasing={{6}: (4, {})} | custom-call | flops 4194304 | bytes 4194304 | tf_op jit(solution)/shard_map/primal_1/pallas_call | solution.py:364
  34.5 0.1 collective-permute-start.10
  34.5 1.2 %collective-permute-done.10.refs_1_ = f32[128,128]{1,0:T(8,128)S(1)} collective-permute-done((f32[128,128]{1,0:T(8,128)S(1)}, f32[128,128]{1,0:T(8,128)S(1)}, u32[]{:S(2)}, u32[]{:S(2)}) %collective-permute-start.10) | collective-permute-done | bytes 65568 | tf_op jit(solution)/shard_map/ppermute | solution.py:379
  35.8 0.1 pair_1.1.refs_6_
  35.8 1.6 %collective-permute-start.13 = (s16[144,128]{1,0:T(8,128)(2,1)S(1)}, s16[144,128]{1,0:T(8,128)(2,1)S(1)}, u32[]{:S(2)}, u32[]{:S(2)}) collective-permute-start(s16[144,128]{1,0:T(8,128)(2,1)S(1)} %pair_1.1.refs_6_), channel_id=1, source_target_pairs={{0,6},{1,7},{2,4},{3,5},{4,2},{5,3},{6,0},{7,1},{8,14},{9,15},{10,... | collective-permute-start | bytes 110600 | tf_op jit(solution)/shard_map/ppermute | solution.py:379
  37.4 0.5 collective-permute-start.12
  37.9 1.5 %collective-permute-start.11 = (s16[144,128]{1,0:T(8,128)(2,1)S(1)}, s16[144,128]{1,0:T(8,128)(2,1)S(1)}, u32[]{:S(2)}, u32[]{:S(2)}) collective-permute-start(s16[144,128]{1,0:T(8,128)(2,1)S(1)} %pair_1.1.refs_6_), channel_id=1, source_target_pairs={{0,2},{1,3},{2,0},{3,1},{4,6},{5,7},{6,4},{7,5},{8,10},{9,11},{10,... | collective-permute-start | bytes 110600 | tf_op jit(solution)/shard_map/ppermute | solution.py:379
  39.4 1.4 %collective-permute-done.13.refs_9_ = s16[144,128]{1,0:T(8,128)(2,1)S(1)} collective-permute-done((s16[144,128]{1,0:T(8,128)(2,1)S(1)}, s16[144,128]{1,0:T(8,128)(2,1)S(1)}, u32[]{:S(2)}, u32[]{:S(2)}) %collective-permute-start.13) | collective-permute-done | bytes 36896 | tf_op jit(solution)/shard_map/ppermute | solution.py:379
  40.8 0.6 collective-permute-done.12.refs_8_
  41.4 0.5 collective-permute-done.11.refs_7_
  41.9 0.0 copy-done.6
  41.9 0.9 %dual_0.1 = (f32[128,128]{1,0:T(8,128)S(1)}, f32[128,128]{1,0:T(8,128)S(1)}, s16[160,128]{1,0:T(8,128)(2,1)S(1)}, bf16[32,256,256]{2,1,0:T(8,128)(2,1)S(1)}) custom-call(s32[1,1,32]{2,1,0:T(1,128)S(4)} %get-tuple-element.45.refs_0_, s32[1,1,32]{2,1,0:T(1,128)S(4)} %get-tuple-element.46.refs_1_, ...), custom_call_target="tpu_custom_call", output_to_operand_aliasing={{3}: (4, {})} | custom-call | flops 4194304 | bytes 4194304 | tf_op jit(solution)/shard_map/dual_0/pallas_call | solution.py:364
  42.7 2.1 %collective-permute-start.16 = (s16[160,128]{1,0:T(8,128)(2,1)S(1)}, s16[160,128]{1,0:T(8,128)(2,1)S(1)}, u32[]{:S(2)}, u32[]{:S(2)}) collective-permute-start(s16[160,128]{1,0:T(8,128)(2,1)S(1)} %get-tuple-element.70.refs_6_), channel_id=1, source_target_pairs={{0,24},{8,16},{16,8},{24,0},{1,25},{9,17},{17,9},{25,1},{2,26},{10... | collective-permute-start | bytes 122888 | tf_op jit(solution)/shard_map/ppermute | solution.py:379
  44.9 0.6 collective-permute-start.15
  45.4 1.8 %collective-permute-start.14 = (s16[160,128]{1,0:T(8,128)(2,1)S(1)}, s16[160,128]{1,0:T(8,128)(2,1)S(1)}, u32[]{:S(2)}, u32[]{:S(2)}) collective-permute-start(s16[160,128]{1,0:T(8,128)(2,1)S(1)} %get-tuple-element.70.refs_6_), channel_id=1, source_target_pairs={{0,8},{8,0},{16,24},{24,16},{1,9},{9,1},{17,25},{25,17},{2,10},{10... | collective-permute-start | bytes 122888 | tf_op jit(solution)/shard_map/ppermute | solution.py:379
  47.2 1.8 %collective-permute-done.16.refs_9_ = s16[160,128]{1,0:T(8,128)(2,1)S(1)} collective-permute-done((s16[160,128]{1,0:T(8,128)(2,1)S(1)}, s16[160,128]{1,0:T(8,128)(2,1)S(1)}, u32[]{:S(2)}, u32[]{:S(2)}) %collective-permute-start.16) | collective-permute-done | bytes 40992 | tf_op jit(solution)/shard_map/ppermute | solution.py:379
  49.0 0.9 %collective-permute-done.15.refs_8_ = s16[160,128]{1,0:T(8,128)(2,1)S(1)} collective-permute-done((s16[160,128]{1,0:T(8,128)(2,1)S(1)}, s16[160,128]{1,0:T(8,128)(2,1)S(1)}, u32[]{:S(2)}, u32[]{:S(2)}) %collective-permute-start.15) | collective-permute-done | bytes 40992 | tf_op jit(solution)/shard_map/ppermute | solution.py:379
  49.9 0.0 collective-permute-done.14.refs_7_
  49.9 0.8 %primal_0.1 = (f32[128,128]{1,0:T(8,128)S(1)}, f32[80,128]{1,0:T(8,128)S(1)}, f32[80,128]{1,0:T(8,128)S(1)}, bf16[32,256,256]{2,1,0:T(8,128)(2,1)S(1)}) custom-call(s32[1,1,32]{2,1,0:T(1,128)S(4)} %get-tuple-element.45.refs_0_, s32[1,1,32]{2,1,0:T(1,128)S(4)} %get-tuple-element.46.refs_1_, ...), custom_call_target="tpu_custom_call", output_to_operand_aliasing={{3}: (4, {})} | custom-call | flops 4194304 | bytes 4194304 | tf_op jit(solution)/shard_map/primal_0/pallas_call | solution.py:364
  50.7 0.1 collective-permute-start.17
  50.8 1.2 %collective-permute-done.17.refs_1_ = f32[80,128]{1,0:T(8,128)S(1)} collective-permute-done((f32[80,128]{1,0:T(8,128)S(1)}, f32[80,128]{1,0:T(8,128)S(1)}, u32[]{:S(2)}, u32[]{:S(2)}) %collective-permute-start.17) | collective-permute-done | bytes 40992 | tf_op jit(solution)/shard_map/ppermute | solution.py:379
  52.0 1.5 %collective-permute-start.18 = (f32[32,128]{1,0:T(8,128)S(1)}, f32[32,128]{1,0:T(8,128)S(1)}, u32[]{:S(2)}, u32[]{:S(2)}) collective-permute-start(f32[32,128]{1,0:T(8,128)S(1)} %get-tuple-element.80), channel_id=1, source_target_pairs={{0,2},{1,3},{2,0},{3,1},{4,6},{5,7},{6,4},{7,5},{8,10},{9,11},{10,... | collective-permute-start | bytes 49160 | tf_op jit(solution)/shard_map/ppermute | solution.py:379
  53.5 1.5 %collective-permute-start.19 = (f32[32,128]{1,0:T(8,128)S(1)}, f32[32,128]{1,0:T(8,128)S(1)}, u32[]{:S(2)}, u32[]{:S(2)}) collective-permute-start(f32[32,128]{1,0:T(8,128)S(1)} %get-tuple-element.81), channel_id=1, source_target_pairs={{0,4},{1,5},{2,6},{3,7},{4,0},{5,1},{6,2},{7,3},{8,12},{9,13},{10,... | collective-permute-start | bytes 49160 | tf_op jit(solution)/shard_map/ppermute | solution.py:379
  55.1 0.5 collective-permute-start.20
  55.6 0.6 %copy.29 = f32[16384]{0:T(1024)} copy(f32[16384]{0:T(1024)S(1)} %bitcast.19) | data formatting | bytes 131072
  56.2 0.0 collective-permute-done.18.refs_2_
  56.2 1.1 %collective-permute-done.19.refs_3_ = f32[32,128]{1,0:T(8,128)S(1)} collective-permute-done((f32[32,128]{1,0:T(8,128)S(1)}, f32[32,128]{1,0:T(8,128)S(1)}, u32[]{:S(2)}, u32[]{:S(2)}) %collective-permute-start.19) | collective-permute-done | bytes 16416 | tf_op jit(solution)/shard_map/ppermute | solution.py:379
  57.3 2.4 %collective-permute-done.20.refs_4_ = f32[32,128]{1,0:T(8,128)S(1)} collective-permute-done((f32[32,128]{1,0:T(8,128)S(1)}, f32[32,128]{1,0:T(8,128)S(1)}, u32[]{:S(2)}, u32[]{:S(2)}) %collective-permute-start.20) | collective-permute-done | bytes 16416 | tf_op jit(solution)/shard_map/ppermute | solution.py:379
  59.7 0.7 %last.1 = (f32[16,128]{1,0:T(8,128)}, f32[2]{0:T(128)}) custom-call(f32[2]{0:T(128)S(4)} %get-tuple-element.48.refs_3_.refs_0_, f32[32,128]{1,0:T(8,128)S(1)} %get-tuple-element.79.refs_1_, f32[32,128]{1,0:T(8,128)S(1)} %collective-permute-done.18.refs_2_, f32[32,128]{1,0:T(8,128)S(1)} %collective-permute-done.19.refs_3_, ...), custom_call_target="tpu_custom_call" | custom-call | tf_op jit(solution)/shard_map/last/pallas_call | solution.py:364
  (4 shorter events, 0.1 us)
Async XLA Ops:
  1.3 14.6 %copy-start.1 = (s32[3,16384]{1,0:T(4,128)S(1)}, s32[3,16384]{1,0:T(4,128)}, u32[]{:S(2)}) copy-start(s32[3,16384]{1,0:T(4,128)} %param.20) | copy-start | bytes 589828
  1.3 14.6 %copy-start.3 = (f32[16384]{0:T(1024)S(1)}, f32[16384]{0:T(1024)}, u32[]{:S(2)}) copy-start(f32[16384]{0:T(1024)} %param.26) | copy-start | bytes 196612
  4.2 6.8 %collective-permute-start = (s16[240,128]{1,0:T(8,128)(2,1)S(1)}, s16[240,128]{1,0:T(8,128)(2,1)S(1)}, u32[]{:S(2)}, u32[]{:S(2)}) collective-permute-start(s16[240,128]{1,0:T(8,128)(2,1)S(1)} %get-tuple-element.52), channel_id=1, source_target_pairs={{0,8},{8,0},{16,24},{24,16},{1,9},{9,1},{17,25},{25,17},{2,10},{10... | collective-permute-start | bytes 184328 | tf_op jit(solution)/shard_map/ppermute | solution.py:379
  7.2 6.4 %collective-permute-start.1 = (s16[240,128]{1,0:T(8,128)(2,1)S(1)}, s16[240,128]{1,0:T(8,128)(2,1)S(1)}, u32[]{:S(2)}, u32[]{:S(2)}) collective-permute-start(s16[240,128]{1,0:T(8,128)(2,1)S(1)} %get-tuple-element.53), channel_id=1, source_target_pairs={{0,16},{8,24},{16,0},{24,8},{1,17},{9,25},{17,1},{25,9},{2,18},{10... | collective-permute-start | bytes 184328 | tf_op jit(solution)/shard_map/ppermute | solution.py:379
  9.8 6.0 %collective-permute-start.2 = (s16[240,128]{1,0:T(8,128)(2,1)S(1)}, s16[240,128]{1,0:T(8,128)(2,1)S(1)}, u32[]{:S(2)}, u32[]{:S(2)}) collective-permute-start(s16[240,128]{1,0:T(8,128)(2,1)S(1)} %get-tuple-element.54), channel_id=1, source_target_pairs={{0,24},{8,16},{16,8},{24,0},{1,25},{9,17},{17,9},{25,1},{2,26},{10... | collective-permute-start | bytes 184328 | tf_op jit(solution)/shard_map/ppermute | solution.py:379
  9.8 15.2 %copy-start = (s32[3,16384]{1,0:T(4,128)S(1)}, s32[3,16384]{1,0:T(4,128)}, u32[]{:S(2)}) copy-start(s32[3,16384]{1,0:T(4,128)} %param.21) | copy-start | bytes 589828
  15.9 17.5 %copy-start.2 = (f32[3,16384]{1,0:T(4,128)S(1)}, f32[3,16384]{1,0:T(4,128)}, u32[]{:S(2)}) copy-start(f32[3,16384]{1,0:T(4,128)} %param.18) | copy-start | bytes 589828
  15.9 17.5 %copy-start.4 = (f32[16384]{0:T(1024)S(1)}, f32[16384]{0:T(1024)}, u32[]{:S(2)}) copy-start(f32[16384]{0:T(1024)} %param.22) | copy-start | bytes 196612
  15.9 17.5 %copy-start.5 = (f32[16384]{0:T(1024)S(1)}, f32[16384]{0:T(1024)}, u32[]{:S(2)}) copy-start(f32[16384]{0:T(1024)} %param.24) | copy-start | bytes 196612
  16.7 1.3 %collective-permute-start.3 = (f32[128,128]{1,0:T(8,128)S(1)}, f32[128,128]{1,0:T(8,128)S(1)}, u32[]{:S(2)}, u32[]{:S(2)}) collective-permute-start(f32[128,128]{1,0:T(8,128)S(1)} %get-tuple-element.57.refs_0_), channel_id=1, source_target_pairs={{0,1},{1,0},{2,3},{3,2},{4,5},{5,4},{6,7},{7,6},{8,9},{9,8},{10,11... | collective-permute-start | bytes 196616 | tf_op jit(solution)/shard_map/ppermute | solution.py:379
  18.0 4.9 %collective-permute-start.6 = (s16[144,128]{1,0:T(8,128)(2,1)S(1)}, s16[144,128]{1,0:T(8,128)(2,1)S(1)}, u32[]{:S(2)}, u32[]{:S(2)}) collective-permute-start(s16[144,128]{1,0:T(8,128)(2,1)S(1)} %pair_2.1.refs_6_), channel_id=1, source_target_pairs={{0,6},{1,7},{2,4},{3,5},{4,2},{5,3},{6,0},{7,1},{8,14},{9,15},{10,... | collective-permute-start | bytes 110600 | tf_op jit(solution)/shard_map/ppermute | solution.py:379
  20.6 4.0 %collective-permute-start.5 = (s16[144,128]{1,0:T(8,128)(2,1)S(1)}, s16[144,128]{1,0:T(8,128)(2,1)S(1)}, u32[]{:S(2)}, u32[]{:S(2)}) collective-permute-start(s16[144,128]{1,0:T(8,128)(2,1)S(1)} %pair_2.1.refs_6_), channel_id=1, source_target_pairs={{0,4},{1,5},{2,6},{3,7},{4,0},{5,1},{6,2},{7,3},{8,12},{9,13},{10,... | collective-permute-start | bytes 110600 | tf_op jit(solution)/shard_map/ppermute | solution.py:379
  21.1 4.0 %collective-permute-start.4 = (s16[144,128]{1,0:T(8,128)(2,1)S(1)}, s16[144,128]{1,0:T(8,128)(2,1)S(1)}, u32[]{:S(2)}, u32[]{:S(2)}) collective-permute-start(s16[144,128]{1,0:T(8,128)(2,1)S(1)} %pair_2.1.refs_6_), channel_id=1, source_target_pairs={{0,2},{1,3},{2,0},{3,1},{4,6},{5,7},{6,4},{7,5},{8,10},{9,11},{10,... | collective-permute-start | bytes 110600 | tf_op jit(solution)/shard_map/ppermute | solution.py:379
  25.0 16.8 %copy-start.6 = (f32[16384]{0:T(1024)S(1)}, f32[16384]{0:T(1024)}, u32[]{:S(2)}) copy-start(f32[16384]{0:T(1024)} %param.23) | copy-start | bytes 196612
  25.9 6.2 %collective-permute-start.9 = (s16[240,128]{1,0:T(8,128)(2,1)S(1)}, s16[240,128]{1,0:T(8,128)(2,1)S(1)}, u32[]{:S(2)}, u32[]{:S(2)}) collective-permute-start(s16[240,128]{1,0:T(8,128)(2,1)S(1)} %get-tuple-element.61.refs_6_), channel_id=1, source_target_pairs={{0,24},{8,16},{16,8},{24,0},{1,25},{9,17},{17,9},{25,1},{2,26},{10... | collective-permute-start | bytes 184328 | tf_op jit(solution)/shard_map/ppermute | solution.py:379
  27.5 5.9 %collective-permute-start.8 = (s16[240,128]{1,0:T(8,128)(2,1)S(1)}, s16[240,128]{1,0:T(8,128)(2,1)S(1)}, u32[]{:S(2)}, u32[]{:S(2)}) collective-permute-start(s16[240,128]{1,0:T(8,128)(2,1)S(1)} %get-tuple-element.61.refs_6_), channel_id=1, source_target_pairs={{0,16},{8,24},{16,0},{24,8},{1,17},{9,25},{17,1},{25,9},{2,18},{10... | collective-permute-start | bytes 184328 | tf_op jit(solution)/shard_map/ppermute | solution.py:379
  27.5 5.9 %collective-permute-start.7 = (s16[240,128]{1,0:T(8,128)(2,1)S(1)}, s16[240,128]{1,0:T(8,128)(2,1)S(1)}, u32[]{:S(2)}, u32[]{:S(2)}) collective-permute-start(s16[240,128]{1,0:T(8,128)(2,1)S(1)} %get-tuple-element.61.refs_6_), channel_id=1, source_target_pairs={{0,8},{8,0},{16,24},{24,16},{1,9},{9,1},{17,25},{25,17},{2,10},{10... | collective-permute-start | bytes 184328 | tf_op jit(solution)/shard_map/ppermute | solution.py:379
  34.5 1.3 %collective-permute-start.10 = (f32[128,128]{1,0:T(8,128)S(1)}, f32[128,128]{1,0:T(8,128)S(1)}, u32[]{:S(2)}, u32[]{:S(2)}) collective-permute-start(f32[128,128]{1,0:T(8,128)S(1)} %get-tuple-element.66.refs_0_), channel_id=1, source_target_pairs={{0,1},{1,0},{2,3},{3,2},{4,5},{5,4},{6,7},{7,6},{8,9},{9,8},{10,11... | collective-permute-start | bytes 196616 | tf_op jit(solution)/shard_map/ppermute | solution.py:379
  35.8 4.9 %collective-permute-start.13 = (s16[144,128]{1,0:T(8,128)(2,1)S(1)}, s16[144,128]{1,0:T(8,128)(2,1)S(1)}, u32[]{:S(2)}, u32[]{:S(2)}) collective-permute-start(s16[144,128]{1,0:T(8,128)(2,1)S(1)} %pair_1.1.refs_6_), channel_id=1, source_target_pairs={{0,6},{1,7},{2,4},{3,5},{4,2},{5,3},{6,0},{7,1},{8,14},{9,15},{10,... | collective-permute-start | bytes 110600 | tf_op jit(solution)/shard_map/ppermute | solution.py:379
  37.4 4.0 %collective-permute-start.12 = (s16[144,128]{1,0:T(8,128)(2,1)S(1)}, s16[144,128]{1,0:T(8,128)(2,1)S(1)}, u32[]{:S(2)}, u32[]{:S(2)}) collective-permute-start(s16[144,128]{1,0:T(8,128)(2,1)S(1)} %pair_1.1.refs_6_), channel_id=1, source_target_pairs={{0,4},{1,5},{2,6},{3,7},{4,0},{5,1},{6,2},{7,3},{8,12},{9,13},{10,... | collective-permute-start | bytes 110600 | tf_op jit(solution)/shard_map/ppermute | solution.py:379
  37.9 4.0 %collective-permute-start.11 = (s16[144,128]{1,0:T(8,128)(2,1)S(1)}, s16[144,128]{1,0:T(8,128)(2,1)S(1)}, u32[]{:S(2)}, u32[]{:S(2)}) collective-permute-start(s16[144,128]{1,0:T(8,128)(2,1)S(1)} %pair_1.1.refs_6_), channel_id=1, source_target_pairs={{0,2},{1,3},{2,0},{3,1},{4,6},{5,7},{6,4},{7,5},{8,10},{9,11},{10,... | collective-permute-start | bytes 110600 | tf_op jit(solution)/shard_map/ppermute | solution.py:379
  42.7 6.2 %collective-permute-start.16 = (s16[160,128]{1,0:T(8,128)(2,1)S(1)}, s16[160,128]{1,0:T(8,128)(2,1)S(1)}, u32[]{:S(2)}, u32[]{:S(2)}) collective-permute-start(s16[160,128]{1,0:T(8,128)(2,1)S(1)} %get-tuple-element.70.refs_6_), channel_id=1, source_target_pairs={{0,24},{8,16},{16,8},{24,0},{1,25},{9,17},{17,9},{25,1},{2,26},{10... | collective-permute-start | bytes 122888 | tf_op jit(solution)/shard_map/ppermute | solution.py:379
  44.9 5.0 %collective-permute-start.15 = (s16[160,128]{1,0:T(8,128)(2,1)S(1)}, s16[160,128]{1,0:T(8,128)(2,1)S(1)}, u32[]{:S(2)}, u32[]{:S(2)}) collective-permute-start(s16[160,128]{1,0:T(8,128)(2,1)S(1)} %get-tuple-element.70.refs_6_), channel_id=1, source_target_pairs={{0,16},{8,24},{16,0},{24,8},{1,17},{9,25},{17,1},{25,9},{2,18},{10... | collective-permute-start | bytes 122888 | tf_op jit(solution)/shard_map/ppermute | solution.py:379
  45.4 4.4 %collective-permute-start.14 = (s16[160,128]{1,0:T(8,128)(2,1)S(1)}, s16[160,128]{1,0:T(8,128)(2,1)S(1)}, u32[]{:S(2)}, u32[]{:S(2)}) collective-permute-start(s16[160,128]{1,0:T(8,128)(2,1)S(1)} %get-tuple-element.70.refs_6_), channel_id=1, source_target_pairs={{0,8},{8,0},{16,24},{24,16},{1,9},{9,1},{17,25},{25,17},{2,10},{10... | collective-permute-start | bytes 122888 | tf_op jit(solution)/shard_map/ppermute | solution.py:379
  50.7 1.3 %collective-permute-start.17 = (f32[80,128]{1,0:T(8,128)S(1)}, f32[80,128]{1,0:T(8,128)S(1)}, u32[]{:S(2)}, u32[]{:S(2)}) collective-permute-start(f32[80,128]{1,0:T(8,128)S(1)} %get-tuple-element.78), channel_id=1, source_target_pairs={{0,1},{1,0},{2,3},{3,2},{4,5},{5,4},{6,7},{7,6},{8,9},{9,8},{10,11... | collective-permute-start | bytes 122888 | tf_op jit(solution)/shard_map/ppermute | solution.py:379
  52.0 4.2 %collective-permute-start.18 = (f32[32,128]{1,0:T(8,128)S(1)}, f32[32,128]{1,0:T(8,128)S(1)}, u32[]{:S(2)}, u32[]{:S(2)}) collective-permute-start(f32[32,128]{1,0:T(8,128)S(1)} %get-tuple-element.80), channel_id=1, source_target_pairs={{0,2},{1,3},{2,0},{3,1},{4,6},{5,7},{6,4},{7,5},{8,10},{9,11},{10,... | collective-permute-start | bytes 49160 | tf_op jit(solution)/shard_map/ppermute | solution.py:379
  53.5 3.7 %collective-permute-start.19 = (f32[32,128]{1,0:T(8,128)S(1)}, f32[32,128]{1,0:T(8,128)S(1)}, u32[]{:S(2)}, u32[]{:S(2)}) collective-permute-start(f32[32,128]{1,0:T(8,128)S(1)} %get-tuple-element.81), channel_id=1, source_target_pairs={{0,4},{1,5},{2,6},{3,7},{4,0},{5,1},{6,2},{7,3},{8,12},{9,13},{10,... | collective-permute-start | bytes 49160 | tf_op jit(solution)/shard_map/ppermute | solution.py:379
  55.1 4.6 %collective-permute-start.20 = (f32[32,128]{1,0:T(8,128)S(1)}, f32[32,128]{1,0:T(8,128)S(1)}, u32[]{:S(2)}, u32[]{:S(2)}) collective-permute-start(f32[32,128]{1,0:T(8,128)S(1)} %get-tuple-element.82), channel_id=1, source_target_pairs={{0,6},{1,7},{2,4},{3,5},{4,2},{5,3},{6,0},{7,1},{8,14},{9,15},{10,... | collective-permute-start | bytes 49160 | tf_op jit(solution)/shard_map/ppermute | solution.py:379

commit v11 on v10

--- a/solution.py
+++ b/solution.py
@@ -10,7 +10,7 @@
 
 LANES = 128
 EXTRA = 16
-BOUNDS = (0, 5, 11, 16)
+BOUNDS = (0, 6, 12, 16)
 SCALES = 16
 STEPS = 64.0
 LIMIT = 32760.0
@@ -470,6 +470,8 @@
     for step in reversed(range(iterations)):
         parts = exchange(parts, "row")
         kind = {0: "last", last: "sums", last - 1: "shares"}.get(step, "plain")
+        if kind == "sums":
+            parts = parts[::-1]
         groups = where + [sizes, (VMEM, turned), (VMEM, mask_x), (VMEM, parts)]
         groups += [(VMEM, adjoint_x), (VMEM, anchor_x)]
         body = functools.partial(primal_body, kind, step, n_row, n_col)
@@ -546,7 +548,7 @@
     dual_adjoint, gradients = run(
         functools.partial(last_body, scales),
         [(ANY, f32(share_y, LANES)), (ANY, f32(2))],
-        [sizes, (VMEM, parts), (VMEM, term_y), (VMEM, anchor_y)],
+        [sizes, (VMEM, parts[::-1]), (VMEM, term_y), (VMEM, anchor_y)],
         [
             scratch(share_y, LANES),
             pltpu.SMEM((2,), jnp.float32),

time: 60.5 us -> 59.1 us (0.977)
  waiting for transfers between devices: 23.7 us -> 22.1 us
    ppermute x21, waiting for transfers between devices: 23.7 us -> 22.1 us  [swap(): return lax.ppermute(array, axis, [(i, i ^ stride) for i in range(size)])]
  transfers between devices with their start and end apart: 21 -> 21, of which waited for: 17 -> 18; matrix products, arithmetic and copies ran while one was open for 1% -> 1% of each run, Pallas kernels for 2% -> 2%
where the time goes in v11:
time: 59.1 us; the launch traced here: 58.9 us
  starting transfers between devices  25.5 us (43%)
  waiting for transfers between devices  22.1 us (37%)
  Pallas kernels  9.2 us (16%)
  between operations  1.45 us (2%)
  local copies, waits for them, and re-layouts  0.67 us (1%)
    ppermute x21, starting transfers between devices, swap(): return lax.ppermute(array, axis, [(i, i ^ stride) for i in range(size)])  25.5 us
    ppermute x21, waiting for transfers between devices, swap(): return lax.ppermute(array, axis, [(i, i ^ stride) for i in range(size)])  22.1 us
    pallas_call x11, Pallas kernels, run(): pl.pallas_call(kernel, out_shape=shapes, in_specs=specs, out_specs=out_sp...  9.2 us
  transfers between devices with their start and end apart: 21, of which 18 were waited for; matrix products, arithmetic and copies ran while one was open for 1% of the time, Pallas kernels for 2%

profile of v11, /device:TPU:0, one launch (start us, length us, event | category | flops | bytes accessed | tf_op | source)
XLA Modules:
  0.0 58.9 jit_solution(14267782174708282298)
XLA Ops:
  1.3 0.0 copy-start.1
  1.3 0.0 copy-start.3
  1.3 2.9 %first.1 = (bf16[32,256,256]{2,1,0:T(8,128)(2,1)S(1)}, f32[128,128]{1,0:T(8,128)S(1)}, f32[128,128]{1,0:T(8,128)S(1)}, s32[1,1,32]{2,1,0:T(1,128)S(4)}, s32[1,1,...) custom-call(s32[1,1,32]{2,1,0:T(1,128)} %refs_0_.1, ...), custom_call_target="tpu_custom_call" | custom-call | flops 4194304 | bytes 4194304 | tf_op jit(solution)/shard_map/first/pallas_call | solution.py:364
  4.2 5.1 %collective-permute-start = (s16[240,128]{1,0:T(8,128)(2,1)S(1)}, s16[240,128]{1,0:T(8,128)(2,1)S(1)}, u32[]{:S(2)}, u32[]{:S(2)}) collective-permute-start(s16[240,128]{1,0:T(8,128)(2,1)S(1)} %get-tuple-element.51), channel_id=1, source_target_pairs={{0,24},{8,16},{16,8},{24,0},{1,25},{9,17},{17,9},{25,1},{2,26},{10... | collective-permute-start | bytes 184328 | tf_op jit(solution)/shard_map/ppermute | solution.py:379
  9.4 0.0 collective-permute-start.1
  9.4 0.6 %collective-permute-start.2 = (s16[240,128]{1,0:T(8,128)(2,1)S(1)}, s16[240,128]{1,0:T(8,128)(2,1)S(1)}, u32[]{:S(2)}, u32[]{:S(2)}) collective-permute-start(s16[240,128]{1,0:T(8,128)(2,1)S(1)} %get-tuple-element.53), channel_id=1, source_target_pairs={{0,8},{8,0},{16,24},{24,16},{1,9},{9,1},{17,25},{25,17},{2,10},{10... | collective-permute-start | bytes 184328 | tf_op jit(solution)/shard_map/ppermute | solution.py:379
  10.0 1.1 %turn.1 = (bf16[32,256,256]{2,1,0:T(8,128)(2,1)S(1)}, bf16[32,256,256]{2,1,0:T(8,128)(2,1)S(1)}) custom-call(bf16[32,256,256]{2,1,0:T(8,128)(2,1)S(1)} %get-tuple-element.49.refs_0_), custom_call_target="tpu_custom_call", output_to_operand_aliasing={{1}: (0, {})} | custom-call | flops 4194304 | bytes 4194304 | tf_op jit(solution)/shard_map/turn/pallas_call | solution.py:364
  11.1 0.7 %collective-permute-done.refs_6_ = s16[240,128]{1,0:T(8,128)(2,1)S(1)} collective-permute-done((s16[240,128]{1,0:T(8,128)(2,1)S(1)}, s16[240,128]{1,0:T(8,128)(2,1)S(1)}, u32[]{:S(2)}, u32[]{:S(2)}) %collective-permute-start) | collective-permute-done | bytes 61472 | tf_op jit(solution)/shard_map/ppermute | solution.py:379
  11.9 2.8 %collective-permute-done.1.refs_7_ = s16[240,128]{1,0:T(8,128)(2,1)S(1)} collective-permute-done((s16[240,128]{1,0:T(8,128)(2,1)S(1)}, s16[240,128]{1,0:T(8,128)(2,1)S(1)}, u32[]{:S(2)}, u32[]{:S(2)}) %collective-permute-start.1) | collective-permute-done | bytes 61472 | tf_op jit(solution)/shard_map/ppermute | solution.py:379
  14.7 0.0 collective-permute-done.2.refs_8_
  14.7 0.0 copy-done.1
  14.7 0.0 copy-done.3
  14.7 0.0 copy-start.2
  14.7 0.0 copy-start.4
  14.7 0.0 copy-start.5
  14.7 0.8 %primal_2.1 = (f32[128,128]{1,0:T(8,128)S(1)}, f32[128,128]{1,0:T(8,128)S(1)}, f32[128,128]{1,0:T(8,128)S(1)}, f32[128,128]{1,0:T(8,128)S(1)}, f32[96,128]{1,0:T(8,128)S(1)}, /*index=5*/bf16[32,256,256]{2,1,0:T(8,128)(2,1)S(1)}) custom-call(s32[1,1,32]{2,1,0:T(1,128)S(4)} %get-tuple-element.45.refs_0_, ...), custom_call_target="tpu_custom_call", output_to_operand_aliasing={{5}: (4, {})} | custom-call | flops 4194304 | bytes 4194304 | tf_op jit(solution)/shard_map/primal_2/pallas_call | solution.py:364
  15.5 0.0 collective-permute-start.3
  15.6 1.2 %collective-permute-done.3.refs_1_ = f32[128,128]{1,0:T(8,128)S(1)} collective-permute-done((f32[128,128]{1,0:T(8,128)S(1)}, f32[128,128]{1,0:T(8,128)S(1)}, u32[]{:S(2)}, u32[]{:S(2)}) %collective-permute-start.3) | collective-permute-done | bytes 65568 | tf_op jit(solution)/shard_map/ppermute | solution.py:379
  16.9 2.6 %collective-permute-start.6 = (s16[144,128]{1,0:T(8,128)(2,1)S(1)}, s16[144,128]{1,0:T(8,128)(2,1)S(1)}, u32[]{:S(2)}, u32[]{:S(2)}) collective-permute-start(s16[144,128]{1,0:T(8,128)(2,1)S(1)} %pair_2.1.refs_6_), channel_id=1, source_target_pairs={{0,6},{1,7},{2,4},{3,5},{4,2},{5,3},{6,0},{7,1},{8,14},{9,15},{10,... | collective-permute-start | bytes 110600 | tf_op jit(solution)/shard_map/ppermute | solution.py:379
  19.5 0.5 collective-permute-start.5
  20.0 0.5 collective-permute-start.4
  20.4 1.4 %collective-permute-done.6.refs_9_ = s16[144,128]{1,0:T(8,128)(2,1)S(1)} collective-permute-done((s16[144,128]{1,0:T(8,128)(2,1)S(1)}, s16[144,128]{1,0:T(8,128)(2,1)S(1)}, u32[]{:S(2)}, u32[]{:S(2)}) %collective-permute-start.6) | collective-permute-done | bytes 36896 | tf_op jit(solution)/shard_map/ppermute | solution.py:379
  21.8 1.6 %collective-permute-done.5.refs_8_ = s16[144,128]{1,0:T(8,128)(2,1)S(1)} collective-permute-done((s16[144,128]{1,0:T(8,128)(2,1)S(1)}, s16[144,128]{1,0:T(8,128)(2,1)S(1)}, u32[]{:S(2)}, u32[]{:S(2)}) %collective-permute-start.5) | collective-permute-done | bytes 36896 | tf_op jit(solution)/shard_map/ppermute | solution.py:379
  23.4 0.5 collective-permute-done.4.refs_7_
  23.9 0.0 copy-done
  23.9 0.9 %dual_1.1 = (f32[128,128]{1,0:T(8,128)S(1)}, f32[128,128]{1,0:T(8,128)S(1)}, s16[240,128]{1,0:T(8,128)(2,1)S(1)}, bf16[32,256,256]{2,1,0:T(8,128)(2,1)S(1)}) custom-call(s32[1,1,32]{2,1,0:T(1,128)S(4)} %get-tuple-element.45.refs_0_, s32[1,1,32]{2,1,0:T(1,128)S(4)} %get-tuple-element.46.refs_1_, ...), custom_call_target="tpu_custom_call", output_to_operand_aliasing={{3}: (4, {})} | custom-call | flops 4194304 | bytes 4194304 | tf_op jit(solution)/shard_map/dual_1/pallas_call | solution.py:364
  24.8 2.7 %collective-permute-start.9 = (s16[240,128]{1,0:T(8,128)(2,1)S(1)}, s16[240,128]{1,0:T(8,128)(2,1)S(1)}, u32[]{:S(2)}, u32[]{:S(2)}) collective-permute-start(s16[240,128]{1,0:T(8,128)(2,1)S(1)} %get-tuple-element.61.refs_6_), channel_id=1, source_target_pairs={{0,24},{8,16},{16,8},{24,0},{1,25},{9,17},{17,9},{25,1},{2,26},{10... | collective-permute-start | bytes 184328 | tf_op jit(solution)/shard_map/ppermute | solution.py:379
  27.5 0.0 collective-permute-start.8
  27.5 1.8 %collective-permute-start.7 = (s16[240,128]{1,0:T(8,128)(2,1)S(1)}, s16[240,128]{1,0:T(8,128)(2,1)S(1)}, u32[]{:S(2)}, u32[]{:S(2)}) collective-permute-start(s16[240,128]{1,0:T(8,128)(2,1)S(1)} %get-tuple-element.61.refs_6_), channel_id=1, source_target_pairs={{0,8},{8,0},{16,24},{24,16},{1,9},{9,1},{17,25},{25,17},{2,10},{10... | collective-permute-start | bytes 184328 | tf_op jit(solution)/shard_map/ppermute | solution.py:379
  29.3 2.2 %collective-permute-done.9.refs_9_ = s16[240,128]{1,0:T(8,128)(2,1)S(1)} collective-permute-done((s16[240,128]{1,0:T(8,128)(2,1)S(1)}, s16[240,128]{1,0:T(8,128)(2,1)S(1)}, u32[]{:S(2)}, u32[]{:S(2)}) %collective-permute-start.9) | collective-permute-done | bytes 61472 | tf_op jit(solution)/shard_map/ppermute | solution.py:379
  31.5 1.4 %collective-permute-done.8.refs_8_ = s16[240,128]{1,0:T(8,128)(2,1)S(1)} collective-permute-done((s16[240,128]{1,0:T(8,128)(2,1)S(1)}, s16[240,128]{1,0:T(8,128)(2,1)S(1)}, u32[]{:S(2)}, u32[]{:S(2)}) %collective-permute-start.8) | collective-permute-done | bytes 61472 | tf_op jit(solution)/shard_map/ppermute | solution.py:379
  32.9 0.0 collective-permute-done.7.refs_7_
  32.9 0.0 copy-done.2
  32.9 0.0 copy-done.4
  32.9 0.0 copy-done.5
  32.9 1.0 %primal_1.1 = (f32[128,128]{1,0:T(8,128)S(1)}, f32[128,128]{1,0:T(8,128)S(1)}, f32[128,128]{1,0:T(8,128)S(1)}, f32[128,128]{1,0:T(8,128)S(1)}, f32[3,128,128]{2,...) custom-call(s32[1,1,32]{2,1,0:T(1,128)S(4)} %get-tuple-element.45.re, ...), custom_call_target="tpu_custom_call", output_to_operand_aliasing={{6}: (4, {})} | custom-call | flops 4194304 | bytes 4194304 | tf_op jit(solution)/shard_map/primal_1/pallas_call | solution.py:364
  33.9 0.1 collective-permute-start.10
  34.0 1.2 %collective-permute-done.10.refs_1_ = f32[128,128]{1,0:T(8,128)S(1)} collective-permute-done((f32[128,128]{1,0:T(8,128)S(1)}, f32[128,128]{1,0:T(8,128)S(1)}, u32[]{:S(2)}, u32[]{:S(2)}) %collective-permute-start.10) | collective-permute-done | bytes 65568 | tf_op jit(solution)/shard_map/ppermute | solution.py:379
  35.3 0.1 pair_1.1.refs_6_
  35.3 1.6 %collective-permute-start.13 = (s16[144,128]{1,0:T(8,128)(2,1)S(1)}, s16[144,128]{1,0:T(8,128)(2,1)S(1)}, u32[]{:S(2)}, u32[]{:S(2)}) collective-permute-start(s16[144,128]{1,0:T(8,128)(2,1)S(1)} %pair_1.1.refs_6_), channel_id=1, source_target_pairs={{0,6},{1,7},{2,4},{3,5},{4,2},{5,3},{6,0},{7,1},{8,14},{9,15},{10,... | collective-permute-start | bytes 110600 | tf_op jit(solution)/shard_map/ppermute | solution.py:379
  36.9 0.4 collective-permute-start.12
  37.3 1.6 %collective-permute-start.11 = (s16[144,128]{1,0:T(8,128)(2,1)S(1)}, s16[144,128]{1,0:T(8,128)(2,1)S(1)}, u32[]{:S(2)}, u32[]{:S(2)}) collective-permute-start(s16[144,128]{1,0:T(8,128)(2,1)S(1)} %pair_1.1.refs_6_), channel_id=1, source_target_pairs={{0,2},{1,3},{2,0},{3,1},{4,6},{5,7},{6,4},{7,5},{8,10},{9,11},{10,... | collective-permute-start | bytes 110600 | tf_op jit(solution)/shard_map/ppermute | solution.py:379
  38.9 1.4 %collective-permute-done.13.refs_9_ = s16[144,128]{1,0:T(8,128)(2,1)S(1)} collective-permute-done((s16[144,128]{1,0:T(8,128)(2,1)S(1)}, s16[144,128]{1,0:T(8,128)(2,1)S(1)}, u32[]{:S(2)}, u32[]{:S(2)}) %collective-permute-start.13) | collective-permute-done | bytes 36896 | tf_op jit(solution)/shard_map/ppermute | solution.py:379
  40.2 0.6 %collective-permute-done.12.refs_8_ = s16[144,128]{1,0:T(8,128)(2,1)S(1)} collective-permute-done((s16[144,128]{1,0:T(8,128)(2,1)S(1)}, s16[144,128]{1,0:T(8,128)(2,1)S(1)}, u32[]{:S(2)}, u32[]{:S(2)}) %collective-permute-start.12) | collective-permute-done | bytes 36896 | tf_op jit(solution)/shard_map/ppermute | solution.py:379
  40.8 0.4 collective-permute-done.11.refs_7_
  41.3 0.0 copy-done.6
  41.3 0.9 %dual_0.1 = (f32[128,128]{1,0:T(8,128)S(1)}, f32[128,128]{1,0:T(8,128)S(1)}, s16[160,128]{1,0:T(8,128)(2,1)S(1)}, bf16[32,256,256]{2,1,0:T(8,128)(2,1)S(1)}) custom-call(s32[1,1,32]{2,1,0:T(1,128)S(4)} %get-tuple-element.45.refs_0_, s32[1,1,32]{2,1,0:T(1,128)S(4)} %get-tuple-element.46.refs_1_, ...), custom_call_target="tpu_custom_call", output_to_operand_aliasing={{3}: (4, {})} | custom-call | flops 4194304 | bytes 4194304 | tf_op jit(solution)/shard_map/dual_0/pallas_call | solution.py:364
  42.1 2.5 %collective-permute-start.16 = (s16[160,128]{1,0:T(8,128)(2,1)S(1)}, s16[160,128]{1,0:T(8,128)(2,1)S(1)}, u32[]{:S(2)}, u32[]{:S(2)}) collective-permute-start(s16[160,128]{1,0:T(8,128)(2,1)S(1)} %get-tuple-element.70.refs_6_), channel_id=1, source_target_pairs={{0,24},{8,16},{16,8},{24,0},{1,25},{9,17},{17,9},{25,1},{2,26},{10... | collective-permute-start | bytes 122888 | tf_op jit(solution)/shard_map/ppermute | solution.py:379
  44.6 0.0 collective-permute-start.15
  44.6 2.0 %collective-permute-start.14 = (s16[160,128]{1,0:T(8,128)(2,1)S(1)}, s16[160,128]{1,0:T(8,128)(2,1)S(1)}, u32[]{:S(2)}, u32[]{:S(2)}) collective-permute-start(s16[160,128]{1,0:T(8,128)(2,1)S(1)} %get-tuple-element.70.refs_6_), channel_id=1, source_target_pairs={{0,8},{8,0},{16,24},{24,16},{1,9},{9,1},{17,25},{25,17},{2,10},{10... | collective-permute-start | bytes 122888 | tf_op jit(solution)/shard_map/ppermute | solution.py:379
  46.6 1.6 %collective-permute-done.16.refs_9_ = s16[160,128]{1,0:T(8,128)(2,1)S(1)} collective-permute-done((s16[160,128]{1,0:T(8,128)(2,1)S(1)}, s16[160,128]{1,0:T(8,128)(2,1)S(1)}, u32[]{:S(2)}, u32[]{:S(2)}) %collective-permute-start.16) | collective-permute-done | bytes 40992 | tf_op jit(solution)/shard_map/ppermute | solution.py:379
  48.2 1.3 %collective-permute-done.15.refs_8_ = s16[160,128]{1,0:T(8,128)(2,1)S(1)} collective-permute-done((s16[160,128]{1,0:T(8,128)(2,1)S(1)}, s16[160,128]{1,0:T(8,128)(2,1)S(1)}, u32[]{:S(2)}, u32[]{:S(2)}) %collective-permute-start.15) | collective-permute-done | bytes 40992 | tf_op jit(solution)/shard_map/ppermute | solution.py:379
  49.5 0.0 collective-permute-done.14.refs_7_
  49.5 0.8 %primal_0.1 = (f32[128,128]{1,0:T(8,128)S(1)}, f32[80,128]{1,0:T(8,128)S(1)}, f32[80,128]{1,0:T(8,128)S(1)}, bf16[32,256,256]{2,1,0:T(8,128)(2,1)S(1)}) custom-call(s32[1,1,32]{2,1,0:T(1,128)S(4)} %get-tuple-element.45.refs_0_, s32[1,1,32]{2,1,0:T(1,128)S(4)} %get-tuple-element.46.refs_1_, ...), custom_call_target="tpu_custom_call", output_to_operand_aliasing={{3}: (4, {})} | custom-call | flops 4194304 | bytes 4194304 | tf_op jit(solution)/shard_map/primal_0/pallas_call | solution.py:364
  50.3 0.1 collective-permute-start.17
  50.4 1.2 %collective-permute-done.17.refs_1_ = f32[80,128]{1,0:T(8,128)S(1)} collective-permute-done((f32[80,128]{1,0:T(8,128)S(1)}, f32[80,128]{1,0:T(8,128)S(1)}, u32[]{:S(2)}, u32[]{:S(2)}) %collective-permute-start.17) | collective-permute-done | bytes 40992 | tf_op jit(solution)/shard_map/ppermute | solution.py:379
  51.6 2.4 %collective-permute-start.18 = (f32[32,128]{1,0:T(8,128)S(1)}, f32[32,128]{1,0:T(8,128)S(1)}, u32[]{:S(2)}, u32[]{:S(2)}) collective-permute-start(f32[32,128]{1,0:T(8,128)S(1)} %get-tuple-element.79), channel_id=1, source_target_pairs={{0,6},{1,7},{2,4},{3,5},{4,2},{5,3},{6,0},{7,1},{8,14},{9,15},{10,... | collective-permute-start | bytes 49160 | tf_op jit(solution)/shard_map/ppermute | solution.py:379
  54.0 0.5 collective-permute-start.19
  54.5 0.7 %collective-permute-start.20 = (f32[32,128]{1,0:T(8,128)S(1)}, f32[32,128]{1,0:T(8,128)S(1)}, u32[]{:S(2)}, u32[]{:S(2)}) collective-permute-start(f32[32,128]{1,0:T(8,128)S(1)} %get-tuple-element.81), channel_id=1, source_target_pairs={{0,2},{1,3},{2,0},{3,1},{4,6},{5,7},{6,4},{7,5},{8,10},{9,11},{10,... | collective-permute-start | bytes 49160 | tf_op jit(solution)/shard_map/ppermute | solution.py:379
  55.2 0.6 %copy.29 = f32[16384]{0:T(1024)} copy(f32[16384]{0:T(1024)S(1)} %bitcast.19) | data formatting | bytes 131072
  55.8 0.5 collective-permute-done.18.refs_1_
  56.3 1.4 %collective-permute-done.19.refs_2_ = f32[32,128]{1,0:T(8,128)S(1)} collective-permute-done((f32[32,128]{1,0:T(8,128)S(1)}, f32[32,128]{1,0:T(8,128)S(1)}, u32[]{:S(2)}, u32[]{:S(2)}) %collective-permute-start.19) | collective-permute-done | bytes 16416 | tf_op jit(solution)/shard_map/ppermute | solution.py:379
  57.8 0.5 collective-permute-done.20.refs_3_
  58.3 0.7 %last.1 = (f32[16,128]{1,0:T(8,128)}, f32[2]{0:T(128)}) custom-call(f32[2]{0:T(128)S(4)} %get-tuple-element.48.refs_3_.refs_0_, f32[32,128]{1,0:T(8,128)S(1)} %collective-permute-done.18.refs_1_, f32[32,128]{1,0:T(8,128)S(1)} %collective-permute-done.19.refs_2_, f32[32,128]{1,0:T(8,128)S(1)} %collective-permute-done.20.refs_3_, ...), custom_call_target="tpu_custom_call" | custom-call | tf_op jit(solution)/shard_map/last/pallas_call | solution.py:364
  (4 shorter events, 0.1 us)
Async XLA Ops:
  1.3 13.4 %copy-start.1 = (s32[3,16384]{1,0:T(4,128)S(1)}, s32[3,16384]{1,0:T(4,128)}, u32[]{:S(2)}) copy-start(s32[3,16384]{1,0:T(4,128)} %param.20) | copy-start | bytes 589828
  1.3 13.4 %copy-start.3 = (f32[16384]{0:T(1024)S(1)}, f32[16384]{0:T(1024)}, u32[]{:S(2)}) copy-start(f32[16384]{0:T(1024)} %param.26) | copy-start | bytes 196612
  4.2 7.6 %collective-permute-start = (s16[240,128]{1,0:T(8,128)(2,1)S(1)}, s16[240,128]{1,0:T(8,128)(2,1)S(1)}, u32[]{:S(2)}, u32[]{:S(2)}) collective-permute-start(s16[240,128]{1,0:T(8,128)(2,1)S(1)} %get-tuple-element.51), channel_id=1, source_target_pairs={{0,24},{8,16},{16,8},{24,0},{1,25},{9,17},{17,9},{25,1},{2,26},{10... | collective-permute-start | bytes 184328 | tf_op jit(solution)/shard_map/ppermute | solution.py:379
  9.4 5.3 %collective-permute-start.1 = (s16[240,128]{1,0:T(8,128)(2,1)S(1)}, s16[240,128]{1,0:T(8,128)(2,1)S(1)}, u32[]{:S(2)}, u32[]{:S(2)}) collective-permute-start(s16[240,128]{1,0:T(8,128)(2,1)S(1)} %get-tuple-element.52), channel_id=1, source_target_pairs={{0,16},{8,24},{16,0},{24,8},{1,17},{9,25},{17,1},{25,9},{2,18},{10... | collective-permute-start | bytes 184328 | tf_op jit(solution)/shard_map/ppermute | solution.py:379
  9.4 5.3 %collective-permute-start.2 = (s16[240,128]{1,0:T(8,128)(2,1)S(1)}, s16[240,128]{1,0:T(8,128)(2,1)S(1)}, u32[]{:S(2)}, u32[]{:S(2)}) collective-permute-start(s16[240,128]{1,0:T(8,128)(2,1)S(1)} %get-tuple-element.53), channel_id=1, source_target_pairs={{0,8},{8,0},{16,24},{24,16},{1,9},{9,1},{17,25},{25,17},{2,10},{10... | collective-permute-start | bytes 184328 | tf_op jit(solution)/shard_map/ppermute | solution.py:379
  10.0 13.9 %copy-start = (s32[3,16384]{1,0:T(4,128)S(1)}, s32[3,16384]{1,0:T(4,128)}, u32[]{:S(2)}) copy-start(s32[3,16384]{1,0:T(4,128)} %param.21) | copy-start | bytes 589828
  14.7 18.2 %copy-start.2 = (f32[3,16384]{1,0:T(4,128)S(1)}, f32[3,16384]{1,0:T(4,128)}, u32[]{:S(2)}) copy-start(f32[3,16384]{1,0:T(4,128)} %param.18) | copy-start | bytes 589828
  14.7 18.2 %copy-start.4 = (f32[16384]{0:T(1024)S(1)}, f32[16384]{0:T(1024)}, u32[]{:S(2)}) copy-start(f32[16384]{0:T(1024)} %param.22) | copy-start | bytes 196612
  14.7 18.2 %copy-start.5 = (f32[16384]{0:T(1024)S(1)}, f32[16384]{0:T(1024)}, u32[]{:S(2)}) copy-start(f32[16384]{0:T(1024)} %param.24) | copy-start | bytes 196612
  15.5 1.3 %collective-permute-start.3 = (f32[128,128]{1,0:T(8,128)S(1)}, f32[128,128]{1,0:T(8,128)S(1)}, u32[]{:S(2)}, u32[]{:S(2)}) collective-permute-start(f32[128,128]{1,0:T(8,128)S(1)} %get-tuple-element.57.refs_0_), channel_id=1, source_target_pairs={{0,1},{1,0},{2,3},{3,2},{4,5},{5,4},{6,7},{7,6},{8,9},{9,8},{10,11... | collective-permute-start | bytes 196616 | tf_op jit(solution)/shard_map/ppermute | solution.py:379
  16.9 4.9 %collective-permute-start.6 = (s16[144,128]{1,0:T(8,128)(2,1)S(1)}, s16[144,128]{1,0:T(8,128)(2,1)S(1)}, u32[]{:S(2)}, u32[]{:S(2)}) collective-permute-start(s16[144,128]{1,0:T(8,128)(2,1)S(1)} %pair_2.1.refs_6_), channel_id=1, source_target_pairs={{0,6},{1,7},{2,4},{3,5},{4,2},{5,3},{6,0},{7,1},{8,14},{9,15},{10,... | collective-permute-start | bytes 110600 | tf_op jit(solution)/shard_map/ppermute | solution.py:379
  19.5 4.0 %collective-permute-start.5 = (s16[144,128]{1,0:T(8,128)(2,1)S(1)}, s16[144,128]{1,0:T(8,128)(2,1)S(1)}, u32[]{:S(2)}, u32[]{:S(2)}) collective-permute-start(s16[144,128]{1,0:T(8,128)(2,1)S(1)} %pair_2.1.refs_6_), channel_id=1, source_target_pairs={{0,4},{1,5},{2,6},{3,7},{4,0},{5,1},{6,2},{7,3},{8,12},{9,13},{10,... | collective-permute-start | bytes 110600 | tf_op jit(solution)/shard_map/ppermute | solution.py:379
  20.0 4.0 %collective-permute-start.4 = (s16[144,128]{1,0:T(8,128)(2,1)S(1)}, s16[144,128]{1,0:T(8,128)(2,1)S(1)}, u32[]{:S(2)}, u32[]{:S(2)}) collective-permute-start(s16[144,128]{1,0:T(8,128)(2,1)S(1)} %pair_2.1.refs_6_), channel_id=1, source_target_pairs={{0,2},{1,3},{2,0},{3,1},{4,6},{5,7},{6,4},{7,5},{8,10},{9,11},{10,... | collective-permute-start | bytes 110600 | tf_op jit(solution)/shard_map/ppermute | solution.py:379
  23.9 17.3 %copy-start.6 = (f32[16384]{0:T(1024)S(1)}, f32[16384]{0:T(1024)}, u32[]{:S(2)}) copy-start(f32[16384]{0:T(1024)} %param.23) | copy-start | bytes 196612
  24.8 6.6 %collective-permute-start.9 = (s16[240,128]{1,0:T(8,128)(2,1)S(1)}, s16[240,128]{1,0:T(8,128)(2,1)S(1)}, u32[]{:S(2)}, u32[]{:S(2)}) collective-permute-start(s16[240,128]{1,0:T(8,128)(2,1)S(1)} %get-tuple-element.61.refs_6_), channel_id=1, source_target_pairs={{0,24},{8,16},{16,8},{24,0},{1,25},{9,17},{17,9},{25,1},{2,26},{10... | collective-permute-start | bytes 184328 | tf_op jit(solution)/shard_map/ppermute | solution.py:379
  27.5 5.4 %collective-permute-start.8 = (s16[240,128]{1,0:T(8,128)(2,1)S(1)}, s16[240,128]{1,0:T(8,128)(2,1)S(1)}, u32[]{:S(2)}, u32[]{:S(2)}) collective-permute-start(s16[240,128]{1,0:T(8,128)(2,1)S(1)} %get-tuple-element.61.refs_6_), channel_id=1, source_target_pairs={{0,16},{8,24},{16,0},{24,8},{1,17},{9,25},{17,1},{25,9},{2,18},{10... | collective-permute-start | bytes 184328 | tf_op jit(solution)/shard_map/ppermute | solution.py:379
  27.5 5.4 %collective-permute-start.7 = (s16[240,128]{1,0:T(8,128)(2,1)S(1)}, s16[240,128]{1,0:T(8,128)(2,1)S(1)}, u32[]{:S(2)}, u32[]{:S(2)}) collective-permute-start(s16[240,128]{1,0:T(8,128)(2,1)S(1)} %get-tuple-element.61.refs_6_), channel_id=1, source_target_pairs={{0,8},{8,0},{16,24},{24,16},{1,9},{9,1},{17,25},{25,17},{2,10},{10... | collective-permute-start | bytes 184328 | tf_op jit(solution)/shard_map/ppermute | solution.py:379
  33.9 1.3 %collective-permute-start.10 = (f32[128,128]{1,0:T(8,128)S(1)}, f32[128,128]{1,0:T(8,128)S(1)}, u32[]{:S(2)}, u32[]{:S(2)}) collective-permute-start(f32[128,128]{1,0:T(8,128)S(1)} %get-tuple-element.66.refs_0_), channel_id=1, source_target_pairs={{0,1},{1,0},{2,3},{3,2},{4,5},{5,4},{6,7},{7,6},{8,9},{9,8},{10,11... | collective-permute-start | bytes 196616 | tf_op jit(solution)/shard_map/ppermute | solution.py:379
  35.3 4.9 %collective-permute-start.13 = (s16[144,128]{1,0:T(8,128)(2,1)S(1)}, s16[144,128]{1,0:T(8,128)(2,1)S(1)}, u32[]{:S(2)}, u32[]{:S(2)}) collective-permute-start(s16[144,128]{1,0:T(8,128)(2,1)S(1)} %pair_1.1.refs_6_), channel_id=1, source_target_pairs={{0,6},{1,7},{2,4},{3,5},{4,2},{5,3},{6,0},{7,1},{8,14},{9,15},{10,... | collective-permute-start | bytes 110600 | tf_op jit(solution)/shard_map/ppermute | solution.py:379
  36.9 4.0 %collective-permute-start.12 = (s16[144,128]{1,0:T(8,128)(2,1)S(1)}, s16[144,128]{1,0:T(8,128)(2,1)S(1)}, u32[]{:S(2)}, u32[]{:S(2)}) collective-permute-start(s16[144,128]{1,0:T(8,128)(2,1)S(1)} %pair_1.1.refs_6_), channel_id=1, source_target_pairs={{0,4},{1,5},{2,6},{3,7},{4,0},{5,1},{6,2},{7,3},{8,12},{9,13},{10,... | collective-permute-start | bytes 110600 | tf_op jit(solution)/shard_map/ppermute | solution.py:379
  37.3 4.0 %collective-permute-start.11 = (s16[144,128]{1,0:T(8,128)(2,1)S(1)}, s16[144,128]{1,0:T(8,128)(2,1)S(1)}, u32[]{:S(2)}, u32[]{:S(2)}) collective-permute-start(s16[144,128]{1,0:T(8,128)(2,1)S(1)} %pair_1.1.refs_6_), channel_id=1, source_target_pairs={{0,2},{1,3},{2,0},{3,1},{4,6},{5,7},{6,4},{7,5},{8,10},{9,11},{10,... | collective-permute-start | bytes 110600 | tf_op jit(solution)/shard_map/ppermute | solution.py:379
  42.1 6.1 %collective-permute-start.16 = (s16[160,128]{1,0:T(8,128)(2,1)S(1)}, s16[160,128]{1,0:T(8,128)(2,1)S(1)}, u32[]{:S(2)}, u32[]{:S(2)}) collective-permute-start(s16[160,128]{1,0:T(8,128)(2,1)S(1)} %get-tuple-element.70.refs_6_), channel_id=1, source_target_pairs={{0,24},{8,16},{16,8},{24,0},{1,25},{9,17},{17,9},{25,1},{2,26},{10... | collective-permute-start | bytes 122888 | tf_op jit(solution)/shard_map/ppermute | solution.py:379
  44.6 4.9 %collective-permute-start.15 = (s16[160,128]{1,0:T(8,128)(2,1)S(1)}, s16[160,128]{1,0:T(8,128)(2,1)S(1)}, u32[]{:S(2)}, u32[]{:S(2)}) collective-permute-start(s16[160,128]{1,0:T(8,128)(2,1)S(1)} %get-tuple-element.70.refs_6_), channel_id=1, source_target_pairs={{0,16},{8,24},{16,0},{24,8},{1,17},{9,25},{17,1},{25,9},{2,18},{10... | collective-permute-start | bytes 122888 | tf_op jit(solution)/shard_map/ppermute | solution.py:379
  44.6 4.9 %collective-permute-start.14 = (s16[160,128]{1,0:T(8,128)(2,1)S(1)}, s16[160,128]{1,0:T(8,128)(2,1)S(1)}, u32[]{:S(2)}, u32[]{:S(2)}) collective-permute-start(s16[160,128]{1,0:T(8,128)(2,1)S(1)} %get-tuple-element.70.refs_6_), channel_id=1, source_target_pairs={{0,8},{8,0},{16,24},{24,16},{1,9},{9,1},{17,25},{25,17},{2,10},{10... | collective-permute-start | bytes 122888 | tf_op jit(solution)/shard_map/ppermute | solution.py:379
  50.3 1.3 %collective-permute-start.17 = (f32[80,128]{1,0:T(8,128)S(1)}, f32[80,128]{1,0:T(8,128)S(1)}, u32[]{:S(2)}, u32[]{:S(2)}) collective-permute-start(f32[80,128]{1,0:T(8,128)S(1)} %get-tuple-element.78), channel_id=1, source_target_pairs={{0,1},{1,0},{2,3},{3,2},{4,5},{5,4},{6,7},{7,6},{8,9},{9,8},{10,11... | collective-permute-start | bytes 122888 | tf_op jit(solution)/shard_map/ppermute | solution.py:379
  51.6 4.7 %collective-permute-start.18 = (f32[32,128]{1,0:T(8,128)S(1)}, f32[32,128]{1,0:T(8,128)S(1)}, u32[]{:S(2)}, u32[]{:S(2)}) collective-permute-start(f32[32,128]{1,0:T(8,128)S(1)} %get-tuple-element.79), channel_id=1, source_target_pairs={{0,6},{1,7},{2,4},{3,5},{4,2},{5,3},{6,0},{7,1},{8,14},{9,15},{10,... | collective-permute-start | bytes 49160 | tf_op jit(solution)/shard_map/ppermute | solution.py:379
  54.0 3.7 %collective-permute-start.19 = (f32[32,128]{1,0:T(8,128)S(1)}, f32[32,128]{1,0:T(8,128)S(1)}, u32[]{:S(2)}, u32[]{:S(2)}) collective-permute-start(f32[32,128]{1,0:T(8,128)S(1)} %get-tuple-element.80), channel_id=1, source_target_pairs={{0,4},{1,5},{2,6},{3,7},{4,0},{5,1},{6,2},{7,3},{8,12},{9,13},{10,... | collective-permute-start | bytes 49160 | tf_op jit(solution)/shard_map/ppermute | solution.py:379
  54.5 3.7 %collective-permute-start.20 = (f32[32,128]{1,0:T(8,128)S(1)}, f32[32,128]{1,0:T(8,128)S(1)}, u32[]{:S(2)}, u32[]{:S(2)}) collective-permute-start(f32[32,128]{1,0:T(8,128)S(1)} %get-tuple-element.81), channel_id=1, source_target_pairs={{0,2},{1,3},{2,0},{3,1},{4,6},{5,7},{6,4},{7,5},{8,10},{9,11},{10,... | collective-permute-start | bytes 49160 | tf_op jit(solution)/shard_map/ppermute | solution.py:379

commit v12 on v9

--- a/solution.py
+++ b/solution.py
@@ -10,7 +10,7 @@
 
 LANES = 128
 EXTRA = 16
-CHUNKS = 4
+BOUNDS = (0, 6, 12, 16)
 SCALES = 16
 STEPS = 64.0
 LIMIT = 32760.0
@@ -130,14 +130,15 @@
 
 
 def first_body(
-    step, rows_far, columns_far, count, tile_data, mask_far, cotangent_far, saved_far,
-    tiles, term, anchor, *refs
+    step, rows_far, columns_far, count, sizes_far, tile_data, mask_far, cotangent_far,
+    tiles, term, anchor, rows, columns, count_out, sizes, out,
+    source, total, mask, cotangent, arrived, ready,
 ):
-    out, saved_out, source, total, rows, columns, mask, cotangent, saved, arrived, ready = refs
+    count_out[0, 0] = count[0, 0]
     slots = tiles.shape[0]
-    chunk = slots // CHUNKS
-    pairs = [(mask_far, mask), (cotangent_far, cotangent), (saved_far, saved)]
-    pairs += [(rows_far, rows), (columns_far, columns)]
+    bounds = [slots * part // 16 for part in BOUNDS]
+    pairs = [(mask_far, mask), (cotangent_far, cotangent)]
+    pairs += [(rows_far, rows), (columns_far, columns), (sizes_far, sizes)]
     small = [
         pltpu.make_async_copy(far_ref, near, ready.at[spot])
         for spot, (far_ref, near) in enumerate(pairs)
@@ -146,11 +147,11 @@
         copy.start()
 
     def fetch(part):
-        span = pl.ds(part * chunk, chunk)
+        span = pl.ds(bounds[part], bounds[part + 1] - bounds[part])
         return pltpu.make_async_copy(tile_data.at[0, 0, span], tiles.at[span], arrived.at[part])
 
-    for part in range(CHUNKS):
-        fetch(part).start(priority=part % 2)
+    for part in range(len(BOUNDS) - 1):
+        fetch(part).start()
     total[...] = jnp.zeros_like(total)
     for copy in small:
         copy.wait()
@@ -159,17 +160,36 @@
     anchor[...] = (1.0 - weight) * adjoint
     value = mask[:, step, :].astype(jnp.float32) * weight * adjoint
     term[...] = value
-    source[0] = rounded(value)
-    iterations = source.shape[0] - 1
-    for vector in range(iterations):
-        source[vector + 1] = rounded(saved[:, vector, :])
-    for part in range(CHUNKS):
+    source[...] = rounded(value)
+    for part in range(len(BOUNDS) - 1):
         fetch(part).wait()
-        span = range(part * chunk, (part + 1) * chunk)
+        span = range(bounds[part], bounds[part + 1])
         add_products(rows, columns, count, tiles, span, source, total)
-    lines = total.shape[1]
-    write_payload(out, total[0])
-    saved_out[...] = total[1:].reshape(iterations * lines, LANES)
+    write_payload(out, total[...])
+
+
+def saved_back_body(rows, columns, count, tiles, saved, out, _, source, total):
+    for vector in range(source.shape[0]):
+        source[vector] = rounded(saved[:, vector, :])
+    total[...] = jnp.zeros_like(total)
+    add_products(rows, columns, count, tiles, range(tiles.shape[0]), source, total)
+    write_payload(out, total[...].reshape(-1, LANES))
+
+
+def saved_image_body(
+    rows, columns, count, sizes, tiles, parts, cost, upper, primal, reduced, images, _, source
+):
+    vectors, lines, _ = reduced.shape
+    scales = [scales_of(part)[0] for part in parts]
+    for vector in range(vectors):
+        at = slice(vector * lines, (vector + 1) * lines)
+        sums = tree_sum([long(part[at, :]) * scale for part, scale in zip(parts, scales)])
+        reduced[vector] = cost[...] - sums
+        saved = primal[:, vector, :]
+        half = jnp.minimum(jnp.maximum(saved - sizes[0] * reduced[vector], 0.0), upper[...])
+        source[vector] = rounded(2.0 * half - saved)
+    images[...] = jnp.zeros_like(images)
+    add_products(columns, rows, count, tiles, range(tiles.shape[0]), source, images)
 
 
 def turn_body(tiles, turned, _):
@@ -208,12 +228,10 @@
         out[lines:, :] = scale_rows([code])
 
 
-def primal_body(kind, step, n_row, n_col, rows, columns, count, sizes, tiles, mask, parts, before, anchor, *refs):
-    last = kind == "last"
+def primal_body(step, n_col, rows, columns, count, sizes, tiles, mask, parts, before, anchor, *refs):
+    last = step == 0
     if last:
         reduced, terms, final, mine, other, _, source, out = refs
-    elif kind == "saved":
-        gathered, cost, upper, primal, term, adjoint_out, anchor_out, out, reduced, images, _, source, total = refs
     else:
         term, adjoint_out, anchor_out, out, _, source = refs
     sigma = sizes[1]
@@ -234,23 +252,6 @@
         adjoint_out[...] = after
         anchor_out[...] = anchored
     all_slots = range(tiles.shape[0])
-    if kind == "saved":
-        iterations = reduced.shape[0]
-        size = iterations * lines
-        for vector in range(iterations):
-            at = slice(vector * lines, (vector + 1) * lines)
-            sums = [gathered[part, at, :] for part in range(n_row)]
-            reduced[vector] = cost[...] - tree_sum(sums)
-        source[0] = rounded(value)
-        for vector in range(iterations):
-            saved = primal[:, vector, :]
-            half = jnp.minimum(jnp.maximum(saved - sizes[0] * reduced[vector], 0.0), upper[...])
-            source[vector + 1] = rounded(2.0 * half - saved)
-        total[...] = jnp.zeros_like(total)
-        add_products(columns, rows, count, tiles, all_slots, source, total)
-        out[...] = total[0]
-        images[...] = total[1:]
-        return
     source[...] = rounded(value)
     out[...] = jnp.zeros_like(out)
     add_products(columns, rows, count, tiles, all_slots, source, out)
@@ -410,28 +411,37 @@
 
     mask_x, mask_y = lines(primal_mask), lines(dual_mask)
     full_x, full_y = f32(lines_x, LANES), f32(lines_y, LANES)
-    where = [(SMEM, tile_row_block), (SMEM, tile_column_block), (SMEM, tile_count)]
-    saved = lines(saved_dual)
-    tiles, term_y, anchor_y, part, saved_part = run(
+    index = (SMEM, pltpu.SMEM(tile_row_block.shape, jnp.int32))
+    tiles, term_y, anchor_y, *held, part = run(
         functools.partial(first_body, last),
-        [pltpu.VMEM((slots, width, width), jnp.bfloat16), full_y, full_y]
-        + [row_part(0), scratch(iterations * lines_x, LANES)],
+        [pltpu.VMEM((slots, width, width), jnp.bfloat16), full_y, full_y, index, index]
+        + [(SMEM, pltpu.SMEM((1, 1), jnp.int32)), (SMEM, pltpu.SMEM((2,), jnp.float32))]
+        + [row_part(0)],
         [(ANY, far(tile_row_block)), (ANY, far(tile_column_block)), (SMEM, tile_count)]
-        + [(ANY, far(tile_data)), (ANY, far(mask_y)), (ANY, far(lines(dual_cotangent)))]
-        + [(ANY, far(saved))],
+        + [(ANY, far(step_sizes)), (ANY, far(tile_data))]
+        + [(ANY, far(mask_y)), (ANY, far(lines(dual_cotangent)))],
         [
-            scratch(iterations + 1, lines_y, LANES),
-            scratch(iterations + 1, lines_x, LANES),
-            pltpu.SMEM(tile_row_block.shape, jnp.int32),
-            pltpu.SMEM(tile_row_block.shape, jnp.int32),
+            scratch(lines_y, LANES),
+            scratch(lines_x, LANES),
             pltpu.VMEM(mask_y.shape, jnp.int32),
             scratch(lines_y, LANES),
-            scratch(*saved.shape),
-            pltpu.SemaphoreType.DMA((CHUNKS,)),
+            pltpu.SemaphoreType.DMA((len(BOUNDS) - 1,)),
             pltpu.SemaphoreType.DMA((5,)),
         ],
         "first",
         cost,
+    )
+    *where, sizes = [
+        (SMEM, pltpu.with_memory_space_constraint(array, pltpu.SMEM)) for array in held
+    ]
+    saved_part, tiles = run(
+        saved_back_body,
+        [row_part((iterations - 1) * lines_x)],
+        where + [(VMEM, tiles), (VMEM, lines(saved_dual))],
+        [scratch(iterations, lines_y, LANES), scratch(iterations, lines_x, LANES)],
+        "saved_back",
+        cost,
+        tiles,
     )
     turned, tiles = run(
         turn_body,
@@ -442,34 +452,37 @@
         cost,
         tiles,
     )
+    saved_parts = [saved_part] + [None] * (n_row - 1)
     adjoint_x, anchor_x = lines(primal_cotangent), None
     terms_x, terms_y = [], [term_y]
     parts = [part] * n_row
-    gathered = lax.all_gather(saved_part, "row")
     reduced = images = None
+    pending = list(range(n_row - 1, 0, -1))
+
+    def send_saved(parts, count):
+        for _ in range(count):
+            parts[-1], own = lax.optimization_barrier((parts[-1], saved_part))
+            offset = pending.pop(0)
+            saved_parts[offset] = swap(own, "row", offset)
+
     for step in reversed(range(iterations)):
         parts = exchange(parts, "row")
-        kind = {0: "last", last - 1: "saved"}.get(step, "plain")
-        groups = where + [(SMEM, step_sizes), (VMEM, turned), (VMEM, mask_x), (VMEM, parts)]
+        if step < last:
+            send_saved(parts, len(pending))
+        groups = where + [sizes, (VMEM, turned), (VMEM, mask_x), (VMEM, parts[::-1])]
         groups += [(VMEM, adjoint_x), (VMEM, anchor_x)]
-        body = functools.partial(primal_body, kind, step, n_row, n_col)
+        body = functools.partial(primal_body, step, n_col)
         if step == 0:
             break
-        outs = [full_x, full_x, full_x, full_y]
-        extra = [scratch(lines_x, LANES)]
-        if kind == "saved":
-            outs += [f32(iterations, lines_x, LANES), f32(iterations, lines_y, LANES)]
-            groups += [(VMEM, gathered), (VMEM, lines(cost_vector)), (VMEM, lines(upper_bound))]
-            groups += [(VMEM, lines(saved_primal))]
-            extra = [
-                scratch(iterations + 1, lines_x, LANES),
-                scratch(iterations + 1, lines_y, LANES),
-            ]
-        term_x, adjoint_x, anchor_x, partial, *more, turned = run(
-            body, outs, groups, extra, f"primal_{step}", cost, turned
+        term_x, adjoint_x, anchor_x, partial, turned = run(
+            body,
+            [full_x, full_x, full_x, full_y],
+            groups,
+            [scratch(lines_x, LANES)],
+            f"primal_{step}",
+            cost,
+            turned,
         )
-        if kind == "saved":
-            reduced, images = more
         terms_x.insert(0, term_x)
         part = run(
             pair_body,
@@ -479,7 +492,22 @@
             f"pair_{step}",
         )[0]
         parts = exchange([part] * n_chip, "col", 2)
-        groups = where + [(SMEM, step_sizes), (VMEM, tiles), (VMEM, mask_y), (VMEM, parts)]
+        if step == last:
+            send_saved(parts, 1 + len(pending) // 3)
+        if step == 1:
+            reduced, images, turned = run(
+                saved_image_body,
+                [f32(iterations, lines_x, LANES), f32(iterations, lines_y, LANES)],
+                where
+                + [sizes, (VMEM, turned), (VMEM, saved_parts)]
+                + [(VMEM, lines(cost_vector)), (VMEM, lines(upper_bound))]
+                + [(VMEM, lines(saved_primal))],
+                [scratch(iterations, lines_x, LANES)],
+                "saved_image",
+                cost,
+                turned,
+            )
+        groups = where + [sizes, (VMEM, tiles), (VMEM, mask_y), (VMEM, parts[::-1])]
         groups += [(VMEM, term_y), (VMEM, anchor_y)]
         if step == 1:
             groups += [(VMEM, lines(demand)), (VMEM, images), (VMEM, list(terms_y))]
@@ -520,7 +548,7 @@
     dual_adjoint, gradients = run(
         functools.partial(last_body, scales),
         [(ANY, f32(share_y, LANES)), (ANY, f32(2))],
-        [(SMEM, step_sizes), (VMEM, parts), (VMEM, term_y), (VMEM, anchor_y)],
+        [sizes, (VMEM, parts[::-1]), (VMEM, term_y), (VMEM, anchor_y)],
         [
             scratch(share_y, LANES),
             pltpu.SMEM((2,), jnp.float32),

time: 76.8 us -> 59.5 us (0.77)
  blocking collectives: 17.7 us -> 0 us
  starting transfers between devices: 25.5 us -> 29 us
  Pallas kernels: 12.6 us -> 10.8 us
  waiting for transfers between devices: 18.7 us -> 17.5 us
    all_gather x1 -> x0, blocking collectives: 17.7 us -> none  [local(): gathered = lax.all_gather(saved_part, 'row')]
    ppermute x21 -> x24, starting transfers between devices: 25.5 us -> 29 us  [swap(): return lax.ppermute(array, axis, [(i, i ^ stride) for i in range(size)])]
    pallas_call x11 -> x13, Pallas kernels: 12.6 us -> 10.8 us  [run(): pl.pallas_call(kernel, out_shape=shapes, in_specs=specs, out_specs=out_sp...]
    ppermute x21 -> x24, waiting for transfers between devices: 18.7 us -> 17.5 us  [swap(): return lax.ppermute(array, axis, [(i, i ^ stride) for i in range(size)])]
  transfers between devices with their start and end apart: 21 -> 24, of which waited for: 15 -> 16; matrix products, arithmetic and copies ran while one was open for 1% -> 1% of each run, Pallas kernels for 1% -> 7%
where the time goes in v12:
time: 59.5 us; the launch traced here: 59.3 us
  starting transfers between devices  29 us (49%)
  waiting for transfers between devices  17.5 us (29%)
  Pallas kernels  10.8 us (18%)
  between operations  1.49 us (3%)
  local copies, waits for them, and re-layouts  0.67 us (1%)
    ppermute x24, starting transfers between devices, swap(): return lax.ppermute(array, axis, [(i, i ^ stride) for i in range(size)])  29 us
    ppermute x24, waiting for transfers between devices, swap(): return lax.ppermute(array, axis, [(i, i ^ stride) for i in range(size)])  17.5 us
    pallas_call x13, Pallas kernels, run(): pl.pallas_call(kernel, out_shape=shapes, in_specs=specs, out_specs=out_sp...  10.8 us
  transfers between devices with their start and end apart: 24, of which 16 were waited for; matrix products, arithmetic and copies ran while one was open for 1% of the time, Pallas kernels for 7%

profile of v12, /device:TPU:0, one launch (start us, length us, event | category | flops | bytes accessed | tf_op | source)
XLA Modules:
  0.0 59.3 jit_solution(9158194380699434592)
XLA Ops:
  0.6 0.0 copy-start.3
  1.3 2.7 %first.1 = (bf16[32,256,256]{2,1,0:T(8,128)(2,1)S(1)}, f32[128,128]{1,0:T(8,128)S(1)}, f32[128,128]{1,0:T(8,128)S(1)}, s32[1,1,32]{2,1,0:T(1,128)S(4)}, s32[1,1,...) custom-call(s32[1,1,32]{2,1,0:T(1,128)} %refs_0_.1, s32[1,1,32]{2,1,0:T(1,128)} %refs_1_.1, ...), custom_call_target="tpu_custom_call" | custom-call | flops 4194304 | bytes 4194304 | tf_op jit(solution)/shard_map/first/pallas_call | solution.py:347
  4.1 5.1 %collective-permute-start = (s16[144,128]{1,0:T(8,128)(2,1)S(1)}, s16[144,128]{1,0:T(8,128)(2,1)S(1)}, u32[]{:S(2)}, u32[]{:S(2)}) collective-permute-start(s16[144,128]{1,0:T(8,128)(2,1)S(1)} %get-tuple-element.57.refs_9_), channel_id=1, source_target_pairs={{0,24},{8,16},{16,8},{24,0},{1,25},{9,17},{17,9},{25,1},{2,26},{10... | collective-permute-start | bytes 110600 | tf_op jit(solution)/shard_map/ppermute | solution.py:362
  9.2 0.0 collective-permute-start.1
  9.2 0.6 %collective-permute-start.2 = (s16[144,128]{1,0:T(8,128)(2,1)S(1)}, s16[144,128]{1,0:T(8,128)(2,1)S(1)}, u32[]{:S(2)}, u32[]{:S(2)}) collective-permute-start(s16[144,128]{1,0:T(8,128)(2,1)S(1)} %get-tuple-element.57.refs_9_), channel_id=1, source_target_pairs={{0,8},{8,0},{16,24},{24,16},{1,9},{9,1},{17,25},{25,17},{2,10},{10... | collective-permute-start | bytes 110600 | tf_op jit(solution)/shard_map/ppermute | solution.py:362
  9.8 0.0 copy-done.3
  9.8 1.1 %saved_back.1 = (s16[400,128]{1,0:T(8,128)(2,1)S(1)}, bf16[32,256,256]{2,1,0:T(8,128)(2,1)S(1)}) custom-call(s32[1,1,32]{2,1,0:T(1,128)S(4)} %get-tuple-element.50.refs_0_, s32[1,1,32]{2,1,0:T(1,128)S(4)} %get-tuple-element.51.refs_1_, s32[1,1]{1,0:T(1,128)S(4)} %get-tuple-element.52.refs_2_, ...), custom_call_target="tpu_custom_call", output_to_operand_aliasing={{1}: (3, {})} | custom-call | flops 4194304 | bytes 4194304 | tf_op jit(solution)/shard_map/saved_back/pallas_call | solution.py:347
  10.9 0.0 copy-start
  10.9 1.1 %turn.1 = (bf16[32,256,256]{2,1,0:T(8,128)(2,1)S(1)}, bf16[32,256,256]{2,1,0:T(8,128)(2,1)S(1)}) custom-call(bf16[32,256,256]{2,1,0:T(8,128)(2,1)S(1)} %get-tuple-element.55.refs_0_), custom_call_target="tpu_custom_call", output_to_operand_aliasing={{1}: (0, {})} | custom-call | flops 4194304 | bytes 4194304 | tf_op jit(solution)/shard_map/turn/pallas_call | solution.py:347
  12.1 0.0 collective-permute-done.refs_6_
  12.1 2.0 %collective-permute-done.1.refs_7_ = s16[144,128]{1,0:T(8,128)(2,1)S(1)} collective-permute-done((s16[144,128]{1,0:T(8,128)(2,1)S(1)}, s16[144,128]{1,0:T(8,128)(2,1)S(1)}, u32[]{:S(2)}, u32[]{:S(2)}) %collective-permute-start.1) | collective-permute-done | bytes 36896 | tf_op jit(solution)/shard_map/ppermute | solution.py:362
  14.1 0.0 collective-permute-done.2.refs_8_
  14.1 0.0 copy-done.1
  14.1 0.8 %primal_2.1 = (f32[128,128]{1,0:T(8,128)S(1)}, f32[128,128]{1,0:T(8,128)S(1)}, f32[128,128]{1,0:T(8,128)S(1)}, f32[128,128]{1,0:T(8,128)S(1)}, bf16[32,256,256]{2,1,0:T(8,128)(2,1)S(1)}) custom-call(s32[1,1,32]{2,1,0:T(1,128)S(4)} %get-tuple-element.50.refs_0_, s32[1,1,32]{2,1,0:T(1,128)S(4)} %get-tuple-element.51.refs_1_, ...), custom_call_target="tpu_custom_call", output_to_operand_aliasing={{4}: (4, {})} | custom-call | flops 4194304 | bytes 4194304 | tf_op jit(solution)/shard_map/primal_2/pallas_call | solution.py:347
  14.9 0.0 collective-permute-start.3
  14.9 1.2 %collective-permute-done.3.refs_1_ = f32[128,128]{1,0:T(8,128)S(1)} collective-permute-done((f32[128,128]{1,0:T(8,128)S(1)}, f32[128,128]{1,0:T(8,128)S(1)}, u32[]{:S(2)}, u32[]{:S(2)}) %collective-permute-start.3) | collective-permute-done | bytes 65568 | tf_op jit(solution)/shard_map/ppermute | solution.py:362
  16.2 2.5 %collective-permute-start.4 = (s16[144,128]{1,0:T(8,128)(2,1)S(1)}, s16[144,128]{1,0:T(8,128)(2,1)S(1)}, u32[]{:S(2)}, u32[]{:S(2)}) collective-permute-start(s16[144,128]{1,0:T(8,128)(2,1)S(1)} %pair_2.1.refs_9_), channel_id=1, source_target_pairs={{0,6},{1,7},{2,4},{3,5},{4,2},{5,3},{6,0},{7,1},{8,14},{9,15},{10,... | collective-permute-start | bytes 110600 | tf_op jit(solution)/shard_map/ppermute | solution.py:362
  18.7 0.5 collective-permute-start.5
  19.2 0.5 collective-permute-start.6
  19.8 1.4 %collective-permute-done.4.refs_6_ = s16[144,128]{1,0:T(8,128)(2,1)S(1)} collective-permute-done((s16[144,128]{1,0:T(8,128)(2,1)S(1)}, s16[144,128]{1,0:T(8,128)(2,1)S(1)}, u32[]{:S(2)}, u32[]{:S(2)}) %collective-permute-start.4) | collective-permute-done | bytes 36896 | tf_op jit(solution)/shard_map/ppermute | solution.py:362
  21.1 1.5 %collective-permute-done.5.refs_7_ = s16[144,128]{1,0:T(8,128)(2,1)S(1)} collective-permute-done((s16[144,128]{1,0:T(8,128)(2,1)S(1)}, s16[144,128]{1,0:T(8,128)(2,1)S(1)}, u32[]{:S(2)}, u32[]{:S(2)}) %collective-permute-start.5) | collective-permute-done | bytes 36896 | tf_op jit(solution)/shard_map/ppermute | solution.py:362
  22.7 0.5 collective-permute-done.6.refs_8_
  23.2 0.9 %dual_1.1 = (f32[128,128]{1,0:T(8,128)S(1)}, f32[128,128]{1,0:T(8,128)S(1)}, s16[144,128]{1,0:T(8,128)(2,1)S(1)}, bf16[32,256,256]{2,1,0:T(8,128)(2,1)S(1)}) custom-call(s32[1,1,32]{2,1,0:T(1,128)S(4)} %get-tuple-element.50.refs_0_, s32[1,1,32]{2,1,0:T(1,128)S(4)} %get-tuple-element.51.refs_1_, ...), custom_call_target="tpu_custom_call", output_to_operand_aliasing={{3}: (4, {})} | custom-call | flops 4194304 | bytes 4194304 | tf_op jit(solution)/shard_map/dual_1/pallas_call | solution.py:347
  24.1 1.9 %collective-permute-start.7 = (s16[144,128]{1,0:T(8,128)(2,1)S(1)}, s16[144,128]{1,0:T(8,128)(2,1)S(1)}, u32[]{:S(2)}, u32[]{:S(2)}) collective-permute-start(s16[144,128]{1,0:T(8,128)(2,1)S(1)} %get-tuple-element.66.refs_9_), channel_id=1, source_target_pairs={{0,24},{8,16},{16,8},{24,0},{1,25},{9,17},{17,9},{25,1},{2,26},{10... | collective-permute-start | bytes 110600 | tf_op jit(solution)/shard_map/ppermute | solution.py:362
  25.9 0.3 collective-permute-start.8
  26.2 2.3 %collective-permute-start.9 = (s16[144,128]{1,0:T(8,128)(2,1)S(1)}, s16[144,128]{1,0:T(8,128)(2,1)S(1)}, u32[]{:S(2)}, u32[]{:S(2)}) collective-permute-start(s16[144,128]{1,0:T(8,128)(2,1)S(1)} %get-tuple-element.66.refs_9_), channel_id=1, source_target_pairs={{0,8},{8,0},{16,24},{24,16},{1,9},{9,1},{17,25},{25,17},{2,10},{10... | collective-permute-start | bytes 110600 | tf_op jit(solution)/shard_map/ppermute | solution.py:362
  28.5 1.1 %collective-permute-start.11 = (s16[400,128]{1,0:T(8,128)(2,1)S(1)}, s16[400,128]{1,0:T(8,128)(2,1)S(1)}, u32[]{:S(2)}, u32[]{:S(2)}) collective-permute-start(s16[400,128]{1,0:T(8,128)(2,1)S(1)} %get-tuple-element.73.refs_5_), channel_id=1, source_target_pairs={{0,16},{8,24},{16,0},{24,8},{1,17},{9,25},{17,1},{25,9},{2,18},{10... | collective-permute-start | bytes 307208 | tf_op jit(solution)/shard_map/ppermute | solution.py:362
  29.6 1.2 %collective-permute-start.12 = (s16[400,128]{1,0:T(8,128)(2,1)S(1)}, s16[400,128]{1,0:T(8,128)(2,1)S(1)}, u32[]{:S(2)}, u32[]{:S(2)}) collective-permute-start(s16[400,128]{1,0:T(8,128)(2,1)S(1)} %get-tuple-element.73.refs_5_), channel_id=1, source_target_pairs={{0,24},{8,16},{16,8},{24,0},{1,25},{9,17},{17,9},{25,1},{2,26},{10... | collective-permute-start | bytes 307208 | tf_op jit(solution)/shard_map/ppermute | solution.py:362
  30.9 0.0 collective-permute-done.7.refs_6_
  30.9 1.1 %collective-permute-start.10 = (s16[400,128]{1,0:T(8,128)(2,1)S(1)}, s16[400,128]{1,0:T(8,128)(2,1)S(1)}, u32[]{:S(2)}, u32[]{:S(2)}) collective-permute-start(s16[400,128]{1,0:T(8,128)(2,1)S(1)} %get-tuple-element.73.refs_5_), channel_id=1, source_target_pairs={{0,8},{8,0},{16,24},{24,16},{1,9},{9,1},{17,25},{25,17},{2,10},{10... | collective-permute-start | bytes 307208 | tf_op jit(solution)/shard_map/ppermute | solution.py:362
  32.0 1.9 %collective-permute-done.8.refs_7_ = s16[144,128]{1,0:T(8,128)(2,1)S(1)} collective-permute-done((s16[144,128]{1,0:T(8,128)(2,1)S(1)}, s16[144,128]{1,0:T(8,128)(2,1)S(1)}, u32[]{:S(2)}, u32[]{:S(2)}) %collective-permute-start.8) | collective-permute-done | bytes 36896 | tf_op jit(solution)/shard_map/ppermute | solution.py:362
  33.9 0.0 collective-permute-done.9.refs_8_
  33.9 0.8 %primal_1.1 = (f32[128,128]{1,0:T(8,128)S(1)}, f32[128,128]{1,0:T(8,128)S(1)}, f32[128,128]{1,0:T(8,128)S(1)}, f32[128,128]{1,0:T(8,128)S(1)}, bf16[32,256,256]{2,1,0:T(8,128)(2,1)S(1)}) custom-call(s32[1,1,32]{2,1,0:T(1,128)S(4)} %get-tuple-element.50.refs_0_, s32[1,1,32]{2,1,0:T(1,128)S(4)} %get-tuple-element.51.refs_1_, ...), custom_call_target="tpu_custom_call", output_to_operand_aliasing={{4}: (4, {})} | custom-call | flops 4194304 | bytes 4194304 | tf_op jit(solution)/shard_map/primal_1/pallas_call | solution.py:347
  34.7 0.0 collective-permute-start.13
  34.7 1.2 %collective-permute-done.13.refs_1_ = f32[128,128]{1,0:T(8,128)S(1)} collective-permute-done((f32[128,128]{1,0:T(8,128)S(1)}, f32[128,128]{1,0:T(8,128)S(1)}, u32[]{:S(2)}, u32[]{:S(2)}) %collective-permute-start.13) | collective-permute-done | bytes 65568 | tf_op jit(solution)/shard_map/ppermute | solution.py:362
  36.0 0.1 pair_1.1.refs_9_
  36.0 1.7 %collective-permute-start.14 = (s16[144,128]{1,0:T(8,128)(2,1)S(1)}, s16[144,128]{1,0:T(8,128)(2,1)S(1)}, u32[]{:S(2)}, u32[]{:S(2)}) collective-permute-start(s16[144,128]{1,0:T(8,128)(2,1)S(1)} %pair_1.1.refs_9_), channel_id=1, source_target_pairs={{0,6},{1,7},{2,4},{3,5},{4,2},{5,3},{6,0},{7,1},{8,14},{9,15},{10,... | collective-permute-start | bytes 110600 | tf_op jit(solution)/shard_map/ppermute | solution.py:362
  37.8 0.6 collective-permute-start.15
  38.3 0.0 collective-permute-done.11.refs_7_
  38.3 1.3 %collective-permute-start.16 = (s16[144,128]{1,0:T(8,128)(2,1)S(1)}, s16[144,128]{1,0:T(8,128)(2,1)S(1)}, u32[]{:S(2)}, u32[]{:S(2)}) collective-permute-start(s16[144,128]{1,0:T(8,128)(2,1)S(1)} %pair_1.1.refs_9_), channel_id=1, source_target_pairs={{0,2},{1,3},{2,0},{3,1},{4,6},{5,7},{6,4},{7,5},{8,10},{9,11},{10,... | collective-permute-start | bytes 110600 | tf_op jit(solution)/shard_map/ppermute | solution.py:362
  39.6 0.0 collective-permute-done.12.refs_8_
  39.6 0.0 collective-permute-done.10.refs_6_
  39.6 0.9 %saved_image.1 = (f32[3,128,128]{2,1,0:T(8,128)S(1)}, f32[3,128,128]{2,1,0:T(8,128)S(1)}, bf16[32,256,256]{2,1,0:T(8,128)(2,1)S(1)}) custom-call(s32[1,1,32]{2,1,0:T(1,128)S(4)} %get-tuple-element.50.refs_0_, s32[1,1,32]{2,1,0:T(1,128)S(4)} %get-tuple-element.51.refs_1_, s32[1,1]{1,0:T(1,128)S(4)} %get-tuple-element.52.refs_2_, ...), custom_call_target="tpu_custom_call", output_to_operand_aliasing={{2}: (4, {})} | custom-call | flops 4194304 | bytes 4194304 | tf_op jit(solution)/shard_map/saved_image/pallas_call | solution.py:347
  40.5 0.5 collective-permute-done.14.refs_6_
  41.0 0.7 %collective-permute-done.15.refs_7_ = s16[144,128]{1,0:T(8,128)(2,1)S(1)} collective-permute-done((s16[144,128]{1,0:T(8,128)(2,1)S(1)}, s16[144,128]{1,0:T(8,128)(2,1)S(1)}, u32[]{:S(2)}, u32[]{:S(2)}) %collective-permute-start.15) | collective-permute-done | bytes 36896 | tf_op jit(solution)/shard_map/ppermute | solution.py:362
  41.7 0.6 collective-permute-done.16.refs_8_
  42.3 0.9 %dual_0.1 = (f32[128,128]{1,0:T(8,128)S(1)}, f32[128,128]{1,0:T(8,128)S(1)}, s16[160,128]{1,0:T(8,128)(2,1)S(1)}, bf16[32,256,256]{2,1,0:T(8,128)(2,1)S(1)}) custom-call(s32[1,1,32]{2,1,0:T(1,128)S(4)} %get-tuple-element.50.refs_0_, s32[1,1,32]{2,1,0:T(1,128)S(4)} %get-tuple-element.51.refs_1_, ...), custom_call_target="tpu_custom_call", output_to_operand_aliasing={{3}: (4, {})} | custom-call | flops 4194304 | bytes 4194304 | tf_op jit(solution)/shard_map/dual_0/pallas_call | solution.py:347
  43.2 1.8 %collective-permute-start.17 = (s16[160,128]{1,0:T(8,128)(2,1)S(1)}, s16[160,128]{1,0:T(8,128)(2,1)S(1)}, u32[]{:S(2)}, u32[]{:S(2)}) collective-permute-start(s16[160,128]{1,0:T(8,128)(2,1)S(1)} %get-tuple-element.80.refs_9_), channel_id=1, source_target_pairs={{0,24},{8,16},{16,8},{24,0},{1,25},{9,17},{17,9},{25,1},{2,26},{10... | collective-permute-start | bytes 122888 | tf_op jit(solution)/shard_map/ppermute | solution.py:362
  45.0 0.0 collective-permute-start.18
  45.0 2.6 %collective-permute-start.19 = (s16[160,128]{1,0:T(8,128)(2,1)S(1)}, s16[160,128]{1,0:T(8,128)(2,1)S(1)}, u32[]{:S(2)}, u32[]{:S(2)}) collective-permute-start(s16[160,128]{1,0:T(8,128)(2,1)S(1)} %get-tuple-element.80.refs_9_), channel_id=1, source_target_pairs={{0,8},{8,0},{16,24},{24,16},{1,9},{9,1},{17,25},{25,17},{2,10},{10... | collective-permute-start | bytes 122888 | tf_op jit(solution)/shard_map/ppermute | solution.py:362
  47.6 1.4 %collective-permute-done.17.refs_6_ = s16[160,128]{1,0:T(8,128)(2,1)S(1)} collective-permute-done((s16[160,128]{1,0:T(8,128)(2,1)S(1)}, s16[160,128]{1,0:T(8,128)(2,1)S(1)}, u32[]{:S(2)}, u32[]{:S(2)}) %collective-permute-start.17) | collective-permute-done | bytes 40992 | tf_op jit(solution)/shard_map/ppermute | solution.py:362
  49.0 1.0 %collective-permute-done.18.refs_7_ = s16[160,128]{1,0:T(8,128)(2,1)S(1)} collective-permute-done((s16[160,128]{1,0:T(8,128)(2,1)S(1)}, s16[160,128]{1,0:T(8,128)(2,1)S(1)}, u32[]{:S(2)}, u32[]{:S(2)}) %collective-permute-start.18) | collective-permute-done | bytes 40992 | tf_op jit(solution)/shard_map/ppermute | solution.py:362
  50.0 0.0 collective-permute-done.19.refs_8_
  50.0 0.8 %primal_0.1 = (f32[128,128]{1,0:T(8,128)S(1)}, f32[80,128]{1,0:T(8,128)S(1)}, f32[80,128]{1,0:T(8,128)S(1)}, bf16[32,256,256]{2,1,0:T(8,128)(2,1)S(1)}) custom-call(s32[1,1,32]{2,1,0:T(1,128)S(4)} %get-tuple-element.50.refs_0_, s32[1,1,32]{2,1,0:T(1,128)S(4)} %get-tuple-element.51.refs_1_, ...), custom_call_target="tpu_custom_call", output_to_operand_aliasing={{3}: (4, {})} | custom-call | flops 4194304 | bytes 4194304 | tf_op jit(solution)/shard_map/primal_0/pallas_call | solution.py:347
  50.9 0.1 collective-permute-start.20
  50.9 1.2 %collective-permute-done.20.refs_1_ = f32[80,128]{1,0:T(8,128)S(1)} collective-permute-done((f32[80,128]{1,0:T(8,128)S(1)}, f32[80,128]{1,0:T(8,128)S(1)}, u32[]{:S(2)}, u32[]{:S(2)}) %collective-permute-start.20) | collective-permute-done | bytes 40992 | tf_op jit(solution)/shard_map/ppermute | solution.py:362
  52.2 2.5 %collective-permute-start.21 = (f32[32,128]{1,0:T(8,128)S(1)}, f32[32,128]{1,0:T(8,128)S(1)}, u32[]{:S(2)}, u32[]{:S(2)}) collective-permute-start(f32[32,128]{1,0:T(8,128)S(1)} %get-tuple-element.89), channel_id=1, source_target_pairs={{0,6},{1,7},{2,4},{3,5},{4,2},{5,3},{6,0},{7,1},{8,14},{9,15},{10,... | collective-permute-start | bytes 49160 | tf_op jit(solution)/shard_map/ppermute | solution.py:362
  54.7 0.2 collective-permute-start.22
  54.9 0.8 %collective-permute-start.23 = (f32[32,128]{1,0:T(8,128)S(1)}, f32[32,128]{1,0:T(8,128)S(1)}, u32[]{:S(2)}, u32[]{:S(2)}) collective-permute-start(f32[32,128]{1,0:T(8,128)S(1)} %get-tuple-element.91), channel_id=1, source_target_pairs={{0,2},{1,3},{2,0},{3,1},{4,6},{5,7},{6,4},{7,5},{8,10},{9,11},{10,... | collective-permute-start | bytes 49160 | tf_op jit(solution)/shard_map/ppermute | solution.py:362
  55.7 0.6 %copy.33 = f32[16384]{0:T(1024)} copy(f32[16384]{0:T(1024)S(1)} %bitcast.19) | data formatting | bytes 131072
  56.3 0.5 collective-permute-done.21.refs_1_
  56.9 1.6 %collective-permute-done.22.refs_2_ = f32[32,128]{1,0:T(8,128)S(1)} collective-permute-done((f32[32,128]{1,0:T(8,128)S(1)}, f32[32,128]{1,0:T(8,128)S(1)}, u32[]{:S(2)}, u32[]{:S(2)}) %collective-permute-start.22) | collective-permute-done | bytes 16416 | tf_op jit(solution)/shard_map/ppermute | solution.py:362
  58.4 0.2 collective-permute-done.23.refs_3_
  58.7 0.7 %last.1 = (f32[16,128]{1,0:T(8,128)}, f32[2]{0:T(128)}) custom-call(f32[2]{0:T(128)S(4)} %get-tuple-element.53.refs_3_.refs_0_, f32[32,128]{1,0:T(8,128)S(1)} %collective-permute-done.21.refs_1_, f32[32,128]{1,0:T(8,128)S(1)} %collective-permute-done.22.refs_2_, f32[32,128]{1,0:T(8,128)S(1)} %collective-permute-done.23.refs_3_, ...), custom_call_target="tpu_custom_call" | custom-call | tf_op jit(solution)/shard_map/last/pallas_call | solution.py:347
  (14 shorter events, 0.1 us)
Async XLA Ops:
  0.6 9.2 %copy-start.3 = (f32[3,16384]{1,0:T(4,128)S(1)}, f32[3,16384]{1,0:T(4,128)}, u32[]{:S(2)}) copy-start(f32[3,16384]{1,0:T(4,128)} %param.19) | copy-start | bytes 589828
  4.1 8.0 %collective-permute-start = (s16[144,128]{1,0:T(8,128)(2,1)S(1)}, s16[144,128]{1,0:T(8,128)(2,1)S(1)}, u32[]{:S(2)}, u32[]{:S(2)}) collective-permute-start(s16[144,128]{1,0:T(8,128)(2,1)S(1)} %get-tuple-element.57.refs_9_), channel_id=1, source_target_pairs={{0,24},{8,16},{16,8},{24,0},{1,25},{9,17},{17,9},{25,1},{2,26},{10... | collective-permute-start | bytes 110600 | tf_op jit(solution)/shard_map/ppermute | solution.py:362
  9.2 4.9 %collective-permute-start.1 = (s16[144,128]{1,0:T(8,128)(2,1)S(1)}, s16[144,128]{1,0:T(8,128)(2,1)S(1)}, u32[]{:S(2)}, u32[]{:S(2)}) collective-permute-start(s16[144,128]{1,0:T(8,128)(2,1)S(1)} %get-tuple-element.57.refs_9_), channel_id=1, source_target_pairs={{0,16},{8,24},{16,0},{24,8},{1,17},{9,25},{17,1},{25,9},{2,18},{10... | collective-permute-start | bytes 110600 | tf_op jit(solution)/shard_map/ppermute | solution.py:362
  9.2 4.9 %collective-permute-start.2 = (s16[144,128]{1,0:T(8,128)(2,1)S(1)}, s16[144,128]{1,0:T(8,128)(2,1)S(1)}, u32[]{:S(2)}, u32[]{:S(2)}) collective-permute-start(s16[144,128]{1,0:T(8,128)(2,1)S(1)} %get-tuple-element.57.refs_9_), channel_id=1, source_target_pairs={{0,8},{8,0},{16,24},{24,16},{1,9},{9,1},{17,25},{25,17},{2,10},{10... | collective-permute-start | bytes 110600 | tf_op jit(solution)/shard_map/ppermute | solution.py:362
  9.8 4.2 %copy-start.1 = (s32[3,16384]{1,0:T(4,128)S(1)}, s32[3,16384]{1,0:T(4,128)}, u32[]{:S(2)}) copy-start(s32[3,16384]{1,0:T(4,128)} %param.20) | copy-start | bytes 589828
  9.8 4.2 %copy-start.4 = (f32[16384]{0:T(1024)S(1)}, f32[16384]{0:T(1024)}, u32[]{:S(2)}) copy-start(f32[16384]{0:T(1024)} %param.26) | copy-start | bytes 196612
  10.9 12.3 %copy-start = (s32[3,16384]{1,0:T(4,128)S(1)}, s32[3,16384]{1,0:T(4,128)}, u32[]{:S(2)}) copy-start(s32[3,16384]{1,0:T(4,128)} %param.21) | copy-start | bytes 589828
  14.9 1.3 %collective-permute-start.3 = (f32[128,128]{1,0:T(8,128)S(1)}, f32[128,128]{1,0:T(8,128)S(1)}, u32[]{:S(2)}, u32[]{:S(2)}) collective-permute-start(f32[128,128]{1,0:T(8,128)S(1)} %get-tuple-element.60.refs_0_), channel_id=1, source_target_pairs={{0,1},{1,0},{2,3},{3,2},{4,5},{5,4},{6,7},{7,6},{8,9},{9,8},{10,11... | collective-permute-start | bytes 196616 | tf_op jit(solution)/shard_map/ppermute | solution.py:362
  16.2 4.9 %collective-permute-start.4 = (s16[144,128]{1,0:T(8,128)(2,1)S(1)}, s16[144,128]{1,0:T(8,128)(2,1)S(1)}, u32[]{:S(2)}, u32[]{:S(2)}) collective-permute-start(s16[144,128]{1,0:T(8,128)(2,1)S(1)} %pair_2.1.refs_9_), channel_id=1, source_target_pairs={{0,6},{1,7},{2,4},{3,5},{4,2},{5,3},{6,0},{7,1},{8,14},{9,15},{10,... | collective-permute-start | bytes 110600 | tf_op jit(solution)/shard_map/ppermute | solution.py:362
  18.7 4.0 %collective-permute-start.5 = (s16[144,128]{1,0:T(8,128)(2,1)S(1)}, s16[144,128]{1,0:T(8,128)(2,1)S(1)}, u32[]{:S(2)}, u32[]{:S(2)}) collective-permute-start(s16[144,128]{1,0:T(8,128)(2,1)S(1)} %pair_2.1.refs_9_), channel_id=1, source_target_pairs={{0,4},{1,5},{2,6},{3,7},{4,0},{5,1},{6,2},{7,3},{8,12},{9,13},{10,... | collective-permute-start | bytes 110600 | tf_op jit(solution)/shard_map/ppermute | solution.py:362
  19.2 4.0 %collective-permute-start.6 = (s16[144,128]{1,0:T(8,128)(2,1)S(1)}, s16[144,128]{1,0:T(8,128)(2,1)S(1)}, u32[]{:S(2)}, u32[]{:S(2)}) collective-permute-start(s16[144,128]{1,0:T(8,128)(2,1)S(1)} %pair_2.1.refs_9_), channel_id=1, source_target_pairs={{0,2},{1,3},{2,0},{3,1},{4,6},{5,7},{6,4},{7,5},{8,10},{9,11},{10,... | collective-permute-start | bytes 110600 | tf_op jit(solution)/shard_map/ppermute | solution.py:362
  23.2 16.4 %copy-start.2 = (f32[3,16384]{1,0:T(4,128)S(1)}, f32[3,16384]{1,0:T(4,128)}, u32[]{:S(2)}) copy-start(f32[3,16384]{1,0:T(4,128)} %param.18) | copy-start | bytes 589828
  23.2 16.4 %copy-start.5 = (f32[16384]{0:T(1024)S(1)}, f32[16384]{0:T(1024)}, u32[]{:S(2)}) copy-start(f32[16384]{0:T(1024)} %param.22) | copy-start | bytes 196612
  23.2 16.4 %copy-start.6 = (f32[16384]{0:T(1024)S(1)}, f32[16384]{0:T(1024)}, u32[]{:S(2)}) copy-start(f32[16384]{0:T(1024)} %param.24) | copy-start | bytes 196612
  24.1 6.8 %collective-permute-start.7 = (s16[144,128]{1,0:T(8,128)(2,1)S(1)}, s16[144,128]{1,0:T(8,128)(2,1)S(1)}, u32[]{:S(2)}, u32[]{:S(2)}) collective-permute-start(s16[144,128]{1,0:T(8,128)(2,1)S(1)} %get-tuple-element.66.refs_9_), channel_id=1, source_target_pairs={{0,24},{8,16},{16,8},{24,0},{1,25},{9,17},{17,9},{25,1},{2,26},{10... | collective-permute-start | bytes 110600 | tf_op jit(solution)/shard_map/ppermute | solution.py:362
  25.9 7.9 %collective-permute-start.8 = (s16[144,128]{1,0:T(8,128)(2,1)S(1)}, s16[144,128]{1,0:T(8,128)(2,1)S(1)}, u32[]{:S(2)}, u32[]{:S(2)}) collective-permute-start(s16[144,128]{1,0:T(8,128)(2,1)S(1)} %get-tuple-element.66.refs_9_), channel_id=1, source_target_pairs={{0,16},{8,24},{16,0},{24,8},{1,17},{9,25},{17,1},{25,9},{2,18},{10... | collective-permute-start | bytes 110600 | tf_op jit(solution)/shard_map/ppermute | solution.py:362
  26.2 7.6 %collective-permute-start.9 = (s16[144,128]{1,0:T(8,128)(2,1)S(1)}, s16[144,128]{1,0:T(8,128)(2,1)S(1)}, u32[]{:S(2)}, u32[]{:S(2)}) collective-permute-start(s16[144,128]{1,0:T(8,128)(2,1)S(1)} %get-tuple-element.66.refs_9_), channel_id=1, source_target_pairs={{0,8},{8,0},{16,24},{24,16},{1,9},{9,1},{17,25},{25,17},{2,10},{10... | collective-permute-start | bytes 110600 | tf_op jit(solution)/shard_map/ppermute | solution.py:362
  28.5 9.8 %collective-permute-start.11 = (s16[400,128]{1,0:T(8,128)(2,1)S(1)}, s16[400,128]{1,0:T(8,128)(2,1)S(1)}, u32[]{:S(2)}, u32[]{:S(2)}) collective-permute-start(s16[400,128]{1,0:T(8,128)(2,1)S(1)} %get-tuple-element.73.refs_5_), channel_id=1, source_target_pairs={{0,16},{8,24},{16,0},{24,8},{1,17},{9,25},{17,1},{25,9},{2,18},{10... | collective-permute-start | bytes 307208 | tf_op jit(solution)/shard_map/ppermute | solution.py:362
  29.6 9.9 %collective-permute-start.12 = (s16[400,128]{1,0:T(8,128)(2,1)S(1)}, s16[400,128]{1,0:T(8,128)(2,1)S(1)}, u32[]{:S(2)}, u32[]{:S(2)}) collective-permute-start(s16[400,128]{1,0:T(8,128)(2,1)S(1)} %get-tuple-element.73.refs_5_), channel_id=1, source_target_pairs={{0,24},{8,16},{16,8},{24,0},{1,25},{9,17},{17,9},{25,1},{2,26},{10... | collective-permute-start | bytes 307208 | tf_op jit(solution)/shard_map/ppermute | solution.py:362
  30.9 8.7 %collective-permute-start.10 = (s16[400,128]{1,0:T(8,128)(2,1)S(1)}, s16[400,128]{1,0:T(8,128)(2,1)S(1)}, u32[]{:S(2)}, u32[]{:S(2)}) collective-permute-start(s16[400,128]{1,0:T(8,128)(2,1)S(1)} %get-tuple-element.73.refs_5_), channel_id=1, source_target_pairs={{0,8},{8,0},{16,24},{24,16},{1,9},{9,1},{17,25},{25,17},{2,10},{10... | collective-permute-start | bytes 307208 | tf_op jit(solution)/shard_map/ppermute | solution.py:362
  33.9 8.4 %copy-start.7 = (f32[16384]{0:T(1024)S(1)}, f32[16384]{0:T(1024)}, u32[]{:S(2)}) copy-start(f32[16384]{0:T(1024)} %param.23) | copy-start | bytes 196612
  34.7 1.3 %collective-permute-start.13 = (f32[128,128]{1,0:T(8,128)S(1)}, f32[128,128]{1,0:T(8,128)S(1)}, u32[]{:S(2)}, u32[]{:S(2)}) collective-permute-start(f32[128,128]{1,0:T(8,128)S(1)} %get-tuple-element.76.refs_0_), channel_id=1, source_target_pairs={{0,1},{1,0},{2,3},{3,2},{4,5},{5,4},{6,7},{7,6},{8,9},{9,8},{10,11... | collective-permute-start | bytes 196616 | tf_op jit(solution)/shard_map/ppermute | solution.py:362
  36.0 5.0 %collective-permute-start.14 = (s16[144,128]{1,0:T(8,128)(2,1)S(1)}, s16[144,128]{1,0:T(8,128)(2,1)S(1)}, u32[]{:S(2)}, u32[]{:S(2)}) collective-permute-start(s16[144,128]{1,0:T(8,128)(2,1)S(1)} %pair_1.1.refs_9_), channel_id=1, source_target_pairs={{0,6},{1,7},{2,4},{3,5},{4,2},{5,3},{6,0},{7,1},{8,14},{9,15},{10,... | collective-permute-start | bytes 110600 | tf_op jit(solution)/shard_map/ppermute | solution.py:362
  37.8 4.0 %collective-permute-start.15 = (s16[144,128]{1,0:T(8,128)(2,1)S(1)}, s16[144,128]{1,0:T(8,128)(2,1)S(1)}, u32[]{:S(2)}, u32[]{:S(2)}) collective-permute-start(s16[144,128]{1,0:T(8,128)(2,1)S(1)} %pair_1.1.refs_9_), channel_id=1, source_target_pairs={{0,4},{1,5},{2,6},{3,7},{4,0},{5,1},{6,2},{7,3},{8,12},{9,13},{10,... | collective-permute-start | bytes 110600 | tf_op jit(solution)/shard_map/ppermute | solution.py:362
  38.3 4.0 %collective-permute-start.16 = (s16[144,128]{1,0:T(8,128)(2,1)S(1)}, s16[144,128]{1,0:T(8,128)(2,1)S(1)}, u32[]{:S(2)}, u32[]{:S(2)}) collective-permute-start(s16[144,128]{1,0:T(8,128)(2,1)S(1)} %pair_1.1.refs_9_), channel_id=1, source_target_pairs={{0,2},{1,3},{2,0},{3,1},{4,6},{5,7},{6,4},{7,5},{8,10},{9,11},{10,... | collective-permute-start | bytes 110600 | tf_op jit(solution)/shard_map/ppermute | solution.py:362
  43.2 5.9 %collective-permute-start.17 = (s16[160,128]{1,0:T(8,128)(2,1)S(1)}, s16[160,128]{1,0:T(8,128)(2,1)S(1)}, u32[]{:S(2)}, u32[]{:S(2)}) collective-permute-start(s16[160,128]{1,0:T(8,128)(2,1)S(1)} %get-tuple-element.80.refs_9_), channel_id=1, source_target_pairs={{0,24},{8,16},{16,8},{24,0},{1,25},{9,17},{17,9},{25,1},{2,26},{10... | collective-permute-start | bytes 122888 | tf_op jit(solution)/shard_map/ppermute | solution.py:362
  45.0 5.0 %collective-permute-start.18 = (s16[160,128]{1,0:T(8,128)(2,1)S(1)}, s16[160,128]{1,0:T(8,128)(2,1)S(1)}, u32[]{:S(2)}, u32[]{:S(2)}) collective-permute-start(s16[160,128]{1,0:T(8,128)(2,1)S(1)} %get-tuple-element.80.refs_9_), channel_id=1, source_target_pairs={{0,16},{8,24},{16,0},{24,8},{1,17},{9,25},{17,1},{25,9},{2,18},{10... | collective-permute-start | bytes 122888 | tf_op jit(solution)/shard_map/ppermute | solution.py:362
  45.0 5.0 %collective-permute-start.19 = (s16[160,128]{1,0:T(8,128)(2,1)S(1)}, s16[160,128]{1,0:T(8,128)(2,1)S(1)}, u32[]{:S(2)}, u32[]{:S(2)}) collective-permute-start(s16[160,128]{1,0:T(8,128)(2,1)S(1)} %get-tuple-element.80.refs_9_), channel_id=1, source_target_pairs={{0,8},{8,0},{16,24},{24,16},{1,9},{9,1},{17,25},{25,17},{2,10},{10... | collective-permute-start | bytes 122888 | tf_op jit(solution)/shard_map/ppermute | solution.py:362
  50.9 1.3 %collective-permute-start.20 = (f32[80,128]{1,0:T(8,128)S(1)}, f32[80,128]{1,0:T(8,128)S(1)}, u32[]{:S(2)}, u32[]{:S(2)}) collective-permute-start(f32[80,128]{1,0:T(8,128)S(1)} %get-tuple-element.88), channel_id=1, source_target_pairs={{0,1},{1,0},{2,3},{3,2},{4,5},{5,4},{6,7},{7,6},{8,9},{9,8},{10,11... | collective-permute-start | bytes 122888 | tf_op jit(solution)/shard_map/ppermute | solution.py:362
  52.2 4.7 %collective-permute-start.21 = (f32[32,128]{1,0:T(8,128)S(1)}, f32[32,128]{1,0:T(8,128)S(1)}, u32[]{:S(2)}, u32[]{:S(2)}) collective-permute-start(f32[32,128]{1,0:T(8,128)S(1)} %get-tuple-element.89), channel_id=1, source_target_pairs={{0,6},{1,7},{2,4},{3,5},{4,2},{5,3},{6,0},{7,1},{8,14},{9,15},{10,... | collective-permute-start | bytes 49160 | tf_op jit(solution)/shard_map/ppermute | solution.py:362
  54.7 3.7 %collective-permute-start.22 = (f32[32,128]{1,0:T(8,128)S(1)}, f32[32,128]{1,0:T(8,128)S(1)}, u32[]{:S(2)}, u32[]{:S(2)}) collective-permute-start(f32[32,128]{1,0:T(8,128)S(1)} %get-tuple-element.90), channel_id=1, source_target_pairs={{0,4},{1,5},{2,6},{3,7},{4,0},{5,1},{6,2},{7,3},{8,12},{9,13},{10,... | collective-permute-start | bytes 49160 | tf_op jit(solution)/shard_map/ppermute | solution.py:362
  54.9 3.7 %collective-permute-start.23 = (f32[32,128]{1,0:T(8,128)S(1)}, f32[32,128]{1,0:T(8,128)S(1)}, u32[]{:S(2)}, u32[]{:S(2)}) collective-permute-start(f32[32,128]{1,0:T(8,128)S(1)} %get-tuple-element.91), channel_id=1, source_target_pairs={{0,2},{1,3},{2,0},{3,1},{4,6},{5,7},{6,4},{7,5},{8,10},{9,11},{10,... | collective-permute-start | bytes 49160 | tf_op jit(solution)/shard_map/ppermute | solution.py:362

commit v13 on v12

--- a/solution.py
+++ b/solution.py
@@ -312,7 +312,7 @@
     return pltpu.with_memory_space_constraint(array, pltpu.HBM)
 
 
-def run(body, out_shape, groups, scratch, name, cost=None, tiles=None):
+def run(body, out_shape, groups, scratch, name, cost=None, tiles=None, handed=None):
     flat, specs, widths, aliases = [], [], [], {}
     for spec, value in groups:
         if value is None:
@@ -321,6 +321,8 @@
         many = isinstance(value, (list, tuple))
         widths.append(len(value) if many else 0)
         for array in value if many else [value]:
+            if array is handed:
+                aliases[len(flat)] = 0
             if array is tiles:
                 aliases[len(flat)] = len(out_shape)
                 array = pltpu.with_memory_space_constraint(array, pltpu.VMEM)
@@ -459,17 +461,25 @@
     reduced = images = None
     pending = list(range(n_row - 1, 0, -1))
 
-    def send_saved(parts, count):
+    def send_saved(own, after, count):
+        (own,) = run(
+            lambda *refs: None,
+            [jax.ShapeDtypeStruct(own.shape, own.dtype)],
+            [(VMEM, own), (VMEM, after)],
+            [],
+            f"after_{len(pending)}",
+            handed=own,
+        )
         for _ in range(count):
-            parts[-1], own = lax.optimization_barrier((parts[-1], saved_part))
             offset = pending.pop(0)
             saved_parts[offset] = swap(own, "row", offset)
+        saved_parts[0] = own
 
     for step in reversed(range(iterations)):
         parts = exchange(parts, "row")
-        if step < last:
-            send_saved(parts, len(pending))
-        groups = where + [sizes, (VMEM, turned), (VMEM, mask_x), (VMEM, parts[::-1])]
+        if step < last and pending:
+            send_saved(saved_parts[0], saved_parts[n_row - 1], len(pending))
+        groups = where + [sizes, (VMEM, turned), (VMEM, mask_x), (VMEM, parts)]
         groups += [(VMEM, adjoint_x), (VMEM, anchor_x)]
         body = functools.partial(primal_body, step, n_col)
         if step == 0:
@@ -493,7 +503,8 @@
         )[0]
         parts = exchange([part] * n_chip, "col", 2)
         if step == last:
-            send_saved(parts, 1 + len(pending) // 3)
+            saved_parts[pending[0]] = swap(saved_part, "row", pending[0])
+            pending = pending[1:]
         if step == 1:
             reduced, images, turned = run(
                 saved_image_body,
@@ -507,7 +518,7 @@
                 cost,
                 turned,
             )
-        groups = where + [sizes, (VMEM, tiles), (VMEM, mask_y), (VMEM, parts[::-1])]
+        groups = where + [sizes, (VMEM, tiles), (VMEM, mask_y), (VMEM, parts)]
         groups += [(VMEM, term_y), (VMEM, anchor_y)]
         if step == 1:
             groups += [(VMEM, lines(demand)), (VMEM, images), (VMEM, list(terms_y))]

time: 59.5 us -> 58.5 us (0.983)
  waiting for transfers between devices: 17.5 us -> 15.4 us
  starting transfers between devices: 29 us -> 29.9 us
    ppermute x24, waiting for transfers between devices: 17.5 us -> 15.4 us  [swap(): return lax.ppermute(array, axis, [(i, i ^ stride) for i in range(size)])]
    ppermute x24, starting transfers between devices: 29 us -> 29.9 us  [swap(): return lax.ppermute(array, axis, [(i, i ^ stride) for i in range(size)])]
    pallas_call x13 -> x14, Pallas kernels: 10.8 us -> 10.8 us  [run(): pl.pallas_call(kernel, out_shape=shapes, in_specs=specs, out_specs=out_sp...]
  transfers between devices with their start and end apart: 24 -> 24, of which waited for: 16 -> 15; matrix products, arithmetic and copies ran while one was open for 1% -> 1% of each run, Pallas kernels for 7% -> 8%
where the time goes in v13:
time: 58.5 us; the launch traced here: 58.3 us
  starting transfers between devices  29.9 us (51%)
  waiting for transfers between devices  15.4 us (26%)
  Pallas kernels  10.8 us (18%)
  between operations  1.49 us (3%)
  local copies, waits for them, and re-layouts  0.67 us (1%)
    ppermute x24, starting transfers between devices, swap(): return lax.ppermute(array, axis, [(i, i ^ stride) for i in range(size)])  29.9 us
    ppermute x24, waiting for transfers between devices, swap(): return lax.ppermute(array, axis, [(i, i ^ stride) for i in range(size)])  15.4 us
    pallas_call x14, Pallas kernels, run(): pl.pallas_call(kernel, out_shape=shapes, in_specs=specs, out_specs=out_sp...  10.8 us
  transfers between devices with their start and end apart: 24, of which 15 were waited for; matrix products, arithmetic and copies ran while one was open for 1% of the time, Pallas kernels for 8%

profile of v13, /device:TPU:0, one launch (start us, length us, event | category | flops | bytes accessed | tf_op | source)
XLA Modules:
  0.0 58.3 jit_solution(16509420196946256987)
XLA Ops:
  0.6 0.0 copy-start.3
  1.3 2.7 %first.1 = (bf16[32,256,256]{2,1,0:T(8,128)(2,1)S(1)}, f32[128,128]{1,0:T(8,128)S(1)}, f32[128,128]{1,0:T(8,128)S(1)}, s32[1,1,32]{2,1,0:T(1,128)S(4)}, s32[1,1,...) custom-call(s32[1,1,32]{2,1,0:T(1,128)} %refs_0_.1, s32[1,1,32]{2,1,0:T(1,128)} %refs_1_.1, ...), custom_call_target="tpu_custom_call" | custom-call | flops 4194304 | bytes 4194304 | tf_op jit(solution)/shard_map/first/pallas_call | solution.py:349
  4.1 5.1 %collective-permute-start.2 = (s16[144,128]{1,0:T(8,128)(2,1)S(1)}, s16[144,128]{1,0:T(8,128)(2,1)S(1)}, u32[]{:S(2)}, u32[]{:S(2)}) collective-permute-start(s16[144,128]{1,0:T(8,128)(2,1)S(1)} %get-tuple-element.51.refs_6_), channel_id=1, source_target_pairs={{0,24},{8,16},{16,8},{24,0},{1,25},{9,17},{17,9},{25,1},{2,26},{10... | collective-permute-start | bytes 110600 | tf_op jit(solution)/shard_map/ppermute | solution.py:364
  9.2 0.0 collective-permute-start.1
  9.2 0.6 %collective-permute-start = (s16[144,128]{1,0:T(8,128)(2,1)S(1)}, s16[144,128]{1,0:T(8,128)(2,1)S(1)}, u32[]{:S(2)}, u32[]{:S(2)}) collective-permute-start(s16[144,128]{1,0:T(8,128)(2,1)S(1)} %get-tuple-element.51.refs_6_), channel_id=1, source_target_pairs={{0,8},{8,0},{16,24},{24,16},{1,9},{9,1},{17,25},{25,17},{2,10},{10... | collective-permute-start | bytes 110600 | tf_op jit(solution)/shard_map/ppermute | solution.py:364
  9.8 0.0 copy-done.3
  9.8 1.1 %saved_back.1 = (s16[400,128]{1,0:T(8,128)(2,1)S(1)}, bf16[32,256,256]{2,1,0:T(8,128)(2,1)S(1)}) custom-call(s32[1,1,32]{2,1,0:T(1,128)S(4)} %get-tuple-element.44.refs_0_, s32[1,1,32]{2,1,0:T(1,128)S(4)} %get-tuple-element.45.refs_1_, s32[1,1]{1,0:T(1,128)S(4)} %get-tuple-element.46.refs_2_, ...), custom_call_target="tpu_custom_call", output_to_operand_aliasing={{1}: (3, {})} | custom-call | flops 4194304 | bytes 4194304 | tf_op jit(solution)/shard_map/saved_back/pallas_call | solution.py:349
  10.9 0.0 copy-start
  10.9 1.1 %turn.1 = (bf16[32,256,256]{2,1,0:T(8,128)(2,1)S(1)}, bf16[32,256,256]{2,1,0:T(8,128)(2,1)S(1)}) custom-call(bf16[32,256,256]{2,1,0:T(8,128)(2,1)S(1)} %get-tuple-element.49.refs_0_), custom_call_target="tpu_custom_call", output_to_operand_aliasing={{1}: (0, {})} | custom-call | flops 4194304 | bytes 4194304 | tf_op jit(solution)/shard_map/turn/pallas_call | solution.py:349
  12.1 0.0 collective-permute-done.2.refs_9_
  12.1 2.0 %collective-permute-done.1.refs_8_ = s16[144,128]{1,0:T(8,128)(2,1)S(1)} collective-permute-done((s16[144,128]{1,0:T(8,128)(2,1)S(1)}, s16[144,128]{1,0:T(8,128)(2,1)S(1)}, u32[]{:S(2)}, u32[]{:S(2)}) %collective-permute-start.1) | collective-permute-done | bytes 36896 | tf_op jit(solution)/shard_map/ppermute | solution.py:364
  14.1 0.0 collective-permute-done.refs_7_
  14.1 0.0 copy-done.1
  14.1 0.8 %primal_2.1 = (f32[128,128]{1,0:T(8,128)S(1)}, f32[128,128]{1,0:T(8,128)S(1)}, f32[128,128]{1,0:T(8,128)S(1)}, f32[128,128]{1,0:T(8,128)S(1)}, bf16[32,256,256]{2,1,0:T(8,128)(2,1)S(1)}) custom-call(s32[1,1,32]{2,1,0:T(1,128)S(4)} %get-tuple-element.44.refs_0_, s32[1,1,32]{2,1,0:T(1,128)S(4)} %get-tuple-element.45.refs_1_, ...), custom_call_target="tpu_custom_call", output_to_operand_aliasing={{4}: (4, {})} | custom-call | flops 4194304 | bytes 4194304 | tf_op jit(solution)/shard_map/primal_2/pallas_call | solution.py:349
  14.9 0.0 collective-permute-start.3
  14.9 1.9 %collective-permute-start.10 = (s16[400,128]{1,0:T(8,128)(2,1)S(1)}, s16[400,128]{1,0:T(8,128)(2,1)S(1)}, u32[]{:S(2)}, u32[]{:S(2)}) collective-permute-start(s16[400,128]{1,0:T(8,128)(2,1)S(1)} %get-tuple-element.61.refs_0_), channel_id=1, source_target_pairs={{0,24},{8,16},{16,8},{24,0},{1,25},{9,17},{17,9},{25,1},{2,26},{10... | collective-permute-start | bytes 307208 | tf_op jit(solution)/shard_map/ppermute | solution.py:364
  16.8 0.0 collective-permute-done.3.refs_1_
  16.8 2.5 %collective-permute-start.6 = (s16[144,128]{1,0:T(8,128)(2,1)S(1)}, s16[144,128]{1,0:T(8,128)(2,1)S(1)}, u32[]{:S(2)}, u32[]{:S(2)}) collective-permute-start(s16[144,128]{1,0:T(8,128)(2,1)S(1)} %pair_2.1.refs_6_), channel_id=1, source_target_pairs={{0,6},{1,7},{2,4},{3,5},{4,2},{5,3},{6,0},{7,1},{8,14},{9,15},{10,... | collective-permute-start | bytes 110600 | tf_op jit(solution)/shard_map/ppermute | solution.py:364
  19.3 0.5 collective-permute-start.5
  19.8 0.5 collective-permute-start.4
  20.4 1.4 %collective-permute-done.6.refs_9_ = s16[144,128]{1,0:T(8,128)(2,1)S(1)} collective-permute-done((s16[144,128]{1,0:T(8,128)(2,1)S(1)}, s16[144,128]{1,0:T(8,128)(2,1)S(1)}, u32[]{:S(2)}, u32[]{:S(2)}) %collective-permute-start.6) | collective-permute-done | bytes 36896 | tf_op jit(solution)/shard_map/ppermute | solution.py:364
  21.8 1.5 %collective-permute-done.5.refs_8_ = s16[144,128]{1,0:T(8,128)(2,1)S(1)} collective-permute-done((s16[144,128]{1,0:T(8,128)(2,1)S(1)}, s16[144,128]{1,0:T(8,128)(2,1)S(1)}, u32[]{:S(2)}, u32[]{:S(2)}) %collective-permute-start.5) | collective-permute-done | bytes 36896 | tf_op jit(solution)/shard_map/ppermute | solution.py:364
  23.3 0.5 collective-permute-done.4.refs_7_
  23.8 0.9 %dual_1.1 = (f32[128,128]{1,0:T(8,128)S(1)}, f32[128,128]{1,0:T(8,128)S(1)}, s16[144,128]{1,0:T(8,128)(2,1)S(1)}, bf16[32,256,256]{2,1,0:T(8,128)(2,1)S(1)}) custom-call(s32[1,1,32]{2,1,0:T(1,128)S(4)} %get-tuple-element.44.refs_0_, s32[1,1,32]{2,1,0:T(1,128)S(4)} %get-tuple-element.45.refs_1_, ...), custom_call_target="tpu_custom_call", output_to_operand_aliasing={{3}: (4, {})} | custom-call | flops 4194304 | bytes 4194304 | tf_op jit(solution)/shard_map/dual_1/pallas_call | solution.py:349
  24.7 2.1 %collective-permute-start.9 = (s16[144,128]{1,0:T(8,128)(2,1)S(1)}, s16[144,128]{1,0:T(8,128)(2,1)S(1)}, u32[]{:S(2)}, u32[]{:S(2)}) collective-permute-start(s16[144,128]{1,0:T(8,128)(2,1)S(1)} %get-tuple-element.57.refs_6_), channel_id=1, source_target_pairs={{0,24},{8,16},{16,8},{24,0},{1,25},{9,17},{17,9},{25,1},{2,26},{10... | collective-permute-start | bytes 110600 | tf_op jit(solution)/shard_map/ppermute | solution.py:364
  26.8 0.2 collective-permute-start.8
  27.0 2.1 %collective-permute-start.7 = (s16[144,128]{1,0:T(8,128)(2,1)S(1)}, s16[144,128]{1,0:T(8,128)(2,1)S(1)}, u32[]{:S(2)}, u32[]{:S(2)}) collective-permute-start(s16[144,128]{1,0:T(8,128)(2,1)S(1)} %get-tuple-element.57.refs_6_), channel_id=1, source_target_pairs={{0,8},{8,0},{16,24},{24,16},{1,9},{9,1},{17,25},{25,17},{2,10},{10... | collective-permute-start | bytes 110600 | tf_op jit(solution)/shard_map/ppermute | solution.py:364
  29.1 0.0 collective-permute-done.10.refs_1_.refs_8_
  29.1 0.6 collective-permute-start.12
  29.7 2.0 %collective-permute-start.11 = (s16[400,128]{1,0:T(8,128)(2,1)S(1)}, s16[400,128]{1,0:T(8,128)(2,1)S(1)}, u32[]{:S(2)}, u32[]{:S(2)}) collective-permute-start(s16[400,128]{1,0:T(8,128)(2,1)S(1)} %after_2.1.refs_5_), channel_id=1, source_target_pairs={{0,8},{8,0},{16,24},{24,16},{1,9},{9,1},{17,25},{25,17},{2,10},{10... | collective-permute-start | bytes 307208 | tf_op jit(solution)/shard_map/ppermute | solution.py:364
  31.7 0.0 collective-permute-done.9.refs_9_
  31.7 1.0 %collective-permute-done.8.refs_8_ = s16[144,128]{1,0:T(8,128)(2,1)S(1)} collective-permute-done((s16[144,128]{1,0:T(8,128)(2,1)S(1)}, s16[144,128]{1,0:T(8,128)(2,1)S(1)}, u32[]{:S(2)}, u32[]{:S(2)}) %collective-permute-start.8) | collective-permute-done | bytes 36896 | tf_op jit(solution)/shard_map/ppermute | solution.py:364
  32.8 0.0 collective-permute-done.7.refs_7_
  32.8 0.8 %primal_1.1 = (f32[128,128]{1,0:T(8,128)S(1)}, f32[128,128]{1,0:T(8,128)S(1)}, f32[128,128]{1,0:T(8,128)S(1)}, f32[128,128]{1,0:T(8,128)S(1)}, bf16[32,256,256]{2,1,0:T(8,128)(2,1)S(1)}) custom-call(s32[1,1,32]{2,1,0:T(1,128)S(4)} %get-tuple-element.44.refs_0_, s32[1,1,32]{2,1,0:T(1,128)S(4)} %get-tuple-element.45.refs_1_, ...), custom_call_target="tpu_custom_call", output_to_operand_aliasing={{4}: (4, {})} | custom-call | flops 4194304 | bytes 4194304 | tf_op jit(solution)/shard_map/primal_1/pallas_call | solution.py:349
  33.6 0.0 collective-permute-start.13
  33.6 1.2 %collective-permute-done.13.refs_1_ = f32[128,128]{1,0:T(8,128)S(1)} collective-permute-done((f32[128,128]{1,0:T(8,128)S(1)}, f32[128,128]{1,0:T(8,128)S(1)}, u32[]{:S(2)}, u32[]{:S(2)}) %collective-permute-start.13) | collective-permute-done | bytes 65568 | tf_op jit(solution)/shard_map/ppermute | solution.py:364
  34.9 0.1 pair_1.1.refs_6_
  34.9 1.8 %collective-permute-start.16 = (s16[144,128]{1,0:T(8,128)(2,1)S(1)}, s16[144,128]{1,0:T(8,128)(2,1)S(1)}, u32[]{:S(2)}, u32[]{:S(2)}) collective-permute-start(s16[144,128]{1,0:T(8,128)(2,1)S(1)} %pair_1.1.refs_6_), channel_id=1, source_target_pairs={{0,6},{1,7},{2,4},{3,5},{4,2},{5,3},{6,0},{7,1},{8,14},{9,15},{10,... | collective-permute-start | bytes 110600 | tf_op jit(solution)/shard_map/ppermute | solution.py:364
  36.8 0.6 %collective-permute-start.15 = (s16[144,128]{1,0:T(8,128)(2,1)S(1)}, s16[144,128]{1,0:T(8,128)(2,1)S(1)}, u32[]{:S(2)}, u32[]{:S(2)}) collective-permute-start(s16[144,128]{1,0:T(8,128)(2,1)S(1)} %pair_1.1.refs_6_), channel_id=1, source_target_pairs={{0,4},{1,5},{2,6},{3,7},{4,0},{5,1},{6,2},{7,3},{8,12},{9,13},{10,... | collective-permute-start | bytes 110600 | tf_op jit(solution)/shard_map/ppermute | solution.py:364
  37.4 1.1 %collective-permute-start.14 = (s16[144,128]{1,0:T(8,128)(2,1)S(1)}, s16[144,128]{1,0:T(8,128)(2,1)S(1)}, u32[]{:S(2)}, u32[]{:S(2)}) collective-permute-start(s16[144,128]{1,0:T(8,128)(2,1)S(1)} %pair_1.1.refs_6_), channel_id=1, source_target_pairs={{0,2},{1,3},{2,0},{3,1},{4,6},{5,7},{6,4},{7,5},{8,10},{9,11},{10,... | collective-permute-start | bytes 110600 | tf_op jit(solution)/shard_map/ppermute | solution.py:364
  38.5 0.0 collective-permute-done.12.refs_7_
  38.5 0.0 collective-permute-done.11.refs_6_
  38.5 0.9 %saved_image.1 = (f32[3,128,128]{2,1,0:T(8,128)S(1)}, f32[3,128,128]{2,1,0:T(8,128)S(1)}, bf16[32,256,256]{2,1,0:T(8,128)(2,1)S(1)}) custom-call(s32[1,1,32]{2,1,0:T(1,128)S(4)} %get-tuple-element.44.refs_0_, s32[1,1,32]{2,1,0:T(1,128)S(4)} %get-tuple-element.45.refs_1_, s32[1,1]{1,0:T(1,128)S(4)} %get-tuple-element.46.refs_2_, ...), custom_call_target="tpu_custom_call", output_to_operand_aliasing={{2}: (4, {})} | custom-call | flops 4194304 | bytes 4194304 | tf_op jit(solution)/shard_map/saved_image/pallas_call | solution.py:349
  39.5 0.5 collective-permute-done.16.refs_9_
  40.0 0.8 %collective-permute-done.15.refs_8_ = s16[144,128]{1,0:T(8,128)(2,1)S(1)} collective-permute-done((s16[144,128]{1,0:T(8,128)(2,1)S(1)}, s16[144,128]{1,0:T(8,128)(2,1)S(1)}, u32[]{:S(2)}, u32[]{:S(2)}) %collective-permute-start.15) | collective-permute-done | bytes 36896 | tf_op jit(solution)/shard_map/ppermute | solution.py:364
  40.7 0.6 %collective-permute-done.14.refs_7_ = s16[144,128]{1,0:T(8,128)(2,1)S(1)} collective-permute-done((s16[144,128]{1,0:T(8,128)(2,1)S(1)}, s16[144,128]{1,0:T(8,128)(2,1)S(1)}, u32[]{:S(2)}, u32[]{:S(2)}) %collective-permute-start.14) | collective-permute-done | bytes 36896 | tf_op jit(solution)/shard_map/ppermute | solution.py:364
  41.4 0.9 %dual_0.1 = (f32[128,128]{1,0:T(8,128)S(1)}, f32[128,128]{1,0:T(8,128)S(1)}, s16[160,128]{1,0:T(8,128)(2,1)S(1)}, bf16[32,256,256]{2,1,0:T(8,128)(2,1)S(1)}) custom-call(s32[1,1,32]{2,1,0:T(1,128)S(4)} %get-tuple-element.44.refs_0_, s32[1,1,32]{2,1,0:T(1,128)S(4)} %get-tuple-element.45.refs_1_, ...), custom_call_target="tpu_custom_call", output_to_operand_aliasing={{3}: (4, {})} | custom-call | flops 4194304 | bytes 4194304 | tf_op jit(solution)/shard_map/dual_0/pallas_call | solution.py:349
  42.2 1.8 %collective-permute-start.19 = (s16[160,128]{1,0:T(8,128)(2,1)S(1)}, s16[160,128]{1,0:T(8,128)(2,1)S(1)}, u32[]{:S(2)}, u32[]{:S(2)}) collective-permute-start(s16[160,128]{1,0:T(8,128)(2,1)S(1)} %get-tuple-element.68.refs_6_), channel_id=1, source_target_pairs={{0,24},{8,16},{16,8},{24,0},{1,25},{9,17},{17,9},{25,1},{2,26},{10... | collective-permute-start | bytes 122888 | tf_op jit(solution)/shard_map/ppermute | solution.py:364
  44.0 0.1 collective-permute-start.18
  44.1 2.6 %collective-permute-start.17 = (s16[160,128]{1,0:T(8,128)(2,1)S(1)}, s16[160,128]{1,0:T(8,128)(2,1)S(1)}, u32[]{:S(2)}, u32[]{:S(2)}) collective-permute-start(s16[160,128]{1,0:T(8,128)(2,1)S(1)} %get-tuple-element.68.refs_6_), channel_id=1, source_target_pairs={{0,8},{8,0},{16,24},{24,16},{1,9},{9,1},{17,25},{25,17},{2,10},{10... | collective-permute-start | bytes 122888 | tf_op jit(solution)/shard_map/ppermute | solution.py:364
  46.7 1.4 %collective-permute-done.19.refs_9_ = s16[160,128]{1,0:T(8,128)(2,1)S(1)} collective-permute-done((s16[160,128]{1,0:T(8,128)(2,1)S(1)}, s16[160,128]{1,0:T(8,128)(2,1)S(1)}, u32[]{:S(2)}, u32[]{:S(2)}) %collective-permute-start.19) | collective-permute-done | bytes 40992 | tf_op jit(solution)/shard_map/ppermute | solution.py:364
  48.1 1.0 %collective-permute-done.18.refs_8_ = s16[160,128]{1,0:T(8,128)(2,1)S(1)} collective-permute-done((s16[160,128]{1,0:T(8,128)(2,1)S(1)}, s16[160,128]{1,0:T(8,128)(2,1)S(1)}, u32[]{:S(2)}, u32[]{:S(2)}) %collective-permute-start.18) | collective-permute-done | bytes 40992 | tf_op jit(solution)/shard_map/ppermute | solution.py:364
  49.1 0.0 collective-permute-done.17.refs_7_
  49.1 0.8 %primal_0.1 = (f32[128,128]{1,0:T(8,128)S(1)}, f32[80,128]{1,0:T(8,128)S(1)}, f32[80,128]{1,0:T(8,128)S(1)}, bf16[32,256,256]{2,1,0:T(8,128)(2,1)S(1)}) custom-call(s32[1,1,32]{2,1,0:T(1,128)S(4)} %get-tuple-element.44.refs_0_, s32[1,1,32]{2,1,0:T(1,128)S(4)} %get-tuple-element.45.refs_1_, ...), custom_call_target="tpu_custom_call", output_to_operand_aliasing={{3}: (4, {})} | custom-call | flops 4194304 | bytes 4194304 | tf_op jit(solution)/shard_map/primal_0/pallas_call | solution.py:349
  49.9 0.1 collective-permute-start.20
  50.0 1.2 %collective-permute-done.20.refs_1_ = f32[80,128]{1,0:T(8,128)S(1)} collective-permute-done((f32[80,128]{1,0:T(8,128)S(1)}, f32[80,128]{1,0:T(8,128)S(1)}, u32[]{:S(2)}, u32[]{:S(2)}) %collective-permute-start.20) | collective-permute-done | bytes 40992 | tf_op jit(solution)/shard_map/ppermute | solution.py:364
  51.2 2.3 %collective-permute-start.21 = (f32[32,128]{1,0:T(8,128)S(1)}, f32[32,128]{1,0:T(8,128)S(1)}, u32[]{:S(2)}, u32[]{:S(2)}) collective-permute-start(f32[32,128]{1,0:T(8,128)S(1)} %get-tuple-element.77), channel_id=1, source_target_pairs={{0,6},{1,7},{2,4},{3,5},{4,2},{5,3},{6,0},{7,1},{8,14},{9,15},{10,... | collective-permute-start | bytes 49160 | tf_op jit(solution)/shard_map/ppermute | solution.py:364
  53.5 0.4 collective-permute-start.22
  53.9 0.9 %collective-permute-start.23 = (f32[32,128]{1,0:T(8,128)S(1)}, f32[32,128]{1,0:T(8,128)S(1)}, u32[]{:S(2)}, u32[]{:S(2)}) collective-permute-start(f32[32,128]{1,0:T(8,128)S(1)} %get-tuple-element.79), channel_id=1, source_target_pairs={{0,2},{1,3},{2,0},{3,1},{4,6},{5,7},{6,4},{7,5},{8,10},{9,11},{10,... | collective-permute-start | bytes 49160 | tf_op jit(solution)/shard_map/ppermute | solution.py:364
  54.8 0.6 %copy.35 = f32[16384]{0:T(1024)} copy(f32[16384]{0:T(1024)S(1)} %bitcast.19) | data formatting | bytes 131072
  55.4 0.5 collective-permute-done.21.refs_1_
  55.9 1.3 %collective-permute-done.22.refs_2_ = f32[32,128]{1,0:T(8,128)S(1)} collective-permute-done((f32[32,128]{1,0:T(8,128)S(1)}, f32[32,128]{1,0:T(8,128)S(1)}, u32[]{:S(2)}, u32[]{:S(2)}) %collective-permute-start.22) | collective-permute-done | bytes 16416 | tf_op jit(solution)/shard_map/ppermute | solution.py:364
  57.3 0.4 collective-permute-done.23.refs_3_
  57.6 0.7 %last.1 = (f32[16,128]{1,0:T(8,128)}, f32[2]{0:T(128)}) custom-call(f32[2]{0:T(128)S(4)} %get-tuple-element.47.refs_3_.refs_0_, f32[32,128]{1,0:T(8,128)S(1)} %collective-permute-done.21.refs_1_, f32[32,128]{1,0:T(8,128)S(1)} %collective-permute-done.22.refs_2_, f32[32,128]{1,0:T(8,128)S(1)} %collective-permute-done.23.refs_3_, ...), custom_call_target="tpu_custom_call" | custom-call | tf_op jit(solution)/shard_map/last/pallas_call | solution.py:349
  (15 shorter events, 0.1 us)
Async XLA Ops:
  0.6 9.2 %copy-start.3 = (f32[3,16384]{1,0:T(4,128)S(1)}, f32[3,16384]{1,0:T(4,128)}, u32[]{:S(2)}) copy-start(f32[3,16384]{1,0:T(4,128)} %param.19) | copy-start | bytes 589828
  4.1 8.0 %collective-permute-start.2 = (s16[144,128]{1,0:T(8,128)(2,1)S(1)}, s16[144,128]{1,0:T(8,128)(2,1)S(1)}, u32[]{:S(2)}, u32[]{:S(2)}) collective-permute-start(s16[144,128]{1,0:T(8,128)(2,1)S(1)} %get-tuple-element.51.refs_6_), channel_id=1, source_target_pairs={{0,24},{8,16},{16,8},{24,0},{1,25},{9,17},{17,9},{25,1},{2,26},{10... | collective-permute-start | bytes 110600 | tf_op jit(solution)/shard_map/ppermute | solution.py:364
  9.2 4.9 %collective-permute-start.1 = (s16[144,128]{1,0:T(8,128)(2,1)S(1)}, s16[144,128]{1,0:T(8,128)(2,1)S(1)}, u32[]{:S(2)}, u32[]{:S(2)}) collective-permute-start(s16[144,128]{1,0:T(8,128)(2,1)S(1)} %get-tuple-element.51.refs_6_), channel_id=1, source_target_pairs={{0,16},{8,24},{16,0},{24,8},{1,17},{9,25},{17,1},{25,9},{2,18},{10... | collective-permute-start | bytes 110600 | tf_op jit(solution)/shard_map/ppermute | solution.py:364
  9.2 4.9 %collective-permute-start = (s16[144,128]{1,0:T(8,128)(2,1)S(1)}, s16[144,128]{1,0:T(8,128)(2,1)S(1)}, u32[]{:S(2)}, u32[]{:S(2)}) collective-permute-start(s16[144,128]{1,0:T(8,128)(2,1)S(1)} %get-tuple-element.51.refs_6_), channel_id=1, source_target_pairs={{0,8},{8,0},{16,24},{24,16},{1,9},{9,1},{17,25},{25,17},{2,10},{10... | collective-permute-start | bytes 110600 | tf_op jit(solution)/shard_map/ppermute | solution.py:364
  9.8 4.2 %copy-start.1 = (s32[3,16384]{1,0:T(4,128)S(1)}, s32[3,16384]{1,0:T(4,128)}, u32[]{:S(2)}) copy-start(s32[3,16384]{1,0:T(4,128)} %param.20) | copy-start | bytes 589828
  9.8 4.2 %copy-start.4 = (f32[16384]{0:T(1024)S(1)}, f32[16384]{0:T(1024)}, u32[]{:S(2)}) copy-start(f32[16384]{0:T(1024)} %param.26) | copy-start | bytes 196612
  10.9 12.9 %copy-start = (s32[3,16384]{1,0:T(4,128)S(1)}, s32[3,16384]{1,0:T(4,128)}, u32[]{:S(2)}) copy-start(s32[3,16384]{1,0:T(4,128)} %param.21) | copy-start | bytes 589828
  14.9 1.9 %collective-permute-start.3 = (f32[128,128]{1,0:T(8,128)S(1)}, f32[128,128]{1,0:T(8,128)S(1)}, u32[]{:S(2)}, u32[]{:S(2)}) collective-permute-start(f32[128,128]{1,0:T(8,128)S(1)} %get-tuple-element.54.refs_0_), channel_id=1, source_target_pairs={{0,1},{1,0},{2,3},{3,2},{4,5},{5,4},{6,7},{7,6},{8,9},{9,8},{10,11... | collective-permute-start | bytes 196616 | tf_op jit(solution)/shard_map/ppermute | solution.py:364
  14.9 14.2 %collective-permute-start.10 = (s16[400,128]{1,0:T(8,128)(2,1)S(1)}, s16[400,128]{1,0:T(8,128)(2,1)S(1)}, u32[]{:S(2)}, u32[]{:S(2)}) collective-permute-start(s16[400,128]{1,0:T(8,128)(2,1)S(1)} %get-tuple-element.61.refs_0_), channel_id=1, source_target_pairs={{0,24},{8,16},{16,8},{24,0},{1,25},{9,17},{17,9},{25,1},{2,26},{10... | collective-permute-start | bytes 307208 | tf_op jit(solution)/shard_map/ppermute | solution.py:364
  16.8 4.9 %collective-permute-start.6 = (s16[144,128]{1,0:T(8,128)(2,1)S(1)}, s16[144,128]{1,0:T(8,128)(2,1)S(1)}, u32[]{:S(2)}, u32[]{:S(2)}) collective-permute-start(s16[144,128]{1,0:T(8,128)(2,1)S(1)} %pair_2.1.refs_6_), channel_id=1, source_target_pairs={{0,6},{1,7},{2,4},{3,5},{4,2},{5,3},{6,0},{7,1},{8,14},{9,15},{10,... | collective-permute-start | bytes 110600 | tf_op jit(solution)/shard_map/ppermute | solution.py:364
  19.3 4.0 %collective-permute-start.5 = (s16[144,128]{1,0:T(8,128)(2,1)S(1)}, s16[144,128]{1,0:T(8,128)(2,1)S(1)}, u32[]{:S(2)}, u32[]{:S(2)}) collective-permute-start(s16[144,128]{1,0:T(8,128)(2,1)S(1)} %pair_2.1.refs_6_), channel_id=1, source_target_pairs={{0,4},{1,5},{2,6},{3,7},{4,0},{5,1},{6,2},{7,3},{8,12},{9,13},{10,... | collective-permute-start | bytes 110600 | tf_op jit(solution)/shard_map/ppermute | solution.py:364
  19.8 4.0 %collective-permute-start.4 = (s16[144,128]{1,0:T(8,128)(2,1)S(1)}, s16[144,128]{1,0:T(8,128)(2,1)S(1)}, u32[]{:S(2)}, u32[]{:S(2)}) collective-permute-start(s16[144,128]{1,0:T(8,128)(2,1)S(1)} %pair_2.1.refs_6_), channel_id=1, source_target_pairs={{0,2},{1,3},{2,0},{3,1},{4,6},{5,7},{6,4},{7,5},{8,10},{9,11},{10,... | collective-permute-start | bytes 110600 | tf_op jit(solution)/shard_map/ppermute | solution.py:364
  23.8 14.7 %copy-start.2 = (f32[3,16384]{1,0:T(4,128)S(1)}, f32[3,16384]{1,0:T(4,128)}, u32[]{:S(2)}) copy-start(f32[3,16384]{1,0:T(4,128)} %param.18) | copy-start | bytes 589828
  23.8 14.7 %copy-start.5 = (f32[16384]{0:T(1024)S(1)}, f32[16384]{0:T(1024)}, u32[]{:S(2)}) copy-start(f32[16384]{0:T(1024)} %param.22) | copy-start | bytes 196612
  23.8 14.7 %copy-start.6 = (f32[16384]{0:T(1024)S(1)}, f32[16384]{0:T(1024)}, u32[]{:S(2)}) copy-start(f32[16384]{0:T(1024)} %param.24) | copy-start | bytes 196612
  24.7 7.1 %collective-permute-start.9 = (s16[144,128]{1,0:T(8,128)(2,1)S(1)}, s16[144,128]{1,0:T(8,128)(2,1)S(1)}, u32[]{:S(2)}, u32[]{:S(2)}) collective-permute-start(s16[144,128]{1,0:T(8,128)(2,1)S(1)} %get-tuple-element.57.refs_6_), channel_id=1, source_target_pairs={{0,24},{8,16},{16,8},{24,0},{1,25},{9,17},{17,9},{25,1},{2,26},{10... | collective-permute-start | bytes 110600 | tf_op jit(solution)/shard_map/ppermute | solution.py:364
  26.8 6.0 %collective-permute-start.8 = (s16[144,128]{1,0:T(8,128)(2,1)S(1)}, s16[144,128]{1,0:T(8,128)(2,1)S(1)}, u32[]{:S(2)}, u32[]{:S(2)}) collective-permute-start(s16[144,128]{1,0:T(8,128)(2,1)S(1)} %get-tuple-element.57.refs_6_), channel_id=1, source_target_pairs={{0,16},{8,24},{16,0},{24,8},{1,17},{9,25},{17,1},{25,9},{2,18},{10... | collective-permute-start | bytes 110600 | tf_op jit(solution)/shard_map/ppermute | solution.py:364
  27.0 5.8 %collective-permute-start.7 = (s16[144,128]{1,0:T(8,128)(2,1)S(1)}, s16[144,128]{1,0:T(8,128)(2,1)S(1)}, u32[]{:S(2)}, u32[]{:S(2)}) collective-permute-start(s16[144,128]{1,0:T(8,128)(2,1)S(1)} %get-tuple-element.57.refs_6_), channel_id=1, source_target_pairs={{0,8},{8,0},{16,24},{24,16},{1,9},{9,1},{17,25},{25,17},{2,10},{10... | collective-permute-start | bytes 110600 | tf_op jit(solution)/shard_map/ppermute | solution.py:364
  29.1 9.4 %collective-permute-start.12 = (s16[400,128]{1,0:T(8,128)(2,1)S(1)}, s16[400,128]{1,0:T(8,128)(2,1)S(1)}, u32[]{:S(2)}, u32[]{:S(2)}) collective-permute-start(s16[400,128]{1,0:T(8,128)(2,1)S(1)} %after_2.1.refs_5_), channel_id=1, source_target_pairs={{0,16},{8,24},{16,0},{24,8},{1,17},{9,25},{17,1},{25,9},{2,18},{10... | collective-permute-start | bytes 307208 | tf_op jit(solution)/shard_map/ppermute | solution.py:364
  29.7 8.8 %collective-permute-start.11 = (s16[400,128]{1,0:T(8,128)(2,1)S(1)}, s16[400,128]{1,0:T(8,128)(2,1)S(1)}, u32[]{:S(2)}, u32[]{:S(2)}) collective-permute-start(s16[400,128]{1,0:T(8,128)(2,1)S(1)} %after_2.1.refs_5_), channel_id=1, source_target_pairs={{0,8},{8,0},{16,24},{24,16},{1,9},{9,1},{17,25},{25,17},{2,10},{10... | collective-permute-start | bytes 307208 | tf_op jit(solution)/shard_map/ppermute | solution.py:364
  32.8 8.6 %copy-start.7 = (f32[16384]{0:T(1024)S(1)}, f32[16384]{0:T(1024)}, u32[]{:S(2)}) copy-start(f32[16384]{0:T(1024)} %param.23) | copy-start | bytes 196612
  33.6 1.3 %collective-permute-start.13 = (f32[128,128]{1,0:T(8,128)S(1)}, f32[128,128]{1,0:T(8,128)S(1)}, u32[]{:S(2)}, u32[]{:S(2)}) collective-permute-start(f32[128,128]{1,0:T(8,128)S(1)} %get-tuple-element.64.refs_0_), channel_id=1, source_target_pairs={{0,1},{1,0},{2,3},{3,2},{4,5},{5,4},{6,7},{7,6},{8,9},{9,8},{10,11... | collective-permute-start | bytes 196616 | tf_op jit(solution)/shard_map/ppermute | solution.py:364
  34.9 5.0 %collective-permute-start.16 = (s16[144,128]{1,0:T(8,128)(2,1)S(1)}, s16[144,128]{1,0:T(8,128)(2,1)S(1)}, u32[]{:S(2)}, u32[]{:S(2)}) collective-permute-start(s16[144,128]{1,0:T(8,128)(2,1)S(1)} %pair_1.1.refs_6_), channel_id=1, source_target_pairs={{0,6},{1,7},{2,4},{3,5},{4,2},{5,3},{6,0},{7,1},{8,14},{9,15},{10,... | collective-permute-start | bytes 110600 | tf_op jit(solution)/shard_map/ppermute | solution.py:364
  36.8 4.0 %collective-permute-start.15 = (s16[144,128]{1,0:T(8,128)(2,1)S(1)}, s16[144,128]{1,0:T(8,128)(2,1)S(1)}, u32[]{:S(2)}, u32[]{:S(2)}) collective-permute-start(s16[144,128]{1,0:T(8,128)(2,1)S(1)} %pair_1.1.refs_6_), channel_id=1, source_target_pairs={{0,4},{1,5},{2,6},{3,7},{4,0},{5,1},{6,2},{7,3},{8,12},{9,13},{10,... | collective-permute-start | bytes 110600 | tf_op jit(solution)/shard_map/ppermute | solution.py:364
  37.4 4.0 %collective-permute-start.14 = (s16[144,128]{1,0:T(8,128)(2,1)S(1)}, s16[144,128]{1,0:T(8,128)(2,1)S(1)}, u32[]{:S(2)}, u32[]{:S(2)}) collective-permute-start(s16[144,128]{1,0:T(8,128)(2,1)S(1)} %pair_1.1.refs_6_), channel_id=1, source_target_pairs={{0,2},{1,3},{2,0},{3,1},{4,6},{5,7},{6,4},{7,5},{8,10},{9,11},{10,... | collective-permute-start | bytes 110600 | tf_op jit(solution)/shard_map/ppermute | solution.py:364
  42.2 5.9 %collective-permute-start.19 = (s16[160,128]{1,0:T(8,128)(2,1)S(1)}, s16[160,128]{1,0:T(8,128)(2,1)S(1)}, u32[]{:S(2)}, u32[]{:S(2)}) collective-permute-start(s16[160,128]{1,0:T(8,128)(2,1)S(1)} %get-tuple-element.68.refs_6_), channel_id=1, source_target_pairs={{0,24},{8,16},{16,8},{24,0},{1,25},{9,17},{17,9},{25,1},{2,26},{10... | collective-permute-start | bytes 122888 | tf_op jit(solution)/shard_map/ppermute | solution.py:364
  44.0 5.1 %collective-permute-start.18 = (s16[160,128]{1,0:T(8,128)(2,1)S(1)}, s16[160,128]{1,0:T(8,128)(2,1)S(1)}, u32[]{:S(2)}, u32[]{:S(2)}) collective-permute-start(s16[160,128]{1,0:T(8,128)(2,1)S(1)} %get-tuple-element.68.refs_6_), channel_id=1, source_target_pairs={{0,16},{8,24},{16,0},{24,8},{1,17},{9,25},{17,1},{25,9},{2,18},{10... | collective-permute-start | bytes 122888 | tf_op jit(solution)/shard_map/ppermute | solution.py:364
  44.1 5.0 %collective-permute-start.17 = (s16[160,128]{1,0:T(8,128)(2,1)S(1)}, s16[160,128]{1,0:T(8,128)(2,1)S(1)}, u32[]{:S(2)}, u32[]{:S(2)}) collective-permute-start(s16[160,128]{1,0:T(8,128)(2,1)S(1)} %get-tuple-element.68.refs_6_), channel_id=1, source_target_pairs={{0,8},{8,0},{16,24},{24,16},{1,9},{9,1},{17,25},{25,17},{2,10},{10... | collective-permute-start | bytes 122888 | tf_op jit(solution)/shard_map/ppermute | solution.py:364
  49.9 1.3 %collective-permute-start.20 = (f32[80,128]{1,0:T(8,128)S(1)}, f32[80,128]{1,0:T(8,128)S(1)}, u32[]{:S(2)}, u32[]{:S(2)}) collective-permute-start(f32[80,128]{1,0:T(8,128)S(1)} %get-tuple-element.76), channel_id=1, source_target_pairs={{0,1},{1,0},{2,3},{3,2},{4,5},{5,4},{6,7},{7,6},{8,9},{9,8},{10,11... | collective-permute-start | bytes 122888 | tf_op jit(solution)/shard_map/ppermute | solution.py:364
  51.2 4.7 %collective-permute-start.21 = (f32[32,128]{1,0:T(8,128)S(1)}, f32[32,128]{1,0:T(8,128)S(1)}, u32[]{:S(2)}, u32[]{:S(2)}) collective-permute-start(f32[32,128]{1,0:T(8,128)S(1)} %get-tuple-element.77), channel_id=1, source_target_pairs={{0,6},{1,7},{2,4},{3,5},{4,2},{5,3},{6,0},{7,1},{8,14},{9,15},{10,... | collective-permute-start | bytes 49160 | tf_op jit(solution)/shard_map/ppermute | solution.py:364
  53.5 3.7 %collective-permute-start.22 = (f32[32,128]{1,0:T(8,128)S(1)}, f32[32,128]{1,0:T(8,128)S(1)}, u32[]{:S(2)}, u32[]{:S(2)}) collective-permute-start(f32[32,128]{1,0:T(8,128)S(1)} %get-tuple-element.78), channel_id=1, source_target_pairs={{0,4},{1,5},{2,6},{3,7},{4,0},{5,1},{6,2},{7,3},{8,12},{9,13},{10,... | collective-permute-start | bytes 49160 | tf_op jit(solution)/shard_map/ppermute | solution.py:364
  53.9 3.7 %collective-permute-start.23 = (f32[32,128]{1,0:T(8,128)S(1)}, f32[32,128]{1,0:T(8,128)S(1)}, u32[]{:S(2)}, u32[]{:S(2)}) collective-permute-start(f32[32,128]{1,0:T(8,128)S(1)} %get-tuple-element.79), channel_id=1, source_target_pairs={{0,2},{1,3},{2,0},{3,1},{4,6},{5,7},{6,4},{7,5},{8,10},{9,11},{10,... | collective-permute-start | bytes 49160 | tf_op jit(solution)/shard_map/ppermute | solution.py:364

commit v14 on v13

--- a/solution.py
+++ b/solution.py
@@ -478,7 +478,7 @@
     for step in reversed(range(iterations)):
         parts = exchange(parts, "row")
         if step < last and pending:
-            send_saved(saved_parts[0], saved_parts[n_row - 1], len(pending))
+            send_saved(saved_parts[0], saved_parts[1], len(pending))
         groups = where + [sizes, (VMEM, turned), (VMEM, mask_x), (VMEM, parts)]
         groups += [(VMEM, adjoint_x), (VMEM, anchor_x)]
         body = functools.partial(primal_body, step, n_col)
@@ -503,8 +503,8 @@
         )[0]
         parts = exchange([part] * n_chip, "col", 2)
         if step == last:
-            saved_parts[pending[0]] = swap(saved_part, "row", pending[0])
-            pending = pending[1:]
+            saved_parts[1] = swap(saved_part, "row", 1)
+            pending = pending[:-1]
         if step == 1:
             reduced, images, turned = run(
                 saved_image_body,

time: 58.5 us -> 61.3 us (1.048)
  waiting for transfers between devices: 15.4 us -> 20.3 us
  starting transfers between devices: 29.9 us -> 27.8 us
    ppermute x24, waiting for transfers between devices: 15.4 us -> 20.3 us  [swap(): return lax.ppermute(array, axis, [(i, i ^ stride) for i in range(size)])]
    ppermute x24, starting transfers between devices: 29.9 us -> 27.8 us  [swap(): return lax.ppermute(array, axis, [(i, i ^ stride) for i in range(size)])]
  transfers between devices with their start and end apart: 24 -> 24, of which waited for: 15 -> 16; matrix products, arithmetic and copies ran while one was open for 1% -> 1% of each run, Pallas kernels for 8% -> 8%
where the time goes in v14:
time: 61.3 us; the launch traced here: 61.1 us
  starting transfers between devices  27.8 us (45%)
  waiting for transfers between devices  20.3 us (33%)
  Pallas kernels  10.8 us (18%)
  between operations  1.51 us (2%)
  local copies, waits for them, and re-layouts  0.67 us (1%)
    ppermute x24, starting transfers between devices, swap(): return lax.ppermute(array, axis, [(i, i ^ stride) for i in range(size)])  27.8 us
    ppermute x24, waiting for transfers between devices, swap(): return lax.ppermute(array, axis, [(i, i ^ stride) for i in range(size)])  20.3 us
    pallas_call x14, Pallas kernels, run(): pl.pallas_call(kernel, out_shape=shapes, in_specs=specs, out_specs=out_sp...  10.8 us
  transfers between devices with their start and end apart: 24, of which 16 were waited for; matrix products, arithmetic and copies ran while one was open for 1% of the time, Pallas kernels for 8%

profile of v14, /device:TPU:0, one launch (start us, length us, event | category | flops | bytes accessed | tf_op | source)
XLA Modules:
  0.0 61.1 jit_solution(13702299367827190190)
XLA Ops:
  0.6 0.0 copy-start.3
  1.3 2.7 %first.1 = (bf16[32,256,256]{2,1,0:T(8,128)(2,1)S(1)}, f32[128,128]{1,0:T(8,128)S(1)}, f32[128,128]{1,0:T(8,128)S(1)}, s32[1,1,32]{2,1,0:T(1,128)S(4)}, s32[1,1,...) custom-call(s32[1,1,32]{2,1,0:T(1,128)} %refs_0_.1, s32[1,1,32]{2,1,0:T(1,128)} %refs_1_.1, ...), custom_call_target="tpu_custom_call" | custom-call | flops 4194304 | bytes 4194304 | tf_op jit(solution)/shard_map/first/pallas_call | solution.py:349
  4.1 5.1 %collective-permute-start.2 = (s16[144,128]{1,0:T(8,128)(2,1)S(1)}, s16[144,128]{1,0:T(8,128)(2,1)S(1)}, u32[]{:S(2)}, u32[]{:S(2)}) collective-permute-start(s16[144,128]{1,0:T(8,128)(2,1)S(1)} %get-tuple-element.51.refs_6_), channel_id=1, source_target_pairs={{0,24},{8,16},{16,8},{24,0},{1,25},{9,17},{17,9},{25,1},{2,26},{10... | collective-permute-start | bytes 110600 | tf_op jit(solution)/shard_map/ppermute | solution.py:364
  9.2 0.0 collective-permute-start.1
  9.2 0.6 %collective-permute-start = (s16[144,128]{1,0:T(8,128)(2,1)S(1)}, s16[144,128]{1,0:T(8,128)(2,1)S(1)}, u32[]{:S(2)}, u32[]{:S(2)}) collective-permute-start(s16[144,128]{1,0:T(8,128)(2,1)S(1)} %get-tuple-element.51.refs_6_), channel_id=1, source_target_pairs={{0,8},{8,0},{16,24},{24,16},{1,9},{9,1},{17,25},{25,17},{2,10},{10... | collective-permute-start | bytes 110600 | tf_op jit(solution)/shard_map/ppermute | solution.py:364
  9.8 0.0 copy-done.3
  9.8 1.1 %saved_back.1 = (s16[400,128]{1,0:T(8,128)(2,1)S(1)}, bf16[32,256,256]{2,1,0:T(8,128)(2,1)S(1)}) custom-call(s32[1,1,32]{2,1,0:T(1,128)S(4)} %get-tuple-element.44.refs_0_, s32[1,1,32]{2,1,0:T(1,128)S(4)} %get-tuple-element.45.refs_1_, s32[1,1]{1,0:T(1,128)S(4)} %get-tuple-element.46.refs_2_, ...), custom_call_target="tpu_custom_call", output_to_operand_aliasing={{1}: (3, {})} | custom-call | flops 4194304 | bytes 4194304 | tf_op jit(solution)/shard_map/saved_back/pallas_call | solution.py:349
  10.9 0.0 copy-start
  10.9 1.1 %turn.1 = (bf16[32,256,256]{2,1,0:T(8,128)(2,1)S(1)}, bf16[32,256,256]{2,1,0:T(8,128)(2,1)S(1)}) custom-call(bf16[32,256,256]{2,1,0:T(8,128)(2,1)S(1)} %get-tuple-element.49.refs_0_), custom_call_target="tpu_custom_call", output_to_operand_aliasing={{1}: (0, {})} | custom-call | flops 4194304 | bytes 4194304 | tf_op jit(solution)/shard_map/turn/pallas_call | solution.py:349
  12.1 0.0 collective-permute-done.2.refs_9_
  12.1 2.0 %collective-permute-done.1.refs_8_ = s16[144,128]{1,0:T(8,128)(2,1)S(1)} collective-permute-done((s16[144,128]{1,0:T(8,128)(2,1)S(1)}, s16[144,128]{1,0:T(8,128)(2,1)S(1)}, u32[]{:S(2)}, u32[]{:S(2)}) %collective-permute-start.1) | collective-permute-done | bytes 36896 | tf_op jit(solution)/shard_map/ppermute | solution.py:364
  14.1 0.0 collective-permute-done.refs_7_
  14.1 0.0 copy-done.4
  14.1 0.8 %primal_2.1 = (f32[128,128]{1,0:T(8,128)S(1)}, f32[128,128]{1,0:T(8,128)S(1)}, f32[128,128]{1,0:T(8,128)S(1)}, f32[128,128]{1,0:T(8,128)S(1)}, bf16[32,256,256]{2,1,0:T(8,128)(2,1)S(1)}) custom-call(s32[1,1,32]{2,1,0:T(1,128)S(4)} %get-tuple-element.44.refs_0_, s32[1,1,32]{2,1,0:T(1,128)S(4)} %get-tuple-element.45.refs_1_, ...), custom_call_target="tpu_custom_call", output_to_operand_aliasing={{4}: (4, {})} | custom-call | flops 4194304 | bytes 4194304 | tf_op jit(solution)/shard_map/primal_2/pallas_call | solution.py:349
  14.9 0.0 collective-permute-start.3
  14.9 0.1 collective-permute-start.10
  15.0 1.2 %collective-permute-done.3.refs_1_ = f32[128,128]{1,0:T(8,128)S(1)} collective-permute-done((f32[128,128]{1,0:T(8,128)S(1)}, f32[128,128]{1,0:T(8,128)S(1)}, u32[]{:S(2)}, u32[]{:S(2)}) %collective-permute-start.3) | collective-permute-done | bytes 65568 | tf_op jit(solution)/shard_map/ppermute | solution.py:364
  16.2 2.5 %collective-permute-start.6 = (s16[144,128]{1,0:T(8,128)(2,1)S(1)}, s16[144,128]{1,0:T(8,128)(2,1)S(1)}, u32[]{:S(2)}, u32[]{:S(2)}) collective-permute-start(s16[144,128]{1,0:T(8,128)(2,1)S(1)} %pair_2.1.refs_6_), channel_id=1, source_target_pairs={{0,6},{1,7},{2,4},{3,5},{4,2},{5,3},{6,0},{7,1},{8,14},{9,15},{10,... | collective-permute-start | bytes 110600 | tf_op jit(solution)/shard_map/ppermute | solution.py:364
  18.7 0.5 collective-permute-start.5
  19.2 0.5 collective-permute-start.4
  19.8 1.4 %collective-permute-done.6.refs_9_ = s16[144,128]{1,0:T(8,128)(2,1)S(1)} collective-permute-done((s16[144,128]{1,0:T(8,128)(2,1)S(1)}, s16[144,128]{1,0:T(8,128)(2,1)S(1)}, u32[]{:S(2)}, u32[]{:S(2)}) %collective-permute-start.6) | collective-permute-done | bytes 36896 | tf_op jit(solution)/shard_map/ppermute | solution.py:364
  21.1 1.6 %collective-permute-done.5.refs_8_ = s16[144,128]{1,0:T(8,128)(2,1)S(1)} collective-permute-done((s16[144,128]{1,0:T(8,128)(2,1)S(1)}, s16[144,128]{1,0:T(8,128)(2,1)S(1)}, u32[]{:S(2)}, u32[]{:S(2)}) %collective-permute-start.5) | collective-permute-done | bytes 36896 | tf_op jit(solution)/shard_map/ppermute | solution.py:364
  22.7 0.5 collective-permute-done.4.refs_7_
  23.2 0.9 %dual_1.1 = (f32[128,128]{1,0:T(8,128)S(1)}, f32[128,128]{1,0:T(8,128)S(1)}, s16[144,128]{1,0:T(8,128)(2,1)S(1)}, bf16[32,256,256]{2,1,0:T(8,128)(2,1)S(1)}) custom-call(s32[1,1,32]{2,1,0:T(1,128)S(4)} %get-tuple-element.44.refs_0_, s32[1,1,32]{2,1,0:T(1,128)S(4)} %get-tuple-element.45.refs_1_, ...), custom_call_target="tpu_custom_call", output_to_operand_aliasing={{3}: (4, {})} | custom-call | flops 4194304 | bytes 4194304 | tf_op jit(solution)/shard_map/dual_1/pallas_call | solution.py:349
  24.1 2.4 %collective-permute-start.9 = (s16[144,128]{1,0:T(8,128)(2,1)S(1)}, s16[144,128]{1,0:T(8,128)(2,1)S(1)}, u32[]{:S(2)}, u32[]{:S(2)}) collective-permute-start(s16[144,128]{1,0:T(8,128)(2,1)S(1)} %get-tuple-element.57.refs_6_), channel_id=1, source_target_pairs={{0,24},{8,16},{16,8},{24,0},{1,25},{9,17},{17,9},{25,1},{2,26},{10... | collective-permute-start | bytes 110600 | tf_op jit(solution)/shard_map/ppermute | solution.py:364
  26.4 0.0 collective-permute-start.8
  26.4 2.1 %collective-permute-start.7 = (s16[144,128]{1,0:T(8,128)(2,1)S(1)}, s16[144,128]{1,0:T(8,128)(2,1)S(1)}, u32[]{:S(2)}, u32[]{:S(2)}) collective-permute-start(s16[144,128]{1,0:T(8,128)(2,1)S(1)} %get-tuple-element.57.refs_6_), channel_id=1, source_target_pairs={{0,8},{8,0},{16,24},{24,16},{1,9},{9,1},{17,25},{25,17},{2,10},{10... | collective-permute-start | bytes 110600 | tf_op jit(solution)/shard_map/ppermute | solution.py:364
  28.5 0.0 collective-permute-done.10.refs_1_.refs_6_
  28.5 2.3 %collective-permute-start.12 = (s16[400,128]{1,0:T(8,128)(2,1)S(1)}, s16[400,128]{1,0:T(8,128)(2,1)S(1)}, u32[]{:S(2)}, u32[]{:S(2)}) collective-permute-start(s16[400,128]{1,0:T(8,128)(2,1)S(1)} %after_2.1.refs_5_), channel_id=1, source_target_pairs={{0,24},{8,16},{16,8},{24,0},{1,25},{9,17},{17,9},{25,1},{2,26},{10... | collective-permute-start | bytes 307208 | tf_op jit(solution)/shard_map/ppermute | solution.py:364
  30.8 0.0 collective-permute-start.11
  30.8 0.0 collective-permute-done.9.refs_9_
  30.8 5.3 %collective-permute-done.8.refs_8_ = s16[144,128]{1,0:T(8,128)(2,1)S(1)} collective-permute-done((s16[144,128]{1,0:T(8,128)(2,1)S(1)}, s16[144,128]{1,0:T(8,128)(2,1)S(1)}, u32[]{:S(2)}, u32[]{:S(2)}) %collective-permute-start.8) | collective-permute-done | bytes 36896 | tf_op jit(solution)/shard_map/ppermute | solution.py:364
  36.1 0.0 collective-permute-done.7.refs_7_
  36.1 0.8 %primal_1.1 = (f32[128,128]{1,0:T(8,128)S(1)}, f32[128,128]{1,0:T(8,128)S(1)}, f32[128,128]{1,0:T(8,128)S(1)}, f32[128,128]{1,0:T(8,128)S(1)}, bf16[32,256,256]{2,1,0:T(8,128)(2,1)S(1)}) custom-call(s32[1,1,32]{2,1,0:T(1,128)S(4)} %get-tuple-element.44.refs_0_, s32[1,1,32]{2,1,0:T(1,128)S(4)} %get-tuple-element.45.refs_1_, ...), custom_call_target="tpu_custom_call", output_to_operand_aliasing={{4}: (4, {})} | custom-call | flops 4194304 | bytes 4194304 | tf_op jit(solution)/shard_map/primal_1/pallas_call | solution.py:349
  36.9 0.0 collective-permute-start.13
  36.9 1.2 %collective-permute-done.13.refs_1_ = f32[128,128]{1,0:T(8,128)S(1)} collective-permute-done((f32[128,128]{1,0:T(8,128)S(1)}, f32[128,128]{1,0:T(8,128)S(1)}, u32[]{:S(2)}, u32[]{:S(2)}) %collective-permute-start.13) | collective-permute-done | bytes 65568 | tf_op jit(solution)/shard_map/ppermute | solution.py:364
  38.2 0.1 pair_1.1.refs_6_
  38.2 1.7 %collective-permute-start.16 = (s16[144,128]{1,0:T(8,128)(2,1)S(1)}, s16[144,128]{1,0:T(8,128)(2,1)S(1)}, u32[]{:S(2)}, u32[]{:S(2)}) collective-permute-start(s16[144,128]{1,0:T(8,128)(2,1)S(1)} %pair_1.1.refs_6_), channel_id=1, source_target_pairs={{0,6},{1,7},{2,4},{3,5},{4,2},{5,3},{6,0},{7,1},{8,14},{9,15},{10,... | collective-permute-start | bytes 110600 | tf_op jit(solution)/shard_map/ppermute | solution.py:364
  40.0 0.4 collective-permute-start.15
  40.4 1.4 %collective-permute-start.14 = (s16[144,128]{1,0:T(8,128)(2,1)S(1)}, s16[144,128]{1,0:T(8,128)(2,1)S(1)}, u32[]{:S(2)}, u32[]{:S(2)}) collective-permute-start(s16[144,128]{1,0:T(8,128)(2,1)S(1)} %pair_1.1.refs_6_), channel_id=1, source_target_pairs={{0,2},{1,3},{2,0},{3,1},{4,6},{5,7},{6,4},{7,5},{8,10},{9,11},{10,... | collective-permute-start | bytes 110600 | tf_op jit(solution)/shard_map/ppermute | solution.py:364
  41.8 0.0 collective-permute-done.12.refs_8_
  41.8 0.0 collective-permute-done.11.refs_7_
  41.8 0.9 %saved_image.1 = (f32[3,128,128]{2,1,0:T(8,128)S(1)}, f32[3,128,128]{2,1,0:T(8,128)S(1)}, bf16[32,256,256]{2,1,0:T(8,128)(2,1)S(1)}) custom-call(s32[1,1,32]{2,1,0:T(1,128)S(4)} %get-tuple-element.44.refs_0_, s32[1,1,32]{2,1,0:T(1,128)S(4)} %get-tuple-element.45.refs_1_, s32[1,1]{1,0:T(1,128)S(4)} %get-tuple-element.46.refs_2_, ...), custom_call_target="tpu_custom_call", output_to_operand_aliasing={{2}: (4, {})} | custom-call | flops 4194304 | bytes 4194304 | tf_op jit(solution)/shard_map/saved_image/pallas_call | solution.py:349
  42.8 0.5 collective-permute-done.16.refs_9_
  43.3 0.7 %collective-permute-done.15.refs_8_ = s16[144,128]{1,0:T(8,128)(2,1)S(1)} collective-permute-done((s16[144,128]{1,0:T(8,128)(2,1)S(1)}, s16[144,128]{1,0:T(8,128)(2,1)S(1)}, u32[]{:S(2)}, u32[]{:S(2)}) %collective-permute-start.15) | collective-permute-done | bytes 36896 | tf_op jit(solution)/shard_map/ppermute | solution.py:364
  43.9 0.4 collective-permute-done.14.refs_7_
  44.4 0.9 %dual_0.1 = (f32[128,128]{1,0:T(8,128)S(1)}, f32[128,128]{1,0:T(8,128)S(1)}, s16[160,128]{1,0:T(8,128)(2,1)S(1)}, bf16[32,256,256]{2,1,0:T(8,128)(2,1)S(1)}) custom-call(s32[1,1,32]{2,1,0:T(1,128)S(4)} %get-tuple-element.44.refs_0_, s32[1,1,32]{2,1,0:T(1,128)S(4)} %get-tuple-element.45.refs_1_, ...), custom_call_target="tpu_custom_call", output_to_operand_aliasing={{3}: (4, {})} | custom-call | flops 4194304 | bytes 4194304 | tf_op jit(solution)/shard_map/dual_0/pallas_call | solution.py:349
  45.2 0.1 collective-permute-start.19
  45.3 0.1 collective-permute-start.18
  45.4 4.3 %collective-permute-start.17 = (s16[160,128]{1,0:T(8,128)(2,1)S(1)}, s16[160,128]{1,0:T(8,128)(2,1)S(1)}, u32[]{:S(2)}, u32[]{:S(2)}) collective-permute-start(s16[160,128]{1,0:T(8,128)(2,1)S(1)} %get-tuple-element.68.refs_6_), channel_id=1, source_target_pairs={{0,8},{8,0},{16,24},{24,16},{1,9},{9,1},{17,25},{25,17},{2,10},{10... | collective-permute-start | bytes 122888 | tf_op jit(solution)/shard_map/ppermute | solution.py:364
  49.7 1.4 %collective-permute-done.19.refs_9_ = s16[160,128]{1,0:T(8,128)(2,1)S(1)} collective-permute-done((s16[160,128]{1,0:T(8,128)(2,1)S(1)}, s16[160,128]{1,0:T(8,128)(2,1)S(1)}, u32[]{:S(2)}, u32[]{:S(2)}) %collective-permute-start.19) | collective-permute-done | bytes 40992 | tf_op jit(solution)/shard_map/ppermute | solution.py:364
  51.1 0.0 collective-permute-done.18.refs_8_
  51.1 0.6 collective-permute-done.17.refs_7_
  51.7 0.8 %primal_0.1 = (f32[128,128]{1,0:T(8,128)S(1)}, f32[80,128]{1,0:T(8,128)S(1)}, f32[80,128]{1,0:T(8,128)S(1)}, bf16[32,256,256]{2,1,0:T(8,128)(2,1)S(1)}) custom-call(s32[1,1,32]{2,1,0:T(1,128)S(4)} %get-tuple-element.44.refs_0_, s32[1,1,32]{2,1,0:T(1,128)S(4)} %get-tuple-element.45.refs_1_, ...), custom_call_target="tpu_custom_call", output_to_operand_aliasing={{3}: (4, {})} | custom-call | flops 4194304 | bytes 4194304 | tf_op jit(solution)/shard_map/primal_0/pallas_call | solution.py:349
  52.5 0.1 collective-permute-start.20
  52.6 1.2 %collective-permute-done.20.refs_1_ = f32[80,128]{1,0:T(8,128)S(1)} collective-permute-done((f32[80,128]{1,0:T(8,128)S(1)}, f32[80,128]{1,0:T(8,128)S(1)}, u32[]{:S(2)}, u32[]{:S(2)}) %collective-permute-start.20) | collective-permute-done | bytes 40992 | tf_op jit(solution)/shard_map/ppermute | solution.py:364
  53.8 2.5 %collective-permute-start.21 = (f32[32,128]{1,0:T(8,128)S(1)}, f32[32,128]{1,0:T(8,128)S(1)}, u32[]{:S(2)}, u32[]{:S(2)}) collective-permute-start(f32[32,128]{1,0:T(8,128)S(1)} %get-tuple-element.77), channel_id=1, source_target_pairs={{0,6},{1,7},{2,4},{3,5},{4,2},{5,3},{6,0},{7,1},{8,14},{9,15},{10,... | collective-permute-start | bytes 49160 | tf_op jit(solution)/shard_map/ppermute | solution.py:364
  56.3 0.4 collective-permute-start.22
  56.7 0.6 %collective-permute-start.23 = (f32[32,128]{1,0:T(8,128)S(1)}, f32[32,128]{1,0:T(8,128)S(1)}, u32[]{:S(2)}, u32[]{:S(2)}) collective-permute-start(f32[32,128]{1,0:T(8,128)S(1)} %get-tuple-element.79), channel_id=1, source_target_pairs={{0,2},{1,3},{2,0},{3,1},{4,6},{5,7},{6,4},{7,5},{8,10},{9,11},{10,... | collective-permute-start | bytes 49160 | tf_op jit(solution)/shard_map/ppermute | solution.py:364
  57.3 0.6 %copy.35 = f32[16384]{0:T(1024)} copy(f32[16384]{0:T(1024)S(1)} %bitcast.19) | data formatting | bytes 131072
  58.0 0.5 collective-permute-done.21.refs_1_
  58.5 1.6 %collective-permute-done.22.refs_2_ = f32[32,128]{1,0:T(8,128)S(1)} collective-permute-done((f32[32,128]{1,0:T(8,128)S(1)}, f32[32,128]{1,0:T(8,128)S(1)}, u32[]{:S(2)}, u32[]{:S(2)}) %collective-permute-start.22) | collective-permute-done | bytes 16416 | tf_op jit(solution)/shard_map/ppermute | solution.py:364
  60.1 0.4 collective-permute-done.23.refs_3_
  60.4 0.7 %last.1 = (f32[16,128]{1,0:T(8,128)}, f32[2]{0:T(128)}) custom-call(f32[2]{0:T(128)S(4)} %get-tuple-element.47.refs_3_.refs_0_, f32[32,128]{1,0:T(8,128)S(1)} %collective-permute-done.21.refs_1_, f32[32,128]{1,0:T(8,128)S(1)} %collective-permute-done.22.refs_2_, f32[32,128]{1,0:T(8,128)S(1)} %collective-permute-done.23.refs_3_, ...), custom_call_target="tpu_custom_call" | custom-call | tf_op jit(solution)/shard_map/last/pallas_call | solution.py:349
  (15 shorter events, 0.1 us)
Async XLA Ops:
  0.6 9.2 %copy-start.3 = (f32[3,16384]{1,0:T(4,128)S(1)}, f32[3,16384]{1,0:T(4,128)}, u32[]{:S(2)}) copy-start(f32[3,16384]{1,0:T(4,128)} %param.19) | copy-start | bytes 589828
  4.1 8.0 %collective-permute-start.2 = (s16[144,128]{1,0:T(8,128)(2,1)S(1)}, s16[144,128]{1,0:T(8,128)(2,1)S(1)}, u32[]{:S(2)}, u32[]{:S(2)}) collective-permute-start(s16[144,128]{1,0:T(8,128)(2,1)S(1)} %get-tuple-element.51.refs_6_), channel_id=1, source_target_pairs={{0,24},{8,16},{16,8},{24,0},{1,25},{9,17},{17,9},{25,1},{2,26},{10... | collective-permute-start | bytes 110600 | tf_op jit(solution)/shard_map/ppermute | solution.py:364
  9.2 4.9 %collective-permute-start.1 = (s16[144,128]{1,0:T(8,128)(2,1)S(1)}, s16[144,128]{1,0:T(8,128)(2,1)S(1)}, u32[]{:S(2)}, u32[]{:S(2)}) collective-permute-start(s16[144,128]{1,0:T(8,128)(2,1)S(1)} %get-tuple-element.51.refs_6_), channel_id=1, source_target_pairs={{0,16},{8,24},{16,0},{24,8},{1,17},{9,25},{17,1},{25,9},{2,18},{10... | collective-permute-start | bytes 110600 | tf_op jit(solution)/shard_map/ppermute | solution.py:364
  9.2 4.9 %collective-permute-start = (s16[144,128]{1,0:T(8,128)(2,1)S(1)}, s16[144,128]{1,0:T(8,128)(2,1)S(1)}, u32[]{:S(2)}, u32[]{:S(2)}) collective-permute-start(s16[144,128]{1,0:T(8,128)(2,1)S(1)} %get-tuple-element.51.refs_6_), channel_id=1, source_target_pairs={{0,8},{8,0},{16,24},{24,16},{1,9},{9,1},{17,25},{25,17},{2,10},{10... | collective-permute-start | bytes 110600 | tf_op jit(solution)/shard_map/ppermute | solution.py:364
  9.8 4.2 %copy-start.1 = (s32[3,16384]{1,0:T(4,128)S(1)}, s32[3,16384]{1,0:T(4,128)}, u32[]{:S(2)}) copy-start(s32[3,16384]{1,0:T(4,128)} %param.20) | copy-start | bytes 589828
  9.8 4.2 %copy-start.4 = (f32[16384]{0:T(1024)S(1)}, f32[16384]{0:T(1024)}, u32[]{:S(2)}) copy-start(f32[16384]{0:T(1024)} %param.26) | copy-start | bytes 196612
  10.9 12.3 %copy-start = (s32[3,16384]{1,0:T(4,128)S(1)}, s32[3,16384]{1,0:T(4,128)}, u32[]{:S(2)}) copy-start(s32[3,16384]{1,0:T(4,128)} %param.21) | copy-start | bytes 589828
  14.9 1.3 %collective-permute-start.3 = (f32[128,128]{1,0:T(8,128)S(1)}, f32[128,128]{1,0:T(8,128)S(1)}, u32[]{:S(2)}, u32[]{:S(2)}) collective-permute-start(f32[128,128]{1,0:T(8,128)S(1)} %get-tuple-element.54.refs_0_), channel_id=1, source_target_pairs={{0,1},{1,0},{2,3},{3,2},{4,5},{5,4},{6,7},{7,6},{8,9},{9,8},{10,11... | collective-permute-start | bytes 196616 | tf_op jit(solution)/shard_map/ppermute | solution.py:364
  14.9 13.6 %collective-permute-start.10 = (s16[400,128]{1,0:T(8,128)(2,1)S(1)}, s16[400,128]{1,0:T(8,128)(2,1)S(1)}, u32[]{:S(2)}, u32[]{:S(2)}) collective-permute-start(s16[400,128]{1,0:T(8,128)(2,1)S(1)} %get-tuple-element.61.refs_0_), channel_id=1, source_target_pairs={{0,8},{8,0},{16,24},{24,16},{1,9},{9,1},{17,25},{25,17},{2,10},{10... | collective-permute-start | bytes 307208 | tf_op jit(solution)/shard_map/ppermute | solution.py:364
  16.2 4.9 %collective-permute-start.6 = (s16[144,128]{1,0:T(8,128)(2,1)S(1)}, s16[144,128]{1,0:T(8,128)(2,1)S(1)}, u32[]{:S(2)}, u32[]{:S(2)}) collective-permute-start(s16[144,128]{1,0:T(8,128)(2,1)S(1)} %pair_2.1.refs_6_), channel_id=1, source_target_pairs={{0,6},{1,7},{2,4},{3,5},{4,2},{5,3},{6,0},{7,1},{8,14},{9,15},{10,... | collective-permute-start | bytes 110600 | tf_op jit(solution)/shard_map/ppermute | solution.py:364
  18.7 4.0 %collective-permute-start.5 = (s16[144,128]{1,0:T(8,128)(2,1)S(1)}, s16[144,128]{1,0:T(8,128)(2,1)S(1)}, u32[]{:S(2)}, u32[]{:S(2)}) collective-permute-start(s16[144,128]{1,0:T(8,128)(2,1)S(1)} %pair_2.1.refs_6_), channel_id=1, source_target_pairs={{0,4},{1,5},{2,6},{3,7},{4,0},{5,1},{6,2},{7,3},{8,12},{9,13},{10,... | collective-permute-start | bytes 110600 | tf_op jit(solution)/shard_map/ppermute | solution.py:364
  19.2 4.0 %collective-permute-start.4 = (s16[144,128]{1,0:T(8,128)(2,1)S(1)}, s16[144,128]{1,0:T(8,128)(2,1)S(1)}, u32[]{:S(2)}, u32[]{:S(2)}) collective-permute-start(s16[144,128]{1,0:T(8,128)(2,1)S(1)} %pair_2.1.refs_6_), channel_id=1, source_target_pairs={{0,2},{1,3},{2,0},{3,1},{4,6},{5,7},{6,4},{7,5},{8,10},{9,11},{10,... | collective-permute-start | bytes 110600 | tf_op jit(solution)/shard_map/ppermute | solution.py:364
  23.2 18.6 %copy-start.2 = (f32[3,16384]{1,0:T(4,128)S(1)}, f32[3,16384]{1,0:T(4,128)}, u32[]{:S(2)}) copy-start(f32[3,16384]{1,0:T(4,128)} %param.18) | copy-start | bytes 589828
  23.2 18.6 %copy-start.5 = (f32[16384]{0:T(1024)S(1)}, f32[16384]{0:T(1024)}, u32[]{:S(2)}) copy-start(f32[16384]{0:T(1024)} %param.22) | copy-start | bytes 196612
  23.2 18.6 %copy-start.6 = (f32[16384]{0:T(1024)S(1)}, f32[16384]{0:T(1024)}, u32[]{:S(2)}) copy-start(f32[16384]{0:T(1024)} %param.24) | copy-start | bytes 196612
  24.1 6.8 %collective-permute-start.9 = (s16[144,128]{1,0:T(8,128)(2,1)S(1)}, s16[144,128]{1,0:T(8,128)(2,1)S(1)}, u32[]{:S(2)}, u32[]{:S(2)}) collective-permute-start(s16[144,128]{1,0:T(8,128)(2,1)S(1)} %get-tuple-element.57.refs_6_), channel_id=1, source_target_pairs={{0,24},{8,16},{16,8},{24,0},{1,25},{9,17},{17,9},{25,1},{2,26},{10... | collective-permute-start | bytes 110600 | tf_op jit(solution)/shard_map/ppermute | solution.py:364
  26.4 9.7 %collective-permute-start.8 = (s16[144,128]{1,0:T(8,128)(2,1)S(1)}, s16[144,128]{1,0:T(8,128)(2,1)S(1)}, u32[]{:S(2)}, u32[]{:S(2)}) collective-permute-start(s16[144,128]{1,0:T(8,128)(2,1)S(1)} %get-tuple-element.57.refs_6_), channel_id=1, source_target_pairs={{0,16},{8,24},{16,0},{24,8},{1,17},{9,25},{17,1},{25,9},{2,18},{10... | collective-permute-start | bytes 110600 | tf_op jit(solution)/shard_map/ppermute | solution.py:364
  26.4 9.6 %collective-permute-start.7 = (s16[144,128]{1,0:T(8,128)(2,1)S(1)}, s16[144,128]{1,0:T(8,128)(2,1)S(1)}, u32[]{:S(2)}, u32[]{:S(2)}) collective-permute-start(s16[144,128]{1,0:T(8,128)(2,1)S(1)} %get-tuple-element.57.refs_6_), channel_id=1, source_target_pairs={{0,8},{8,0},{16,24},{24,16},{1,9},{9,1},{17,25},{25,17},{2,10},{10... | collective-permute-start | bytes 110600 | tf_op jit(solution)/shard_map/ppermute | solution.py:364
  28.5 13.3 %collective-permute-start.12 = (s16[400,128]{1,0:T(8,128)(2,1)S(1)}, s16[400,128]{1,0:T(8,128)(2,1)S(1)}, u32[]{:S(2)}, u32[]{:S(2)}) collective-permute-start(s16[400,128]{1,0:T(8,128)(2,1)S(1)} %after_2.1.refs_5_), channel_id=1, source_target_pairs={{0,24},{8,16},{16,8},{24,0},{1,25},{9,17},{17,9},{25,1},{2,26},{10... | collective-permute-start | bytes 307208 | tf_op jit(solution)/shard_map/ppermute | solution.py:364
  30.8 11.0 %collective-permute-start.11 = (s16[400,128]{1,0:T(8,128)(2,1)S(1)}, s16[400,128]{1,0:T(8,128)(2,1)S(1)}, u32[]{:S(2)}, u32[]{:S(2)}) collective-permute-start(s16[400,128]{1,0:T(8,128)(2,1)S(1)} %after_2.1.refs_5_), channel_id=1, source_target_pairs={{0,16},{8,24},{16,0},{24,8},{1,17},{9,25},{17,1},{25,9},{2,18},{10... | collective-permute-start | bytes 307208 | tf_op jit(solution)/shard_map/ppermute | solution.py:364
  36.1 8.3 %copy-start.7 = (f32[16384]{0:T(1024)S(1)}, f32[16384]{0:T(1024)}, u32[]{:S(2)}) copy-start(f32[16384]{0:T(1024)} %param.23) | copy-start | bytes 196612
  36.9 1.3 %collective-permute-start.13 = (f32[128,128]{1,0:T(8,128)S(1)}, f32[128,128]{1,0:T(8,128)S(1)}, u32[]{:S(2)}, u32[]{:S(2)}) collective-permute-start(f32[128,128]{1,0:T(8,128)S(1)} %get-tuple-element.64.refs_0_), channel_id=1, source_target_pairs={{0,1},{1,0},{2,3},{3,2},{4,5},{5,4},{6,7},{7,6},{8,9},{9,8},{10,11... | collective-permute-start | bytes 196616 | tf_op jit(solution)/shard_map/ppermute | solution.py:364
  38.2 5.0 %collective-permute-start.16 = (s16[144,128]{1,0:T(8,128)(2,1)S(1)}, s16[144,128]{1,0:T(8,128)(2,1)S(1)}, u32[]{:S(2)}, u32[]{:S(2)}) collective-permute-start(s16[144,128]{1,0:T(8,128)(2,1)S(1)} %pair_1.1.refs_6_), channel_id=1, source_target_pairs={{0,6},{1,7},{2,4},{3,5},{4,2},{5,3},{6,0},{7,1},{8,14},{9,15},{10,... | collective-permute-start | bytes 110600 | tf_op jit(solution)/shard_map/ppermute | solution.py:364
  40.0 4.0 %collective-permute-start.15 = (s16[144,128]{1,0:T(8,128)(2,1)S(1)}, s16[144,128]{1,0:T(8,128)(2,1)S(1)}, u32[]{:S(2)}, u32[]{:S(2)}) collective-permute-start(s16[144,128]{1,0:T(8,128)(2,1)S(1)} %pair_1.1.refs_6_), channel_id=1, source_target_pairs={{0,4},{1,5},{2,6},{3,7},{4,0},{5,1},{6,2},{7,3},{8,12},{9,13},{10,... | collective-permute-start | bytes 110600 | tf_op jit(solution)/shard_map/ppermute | solution.py:364
  40.4 4.0 %collective-permute-start.14 = (s16[144,128]{1,0:T(8,128)(2,1)S(1)}, s16[144,128]{1,0:T(8,128)(2,1)S(1)}, u32[]{:S(2)}, u32[]{:S(2)}) collective-permute-start(s16[144,128]{1,0:T(8,128)(2,1)S(1)} %pair_1.1.refs_6_), channel_id=1, source_target_pairs={{0,2},{1,3},{2,0},{3,1},{4,6},{5,7},{6,4},{7,5},{8,10},{9,11},{10,... | collective-permute-start | bytes 110600 | tf_op jit(solution)/shard_map/ppermute | solution.py:364
  45.2 5.9 %collective-permute-start.19 = (s16[160,128]{1,0:T(8,128)(2,1)S(1)}, s16[160,128]{1,0:T(8,128)(2,1)S(1)}, u32[]{:S(2)}, u32[]{:S(2)}) collective-permute-start(s16[160,128]{1,0:T(8,128)(2,1)S(1)} %get-tuple-element.68.refs_6_), channel_id=1, source_target_pairs={{0,24},{8,16},{16,8},{24,0},{1,25},{9,17},{17,9},{25,1},{2,26},{10... | collective-permute-start | bytes 122888 | tf_op jit(solution)/shard_map/ppermute | solution.py:364
  45.3 5.8 %collective-permute-start.18 = (s16[160,128]{1,0:T(8,128)(2,1)S(1)}, s16[160,128]{1,0:T(8,128)(2,1)S(1)}, u32[]{:S(2)}, u32[]{:S(2)}) collective-permute-start(s16[160,128]{1,0:T(8,128)(2,1)S(1)} %get-tuple-element.68.refs_6_), channel_id=1, source_target_pairs={{0,16},{8,24},{16,0},{24,8},{1,17},{9,25},{17,1},{25,9},{2,18},{10... | collective-permute-start | bytes 122888 | tf_op jit(solution)/shard_map/ppermute | solution.py:364
  45.4 6.3 %collective-permute-start.17 = (s16[160,128]{1,0:T(8,128)(2,1)S(1)}, s16[160,128]{1,0:T(8,128)(2,1)S(1)}, u32[]{:S(2)}, u32[]{:S(2)}) collective-permute-start(s16[160,128]{1,0:T(8,128)(2,1)S(1)} %get-tuple-element.68.refs_6_), channel_id=1, source_target_pairs={{0,8},{8,0},{16,24},{24,16},{1,9},{9,1},{17,25},{25,17},{2,10},{10... | collective-permute-start | bytes 122888 | tf_op jit(solution)/shard_map/ppermute | solution.py:364
  52.5 1.3 %collective-permute-start.20 = (f32[80,128]{1,0:T(8,128)S(1)}, f32[80,128]{1,0:T(8,128)S(1)}, u32[]{:S(2)}, u32[]{:S(2)}) collective-permute-start(f32[80,128]{1,0:T(8,128)S(1)} %get-tuple-element.76), channel_id=1, source_target_pairs={{0,1},{1,0},{2,3},{3,2},{4,5},{5,4},{6,7},{7,6},{8,9},{9,8},{10,11... | collective-permute-start | bytes 122888 | tf_op jit(solution)/shard_map/ppermute | solution.py:364
  53.8 4.7 %collective-permute-start.21 = (f32[32,128]{1,0:T(8,128)S(1)}, f32[32,128]{1,0:T(8,128)S(1)}, u32[]{:S(2)}, u32[]{:S(2)}) collective-permute-start(f32[32,128]{1,0:T(8,128)S(1)} %get-tuple-element.77), channel_id=1, source_target_pairs={{0,6},{1,7},{2,4},{3,5},{4,2},{5,3},{6,0},{7,1},{8,14},{9,15},{10,... | collective-permute-start | bytes 49160 | tf_op jit(solution)/shard_map/ppermute | solution.py:364
  56.3 3.7 %collective-permute-start.22 = (f32[32,128]{1,0:T(8,128)S(1)}, f32[32,128]{1,0:T(8,128)S(1)}, u32[]{:S(2)}, u32[]{:S(2)}) collective-permute-start(f32[32,128]{1,0:T(8,128)S(1)} %get-tuple-element.78), channel_id=1, source_target_pairs={{0,4},{1,5},{2,6},{3,7},{4,0},{5,1},{6,2},{7,3},{8,12},{9,13},{10,... | collective-permute-start | bytes 49160 | tf_op jit(solution)/shard_map/ppermute | solution.py:364
  56.7 3.7 %collective-permute-start.23 = (f32[32,128]{1,0:T(8,128)S(1)}, f32[32,128]{1,0:T(8,128)S(1)}, u32[]{:S(2)}, u32[]{:S(2)}) collective-permute-start(f32[32,128]{1,0:T(8,128)S(1)} %get-tuple-element.79), channel_id=1, source_target_pairs={{0,2},{1,3},{2,0},{3,1},{4,6},{5,7},{6,4},{7,5},{8,10},{9,11},{10,... | collective-permute-start | bytes 49160 | tf_op jit(solution)/shard_map/ppermute | solution.py:364
